TPU v7x, 32 devices: a whole 2x2x4 slice. The times are simulated.
32 devices in a mesh: stn: 8 (over z, core), seg: 4 (over y, x).
Axes of the slice: x: 2, y: 2, z: 4, core: 2. Of those that a mesh axis runs over, the one named last changes fastest.
Arguments:
- traces: float32 [1024, 19200], P(('stn', 'seg')), may hold values from -6 to 6
- fir_taps: float32 [31], replicated, may hold values from -0.9 to 0.9
- seg_flags: int32 [1024, 32], P(('stn', 'seg')), may hold values 0 or 1
- pair_mask: int32 [1024, 1024], P('stn', 'seg'), may hold values 0 or 1
Outputs:
- stacked: float32 [41, 1024, 1024], P(None, 'stn', 'seg')
All inputs are finite; a program needn't handle non-finite values. No bound on the sum of `seg_flags` or of `pair_mask` on one device may be relied on, other than what follows from the above.
Results may differ from a plain program's by a relative error of at most 0.0095.
Values may be sent and summed in bfloat16 or wider, within the bound.
No kernel may reach another device: no remote copies, remote signals or barrier semaphores. Data moves between devices by JAX's collectives and lax.ppermute only.
A program may use at most 192 MiB of HBM per device.

v0:
```python
import math

import jax
import jax.numpy as jnp
from jax import lax
from jax.sharding import PartitionSpec as P

SAMP = 600
LAGS = 41
TAPS = 31
RADIUS = 64


epsilon = 1e-06
lag_group = 8


def preprocess(traces, fir_taps, seg_flags):
    station_count = traces.shape[0]
    record_len = traces.shape[1]
    half_taps = (TAPS - 1) // 2
    padded = jnp.pad(traces, ((0, 0), (half_taps, half_taps)))
    filtered = jnp.zeros_like(traces)
    for tap_index in range(TAPS):
        filtered = filtered + fir_taps[tap_index] * padded[:, tap_index : tap_index + record_len]
    width = 2 * RADIUS + 1
    magnitude = jnp.pad(jnp.abs(filtered), ((0, 0), (RADIUS + 1, RADIUS)))
    running = jnp.cumsum(magnitude, axis=1)
    running_level = (running[:, width:] - running[:, :record_len]) / width
    whitened = filtered / (running_level + epsilon)
    flagged = whitened.reshape(station_count, -1, SAMP) * seg_flags[:, :, None].astype(jnp.float32)
    return flagged.astype(jnp.bfloat16)


def correlate(left_rows, right_rows):
    half_lag = (LAGS - 1) // 2
    row_count = left_rows.shape[0]
    right_flat = right_rows.reshape(right_rows.shape[0], -1)
    left_padded = jnp.pad(left_rows, ((0, 0), (0, 0), (half_lag, half_lag)))
    results = []
    for first_lag in range(0, LAGS, lag_group):
        lag_list = list(range(first_lag, min(first_lag + lag_group, LAGS)))
        shifted = jnp.stack(
            [
                left_padded[:, :, LAGS - 1 - lag_index : LAGS - 1 - lag_index + SAMP]
                for lag_index in lag_list
            ],
            axis=0,
        )
        shifted = shifted.reshape(len(lag_list) * row_count, -1)
        product = lax.dot_general(
            shifted, right_flat, (((1,), (1,)), ((), ())), preferred_element_type=jnp.float32
        )
        results.append(product.reshape(len(lag_list), row_count, right_flat.shape[0]))
    return jnp.concatenate(results, axis=0)


def body(traces, fir_taps, seg_flags, pair_mask):
    seg_count = lax.axis_size("seg")
    total_segments = seg_flags.shape[1]
    seg_dev = total_segments // seg_count
    norm_scale = 1.0 / math.sqrt(SAMP * total_segments)
    whitened = preprocess(traces, fir_taps, seg_flags)
    flat_rows = whitened.reshape(whitened.shape[0], total_segments * SAMP)
    mask_float = pair_mask.astype(jnp.float32)[None]
    regrouped = lax.all_to_all(flat_rows, "seg", split_axis=1, concat_axis=0, tiled=True)
    block_size = regrouped.shape[0]
    own_block = regrouped.reshape(block_size, seg_dev, SAMP)
    shard_piece = lax.all_gather(regrouped, "stn", axis=0, tiled=True)
    partial_value = correlate(own_block, shard_piece.reshape(shard_piece.shape[0], seg_dev, SAMP))
    stacked = lax.psum_scatter(
        (partial_value * norm_scale).astype(jnp.bfloat16), "seg", scatter_dimension=2, tiled=True
    ).astype(jnp.float32)
    return stacked * mask_float


def solution(mesh):
    return jax.shard_map(
        body,
        mesh=mesh,
        in_specs=(P(("stn", "seg"), None), P(), P(("stn", "seg"), None), P("stn", "seg")),
        out_specs=P(None, "stn", "seg"),
        check_vma=False,
    )
```

profile of v0, /device:TPU:0, one launch (start us, length us, event | category | flops | bytes accessed | tf_op | source)
XLA Modules:
  0.0 505.5 jit_solution(18046086597664292925)
XLA Ops:
  6.5 1.8 fusion.50
  8.3 2.1 fusion.49
  11.4 2.4 mul.274
  13.8 61.6 %fusion.48 = (f32[32,19200]{1,0:T(8,128)S(1)}, f32[32,19200]{1,0:T(8,128)}) fusion(f32[]{:T(128)} %bitcast.30, f32[]{:T(128)} %bitcast.29, f32[]{:T(128)} %bitcast.28, f32[]{:T(128)} %bitcast.27, f32[]{:T(128)} %bitcast.26, f32[]{:T(128)} %bitcast.25, f32[]{:T(128)} %bitcast.24, f32[]{:T(128)} %bitcast.23, f32[]{:T(128)} %bitcast.22, f32[]{:T(128)} %bitcast.21, ...), kind=kLoop, calls=%fused_computation.142 | loop fusion | flops 38092800 | bytes 7372924 | tf_op jit(solution)/shard_map/abs | solution.py:27
  76.6 3.3 copy.54
  79.9 2.5 fusion.51
  82.4 2.0 copy-done.1
  85.4 5.0 broadcast_add_fusion
  90.4 3.6 copy.57
  98.8 21.8 %all_to_all.19 = bf16[32,4,4800]{2,0,1:T(8,128)(2,1)S(1)} all-to-all(bf16[32,4,4800]{2,0,1:T(8,128)(2,1)S(1)} %copy.58), channel_id=1, replica_groups=mesh['stn'=8,'seg'=4] {'seg'}, dimensions={1} | all-to-all | bytes 2457600 | tf_op jit(solution)/shard_map/all_to_all | solution.py:66
  122.4 3.4 pad_slice_fusion.14
  125.8 6.6 %pad_slice_fusion.10 = (bf16[128,8,600]{2,1,0:T(8,128)(2,1)}, bf16[128,8,600]{2,1,0:T(8,128)(2,1)}, bf16[128,8,600]{2,1,0:T(8,128)(2,1)}, bf16[128,8,600]{2,1,0:...) fusion(bf16[128,8,600]{2,1,0:T(8,128)(2,1)S(1)} %reshape.141), kind=kLoop, calls=%fused_computation.102 | loop fusion | bytes 12288000 | tf_op jit(solution)/shard_map/slice | solution.py:45
  132.4 6.6 %pad_slice_fusion.11 = (bf16[128,8,600]{2,1,0:T(8,128)(2,1)}, bf16[128,8,600]{2,1,0:T(8,128)(2,1)}, bf16[128,8,600]{2,1,0:T(8,128)(2,1)}, bf16[128,8,600]{2,1,0:...) fusion(bf16[128,8,600]{2,1,0:T(8,128)(2,1)S(1)} %reshape.141), kind=kLoop, calls=%fused_computation.103 | loop fusion | bytes 12288000 | tf_op jit(solution)/shard_map/slice | solution.py:45
  139.0 6.6 %pad_slice_fusion.12 = (bf16[128,8,600]{2,1,0:T(8,128)(2,1)}, bf16[128,8,600]{2,1,0:T(8,128)(2,1)}, bf16[128,8,600]{2,1,0:T(8,128)(2,1)}, bf16[128,8,600]{2,1,0:...) fusion(bf16[128,8,600]{2,1,0:T(8,128)(2,1)S(1)} %reshape.141), kind=kLoop, calls=%fused_computation.104 | loop fusion | bytes 12288000 | tf_op jit(solution)/shard_map/slice | solution.py:45
  145.6 6.4 %pad_slice_fusion.13 = (bf16[128,8,600]{2,1,0:T(8,128)(2,1)}, bf16[128,8,600]{2,1,0:T(8,128)(2,1)}, bf16[128,8,600]{2,1,0:T(8,128)(2,1)}, bf16[128,8,600]{2,1,0:...) fusion(bf16[128,8,600]{2,1,0:T(8,128)(2,1)S(1)} %reshape.141), kind=kLoop, calls=%fused_computation.105 | loop fusion | bytes 12288000 | tf_op jit(solution)/shard_map/slice | solution.py:45
  152.0 2.9 copy.59
  154.9 2.4 constant_dynamic-update-slice_fusion.7
  157.3 1.8 copy.60
  159.1 2.9 copy.61
  161.9 2.7 copy.62
  164.7 2.0 copy.63
  166.7 2.9 copy.64
  169.5 2.7 copy.65
  175.5 1.8 copy.68
  177.3 2.5 constant_dynamic-update-slice_fusion.15
  179.8 2.8 copy.69
  182.6 1.8 copy.70
  184.4 2.9 copy.71
  187.3 2.7 copy.72
  190.1 1.8 copy.73
  191.9 2.8 copy.74
  194.7 2.7 copy.75
  199.2 2.5 constant_dynamic-update-slice_fusion.23
  201.7 2.7 copy.77
  204.4 1.8 copy.78
  206.2 2.8 copy.79
  210.5 1.8 copy.80
  212.3 2.8 copy.81
  215.1 1.8 copy.82
  218.7 2.5 constant_dynamic-update-slice_fusion.31
  221.2 1.8 copy.85
  224.8 2.8 copy.87
  227.6 1.8 copy.88
  229.4 2.0 copy.89
  231.4 2.8 copy.90
  234.3 1.8 copy.91
  236.1 1.8 copy.92
  237.9 2.4 constant_dynamic-update-slice_fusion.39
  240.3 1.8 copy.93
  242.1 2.9 copy.94
  245.0 2.9 copy.95
  249.6 1.8 copy.97
  251.4 2.8 copy.98
  254.2 2.7 copy.99
  258.3 2.6 constant_dynamic-update-slice_fusion.6
  299.5 17.9 %fusion.10 = f32[41,128,1024]{2,1,0:T(8,128)} fusion(bf16[8,128,4800]{1,2,0:T(8,128)(2,1)} %constant_dynamic-update-slice_fusion, bf16[1024,4800]{0,1:T(8,128)(2,1)} %all-gather.2.cloned.1.call-done), kind=kOutput, calls=%fused_computation.12 | convolution fusion | flops 10066329600 | bytes 23855104 | tf_op jit(solution)/shard_map/dot_general | solution.py:51
  317.3 14.5 %fusion.13 = f32[41,128,1024]{2,1,0:T(8,128)} fusion(f32[41,128,1024]{2,1,0:T(8,128)} %fusion.10, bf16[8,128,4800]{1,2,0:T(8,128)(2,1)} %constant_dynamic-update-slice_fusion.8, bf16[1024,4800]{0,1:T(8,128)(2,1)S(1)} %copy-done), kind=kOutput, calls=%fused_computation.13 | convolution fusion | flops 10066329600 | bytes 23855104 | tf_op jit(solution)/shard_map/dot_general | solution.py:51
  331.8 14.7 %fusion.16 = f32[41,128,1024]{2,1,0:T(8,128)} fusion(f32[41,128,1024]{2,1,0:T(8,128)} %fusion.13, bf16[8,128,4800]{1,2,0:T(8,128)(2,1)} %constant_dynamic-update-slice_fusion.16, bf16[1024,4800]{0,1:T(8,128)(2,1)S(1)} %copy-done), kind=kOutput, calls=%fused_computation.14 | convolution fusion | flops 10066329600 | bytes 23855104 | tf_op jit(solution)/shard_map/dot_general | solution.py:51
  346.5 14.6 %fusion.19 = f32[41,128,1024]{2,1,0:T(8,128)} fusion(f32[41,128,1024]{2,1,0:T(8,128)} %fusion.16, bf16[8,128,4800]{1,2,0:T(8,128)(2,1)} %constant_dynamic-update-slice_fusion.24, bf16[1024,4800]{0,1:T(8,128)(2,1)S(1)} %copy-done), kind=kOutput, calls=%fused_computation.15 | convolution fusion | flops 10066329600 | bytes 23855104 | tf_op jit(solution)/shard_map/dot_general | solution.py:51
  361.1 12.1 %fusion.22 = f32[41,128,1024]{2,1,0:T(8,128)} fusion(f32[41,128,1024]{2,1,0:T(8,128)} %fusion.19, bf16[8,128,4800]{1,2,0:T(8,128)(2,1)S(1)} %bitcast.176, bf16[1024,4800]{0,1:T(8,128)(2,1)S(1)} %copy-done), kind=kOutput, calls=%fused_computation.16 | convolution fusion | flops 10066329600 | bytes 23855104 | tf_op jit(solution)/shard_map/dot_general | solution.py:51
  373.2 2.3 fusion.47
  375.6 12.5 %multiply_convert_fusion = bf16[41,128,1024]{2,1,0:T(8,128)(2,1)} fusion(f32[41,128,1024]{2,1,0:T(8,128)} %fusion.47), kind=kLoop, calls=%fused_computation | loop fusion | flops 10747904 | bytes 32243712 | tf_op jit(solution)/shard_map/convert_element_type | solution.py:72
  389.0 104.6 %reduce-scatter.2.cloned.1.call-done = bf16[41,128,256]{2,1,0:T(8,128)(2,1)} async-done(((bf16[41,128,1024]{2,1,0:T(8,128)(2,1)}), bf16[41,128,256]{2,1,0:T(8,128)(2,1)}) %reduce-scatter.2.cloned.1.call-update) | async-done | bytes 2686992 | tf_op jit(solution)/shard_map/reduce_scatter | solution.py:71
  493.7 4.8 convert_multiply_fusion
  (191 shorter events, 62.1 us)
Async XLA Ops:
  6.5 292.9 %all-gather.2.cloned.1.call-start = ((), (), s32[]{:S(2)}) async-start(), calls=%async_computation.2 | async-start | bytes 11059200 | tf_op jit(solution)/shard_map/all_gather | solution.py:69
  82.4 2.0 copy-start.1
  94.1 1.7 copy-start.2
  94.1 2.4 copy-start.3
  152.0 5.3 %copy-start.23 = (bf16[128,8,600]{2,1,0:T(8,128)(2,1)S(1)}, bf16[128,8,600]{2,1,0:T(8,128)(2,1)}, u32[]{:S(2)}) copy-start(bf16[128,8,600]{2,1,0:T(8,128)(2,1)} %get-tuple-element.8) | copy-start | bytes 3686404
  159.1 5.6 %copy-start.22 = (bf16[128,8,600]{2,1,0:T(8,128)(2,1)S(1)}, bf16[128,8,600]{2,1,0:T(8,128)(2,1)}, u32[]{:S(2)}) copy-start(bf16[128,8,600]{2,1,0:T(8,128)(2,1)} %get-tuple-element.11) | copy-start | bytes 3686404
  166.7 5.6 %copy-start.21 = (bf16[128,8,600]{2,1,0:T(8,128)(2,1)S(1)}, bf16[128,8,600]{2,1,0:T(8,128)(2,1)}, u32[]{:S(2)}) copy-start(bf16[128,8,600]{2,1,0:T(8,128)(2,1)} %get-tuple-element.14) | copy-start | bytes 3686404
  174.0 1.5 copy-start.20
  175.5 318.2 %reduce-scatter.2.cloned.1.call-start = ((), (), s32[]{:S(2)}) async-start(), calls=%async_computation.3 | async-start | bytes 13434880 | tf_op jit(solution)/shard_map/reduce_scatter | solution.py:71
  177.3 5.2 %copy-start.19 = (bf16[128,8,600]{2,1,0:T(8,128)(2,1)S(1)}, bf16[128,8,600]{2,1,0:T(8,128)(2,1)}, u32[]{:S(2)}) copy-start(bf16[128,8,600]{2,1,0:T(8,128)(2,1)} %get-tuple-element.18) | copy-start | bytes 3686404
  184.4 5.7 %copy-start.18 = (bf16[128,8,600]{2,1,0:T(8,128)(2,1)S(1)}, bf16[128,8,600]{2,1,0:T(8,128)(2,1)}, u32[]{:S(2)}) copy-start(bf16[128,8,600]{2,1,0:T(8,128)(2,1)} %get-tuple-element.21) | copy-start | bytes 3686404
  191.9 5.5 %copy-start.17 = (bf16[128,8,600]{2,1,0:T(8,128)(2,1)S(1)}, bf16[128,8,600]{2,1,0:T(8,128)(2,1)}, u32[]{:S(2)}) copy-start(bf16[128,8,600]{2,1,0:T(8,128)(2,1)} %get-tuple-element.24) | copy-start | bytes 3686404
  199.2 5.2 %copy-start.16 = (bf16[128,8,600]{2,1,0:T(8,128)(2,1)S(1)}, bf16[128,8,600]{2,1,0:T(8,128)(2,1)}, u32[]{:S(2)}) copy-start(bf16[128,8,600]{2,1,0:T(8,128)(2,1)} %get-tuple-element.27) | copy-start | bytes 3686404
  206.2 4.3 copy-start.15
  210.4 4.7 copy-start.14
  212.3 4.6 copy-start.13
  216.9 4.3 copy-start.11
  218.7 4.3 copy-start.12
  223.0 4.6 copy-start.10
  224.8 4.6 copy-start.9
  229.4 4.9 copy-start.8
  231.4 4.6 copy-start.7
  236.1 4.2 copy-start.6
  242.1 5.7 %copy-start.24 = (bf16[128,8,600]{2,1,0:T(8,128)(2,1)S(1)}, bf16[128,8,600]{2,1,0:T(8,128)(2,1)}, u32[]{:S(2)}) copy-start(bf16[128,8,600]{2,1,0:T(8,128)(2,1)} %get-tuple-element.43) | copy-start | bytes 3686404
  245.0 4.6 copy-start.5
  251.4 5.6 %copy-start.4 = (bf16[128,8,600]{2,1,0:T(8,128)(2,1)S(1)}, bf16[128,8,600]{2,1,0:T(8,128)(2,1)}, u32[]{:S(2)}) copy-start(bf16[128,8,600]{2,1,0:T(8,128)(2,1)} %get-tuple-element.7) | copy-start | bytes 3686404
  258.3 2.6 copy-start.40
  258.3 3.7 copy-start.36
  260.9 2.3 copy-start.29
  262.0 2.3 copy-start.27
  263.2 2.3 copy-start.26
  264.3 2.3 copy-start.25
  265.4 2.3 copy-start.57
  266.6 2.3 copy-start.58
  267.8 2.3 copy-start.56
  268.9 2.3 copy-start.55
  270.0 2.2 copy-start.52
  271.2 2.2 copy-start.50
  272.3 2.3 copy-start.48
  273.4 2.3 copy-start.53
  274.6 2.3 copy-start.54
  275.7 2.3 copy-start.51
  276.9 2.2 copy-start.49
  278.0 2.2 copy-start.45
  279.1 2.3 copy-start.43
  280.2 2.3 copy-start.41
  281.4 2.3 copy-start.46
  282.5 2.3 copy-start.47
  283.6 2.3 copy-start.44
  284.8 2.2 copy-start.42
  285.9 2.3 copy-start.37
  287.0 2.3 copy-start.30
  288.2 2.3 copy-start.28
  289.3 2.3 copy-start.38
  290.4 2.2 copy-start.39
  291.6 2.2 copy-start.31
  292.7 2.2 copy-start.32
  293.8 2.2 copy-start.33
  294.9 2.2 copy-start.34
  296.0 2.3 copy-start.35
  299.5 17.9 %copy-start = (bf16[1024,4800]{0,1:T(8,128)(2,1)S(1)}, bf16[1024,4800]{0,1:T(8,128)(2,1)}, u32[]{:S(2)}) copy-start(bf16[1024,4800]{0,1:T(8,128)(2,1)} %all-gather.2.cloned.1.call-done) | copy-start | bytes 29491204
  331.8 29.3 %slice-start = ((s8[9830400]{0:T(1024)(128)(4,1)}), s8[4194304]{0:T(1024)(128)(4,1)S(1)}, s32[]{:S(2)}) async-start(s8[9830400]{0:T(1024)(128)(4,1)} %bitcast.175), calls=%async_computation.4 | async-start | bytes 8388608
  331.8 29.3 %slice-start.1 = ((s8[9830400]{0:T(1024)(128)(4,1)}), s8[4194304]{0:T(1024)(128)(4,1)S(1)}, s32[]{:S(2)}) async-start(s8[9830400]{0:T(1024)(128)(4,1)} %bitcast.175), calls=%async_computation.5 | async-start | bytes 8388608
  346.5 14.6 %slice-start.2 = ((s8[9830400]{0:T(1024)(128)(4,1)}), s8[1441792]{0:T(1024)(128)(4,1)S(1)}, s32[]{:S(2)}) async-start(s8[9830400]{0:T(1024)(128)(4,1)} %bitcast.175), calls=%async_computation.6 | async-start | bytes 2883584
  (1 other events, 0.9 us)
Sparse Core Ops, SparseCore 0:
  175.6 93.9 all-gather.1
  388.2 105.3 reduce-scatter.1
where the time goes:
time: 514 us; the launch traced here: 506 us
  local copies, waits for them, and re-layouts  200 us (39%)
  waiting for transfers between devices  105 us (20%)
  other arithmetic  88.7 us (17%)
  matrix products  76.1 us (15%)
  blocking collectives  21.8 us (4%)
  between operations  13.8 us (3%)
    slice x45, local copies, waits for them, and re-layouts, correlate(): left_padded[:, :, LAGS - 1 - lag_index:LAGS - 1 - lag_index + SAMP]  120 us
    reduce_scatter x1, waiting for transfers between devices, body(): lax.psum_scatter((partial_value * norm_scale).astype(jnp.bfloat16), 'seg'...  105 us
    dot_general x6, matrix products, correlate(): lax.dot_general(shifted, right_flat, (((1,), (1,)), ((), ())), preferred_...  76.1 us
    abs x1, other arithmetic, preprocess(): magnitude = jnp.pad(jnp.abs(filtered), ((0, 0), (RADIUS + 1, RADIUS)))  61.6 us
    unnamed x164, local copies, waits for them, and re-layouts  54.3 us
    all_to_all x1, blocking collectives, body(): lax.all_to_all(flat_rows, 'seg', split_axis=1, concat_axis=0, tiled=True)  21.8 us
    convert_element_type x1, other arithmetic, body(): (partial_value * norm_scale).astype(jnp.bfloat16)  12.5 us
  transfers between devices with their start and end apart: 2, of which 1 were waited for; matrix products, arithmetic and copies ran while one was open for 24% of the time, Pallas kernels for 0%

commit v1 on v0

v1 whole, which is shorter than its diff:
```python
import functools
import math

import jax
import jax.numpy as jnp
from jax import lax
from jax.experimental import pallas as pl
from jax.experimental.pallas import tpu as pltpu
from jax.sharding import PartitionSpec as P

SAMP = 600
LAGS = 41
TAPS = 31
RADIUS = 64
LANES = 128
HALF_LAG = (LAGS - 1) // 2
HALF_TAPS = (TAPS - 1) // 2

epsilon = 1e-06
chunk_segs = 8
lag_group = 7
vmem_bytes = 58 << 20


def split_bf16(value):
    high = value.astype(jnp.bfloat16)
    low = (value - high.astype(jnp.float32)).astype(jnp.bfloat16)
    return high, low


def dot_f32(left, right):
    return jnp.dot(left, right, preferred_element_type=jnp.float32)


def whiten_kernel(chunk_len, taps_ref, traces_ref, flags_ref, *out_refs):
    rows, record_len = traces_ref.shape
    blocks = record_len // LANES
    traces = traces_ref[...]
    stacked = jnp.concatenate(
        [jnp.zeros((rows, LANES), jnp.float32)]
        + [traces[:, j * LANES : (j + 1) * LANES] for j in range(blocks)]
        + [jnp.zeros((2 * rows, LANES), jnp.float32)],
        axis=0,
    )

    def windows(value):
        return jnp.concatenate([value[:-rows], value[rows:]], axis=1)

    offset = lax.broadcasted_iota(jnp.int32, (2 * LANES, LANES), 0) - lax.broadcasted_iota(
        jnp.int32, (2 * LANES, LANES), 1
    )
    band = jnp.zeros((2 * LANES, LANES), jnp.float32)
    for tap_index in range(TAPS):
        band = jnp.where(offset == tap_index, taps_ref[tap_index], band)
    late_band = jnp.concatenate(
        [jnp.zeros((RADIUS, LANES), jnp.float32), band[: 2 * LANES - RADIUS]], axis=0
    )
    band_high, band_low = split_bf16(jnp.concatenate([band, late_band], axis=1))
    high, low = split_bf16(stacked)
    high, low = windows(high), windows(low)
    both = dot_f32(high, band_high) + dot_f32(low, band_high) + dot_f32(high, band_low)

    magnitude = jnp.abs(both[:, :LANES])
    lane = lax.broadcasted_iota(jnp.int32, (rows, LANES), 1)
    magnitude = jnp.concatenate(
        [
            jnp.where(lane >= LANES - HALF_TAPS, magnitude[:rows], 0.0),
            magnitude[rows : blocks * rows],
            jnp.where(
                lane < LANES - HALF_TAPS, magnitude[blocks * rows : (blocks + 1) * rows], 0.0
            ),
            jnp.zeros((rows, LANES), jnp.float32),
        ],
        axis=0,
    )
    ones = jnp.where((offset >= 0) & (offset <= 2 * RADIUS), 1.0, 0.0).astype(jnp.bfloat16)
    high, low = split_bf16(magnitude)
    level = (dot_f32(windows(high), ones) + dot_f32(windows(low), ones)) * (1.0 / (2 * RADIUS + 1))
    filtered = both[: (blocks + 1) * rows, LANES:]
    whitened = filtered / (level + epsilon)

    shift = LANES - HALF_TAPS - RADIUS
    moved = pltpu.roll(whitened, LANES - shift, 1)
    lane = lax.broadcasted_iota(jnp.int32, (blocks * rows, LANES), 1)
    aligned = jnp.where(lane < LANES - shift, moved[: blocks * rows], moved[rows:])
    flat = jnp.concatenate([aligned[j * rows : (j + 1) * rows] for j in range(blocks)], axis=1)

    segments = flags_ref.shape[1]
    first = SAMP * lax.broadcasted_iota(jnp.int32, (segments, record_len), 0)
    sample = lax.broadcasted_iota(jnp.int32, (segments, record_len), 1)
    inside = jnp.where((sample >= first) & (sample < first + SAMP), 1.0, 0.0).astype(jnp.bfloat16)
    kept = dot_f32(flags_ref[...].astype(jnp.float32).astype(jnp.bfloat16), inside)
    flat = (flat * kept).astype(jnp.bfloat16)
    for index, out_ref in enumerate(out_refs):
        out_ref[...] = flat[:, index * chunk_len : (index + 1) * chunk_len]


def whiten(traces, fir_taps, seg_flags, chunk_count):
    rows, record_len = traces.shape
    chunk_len = record_len // chunk_count
    vmem = pl.BlockSpec(memory_space=pltpu.VMEM)
    return pl.pallas_call(
        functools.partial(whiten_kernel, chunk_len),
        in_specs=[pl.BlockSpec(memory_space=pltpu.SMEM), vmem, vmem],
        out_specs=[vmem] * chunk_count,
        out_shape=[jax.ShapeDtypeStruct((rows, chunk_len), jnp.bfloat16)] * chunk_count,
        compiler_params=pltpu.CompilerParams(vmem_limit_bytes=vmem_bytes),
        name="whiten",
    )(fir_taps, traces, seg_flags)


def route_kernel(place_ref, *refs):
    count = len(refs) // 2
    for index, out_ref in enumerate(refs[count:]):
        for source_index, source in enumerate(refs[:count]):

            @pl.when(place_ref[index] == source_index)
            def _(source=source, out_ref=out_ref):
                out_ref[...] = source[...]


def route(place, pieces):
    vmem = pl.BlockSpec(memory_space=pltpu.VMEM)
    return pl.pallas_call(
        route_kernel,
        in_specs=[pl.BlockSpec(memory_space=pltpu.SMEM)] + [vmem] * len(pieces),
        out_specs=[vmem] * len(pieces),
        out_shape=[jax.ShapeDtypeStruct(p.shape, p.dtype) for p in pieces],
        compiler_params=pltpu.CompilerParams(vmem_limit_bytes=vmem_bytes),
        name="route",
    )(place, *pieces)


def correlate_kernel(seg_count, sides, has_total, last, scale, place_ref, *refs):
    refs = list(refs)
    left = [refs.pop(0) for _ in range(seg_count)]
    right = [refs.pop(0) for _ in range(seg_count * sides)]
    total_ref = refs.pop(0) if has_total else None
    mask_ref = refs.pop(0) if last else None
    out_ref, moved, columns, shifted = refs[:4]
    piece_rows, chunk_len = left[0].shape
    row_count, padded_len = moved.shape
    step = pl.program_id(0)

    @pl.when(step == 0)
    def _():
        edge = chunk_len // LANES * LANES
        if padded_len > chunk_len:
            moved[:, edge:] = jnp.zeros((row_count, padded_len - edge), moved.dtype)
            columns[:, edge:] = jnp.zeros((columns.shape[0], padded_len - edge), columns.dtype)
        for index, piece in enumerate(left):
            moved[index * piece_rows : (index + 1) * piece_rows, :chunk_len] = piece[...]
        staged = refs[4] if len(refs) > 4 else columns
        for index, piece in enumerate(right):
            at = pl.multiple_of(place_ref[seg_count + index] * piece_rows, piece_rows)
            staged[pl.ds(at, piece_rows), :chunk_len] = piece[...].astype(staged.dtype)
        if len(refs) > 4:
            columns[:, :chunk_len] = staged[:, :chunk_len].astype(columns.dtype)
        moved[...] = pltpu.roll(moved[...], padded_len - HALF_LAG, 1)

    sample = lax.broadcasted_iota(jnp.int32, (16, padded_len), 1)
    phase = sample
    for segment in range(1, chunk_len // SAMP):
        phase = jnp.where(sample >= segment * SAMP, sample - segment * SAMP, phase)
    phase = jnp.where(sample >= chunk_len, -SAMP, phase)
    base = moved[...]
    for index in range(lag_group):
        lag = step * lag_group + index - HALF_LAG
        rolled = pltpu.roll(base, index, 1) if index else base
        keep = jnp.where((phase >= lag) & (phase < SAMP + lag), 1.0, 0.0).astype(jnp.bfloat16)
        keep = jnp.concatenate([keep] * (row_count // 16), axis=0)
        shifted[index * row_count : (index + 1) * row_count, :] = rolled * keep
    moved[...] = pltpu.roll(base, lag_group, 1)
    product = lax.dot_general(
        shifted[...], columns[...], (((1,), (1,)), ((), ())), preferred_element_type=jnp.float32
    )
    product = product.reshape(lag_group, row_count, columns.shape[0])
    if has_total:
        product = product + total_ref[...]
    if not last:
        out_ref[...] = product
        return
    for index in range(seg_count):
        at = pl.ds(pl.multiple_of(place_ref[index] * piece_rows, piece_rows), piece_rows)
        weight = mask_ref[at, :].astype(jnp.float32) * scale
        out_ref[:, at, :] = product[:, index * piece_rows : (index + 1) * piece_rows] * weight[None]


def correlate(place, left, right, total, mask, last, scale):
    seg_count = len(left)
    piece_rows, chunk_len = left[0].shape
    rows, cols = seg_count * piece_rows, len(right) * piece_rows
    padded_len = pl.cdiv(chunk_len, LANES) * LANES
    whole = pl.BlockSpec((piece_rows, chunk_len), lambda step: (0, 0))
    block = pl.BlockSpec((lag_group, rows, cols), lambda step: (step, 0, 0))
    operands, specs = [place, *left, *right], [pl.BlockSpec(memory_space=pltpu.SMEM)]
    specs += [whole] * (len(left) + len(right))
    aliases = {}
    if total is not None:
        aliases = {len(operands): 0}
        operands.append(total)
        specs.append(block)
    if last:
        operands.append(mask)
        specs.append(pl.BlockSpec((rows, cols), lambda step: (0, 0)))
    scratch = [
        pltpu.VMEM((rows, padded_len), jnp.bfloat16),
        pltpu.VMEM((cols, padded_len), jnp.bfloat16),
        pltpu.VMEM((lag_group * rows, padded_len), jnp.bfloat16),
    ]
    if piece_rows % 16:
        scratch.append(pltpu.VMEM((cols, padded_len), jnp.float32))
    return pl.pallas_call(
        functools.partial(
            correlate_kernel, seg_count, len(right) // seg_count, total is not None, last, scale
        ),
        grid=(pl.cdiv(LAGS, lag_group),),
        in_specs=specs,
        out_specs=block,
        out_shape=jax.ShapeDtypeStruct((LAGS, rows, cols), jnp.float32),
        input_output_aliases=aliases,
        scratch_shapes=scratch,
        compiler_params=pltpu.CompilerParams(vmem_limit_bytes=vmem_bytes),
        cost_estimate=pl.CostEstimate(
            flops=2 * LAGS * rows * cols * chunk_len,
            bytes_accessed=8 * LAGS * rows * cols + 2 * (rows + cols) * chunk_len,
            transcendentals=0,
        ),
        name="correlate",
    )(*operands)


def body(traces, fir_taps, seg_flags, pair_mask):
    stn_count, seg_count = lax.axis_size("stn"), lax.axis_size("seg")
    sides = stn_count // seg_count
    stn, seg = lax.axis_index("stn"), lax.axis_index("seg")
    plane, side = stn // sides, stn % sides
    segments = seg_flags.shape[1]
    chunk_count = segments // chunk_segs
    scale = 1.0 / math.sqrt(SAMP * segments)
    partner = jnp.stack([seg ^ k for k in range(seg_count)]).astype(jnp.int32)
    route_place = plane ^ partner
    place = jnp.concatenate(
        [partner] + [(side ^ j) * seg_count + partner for j in range(sides)]
    ).astype(jnp.int32)

    def to_seg(value, k):
        return lax.ppermute(value, "seg", [(i, i ^ k) for i in range(seg_count)])

    def to_plane(value, k):
        return lax.ppermute(value, "stn", [(i, i ^ (k * sides)) for i in range(stn_count)])

    def to_side(value, j):
        return lax.ppermute(value, "stn", [(i, i ^ j) for i in range(stn_count)])

    pieces = whiten(traces, fir_taps, seg_flags, chunk_count)
    total = None
    for index, piece in enumerate(pieces):
        line = [piece]
        for k in range(1, seg_count):
            low = k & (k - 1)
            line.append(to_plane(line[k ^ low] if low else piece, low or k))
        left = [piece] + [to_seg(piece, k) for k in range(1, seg_count)]
        routed = route(route_place, line)
        own = [routed[0]] + [to_seg(routed[k], k) for k in range(1, seg_count)]
        right = own + [to_side(value, j) for j in range(1, sides) for value in own]
        last = index == chunk_count - 1
        total = correlate(place, left, right, total, pair_mask, last, scale)
    return total


def solution(mesh):
    return jax.shard_map(
        body,
        mesh=mesh,
        in_specs=(P(("stn", "seg"), None), P(), P(("stn", "seg"), None), P("stn", "seg")),
        out_specs=P(None, "stn", "seg"),
        check_vma=False,
    )
```

time: 514 us -> 245 us (0.48); the launches traced: 506 us -> 244 us
  local copies, waits for them, and re-layouts: 200 us -> 3.08 us
  Pallas kernels: 0 us -> 95.1 us
  other arithmetic: 88.7 us -> 0.6 us
  matrix products: 76.1 us -> 0 us
  starting transfers between devices: 0.04 us -> 44.6 us
  blocking collectives: 21.8 us -> 0 us
  between operations: 13.8 us -> 0.41 us
    slice x47 -> x0, local copies, waits for them, and re-layouts: 124 us -> none  [the longest x45 120 us: correlate(): left_padded[:, :, LAGS - 1 - lag_index:LAGS - 1 - lag_index + SAMP]]
    reduce_scatter x1 -> x0, waiting for transfers between devices: 105 us -> none  [body(): lax.psum_scatter((partial_value * norm_scale).astype(jnp.bfloat16), 'seg'...]
    ppermute x0 -> x52, waiting for transfers between devices: none -> 101 us  [the longest x12 81.3 us: to_plane(): lax.ppermute(value, 'stn', [(i, i ^ k * sides) for i in range(stn_count)])]
    pallas_call x0 -> x9, Pallas kernels: none -> 95.1 us  [the longest x4 76.3 us: correlate(): pl.pallas_call(functools.partial(correlate_kernel, seg_count, len(right)...]
    dot_general x6 -> x0, matrix products: 76.1 us -> none  [correlate(): lax.dot_general(shifted, right_flat, (((1,), (1,)), ((), ())), preferred_...]
    abs x1 -> x0, other arithmetic: 61.6 us -> none  [preprocess(): magnitude = jnp.pad(jnp.abs(filtered), ((0, 0), (RADIUS + 1, RADIUS)))]
    unnamed x164 -> x88, local copies, waits for them, and re-layouts: 54.3 us -> 2.47 us
    ppermute x0 -> x52, starting transfers between devices: none -> 44.6 us  [the longest x24 32.4 us: to_seg(): return lax.ppermute(value, 'seg', [(i, i ^ k) for i in range(seg_count)])]
  transfers between devices with their start and end apart: 2 -> 52, of which waited for: 1 -> 17; matrix products, arithmetic and copies ran while one was open for 24% -> 0% of each run, Pallas kernels for 0% -> 28%
where the time goes in v1:
time: 245 us; the launch traced here: 244 us
  waiting for transfers between devices  101 us (41%)
  Pallas kernels  95.1 us (39%)
  starting transfers between devices  44.6 us (18%)
  local copies, waits for them, and re-layouts  3.08 us (1%)
    ppermute x12, waiting for transfers between devices, to_plane(): lax.ppermute(value, 'stn', [(i, i ^ k * sides) for i in range(stn_count)])  81.3 us
    pallas_call x4, Pallas kernels, correlate(): pl.pallas_call(functools.partial(correlate_kernel, seg_count, len(right)...  76.3 us
    ppermute x24, starting transfers between devices, to_seg(): return lax.ppermute(value, 'seg', [(i, i ^ k) for i in range(seg_count)])  32.4 us
    ppermute x24, waiting for transfers between devices, to_seg(): return lax.ppermute(value, 'seg', [(i, i ^ k) for i in range(seg_count)])  19.4 us
    pallas_call x4, Pallas kernels, route(): pl.pallas_call(route_kernel, in_specs=[pl.BlockSpec(memory_space=pltpu.SM...  10.4 us
    ppermute x12, starting transfers between devices, to_plane(): lax.ppermute(value, 'stn', [(i, i ^ k * sides) for i in range(stn_count)])  9.12 us
    pallas_call x1, Pallas kernels, whiten(): pl.pallas_call(functools.partial(whiten_kernel, chunk_len), in_specs=[pl....  8.4 us
  transfers between devices with their start and end apart: 52, of which 17 were waited for; matrix products, arithmetic and copies ran while one was open for 0% of the time, Pallas kernels for 28%

profile of v1, /device:TPU:0, one launch (start us, length us, event | category | flops | bytes accessed | tf_op | source)
XLA Modules:
  0.0 244.5 jit_solution(1317857673177571584)
XLA Ops:
  0.0 8.4 %whiten.1 = (bf16[32,4800]{1,0:T(8,128)(2,1)}, bf16[32,4800]{1,0:T(8,128)(2,1)}, bf16[32,4800]{1,0:T(8,128)(2,1)}, bf16[32,4800]{1,0:T(8,128)(2,1)}) custom-call(f32[31]{0:T(128)} %taps_ref.1, f32[32,19200]{1,0:T(8,128)} %traces_ref.1, s32[32,32]{1,0:T(8,128)} %flags_ref.1), custom_call_target="tpu_custom_call" | custom-call | tf_op jit(solution)/shard_map/whiten/pallas_call | solution.py:102
  8.4 3.0 %collective-permute-start.42 = (bf16[32,4800]{1,0:T(8,128)(2,1)}, bf16[32,4800]{1,0:T(8,128)(2,1)S(1)}, u32[]{:S(2)}, u32[]{:S(2)}) collective-permute-start(bf16[32,4800]{1,0:T(8,128)(2,1)} %get-tuple-element.40.refs_0_), channel_id=1, source_target_pairs={{0,8},{4,12},{8,0},{12,4},{16,24},{20,28},{24,16},{28,20},{1,9},{5... | collective-permute-start | bytes 921608 | tf_op jit(solution)/shard_map/ppermute | solution.py:251
  11.4 2.6 %collective-permute-start.43 = (bf16[32,4800]{1,0:T(8,128)(2,1)}, bf16[32,4800]{1,0:T(8,128)(2,1)S(1)}, u32[]{:S(2)}, u32[]{:S(2)}) collective-permute-start(bf16[32,4800]{1,0:T(8,128)(2,1)} %get-tuple-element.40.refs_0_), channel_id=1, source_target_pairs={{0,16},{4,20},{8,24},{12,28},{16,0},{20,4},{24,8},{28,12},{1,17},{... | collective-permute-start | bytes 921608 | tf_op jit(solution)/shard_map/ppermute | solution.py:251
  14.0 1.5 collective-permute-start.39
  15.5 1.5 collective-permute-start.40
  17.0 0.5 collective-permute-start.41
  17.5 8.0 %collective-permute-done.42.refs_1_ = bf16[32,4800]{1,0:T(8,128)(2,1)S(1)} collective-permute-done((bf16[32,4800]{1,0:T(8,128)(2,1)}, bf16[32,4800]{1,0:T(8,128)(2,1)S(1)}, u32[]{:S(2)}, u32[]{:S(2)}) %collective-permute-start.42) | collective-permute-done | bytes 307232 | tf_op jit(solution)/shard_map/ppermute | solution.py:251
  25.5 2.7 %collective-permute-done.43.refs_2_ = bf16[32,4800]{1,0:T(8,128)(2,1)S(1)} collective-permute-done((bf16[32,4800]{1,0:T(8,128)(2,1)}, bf16[32,4800]{1,0:T(8,128)(2,1)S(1)}, u32[]{:S(2)}, u32[]{:S(2)}) %collective-permute-start.43) | collective-permute-done | bytes 307232 | tf_op jit(solution)/shard_map/ppermute | solution.py:251
  28.2 0.6 collective-permute-start.30
  28.8 1.5 collective-permute-start.26
  30.3 0.5 collective-permute-done.40.refs_2_
  30.8 1.5 collective-permute-start.27
  32.3 7.8 %collective-permute-done.29.refs_1_ = bf16[32,4800]{1,0:T(8,128)(2,1)S(1)} collective-permute-done((bf16[32,4800]{1,0:T(8,128)(2,1)}, bf16[32,4800]{1,0:T(8,128)(2,1)S(1)}, u32[]{:S(2)}, u32[]{:S(2)}) %collective-permute-start.29) | collective-permute-done | bytes 307232 | tf_op jit(solution)/shard_map/ppermute | solution.py:251
  40.1 2.9 %collective-permute-done.30.refs_2_ = bf16[32,4800]{1,0:T(8,128)(2,1)S(1)} collective-permute-done((bf16[32,4800]{1,0:T(8,128)(2,1)}, bf16[32,4800]{1,0:T(8,128)(2,1)S(1)}, u32[]{:S(2)}, u32[]{:S(2)}) %collective-permute-start.30) | collective-permute-done | bytes 307232 | tf_op jit(solution)/shard_map/ppermute | solution.py:251
  43.0 1.6 collective-permute-start.13
  44.6 1.5 collective-permute-start.14
  46.2 0.4 collective-permute-start.15
  46.6 7.9 %collective-permute-done.16.refs_1_ = bf16[32,4800]{1,0:T(8,128)(2,1)S(1)} collective-permute-done((bf16[32,4800]{1,0:T(8,128)(2,1)}, bf16[32,4800]{1,0:T(8,128)(2,1)S(1)}, u32[]{:S(2)}, u32[]{:S(2)}) %collective-permute-start.16) | collective-permute-done | bytes 307232 | tf_op jit(solution)/shard_map/ppermute | solution.py:251
  54.4 3.3 %collective-permute-done.17.refs_2_ = bf16[32,4800]{1,0:T(8,128)(2,1)S(1)} collective-permute-done((bf16[32,4800]{1,0:T(8,128)(2,1)}, bf16[32,4800]{1,0:T(8,128)(2,1)S(1)}, u32[]{:S(2)}, u32[]{:S(2)}) %collective-permute-start.17) | collective-permute-done | bytes 307232 | tf_op jit(solution)/shard_map/ppermute | solution.py:251
  57.7 2.9 %collective-permute-start.4 = (bf16[32,4800]{1,0:T(8,128)(2,1)}, bf16[32,4800]{1,0:T(8,128)(2,1)S(1)}, u32[]{:S(2)}, u32[]{:S(2)}) collective-permute-start(bf16[32,4800]{1,0:T(8,128)(2,1)} %get-tuple-element.25.refs_0_), channel_id=1, source_target_pairs={{0,16},{4,20},{8,24},{12,28},{16,0},{20,4},{24,8},{28,12},{1,17},{... | collective-permute-start | bytes 921608 | tf_op jit(solution)/shard_map/ppermute | solution.py:251
  60.6 1.5 collective-permute-start
  62.2 1.5 collective-permute-start.1
  63.7 7.1 %collective-permute-done.3.refs_1_ = bf16[32,4800]{1,0:T(8,128)(2,1)S(1)} collective-permute-done((bf16[32,4800]{1,0:T(8,128)(2,1)}, bf16[32,4800]{1,0:T(8,128)(2,1)S(1)}, u32[]{:S(2)}, u32[]{:S(2)}) %collective-permute-start.3) | collective-permute-done | bytes 307232 | tf_op jit(solution)/shard_map/ppermute | solution.py:251
  70.8 21.5 %collective-permute-done.44.refs_3_ = bf16[32,4800]{1,0:T(8,128)(2,1)S(1)} collective-permute-done((bf16[32,4800]{1,0:T(8,128)(2,1)S(1)}, bf16[32,4800]{1,0:T(8,128)(2,1)S(1)}, u32[]{:S(2)}, u32[]{:S(2)}) %collective-permute-start.44) | collective-permute-done | bytes 307232 | tf_op jit(solution)/shard_map/ppermute | solution.py:251
  92.3 0.6 broadcast_xor_fusion
  93.0 2.5 %route.7 = (bf16[32,4800]{1,0:T(8,128)(2,1)}, bf16[32,4800]{1,0:T(8,128)(2,1)}, bf16[32,4800]{1,0:T(8,128)(2,1)}, bf16[32,4800]{1,0:T(8,128)(2,1)}) custom-call(s32[4]{0:T(128)} %get-tuple-element.45.place_ref, bf16[32,4800]{1,0:T(8,128)(2,1)} %get-tuple-element.40.refs_0_, bf16[32,4800]{1,0:T(8,128)(2,1)} %copy-done.5, bf16[32,4800]{1,0:T(8,128)(2,1)} %copy-done.6, ...), custom_call_target="tpu_custom_call" | custom-call | tf_op jit(solution)/shard_map/route/pallas_call | solution.py:124
  95.5 10.1 %collective-permute-done.4.refs_2_ = bf16[32,4800]{1,0:T(8,128)(2,1)S(1)} collective-permute-done((bf16[32,4800]{1,0:T(8,128)(2,1)}, bf16[32,4800]{1,0:T(8,128)(2,1)S(1)}, u32[]{:S(2)}, u32[]{:S(2)}) %collective-permute-start.4) | collective-permute-done | bytes 307232 | tf_op jit(solution)/shard_map/ppermute | solution.py:251
  105.6 1.6 collective-permute-start.45
  107.2 1.5 collective-permute-start.46
  108.7 6.9 %collective-permute-done.31.refs_3_ = bf16[32,4800]{1,0:T(8,128)(2,1)S(1)} collective-permute-done((bf16[32,4800]{1,0:T(8,128)(2,1)S(1)}, bf16[32,4800]{1,0:T(8,128)(2,1)S(1)}, u32[]{:S(2)}, u32[]{:S(2)}) %collective-permute-start.31) | collective-permute-done | bytes 307232 | tf_op jit(solution)/shard_map/ppermute | solution.py:251
  115.6 2.5 %collective-permute-start.47 = (bf16[32,4800]{1,0:T(8,128)(2,1)}, bf16[32,4800]{1,0:T(8,128)(2,1)}, u32[]{:S(2)}, u32[]{:S(2)}) collective-permute-start(bf16[32,4800]{1,0:T(8,128)(2,1)} %get-tuple-element.44), channel_id=1, source_target_pairs={{0,3},{1,2},{2,1},{3,0},{4,7},{5,6},{6,5},{7,4},{8,11},{9,10},{10,... | collective-permute-start | bytes 921608 | tf_op jit(solution)/shard_map/ppermute | solution.py:248
  118.1 3.3 %collective-permute-done.18.refs_3_ = bf16[32,4800]{1,0:T(8,128)(2,1)S(1)} collective-permute-done((bf16[32,4800]{1,0:T(8,128)(2,1)S(1)}, bf16[32,4800]{1,0:T(8,128)(2,1)S(1)}, u32[]{:S(2)}, u32[]{:S(2)}) %collective-permute-start.18) | collective-permute-done | bytes 307232 | tf_op jit(solution)/shard_map/ppermute | solution.py:251
  121.4 2.6 %route.6 = (bf16[32,4800]{1,0:T(8,128)(2,1)}, bf16[32,4800]{1,0:T(8,128)(2,1)}, bf16[32,4800]{1,0:T(8,128)(2,1)}, bf16[32,4800]{1,0:T(8,128)(2,1)}) custom-call(s32[4]{0:T(128)} %get-tuple-element.45.place_ref, bf16[32,4800]{1,0:T(8,128)(2,1)} %get-tuple-element.35.refs_0_, bf16[32,4800]{1,0:T(8,128)(2,1)} %copy-done.3, bf16[32,4800]{1,0:T(8,128)(2,1)} %copy-done.4, ...), custom_call_target="tpu_custom_call" | custom-call | tf_op jit(solution)/shard_map/route/pallas_call | solution.py:124
  124.0 2.5 %route.5 = (bf16[32,4800]{1,0:T(8,128)(2,1)}, bf16[32,4800]{1,0:T(8,128)(2,1)}, bf16[32,4800]{1,0:T(8,128)(2,1)}, bf16[32,4800]{1,0:T(8,128)(2,1)}) custom-call(s32[4]{0:T(128)} %get-tuple-element.45.place_ref, bf16[32,4800]{1,0:T(8,128)(2,1)} %get-tuple-element.30.refs_0_, bf16[32,4800]{1,0:T(8,128)(2,1)} %copy-done.7, bf16[32,4800]{1,0:T(8,128)(2,1)} %copy-done.8, ...), custom_call_target="tpu_custom_call" | custom-call | tf_op jit(solution)/shard_map/route/pallas_call | solution.py:124
  126.5 1.6 collective-permute-start.32
  128.1 1.6 collective-permute-start.33
  129.7 0.4 collective-permute-start.34
  130.1 1.6 collective-permute-start.19
  131.7 5.3 %collective-permute-done.32.refs_5_ = bf16[32,4800]{1,0:T(8,128)(2,1)S(1)} collective-permute-done((bf16[32,4800]{1,0:T(8,128)(2,1)}, bf16[32,4800]{1,0:T(8,128)(2,1)S(1)}, u32[]{:S(2)}, u32[]{:S(2)}) %collective-permute-start.32) | collective-permute-done | bytes 307232 | tf_op jit(solution)/shard_map/ppermute | solution.py:248
  137.0 1.6 collective-permute-start.20
  138.6 5.8 %collective-permute-done.33.refs_6_ = bf16[32,4800]{1,0:T(8,128)(2,1)S(1)} collective-permute-done((bf16[32,4800]{1,0:T(8,128)(2,1)}, bf16[32,4800]{1,0:T(8,128)(2,1)S(1)}, u32[]{:S(2)}, u32[]{:S(2)}) %collective-permute-start.33) | collective-permute-done | bytes 307232 | tf_op jit(solution)/shard_map/ppermute | solution.py:248
  144.4 1.7 collective-permute-start.21
  146.2 0.5 collective-permute-start.50
  146.7 3.7 %collective-permute-done.19.refs_5_ = bf16[32,4800]{1,0:T(8,128)(2,1)S(1)} collective-permute-done((bf16[32,4800]{1,0:T(8,128)(2,1)}, bf16[32,4800]{1,0:T(8,128)(2,1)S(1)}, u32[]{:S(2)}, u32[]{:S(2)}) %collective-permute-start.19) | collective-permute-done | bytes 307232 | tf_op jit(solution)/shard_map/ppermute | solution.py:248
  150.4 0.6 concatenate.4.place_ref
  151.0 2.7 %route.4 = (bf16[32,4800]{1,0:T(8,128)(2,1)}, bf16[32,4800]{1,0:T(8,128)(2,1)}, bf16[32,4800]{1,0:T(8,128)(2,1)}, bf16[32,4800]{1,0:T(8,128)(2,1)}) custom-call(s32[4]{0:T(128)} %get-tuple-element.45.place_ref, bf16[32,4800]{1,0:T(8,128)(2,1)} %get-tuple-element.25.refs_0_, bf16[32,4800]{1,0:T(8,128)(2,1)} %copy-done.1, bf16[32,4800]{1,0:T(8,128)(2,1)} %copy-done.2, ...), custom_call_target="tpu_custom_call" | custom-call | tf_op jit(solution)/shard_map/route/pallas_call | solution.py:124
  153.8 3.9 %collective-permute-done.20.refs_6_ = bf16[32,4800]{1,0:T(8,128)(2,1)S(1)} collective-permute-done((bf16[32,4800]{1,0:T(8,128)(2,1)}, bf16[32,4800]{1,0:T(8,128)(2,1)S(1)}, u32[]{:S(2)}, u32[]{:S(2)}) %collective-permute-start.20) | collective-permute-done | bytes 307232 | tf_op jit(solution)/shard_map/ppermute | solution.py:248
  157.8 1.2 collective-permute-start.6
  159.0 0.5 collective-permute-start.37
  159.6 18.7 %correlate.4.refs_12_ = f32[41,128,256]{2,1,0:T(8,128)} custom-call(s32[12]{0:T(128)} %concatenate.4.place_ref, bf16[32,4800]{1,0:T(8,128)(2,1)} %get-tuple-element.40.refs_0_, bf16[32,4800]{1,0:T(8,128)(2,1)} %collective-permute-done.39.refs_1_, bf16[32,4800]{1,0:T(8,128)(2,1)} %collective-permute-done.40.refs_2_, ...), custom_call_target="tpu_custom_call" | custom-call | flops 12897484800 | bytes 14434304 | tf_op jit(solution)/shard_map/correlate/pallas_call | solution.py:213
  178.4 1.1 collective-permute-start.7
  179.5 1.4 collective-permute-start.8
  181.1 0.5 collective-permute-start.24
  181.9 19.1 %correlate.5.refs_12_ = f32[41,128,256]{2,1,0:T(8,128)} custom-call(s32[12]{0:T(128)} %concatenate.4.place_ref, bf16[32,4800]{1,0:T(8,128)(2,1)} %get-tuple-element.35.refs_0_, bf16[32,4800]{1,0:T(8,128)(2,1)} %copy-done.15, bf16[32,4800]{1,0:T(8,128)(2,1)} %copy-done.16, bf16[32,4800]{1,0:T(8,128)(2,1)} %copy-done.17, ...), custom_call_target="tpu_custom_call", output_to_operand_aliasing={{}: (13, {})} | custom-call | flops 12897484800 | bytes 14434304 | tf_op jit(solution)/shard_map/correlate/pallas_call | solution.py:213
  201.0 1.6 collective-permute-start.2
  202.7 0.2 collective-permute-start.9
  202.9 0.4 collective-permute-start.10
  203.5 0.4 collective-permute-start.12
  203.8 0.2 copy-done.36
  204.0 0.2 copy-done.39
  204.2 19.1 %correlate.6.refs_12_ = f32[41,128,256]{2,1,0:T(8,128)} custom-call(s32[12]{0:T(128)} %concatenate.4.place_ref, bf16[32,4800]{1,0:T(8,128)(2,1)} %get-tuple-element.30.refs_0_, bf16[32,4800]{1,0:T(8,128)(2,1)} %collective-permute-done.13.refs_1_, bf16[32,4800]{1,0:T(8,128)(2,1)} %copy-done.13, ...), custom_call_target="tpu_custom_call", output_to_operand_aliasing={{}: (13, {})} | custom-call | flops 12897484800 | bytes 14434304 | tf_op jit(solution)/shard_map/correlate/pallas_call | solution.py:213
  223.4 0.6 copy-done.37
  224.4 0.7 copy-done.43
  225.1 19.4 %correlate.7 = f32[41,128,256]{2,1,0:T(8,128)} custom-call(s32[12]{0:T(128)} %concatenate.4.place_ref, bf16[32,4800]{1,0:T(8,128)(2,1)} %get-tuple-element.25.refs_0_, bf16[32,4800]{1,0:T(8,128)(2,1)} %collective-permute-done.refs_1_, bf16[32,4800]{1,0:T(8,128)(2,1)} %collective-permute-done.1.refs_2_, ...), custom_call_target="tpu_custom_call", output_to_operand_aliasing={{}: (13, {})} | custom-call | flops 12897484800 | bytes 14434304 | tf_op jit(solution)/shard_map/correlate/pallas_call | solution.py:213
  (140 shorter events, 1.4 us)
Async XLA Ops:
  8.4 17.1 %collective-permute-start.42 = (bf16[32,4800]{1,0:T(8,128)(2,1)}, bf16[32,4800]{1,0:T(8,128)(2,1)S(1)}, u32[]{:S(2)}, u32[]{:S(2)}) collective-permute-start(bf16[32,4800]{1,0:T(8,128)(2,1)} %get-tuple-element.40.refs_0_), channel_id=1, source_target_pairs={{0,8},{4,12},{8,0},{12,4},{16,24},{20,28},{24,16},{28,20},{1,9},{5... | collective-permute-start | bytes 921608 | tf_op jit(solution)/shard_map/ppermute | solution.py:251
  11.4 16.8 %collective-permute-start.43 = (bf16[32,4800]{1,0:T(8,128)(2,1)}, bf16[32,4800]{1,0:T(8,128)(2,1)S(1)}, u32[]{:S(2)}, u32[]{:S(2)}) collective-permute-start(bf16[32,4800]{1,0:T(8,128)(2,1)} %get-tuple-element.40.refs_0_), channel_id=1, source_target_pairs={{0,16},{4,20},{8,24},{12,28},{16,0},{20,4},{24,8},{28,12},{1,17},{... | collective-permute-start | bytes 921608 | tf_op jit(solution)/shard_map/ppermute | solution.py:251
  14.0 14.8 %collective-permute-start.39 = (bf16[32,4800]{1,0:T(8,128)(2,1)}, bf16[32,4800]{1,0:T(8,128)(2,1)}, u32[]{:S(2)}, u32[]{:S(2)}) collective-permute-start(bf16[32,4800]{1,0:T(8,128)(2,1)} %get-tuple-element.40.refs_0_), channel_id=1, source_target_pairs={{0,1},{1,0},{2,3},{3,2},{4,5},{5,4},{6,7},{7,6},{8,9},{9,8},{10,11... | collective-permute-start | bytes 921608 | tf_op jit(solution)/shard_map/ppermute | solution.py:248
  15.5 15.2 %collective-permute-start.40 = (bf16[32,4800]{1,0:T(8,128)(2,1)}, bf16[32,4800]{1,0:T(8,128)(2,1)}, u32[]{:S(2)}, u32[]{:S(2)}) collective-permute-start(bf16[32,4800]{1,0:T(8,128)(2,1)} %get-tuple-element.40.refs_0_), channel_id=1, source_target_pairs={{0,2},{1,3},{2,0},{3,1},{4,6},{5,7},{6,4},{7,5},{8,10},{9,11},{10,... | collective-permute-start | bytes 921608 | tf_op jit(solution)/shard_map/ppermute | solution.py:248
  17.0 15.2 %collective-permute-start.41 = (bf16[32,4800]{1,0:T(8,128)(2,1)}, bf16[32,4800]{1,0:T(8,128)(2,1)}, u32[]{:S(2)}, u32[]{:S(2)}) collective-permute-start(bf16[32,4800]{1,0:T(8,128)(2,1)} %get-tuple-element.40.refs_0_), channel_id=1, source_target_pairs={{0,3},{1,2},{2,1},{3,0},{4,7},{5,6},{6,5},{7,4},{8,11},{9,10},{10,... | collective-permute-start | bytes 921608 | tf_op jit(solution)/shard_map/ppermute | solution.py:248
  25.5 67.4 %copy-start.5 = (bf16[32,4800]{1,0:T(8,128)(2,1)}, bf16[32,4800]{1,0:T(8,128)(2,1)S(1)}, u32[]{:S(2)}) copy-start(bf16[32,4800]{1,0:T(8,128)(2,1)S(1)} %collective-permute-done.42.refs_1_) | copy-start | bytes 921604
  25.5 14.6 %collective-permute-start.29 = (bf16[32,4800]{1,0:T(8,128)(2,1)}, bf16[32,4800]{1,0:T(8,128)(2,1)S(1)}, u32[]{:S(2)}, u32[]{:S(2)}) collective-permute-start(bf16[32,4800]{1,0:T(8,128)(2,1)} %get-tuple-element.35.refs_0_), channel_id=1, source_target_pairs={{0,8},{4,12},{8,0},{12,4},{16,24},{20,28},{24,16},{28,20},{1,9},{5... | collective-permute-start | bytes 921608 | tf_op jit(solution)/shard_map/ppermute | solution.py:251
  28.2 64.7 %copy-start.6 = (bf16[32,4800]{1,0:T(8,128)(2,1)}, bf16[32,4800]{1,0:T(8,128)(2,1)S(1)}, u32[]{:S(2)}) copy-start(bf16[32,4800]{1,0:T(8,128)(2,1)S(1)} %collective-permute-done.43.refs_2_) | copy-start | bytes 921604
  28.2 14.8 %collective-permute-start.30 = (bf16[32,4800]{1,0:T(8,128)(2,1)}, bf16[32,4800]{1,0:T(8,128)(2,1)S(1)}, u32[]{:S(2)}, u32[]{:S(2)}) collective-permute-start(bf16[32,4800]{1,0:T(8,128)(2,1)} %get-tuple-element.35.refs_0_), channel_id=1, source_target_pairs={{0,16},{4,20},{8,24},{12,28},{16,0},{20,4},{24,8},{28,12},{1,17},{... | collective-permute-start | bytes 921608 | tf_op jit(solution)/shard_map/ppermute | solution.py:251
  28.8 14.2 %collective-permute-start.26 = (bf16[32,4800]{1,0:T(8,128)(2,1)}, bf16[32,4800]{1,0:T(8,128)(2,1)S(1)}, u32[]{:S(2)}, u32[]{:S(2)}) collective-permute-start(bf16[32,4800]{1,0:T(8,128)(2,1)} %get-tuple-element.35.refs_0_), channel_id=1, source_target_pairs={{0,1},{1,0},{2,3},{3,2},{4,5},{5,4},{6,7},{7,6},{8,9},{9,8},{10,11... | collective-permute-start | bytes 921608 | tf_op jit(solution)/shard_map/ppermute | solution.py:248
  30.8 13.9 %collective-permute-start.27 = (bf16[32,4800]{1,0:T(8,128)(2,1)}, bf16[32,4800]{1,0:T(8,128)(2,1)S(1)}, u32[]{:S(2)}, u32[]{:S(2)}) collective-permute-start(bf16[32,4800]{1,0:T(8,128)(2,1)} %get-tuple-element.35.refs_0_), channel_id=1, source_target_pairs={{0,2},{1,3},{2,0},{3,1},{4,6},{5,7},{6,4},{7,5},{8,10},{9,11},{10,... | collective-permute-start | bytes 921608 | tf_op jit(solution)/shard_map/ppermute | solution.py:248
  32.3 13.9 %collective-permute-start.28 = (bf16[32,4800]{1,0:T(8,128)(2,1)}, bf16[32,4800]{1,0:T(8,128)(2,1)S(1)}, u32[]{:S(2)}, u32[]{:S(2)}) collective-permute-start(bf16[32,4800]{1,0:T(8,128)(2,1)} %get-tuple-element.35.refs_0_), channel_id=1, source_target_pairs={{0,3},{1,2},{2,1},{3,0},{4,7},{5,6},{6,5},{7,4},{8,11},{9,10},{10,... | collective-permute-start | bytes 921608 | tf_op jit(solution)/shard_map/ppermute | solution.py:248
  40.1 81.2 %copy-start.3 = (bf16[32,4800]{1,0:T(8,128)(2,1)}, bf16[32,4800]{1,0:T(8,128)(2,1)S(1)}, u32[]{:S(2)}) copy-start(bf16[32,4800]{1,0:T(8,128)(2,1)S(1)} %collective-permute-done.29.refs_1_) | copy-start | bytes 921604
  40.1 14.3 %collective-permute-start.16 = (bf16[32,4800]{1,0:T(8,128)(2,1)}, bf16[32,4800]{1,0:T(8,128)(2,1)S(1)}, u32[]{:S(2)}, u32[]{:S(2)}) collective-permute-start(bf16[32,4800]{1,0:T(8,128)(2,1)} %get-tuple-element.30.refs_0_), channel_id=1, source_target_pairs={{0,8},{4,12},{8,0},{12,4},{16,24},{20,28},{24,16},{28,20},{1,9},{5... | collective-permute-start | bytes 921608 | tf_op jit(solution)/shard_map/ppermute | solution.py:251
  43.0 78.4 %copy-start.4 = (bf16[32,4800]{1,0:T(8,128)(2,1)}, bf16[32,4800]{1,0:T(8,128)(2,1)S(1)}, u32[]{:S(2)}) copy-start(bf16[32,4800]{1,0:T(8,128)(2,1)S(1)} %collective-permute-done.30.refs_2_) | copy-start | bytes 921604
  43.0 14.7 %collective-permute-start.17 = (bf16[32,4800]{1,0:T(8,128)(2,1)}, bf16[32,4800]{1,0:T(8,128)(2,1)S(1)}, u32[]{:S(2)}, u32[]{:S(2)}) collective-permute-start(bf16[32,4800]{1,0:T(8,128)(2,1)} %get-tuple-element.30.refs_0_), channel_id=1, source_target_pairs={{0,16},{4,20},{8,24},{12,28},{16,0},{20,4},{24,8},{28,12},{1,17},{... | collective-permute-start | bytes 921608 | tf_op jit(solution)/shard_map/ppermute | solution.py:251
  43.0 49.3 %copy-start.15 = (bf16[32,4800]{1,0:T(8,128)(2,1)}, bf16[32,4800]{1,0:T(8,128)(2,1)S(1)}, u32[]{:S(2)}) copy-start(bf16[32,4800]{1,0:T(8,128)(2,1)S(1)} %collective-permute-done.26.refs_1_) | copy-start | bytes 921604
  43.0 14.7 %collective-permute-start.13 = (bf16[32,4800]{1,0:T(8,128)(2,1)}, bf16[32,4800]{1,0:T(8,128)(2,1)}, u32[]{:S(2)}, u32[]{:S(2)}) collective-permute-start(bf16[32,4800]{1,0:T(8,128)(2,1)} %get-tuple-element.30.refs_0_), channel_id=1, source_target_pairs={{0,1},{1,0},{2,3},{3,2},{4,5},{5,4},{6,7},{7,6},{8,9},{9,8},{10,11... | collective-permute-start | bytes 921608 | tf_op jit(solution)/shard_map/ppermute | solution.py:248
  44.6 47.6 %copy-start.16 = (bf16[32,4800]{1,0:T(8,128)(2,1)}, bf16[32,4800]{1,0:T(8,128)(2,1)S(1)}, u32[]{:S(2)}) copy-start(bf16[32,4800]{1,0:T(8,128)(2,1)S(1)} %collective-permute-done.27.refs_2_) | copy-start | bytes 921604
  44.6 16.0 %collective-permute-start.14 = (bf16[32,4800]{1,0:T(8,128)(2,1)}, bf16[32,4800]{1,0:T(8,128)(2,1)S(1)}, u32[]{:S(2)}, u32[]{:S(2)}) collective-permute-start(bf16[32,4800]{1,0:T(8,128)(2,1)} %get-tuple-element.30.refs_0_), channel_id=1, source_target_pairs={{0,2},{1,3},{2,0},{3,1},{4,6},{5,7},{6,4},{7,5},{8,10},{9,11},{10,... | collective-permute-start | bytes 921608 | tf_op jit(solution)/shard_map/ppermute | solution.py:248
  46.2 46.1 %copy-start.17 = (bf16[32,4800]{1,0:T(8,128)(2,1)}, bf16[32,4800]{1,0:T(8,128)(2,1)S(1)}, u32[]{:S(2)}) copy-start(bf16[32,4800]{1,0:T(8,128)(2,1)S(1)} %collective-permute-done.28.refs_3_) | copy-start | bytes 921604
  46.2 16.0 %collective-permute-start.15 = (bf16[32,4800]{1,0:T(8,128)(2,1)}, bf16[32,4800]{1,0:T(8,128)(2,1)S(1)}, u32[]{:S(2)}, u32[]{:S(2)}) collective-permute-start(bf16[32,4800]{1,0:T(8,128)(2,1)} %get-tuple-element.30.refs_0_), channel_id=1, source_target_pairs={{0,3},{1,2},{2,1},{3,0},{4,7},{5,6},{6,5},{7,4},{8,11},{9,10},{10,... | collective-permute-start | bytes 921608 | tf_op jit(solution)/shard_map/ppermute | solution.py:248
  54.4 69.5 %copy-start.7 = (bf16[32,4800]{1,0:T(8,128)(2,1)}, bf16[32,4800]{1,0:T(8,128)(2,1)S(1)}, u32[]{:S(2)}) copy-start(bf16[32,4800]{1,0:T(8,128)(2,1)S(1)} %collective-permute-done.16.refs_1_) | copy-start | bytes 921604
  54.4 16.3 %collective-permute-start.3 = (bf16[32,4800]{1,0:T(8,128)(2,1)}, bf16[32,4800]{1,0:T(8,128)(2,1)S(1)}, u32[]{:S(2)}, u32[]{:S(2)}) collective-permute-start(bf16[32,4800]{1,0:T(8,128)(2,1)} %get-tuple-element.25.refs_0_), channel_id=1, source_target_pairs={{0,8},{4,12},{8,0},{12,4},{16,24},{20,28},{24,16},{28,20},{1,9},{5... | collective-permute-start | bytes 921608 | tf_op jit(solution)/shard_map/ppermute | solution.py:251
  57.7 66.3 %copy-start.8 = (bf16[32,4800]{1,0:T(8,128)(2,1)}, bf16[32,4800]{1,0:T(8,128)(2,1)S(1)}, u32[]{:S(2)}) copy-start(bf16[32,4800]{1,0:T(8,128)(2,1)S(1)} %collective-permute-done.17.refs_2_) | copy-start | bytes 921604
  57.7 34.5 %collective-permute-start.44 = (bf16[32,4800]{1,0:T(8,128)(2,1)S(1)}, bf16[32,4800]{1,0:T(8,128)(2,1)S(1)}, u32[]{:S(2)}, u32[]{:S(2)}) collective-permute-start(bf16[32,4800]{1,0:T(8,128)(2,1)S(1)} %collective-permute-done.42.refs_1_), channel_id=1, source_target_pairs={{0,16},{4,20},{8,24},{12,28},{16,0},{20,4},{24,8},{28,12},{1,17},{... | collective-permute-start | bytes 921608 | tf_op jit(solution)/shard_map/ppermute | solution.py:251
  57.7 47.9 %collective-permute-start.4 = (bf16[32,4800]{1,0:T(8,128)(2,1)}, bf16[32,4800]{1,0:T(8,128)(2,1)S(1)}, u32[]{:S(2)}, u32[]{:S(2)}) collective-permute-start(bf16[32,4800]{1,0:T(8,128)(2,1)} %get-tuple-element.25.refs_0_), channel_id=1, source_target_pairs={{0,16},{4,20},{8,24},{12,28},{16,0},{20,4},{24,8},{28,12},{1,17},{... | collective-permute-start | bytes 921608 | tf_op jit(solution)/shard_map/ppermute | solution.py:251
  60.6 45.0 %collective-permute-start = (bf16[32,4800]{1,0:T(8,128)(2,1)}, bf16[32,4800]{1,0:T(8,128)(2,1)}, u32[]{:S(2)}, u32[]{:S(2)}) collective-permute-start(bf16[32,4800]{1,0:T(8,128)(2,1)} %get-tuple-element.25.refs_0_), channel_id=1, source_target_pairs={{0,1},{1,0},{2,3},{3,2},{4,5},{5,4},{6,7},{7,6},{8,9},{9,8},{10,11... | collective-permute-start | bytes 921608 | tf_op jit(solution)/shard_map/ppermute | solution.py:248
  62.2 45.0 %collective-permute-start.1 = (bf16[32,4800]{1,0:T(8,128)(2,1)}, bf16[32,4800]{1,0:T(8,128)(2,1)}, u32[]{:S(2)}, u32[]{:S(2)}) collective-permute-start(bf16[32,4800]{1,0:T(8,128)(2,1)} %get-tuple-element.25.refs_0_), channel_id=1, source_target_pairs={{0,2},{1,3},{2,0},{3,1},{4,6},{5,7},{6,4},{7,5},{8,10},{9,11},{10,... | collective-permute-start | bytes 921608 | tf_op jit(solution)/shard_map/ppermute | solution.py:248
  70.7 80.3 %copy-start.1 = (bf16[32,4800]{1,0:T(8,128)(2,1)}, bf16[32,4800]{1,0:T(8,128)(2,1)S(1)}, u32[]{:S(2)}) copy-start(bf16[32,4800]{1,0:T(8,128)(2,1)S(1)} %collective-permute-done.3.refs_1_) | copy-start | bytes 921604
  70.7 44.9 %collective-permute-start.31 = (bf16[32,4800]{1,0:T(8,128)(2,1)S(1)}, bf16[32,4800]{1,0:T(8,128)(2,1)S(1)}, u32[]{:S(2)}, u32[]{:S(2)}) collective-permute-start(bf16[32,4800]{1,0:T(8,128)(2,1)S(1)} %collective-permute-done.29.refs_1_), channel_id=1, source_target_pairs={{0,16},{4,20},{8,24},{12,28},{16,0},{20,4},{24,8},{28,12},{1,17},{... | collective-permute-start | bytes 921608 | tf_op jit(solution)/shard_map/ppermute | solution.py:251
  92.3 29.1 %collective-permute-start.18 = (bf16[32,4800]{1,0:T(8,128)(2,1)S(1)}, bf16[32,4800]{1,0:T(8,128)(2,1)S(1)}, u32[]{:S(2)}, u32[]{:S(2)}) collective-permute-start(bf16[32,4800]{1,0:T(8,128)(2,1)S(1)} %collective-permute-done.16.refs_1_), channel_id=1, source_target_pairs={{0,16},{4,20},{8,24},{12,28},{16,0},{20,4},{24,8},{28,12},{1,17},{... | collective-permute-start | bytes 921608 | tf_op jit(solution)/shard_map/ppermute | solution.py:251
  105.6 45.4 %copy-start.2 = (bf16[32,4800]{1,0:T(8,128)(2,1)}, bf16[32,4800]{1,0:T(8,128)(2,1)S(1)}, u32[]{:S(2)}) copy-start(bf16[32,4800]{1,0:T(8,128)(2,1)S(1)} %collective-permute-done.4.refs_2_) | copy-start | bytes 921604
  105.6 20.9 %collective-permute-start.5 = (bf16[32,4800]{1,0:T(8,128)(2,1)S(1)}, bf16[32,4800]{1,0:T(8,128)(2,1)S(1)}, u32[]{:S(2)}, u32[]{:S(2)}) collective-permute-start(bf16[32,4800]{1,0:T(8,128)(2,1)S(1)} %collective-permute-done.3.refs_1_), channel_id=1, source_target_pairs={{0,16},{4,20},{8,24},{12,28},{16,0},{20,4},{24,8},{28,12},{1,17},{... | collective-permute-start | bytes 921608 | tf_op jit(solution)/shard_map/ppermute | solution.py:251
  105.6 22.5 %collective-permute-start.45 = (bf16[32,4800]{1,0:T(8,128)(2,1)}, bf16[32,4800]{1,0:T(8,128)(2,1)S(1)}, u32[]{:S(2)}, u32[]{:S(2)}) collective-permute-start(bf16[32,4800]{1,0:T(8,128)(2,1)} %get-tuple-element.42), channel_id=1, source_target_pairs={{0,1},{1,0},{2,3},{3,2},{4,5},{5,4},{6,7},{7,6},{8,9},{9,8},{10,11... | collective-permute-start | bytes 921608 | tf_op jit(solution)/shard_map/ppermute | solution.py:248
  107.2 22.5 %collective-permute-start.46 = (bf16[32,4800]{1,0:T(8,128)(2,1)}, bf16[32,4800]{1,0:T(8,128)(2,1)}, u32[]{:S(2)}, u32[]{:S(2)}) collective-permute-start(bf16[32,4800]{1,0:T(8,128)(2,1)} %get-tuple-element.43), channel_id=1, source_target_pairs={{0,2},{1,3},{2,0},{3,1},{4,6},{5,7},{6,4},{7,5},{8,10},{9,11},{10,... | collective-permute-start | bytes 921608 | tf_op jit(solution)/shard_map/ppermute | solution.py:248
  115.6 14.5 %collective-permute-start.47 = (bf16[32,4800]{1,0:T(8,128)(2,1)}, bf16[32,4800]{1,0:T(8,128)(2,1)}, u32[]{:S(2)}, u32[]{:S(2)}) collective-permute-start(bf16[32,4800]{1,0:T(8,128)(2,1)} %get-tuple-element.44), channel_id=1, source_target_pairs={{0,3},{1,2},{2,1},{3,0},{4,7},{5,6},{6,5},{7,4},{8,11},{9,10},{10,... | collective-permute-start | bytes 921608 | tf_op jit(solution)/shard_map/ppermute | solution.py:248
  121.3 8.8 %collective-permute-start.48 = (bf16[32,4800]{1,0:T(8,128)(2,1)}, bf16[32,4800]{1,0:T(8,128)(2,1)S(1)}, u32[]{:S(2)}, u32[]{:S(2)}) collective-permute-start(bf16[32,4800]{1,0:T(8,128)(2,1)} %get-tuple-element.41.refs_4_), channel_id=1, source_target_pairs={{0,4},{4,0},{8,12},{12,8},{16,20},{20,16},{24,28},{28,24},{1,5},{5... | collective-permute-start | bytes 921608 | tf_op jit(solution)/shard_map/ppermute | solution.py:254
  126.5 10.5 %collective-permute-start.32 = (bf16[32,4800]{1,0:T(8,128)(2,1)}, bf16[32,4800]{1,0:T(8,128)(2,1)S(1)}, u32[]{:S(2)}, u32[]{:S(2)}) collective-permute-start(bf16[32,4800]{1,0:T(8,128)(2,1)} %get-tuple-element.37), channel_id=1, source_target_pairs={{0,1},{1,0},{2,3},{3,2},{4,5},{5,4},{6,7},{7,6},{8,9},{9,8},{10,11... | collective-permute-start | bytes 921608 | tf_op jit(solution)/shard_map/ppermute | solution.py:248
  128.1 16.3 %collective-permute-start.33 = (bf16[32,4800]{1,0:T(8,128)(2,1)}, bf16[32,4800]{1,0:T(8,128)(2,1)S(1)}, u32[]{:S(2)}, u32[]{:S(2)}) collective-permute-start(bf16[32,4800]{1,0:T(8,128)(2,1)} %get-tuple-element.38), channel_id=1, source_target_pairs={{0,2},{1,3},{2,0},{3,1},{4,6},{5,7},{6,4},{7,5},{8,10},{9,11},{10,... | collective-permute-start | bytes 921608 | tf_op jit(solution)/shard_map/ppermute | solution.py:248
  129.7 16.4 %collective-permute-start.34 = (bf16[32,4800]{1,0:T(8,128)(2,1)}, bf16[32,4800]{1,0:T(8,128)(2,1)S(1)}, u32[]{:S(2)}, u32[]{:S(2)}) collective-permute-start(bf16[32,4800]{1,0:T(8,128)(2,1)} %get-tuple-element.39), channel_id=1, source_target_pairs={{0,3},{1,2},{2,1},{3,0},{4,7},{5,6},{6,5},{7,4},{8,11},{9,10},{10,... | collective-permute-start | bytes 921608 | tf_op jit(solution)/shard_map/ppermute | solution.py:248
  130.1 16.1 %collective-permute-start.35 = (bf16[32,4800]{1,0:T(8,128)(2,1)}, bf16[32,4800]{1,0:T(8,128)(2,1)S(1)}, u32[]{:S(2)}, u32[]{:S(2)}) collective-permute-start(bf16[32,4800]{1,0:T(8,128)(2,1)} %get-tuple-element.36.refs_4_), channel_id=1, source_target_pairs={{0,4},{4,0},{8,12},{12,8},{16,20},{20,16},{24,28},{28,24},{1,5},{5... | collective-permute-start | bytes 921608 | tf_op jit(solution)/shard_map/ppermute | solution.py:254
  130.1 20.3 %collective-permute-start.19 = (bf16[32,4800]{1,0:T(8,128)(2,1)}, bf16[32,4800]{1,0:T(8,128)(2,1)S(1)}, u32[]{:S(2)}, u32[]{:S(2)}) collective-permute-start(bf16[32,4800]{1,0:T(8,128)(2,1)} %get-tuple-element.32), channel_id=1, source_target_pairs={{0,1},{1,0},{2,3},{3,2},{4,5},{5,4},{6,7},{7,6},{8,9},{9,8},{10,11... | collective-permute-start | bytes 921608 | tf_op jit(solution)/shard_map/ppermute | solution.py:248
  137.0 41.4 %copy-start.21 = (bf16[32,4800]{1,0:T(8,128)(2,1)}, bf16[32,4800]{1,0:T(8,128)(2,1)S(1)}, u32[]{:S(2)}) copy-start(bf16[32,4800]{1,0:T(8,128)(2,1)S(1)} %collective-permute-done.32.refs_5_) | copy-start | bytes 921604
  137.0 20.7 %collective-permute-start.20 = (bf16[32,4800]{1,0:T(8,128)(2,1)}, bf16[32,4800]{1,0:T(8,128)(2,1)S(1)}, u32[]{:S(2)}, u32[]{:S(2)}) collective-permute-start(bf16[32,4800]{1,0:T(8,128)(2,1)} %get-tuple-element.33), channel_id=1, source_target_pairs={{0,2},{1,3},{2,0},{3,1},{4,6},{5,7},{6,4},{7,5},{8,10},{9,11},{10,... | collective-permute-start | bytes 921608 | tf_op jit(solution)/shard_map/ppermute | solution.py:248
  144.4 13.4 %collective-permute-start.21 = (bf16[32,4800]{1,0:T(8,128)(2,1)}, bf16[32,4800]{1,0:T(8,128)(2,1)S(1)}, u32[]{:S(2)}, u32[]{:S(2)}) collective-permute-start(bf16[32,4800]{1,0:T(8,128)(2,1)} %get-tuple-element.34), channel_id=1, source_target_pairs={{0,3},{1,2},{2,1},{3,0},{4,7},{5,6},{6,5},{7,4},{8,11},{9,10},{10,... | collective-permute-start | bytes 921608 | tf_op jit(solution)/shard_map/ppermute | solution.py:248
  146.1 12.9 %collective-permute-start.49 = (bf16[32,4800]{1,0:T(8,128)(2,1)S(1)}, bf16[32,4800]{1,0:T(8,128)(2,1)}, u32[]{:S(2)}, u32[]{:S(2)}) collective-permute-start(bf16[32,4800]{1,0:T(8,128)(2,1)S(1)} %collective-permute-done.45.refs_5_), channel_id=1, source_target_pairs={{0,4},{4,0},{8,12},{12,8},{16,20},{20,16},{24,28},{28,24},{1,5},{5... | collective-permute-start | bytes 921608 | tf_op jit(solution)/shard_map/ppermute | solution.py:254
  146.2 12.9 %collective-permute-start.50 = (bf16[32,4800]{1,0:T(8,128)(2,1)}, bf16[32,4800]{1,0:T(8,128)(2,1)}, u32[]{:S(2)}, u32[]{:S(2)}) collective-permute-start(bf16[32,4800]{1,0:T(8,128)(2,1)} %collective-permute-done.46.refs_6_), channel_id=1, source_target_pairs={{0,4},{4,0},{8,12},{12,8},{16,20},{20,16},{24,28},{28,24},{1,5},{5... | collective-permute-start | bytes 921608 | tf_op jit(solution)/shard_map/ppermute | solution.py:254
  150.4 9.2 %collective-permute-start.51 = (bf16[32,4800]{1,0:T(8,128)(2,1)}, bf16[32,4800]{1,0:T(8,128)(2,1)}, u32[]{:S(2)}, u32[]{:S(2)}) collective-permute-start(bf16[32,4800]{1,0:T(8,128)(2,1)} %collective-permute-done.47.refs_7_), channel_id=1, source_target_pairs={{0,4},{4,0},{8,12},{12,8},{16,20},{20,16},{24,28},{28,24},{1,5},{5... | collective-permute-start | bytes 921608 | tf_op jit(solution)/shard_map/ppermute | solution.py:254
  157.7 20.7 %collective-permute-start.22 = (bf16[32,4800]{1,0:T(8,128)(2,1)}, bf16[32,4800]{1,0:T(8,128)(2,1)S(1)}, u32[]{:S(2)}, u32[]{:S(2)}) collective-permute-start(bf16[32,4800]{1,0:T(8,128)(2,1)} %get-tuple-element.31.refs_4_), channel_id=1, source_target_pairs={{0,4},{4,0},{8,12},{12,8},{16,20},{20,16},{24,28},{28,24},{1,5},{5... | collective-permute-start | bytes 921608 | tf_op jit(solution)/shard_map/ppermute | solution.py:254
  157.8 21.7 %collective-permute-start.6 = (bf16[32,4800]{1,0:T(8,128)(2,1)}, bf16[32,4800]{1,0:T(8,128)(2,1)S(1)}, u32[]{:S(2)}, u32[]{:S(2)}) collective-permute-start(bf16[32,4800]{1,0:T(8,128)(2,1)} %get-tuple-element.27), channel_id=1, source_target_pairs={{0,1},{1,0},{2,3},{3,2},{4,5},{5,4},{6,7},{7,6},{8,9},{9,8},{10,11... | collective-permute-start | bytes 921608 | tf_op jit(solution)/shard_map/ppermute | solution.py:248
  159.0 21.9 %collective-permute-start.36 = (bf16[32,4800]{1,0:T(8,128)(2,1)S(1)}, bf16[32,4800]{1,0:T(8,128)(2,1)S(1)}, u32[]{:S(2)}, u32[]{:S(2)}) collective-permute-start(bf16[32,4800]{1,0:T(8,128)(2,1)S(1)} %collective-permute-done.32.refs_5_), channel_id=1, source_target_pairs={{0,4},{4,0},{8,12},{12,8},{16,20},{20,16},{24,28},{28,24},{1,5},{5... | collective-permute-start | bytes 921608 | tf_op jit(solution)/shard_map/ppermute | solution.py:254
  159.0 22.0 %collective-permute-start.37 = (bf16[32,4800]{1,0:T(8,128)(2,1)S(1)}, bf16[32,4800]{1,0:T(8,128)(2,1)S(1)}, u32[]{:S(2)}, u32[]{:S(2)}) collective-permute-start(bf16[32,4800]{1,0:T(8,128)(2,1)S(1)} %collective-permute-done.33.refs_6_), channel_id=1, source_target_pairs={{0,4},{4,0},{8,12},{12,8},{16,20},{20,16},{24,28},{28,24},{1,5},{5... | collective-permute-start | bytes 921608 | tf_op jit(solution)/shard_map/ppermute | solution.py:254
  159.5 22.1 %collective-permute-start.38 = (bf16[32,4800]{1,0:T(8,128)(2,1)S(1)}, bf16[32,4800]{1,0:T(8,128)(2,1)}, u32[]{:S(2)}, u32[]{:S(2)}) collective-permute-start(bf16[32,4800]{1,0:T(8,128)(2,1)S(1)} %collective-permute-done.34.refs_7_), channel_id=1, source_target_pairs={{0,4},{4,0},{8,12},{12,8},{16,20},{20,16},{24,28},{28,24},{1,5},{5... | collective-permute-start | bytes 921608 | tf_op jit(solution)/shard_map/ppermute | solution.py:254
  178.4 22.6 %collective-permute-start.7 = (bf16[32,4800]{1,0:T(8,128)(2,1)S(1)}, bf16[32,4800]{1,0:T(8,128)(2,1)S(1)}, u32[]{:S(2)}, u32[]{:S(2)}) collective-permute-start(bf16[32,4800]{1,0:T(8,128)(2,1)S(1)} %copy-done.33), channel_id=1, source_target_pairs={{0,2},{1,3},{2,0},{3,1},{4,6},{5,7},{6,4},{7,5},{8,10},{9,11},{10,... | collective-permute-start | bytes 921608 | tf_op jit(solution)/shard_map/ppermute | solution.py:248
  179.5 23.1 %collective-permute-start.8 = (bf16[32,4800]{1,0:T(8,128)(2,1)S(1)}, bf16[32,4800]{1,0:T(8,128)(2,1)S(1)}, u32[]{:S(2)}, u32[]{:S(2)}) collective-permute-start(bf16[32,4800]{1,0:T(8,128)(2,1)S(1)} %copy-done.31), channel_id=1, source_target_pairs={{0,3},{1,2},{2,1},{3,0},{4,7},{5,6},{6,5},{7,4},{8,11},{9,10},{10,... | collective-permute-start | bytes 921608 | tf_op jit(solution)/shard_map/ppermute | solution.py:248
  181.0 21.9 %collective-permute-start.23 = (bf16[32,4800]{1,0:T(8,128)(2,1)S(1)}, bf16[32,4800]{1,0:T(8,128)(2,1)S(1)}, u32[]{:S(2)}, u32[]{:S(2)}) collective-permute-start(bf16[32,4800]{1,0:T(8,128)(2,1)S(1)} %collective-permute-done.19.refs_5_), channel_id=1, source_target_pairs={{0,4},{4,0},{8,12},{12,8},{16,20},{20,16},{24,28},{28,24},{1,5},{5... | collective-permute-start | bytes 921608 | tf_op jit(solution)/shard_map/ppermute | solution.py:254
  181.1 22.2 %collective-permute-start.24 = (bf16[32,4800]{1,0:T(8,128)(2,1)S(1)}, bf16[32,4800]{1,0:T(8,128)(2,1)S(1)}, u32[]{:S(2)}, u32[]{:S(2)}) collective-permute-start(bf16[32,4800]{1,0:T(8,128)(2,1)S(1)} %collective-permute-done.20.refs_6_), channel_id=1, source_target_pairs={{0,4},{4,0},{8,12},{12,8},{16,20},{20,16},{24,28},{28,24},{1,5},{5... | collective-permute-start | bytes 921608 | tf_op jit(solution)/shard_map/ppermute | solution.py:254
  181.6 21.8 %collective-permute-start.25 = (bf16[32,4800]{1,0:T(8,128)(2,1)S(1)}, bf16[32,4800]{1,0:T(8,128)(2,1)S(1)}, u32[]{:S(2)}, u32[]{:S(2)}) collective-permute-start(bf16[32,4800]{1,0:T(8,128)(2,1)S(1)} %collective-permute-done.21.refs_7_), channel_id=1, source_target_pairs={{0,4},{4,0},{8,12},{12,8},{16,20},{20,16},{24,28},{28,24},{1,5},{5... | collective-permute-start | bytes 921608 | tf_op jit(solution)/shard_map/ppermute | solution.py:254
  201.0 22.3 %collective-permute-start.2 = (bf16[32,4800]{1,0:T(8,128)(2,1)S(1)}, bf16[32,4800]{1,0:T(8,128)(2,1)S(1)}, u32[]{:S(2)}, u32[]{:S(2)}) collective-permute-start(bf16[32,4800]{1,0:T(8,128)(2,1)S(1)} %copy-done), channel_id=1, source_target_pairs={{0,3},{1,2},{2,1},{3,0},{4,7},{5,6},{6,5},{7,4},{8,11},{9,10},{10,... | collective-permute-start | bytes 921608 | tf_op jit(solution)/shard_map/ppermute | solution.py:248
  202.7 20.7 %collective-permute-start.9 = (bf16[32,4800]{1,0:T(8,128)(2,1)S(1)}, bf16[32,4800]{1,0:T(8,128)(2,1)S(1)}, u32[]{:S(2)}, u32[]{:S(2)}) collective-permute-start(bf16[32,4800]{1,0:T(8,128)(2,1)S(1)} %copy-done.27), channel_id=1, source_target_pairs={{0,4},{4,0},{8,12},{12,8},{16,20},{20,16},{24,28},{28,24},{1,5},{5... | collective-permute-start | bytes 921608 | tf_op jit(solution)/shard_map/ppermute | solution.py:254
  202.9 20.5 %collective-permute-start.10 = (bf16[32,4800]{1,0:T(8,128)(2,1)S(1)}, bf16[32,4800]{1,0:T(8,128)(2,1)S(1)}, u32[]{:S(2)}, u32[]{:S(2)}) collective-permute-start(bf16[32,4800]{1,0:T(8,128)(2,1)S(1)} %collective-permute-done.6.refs_5_), channel_id=1, source_target_pairs={{0,4},{4,0},{8,12},{12,8},{16,20},{20,16},{24,28},{28,24},{1,5},{5... | collective-permute-start | bytes 921608 | tf_op jit(solution)/shard_map/ppermute | solution.py:254
  203.3 20.1 %collective-permute-start.11 = (bf16[32,4800]{1,0:T(8,128)(2,1)S(1)}, bf16[32,4800]{1,0:T(8,128)(2,1)S(1)}, u32[]{:S(2)}, u32[]{:S(2)}) collective-permute-start(bf16[32,4800]{1,0:T(8,128)(2,1)S(1)} %collective-permute-done.7.refs_6_), channel_id=1, source_target_pairs={{0,4},{4,0},{8,12},{12,8},{16,20},{20,16},{24,28},{28,24},{1,5},{5... | collective-permute-start | bytes 921608 | tf_op jit(solution)/shard_map/ppermute | solution.py:254
  203.5 19.9 %collective-permute-start.12 = (bf16[32,4800]{1,0:T(8,128)(2,1)S(1)}, bf16[32,4800]{1,0:T(8,128)(2,1)S(1)}, u32[]{:S(2)}, u32[]{:S(2)}) collective-permute-start(bf16[32,4800]{1,0:T(8,128)(2,1)S(1)} %collective-permute-done.8.refs_7_), channel_id=1, source_target_pairs={{0,4},{4,0},{8,12},{12,8},{16,20},{20,16},{24,28},{28,24},{1,5},{5... | collective-permute-start | bytes 921608 | tf_op jit(solution)/shard_map/ppermute | solution.py:254
  (32 other events, 416.1 us)

commit v2 on v1

--- a/solution.py
+++ b/solution.py
@@ -32,7 +32,7 @@
     return jnp.dot(left, right, preferred_element_type=jnp.float32)
 
 
-def whiten_kernel(chunk_len, taps_ref, traces_ref, flags_ref, *out_refs):
+def whiten_kernel(starts, taps_ref, traces_ref, flags_ref, *out_refs):
     rows, record_len = traces_ref.shape
     blocks = record_len // LANES
     traces = traces_ref[...]
@@ -91,19 +91,17 @@
     inside = jnp.where((sample >= first) & (sample < first + SAMP), 1.0, 0.0).astype(jnp.bfloat16)
     kept = dot_f32(flags_ref[...].astype(jnp.float32).astype(jnp.bfloat16), inside)
     flat = (flat * kept).astype(jnp.bfloat16)
-    for index, out_ref in enumerate(out_refs):
-        out_ref[...] = flat[:, index * chunk_len : (index + 1) * chunk_len]
-
-
-def whiten(traces, fir_taps, seg_flags, chunk_count):
-    rows, record_len = traces.shape
-    chunk_len = record_len // chunk_count
+    for start, out_ref in zip(starts, out_refs):
+        out_ref[...] = flat[:, start : start + out_ref.shape[1]]
+
+
+def whiten(traces, fir_taps, seg_flags, spans):
     vmem = pl.BlockSpec(memory_space=pltpu.VMEM)
     return pl.pallas_call(
-        functools.partial(whiten_kernel, chunk_len),
+        functools.partial(whiten_kernel, [start for start, _ in spans]),
         in_specs=[pl.BlockSpec(memory_space=pltpu.SMEM), vmem, vmem],
-        out_specs=[vmem] * chunk_count,
-        out_shape=[jax.ShapeDtypeStruct((rows, chunk_len), jnp.bfloat16)] * chunk_count,
+        out_specs=[vmem] * len(spans),
+        out_shape=[jax.ShapeDtypeStruct((traces.shape[0], length), jnp.bfloat16) for _, length in spans],
         compiler_params=pltpu.CompilerParams(vmem_limit_bytes=vmem_bytes),
         name="whiten",
     )(fir_taps, traces, seg_flags)
@@ -119,44 +117,56 @@
                 out_ref[...] = source[...]
 
 
-def route(place, pieces):
-    vmem = pl.BlockSpec(memory_space=pltpu.VMEM)
+def route(place, parts, rows):
+    length = parts[0][0].shape[1]
+    kind = parts[0][0].dtype
     return pl.pallas_call(
         route_kernel,
-        in_specs=[pl.BlockSpec(memory_space=pltpu.SMEM)] + [vmem] * len(pieces),
-        out_specs=[vmem] * len(pieces),
-        out_shape=[jax.ShapeDtypeStruct(p.shape, p.dtype) for p in pieces],
+        grid=(1,),
+        in_specs=[pl.BlockSpec(memory_space=pltpu.SMEM)]
+        + [pl.BlockSpec((rows, length), functools.partial(lambda at, step: (at, 0), at)) for _, at in parts],
+        out_specs=[pl.BlockSpec((rows, length), lambda step: (0, 0))] * len(parts),
+        out_shape=[jax.ShapeDtypeStruct((rows, length), kind)] * len(parts),
         compiler_params=pltpu.CompilerParams(vmem_limit_bytes=vmem_bytes),
         name="route",
-    )(place, *pieces)
-
-
-def correlate_kernel(seg_count, sides, has_total, last, scale, place_ref, *refs):
-    refs = list(refs)
-    left = [refs.pop(0) for _ in range(seg_count)]
-    right = [refs.pop(0) for _ in range(seg_count * sides)]
-    total_ref = refs.pop(0) if has_total else None
-    mask_ref = refs.pop(0) if last else None
-    out_ref, moved, columns, shifted = refs[:4]
-    piece_rows, chunk_len = left[0].shape
+    )(place, *[array for array, _ in parts])
+
+
+def correlate_kernel(start, left_count, has_total, last, scale, place_ref, *refs):
+    lefts, refs = refs[:left_count], list(refs[left_count:])
+    piece_rows, chunk_len = refs[0].shape
+    staged = refs.pop() if piece_rows % 16 else None
+    *refs, out_ref, moved, columns, shifted, sems = refs
+    staged = columns if staged is None else staged
+    mask_ref = refs.pop() if last else None
+    total_ref = refs.pop() if has_total else None
     row_count, padded_len = moved.shape
     step = pl.program_id(0)
+    begin = start // LANES * LANES
 
     @pl.when(step == 0)
     def _():
+        copies = [
+            pltpu.make_async_copy(
+                left.at[:, pl.ds(begin, padded_len)],
+                moved.at[pl.ds(index * left.shape[0], left.shape[0])],
+                sems.at[index],
+            )
+            for index, left in enumerate(lefts)
+        ]
+        for copy in copies:
+            copy.start()
         edge = chunk_len // LANES * LANES
         if padded_len > chunk_len:
-            moved[:, edge:] = jnp.zeros((row_count, padded_len - edge), moved.dtype)
             columns[:, edge:] = jnp.zeros((columns.shape[0], padded_len - edge), columns.dtype)
-        for index, piece in enumerate(left):
-            moved[index * piece_rows : (index + 1) * piece_rows, :chunk_len] = piece[...]
-        staged = refs[4] if len(refs) > 4 else columns
-        for index, piece in enumerate(right):
-            at = pl.multiple_of(place_ref[seg_count + index] * piece_rows, piece_rows)
+        for index, piece in enumerate(refs):
+            at = pl.multiple_of(place_ref[index] * piece_rows, piece_rows)
             staged[pl.ds(at, piece_rows), :chunk_len] = piece[...].astype(staged.dtype)
-        if len(refs) > 4:
+        if staged is not columns:
             columns[:, :chunk_len] = staged[:, :chunk_len].astype(columns.dtype)
-        moved[...] = pltpu.roll(moved[...], padded_len - HALF_LAG, 1)
+        for copy in copies:
+            copy.wait()
+        moved[...] = pltpu.roll(moved[...], padded_len - HALF_LAG - (start - begin), 1)
 
     sample = lax.broadcasted_iota(jnp.int32, (16, padded_len), 1)
     phase = sample
@@ -180,21 +190,23 @@
     if not last:
         out_ref[...] = product
         return
-    for index in range(seg_count):
-        at = pl.ds(pl.multiple_of(place_ref[index] * piece_rows, piece_rows), piece_rows)
+    for index, left in enumerate(lefts):
+        rows = left.shape[0]
+        at = pl.ds(pl.multiple_of(place_ref[len(refs) + index] * rows, rows), rows)
         weight = mask_ref[at, :].astype(jnp.float32) * scale
-        out_ref[:, at, :] = product[:, index * piece_rows : (index + 1) * piece_rows] * weight[None]
-
-
-def correlate(place, left, right, total, mask, last, scale):
-    seg_count = len(left)
-    piece_rows, chunk_len = left[0].shape
-    rows, cols = seg_count * piece_rows, len(right) * piece_rows
+        out_ref[:, at, :] = product[:, index * rows : (index + 1) * rows] * weight[None]
+
+
+def correlate(place, lefts, start, right, total, mask, last, scale):
+    rows = sum(left.shape[0] for left in lefts)
+    piece_rows, chunk_len = right[0].shape
+    cols = len(right) * piece_rows
     padded_len = pl.cdiv(chunk_len, LANES) * LANES
     whole = pl.BlockSpec((piece_rows, chunk_len), lambda step: (0, 0))
     block = pl.BlockSpec((lag_group, rows, cols), lambda step: (step, 0, 0))
-    operands, specs = [place, *left, *right], [pl.BlockSpec(memory_space=pltpu.SMEM)]
-    specs += [whole] * (len(left) + len(right))
+    operands = [place, *lefts, *right]
+    specs = [pl.BlockSpec(memory_space=pltpu.SMEM)] + [pl.BlockSpec(memory_space=pl.ANY)] * len(lefts)
+    specs += [whole] * len(right)
     aliases = {}
     if total is not None:
         aliases = {len(operands): 0}
@@ -207,13 +219,12 @@
         pltpu.VMEM((rows, padded_len), jnp.bfloat16),
         pltpu.VMEM((cols, padded_len), jnp.bfloat16),
         pltpu.VMEM((lag_group * rows, padded_len), jnp.bfloat16),
+        pltpu.SemaphoreType.DMA((len(lefts),)),
     ]
     if piece_rows % 16:
         scratch.append(pltpu.VMEM((cols, padded_len), jnp.float32))
     return pl.pallas_call(
-        functools.partial(
-            correlate_kernel, seg_count, len(right) // seg_count, total is not None, last, scale
-        ),
+        functools.partial(correlate_kernel, start, len(lefts), total is not None, last, scale),
         grid=(pl.cdiv(LAGS, lag_group),),
         in_specs=specs,
         out_specs=block,
@@ -221,11 +232,6 @@
         input_output_aliases=aliases,
         scratch_shapes=scratch,
         compiler_params=pltpu.CompilerParams(vmem_limit_bytes=vmem_bytes),
-        cost_estimate=pl.CostEstimate(
-            flops=2 * LAGS * rows * cols * chunk_len,
-            bytes_accessed=8 * LAGS * rows * cols + 2 * (rows + cols) * chunk_len,
-            transcendentals=0,
-        ),
         name="correlate",
     )(*operands)
 
@@ -236,13 +242,12 @@
     stn, seg = lax.axis_index("stn"), lax.axis_index("seg")
     plane, side = stn // sides, stn % sides
     segments = seg_flags.shape[1]
-    chunk_count = segments // chunk_segs
+    count = segments // chunk_segs
     scale = 1.0 / math.sqrt(SAMP * segments)
     partner = jnp.stack([seg ^ k for k in range(seg_count)]).astype(jnp.int32)
     route_place = plane ^ partner
-    place = jnp.concatenate(
-        [partner] + [(side ^ j) * seg_count + partner for j in range(sides)]
-    ).astype(jnp.int32)
+    rows = traces.shape[0]
+    place = [(side ^ j) * seg_count + partner for j in range(sides)]
 
     def to_seg(value, k):
         return lax.ppermute(value, "seg", [(i, i ^ k) for i in range(seg_count)])
@@ -253,20 +258,87 @@
     def to_side(value, j):
         return lax.ppermute(value, "stn", [(i, i ^ j) for i in range(stn_count)])
 
-    pieces = whiten(traces, fir_taps, seg_flags, chunk_count)
-    total = None
-    for index, piece in enumerate(pieces):
-        line = [piece]
-        for k in range(1, seg_count):
-            low = k & (k - 1)
-            line.append(to_plane(line[k ^ low] if low else piece, low or k))
-        left = [piece] + [to_seg(piece, k) for k in range(1, seg_count)]
-        routed = route(route_place, line)
-        own = [routed[0]] + [to_seg(routed[k], k) for k in range(1, seg_count)]
-        right = own + [to_side(value, j) for j in range(1, sides) for value in own]
-        last = index == chunk_count - 1
-        total = correlate(place, left, right, total, pair_mask, last, scale)
-    return total
+    length = chunk_segs * SAMP
+    record_len = traces.shape[1]
+    half_len = record_len // 2
+    spans = [(u * length, length) for u in range(count)] + [(0, half_len), (half_len, half_len)]
+    *units, early, late = whiten(traces, fir_taps, seg_flags, spans)
+    direct = [k for k in range(1, seg_count) if k & (k - 1) == 0][::-1]
+    passed = [k for k in range(1, seg_count) if k & (k - 1)]
+    gathered = rows % 16 > 0
+    place.append(jnp.zeros((1,), jnp.int32) if gathered else partner)
+    place = jnp.concatenate(place).astype(jnp.int32)
+
+    state = {("unit", u): unit for u, unit in enumerate(units)}
+    state["early", 0], state["late", 0] = early, late
+    lines = [{0: (("unit", u), 0)} for u in range(count)]
+
+    def fence():
+        names = list(state)
+        state.update(zip(names, lax.optimization_barrier([state[n] for n in names])))
+
+    def value(u, k):
+        name, at = lines[u][k]
+        return state[name][at * rows : (at + 1) * rows] if at else state[name][:rows]
+
+    def hop(k, *moves):
+        sent = [value(u, slot ^ k) for u, slot in moves]
+        name = ("line", *moves)
+        state[name] = to_plane(jnp.concatenate(sent, axis=0) if len(sent) > 1 else sent[0], k)
+        for at, (u, slot) in enumerate(moves):
+            lines[u][slot] = name, at
+
+    def plane_hops(u):
+        ahead = u + 1 < count
+        if len(passed) == 1 and u >= 0:
+            if ahead:
+                hop(direct[0], (u + 1, direct[0]))
+            if u < count:
+                hop(direct[1], *([(u, passed[0])] + ([(u + 1, direct[1])] if ahead else [])))
+            return
+        for k in passed if 0 <= u < count else []:
+            hop(k & (k - 1), (u, k))
+        for k in direct if ahead else []:
+            hop(k, (u + 1, k))
+
+    def columns(u):
+        parts = [(state[lines[u][k][0]], lines[u][k][1]) for k in range(seg_count)]
+        for k, piece in enumerate(route(route_place, parts, rows)):
+            state["own", u, k] = to_seg(piece, k) if k else piece
+
+    def row_hops(name, which):
+        if not gathered:
+            for k in which:
+                state[name, k] = to_seg(state[name, 0], k)
+        elif which:
+            state[name, 0] = lax.all_gather(state[name, 0], "seg", axis=0, tiled=True)
+
+    def products(u):
+        name, start = ("early", u * length) if u < count // 2 else ("late", u * length - half_len)
+        lefts = [state[name, k] for k in range(1 if gathered else seg_count)]
+        own = [state.pop(("own", u, k)) for k in range(seg_count)]
+        right = own + [to_side(v, j) for j in range(1, sides) for v in own]
+        state["total"] = correlate(
+            place, lefts, start, right, state.pop("total", None), pair_mask, u == count - 1, scale
+        )
+
+    near, far = list(range(1, seg_count - 1)), [seg_count - 1]
+    plane_hops(-1)
+    row_hops("early", near)
+    for u in range(count + 2):
+        fence()
+        plane_hops(u)
+        if 1 <= u <= count:
+            columns(u - 1)
+        if u == 0:
+            row_hops("early", [] if gathered else far)
+            row_hops("late", near)
+        if u == count // 2 + 1:
+            row_hops("late", [] if gathered else far)
+        if 2 <= u <= count:
+            products(u - 2)
+    products(count - 1)
+    return state["total"]
 
 
 def solution(mesh):

time: 245 us -> 203 us (0.83)
  waiting for transfers between devices: 101 us -> 47.9 us
  Pallas kernels: 95.1 us -> 98.6 us
  local copies, waits for them, and re-layouts: 3.08 us -> 6.01 us
  other arithmetic: 0.6 us -> 3.51 us
    ppermute x12 -> x9, waiting for transfers between devices: 81.3 us -> 28.4 us  [to_plane(): lax.ppermute(value, 'stn', [(i, i ^ k * sides) for i in range(stn_count)])]
    ppermute x24 -> x18, starting transfers between devices: 32.4 us -> 23.6 us  [to_seg(): return lax.ppermute(value, 'seg', [(i, i ^ k) for i in range(seg_count)])]
    ppermute x12 -> x9, starting transfers between devices: 9.12 us -> 17.6 us  [to_plane(): lax.ppermute(value, 'stn', [(i, i ^ k * sides) for i in range(stn_count)])]
    pallas_call x9, Pallas kernels: 95.1 us -> 98.6 us  [the longest x4 79.4 us: correlate(): pl.pallas_call(functools.partial(correlate_kernel, start, len(lefts), tot...]
    unnamed x88 -> x90, local copies, waits for them, and re-layouts: 2.47 us -> 5.41 us
    concatenate x0 -> x3, other arithmetic: none -> 2.89 us  [hop(): jnp.concatenate(sent, axis=0)]
    ppermute x24 -> x18, waiting for transfers between devices: 19.4 us -> 17.5 us  [to_seg(): return lax.ppermute(value, 'seg', [(i, i ^ k) for i in range(seg_count)])]
  transfers between devices with their start and end apart: 52 -> 43, of which waited for: 17 -> 13; matrix products, arithmetic and copies ran while one was open for 0% -> 1% of each run, Pallas kernels for 28% -> 35%
where the time goes in v2:
time: 203 us; the launch traced here: 202 us
  Pallas kernels  98.6 us (49%)
  waiting for transfers between devices  47.9 us (24%)
  starting transfers between devices  45.4 us (22%)
  local copies, waits for them, and re-layouts  6.01 us (3%)
  other arithmetic  3.51 us (2%)
    pallas_call x4, Pallas kernels, correlate(): pl.pallas_call(functools.partial(correlate_kernel, start, len(lefts), tot...  79.4 us
    ppermute x9, waiting for transfers between devices, to_plane(): lax.ppermute(value, 'stn', [(i, i ^ k * sides) for i in range(stn_count)])  28.4 us
    ppermute x18, starting transfers between devices, to_seg(): return lax.ppermute(value, 'seg', [(i, i ^ k) for i in range(seg_count)])  23.6 us
    ppermute x9, starting transfers between devices, to_plane(): lax.ppermute(value, 'stn', [(i, i ^ k * sides) for i in range(stn_count)])  17.6 us
    ppermute x18, waiting for transfers between devices, to_seg(): return lax.ppermute(value, 'seg', [(i, i ^ k) for i in range(seg_count)])  17.5 us
    pallas_call x4, Pallas kernels, route(): pl.pallas_call(route_kernel, grid=(1,), in_specs=[pl.BlockSpec(memory_spa...  10.5 us
    pallas_call x1, Pallas kernels, whiten(): pl.pallas_call(functools.partial(whiten_kernel, [start for start, _ in sp...  8.75 us
    unnamed x90, local copies, waits for them, and re-layouts  5.41 us
  transfers between devices with their start and end apart: 43, of which 13 were waited for; matrix products, arithmetic and copies ran while one was open for 1% of the time, Pallas kernels for 35%

profile of v2, /device:TPU:0, one launch (start us, length us, event | category | flops | bytes accessed | tf_op | source)
XLA Modules:
  0.0 202.1 jit_solution(10273036979462903069)
XLA Ops:
  0.0 8.7 %whiten.1 = (bf16[32,4800]{1,0:T(8,128)(2,1)}, bf16[32,4800]{1,0:T(8,128)(2,1)}, bf16[32,4800]{1,0:T(8,128)(2,1)}, bf16[32,4800]{1,0:T(8,128)(2,1)}, bf16[32,9600]{1,0:T(8,128)(2,1)}, /*index=5*/bf16[32,9600]{1,0:T(8,128)(2,1)}) custom-call(f32[31]{0:T(128)} %taps_ref.1, f32[32,19200]{1,0:T(8,128)} %traces_ref.1, s32[32,32]{1,0:T(8,128)} %flags_ref.1), custom_call_target="tpu_custom_call" | custom-call | tf_op jit(solution)/shard_map/whiten/pallas_call | solution.py:100
  8.8 3.0 %collective-permute-start.2 = (bf16[32,9600]{1,0:T(8,128)(2,1)}, bf16[32,9600]{1,0:T(8,128)(2,1)}, u32[]{:S(2)}, u32[]{:S(2)}) collective-permute-start(bf16[32,9600]{1,0:T(8,128)(2,1)} %get-tuple-element.169.refs_0_), channel_id=1, source_target_pairs={{0,1},{1,0},{2,3},{3,2},{4,5},{5,4},{6,7},{7,6},{8,9},{9,8},{10,11... | collective-permute-start | bytes 1843208 | tf_op jit(solution)/shard_map/ppermute | solution.py:253
  11.8 1.5 collective-permute-start.3
  13.3 2.6 %collective-permute-start = (bf16[32,4800]{1,0:T(8,128)(2,1)}, bf16[32,4800]{1,0:T(8,128)(2,1)S(1)}, u32[]{:S(2)}, u32[]{:S(2)}) collective-permute-start(bf16[32,4800]{1,0:T(8,128)(2,1)} %get-tuple-element.126.refs_0_), channel_id=1, source_target_pairs={{0,16},{4,20},{8,24},{12,28},{16,0},{20,4},{24,8},{28,12},{1,17},{... | collective-permute-start | bytes 921608 | tf_op jit(solution)/shard_map/ppermute | solution.py:256
  15.9 1.6 collective-permute-start.1
  17.4 12.3 %collective-permute-done.refs_2_ = bf16[32,4800]{1,0:T(8,128)(2,1)S(1)} collective-permute-done((bf16[32,4800]{1,0:T(8,128)(2,1)}, bf16[32,4800]{1,0:T(8,128)(2,1)S(1)}, u32[]{:S(2)}, u32[]{:S(2)}) %collective-permute-start) | collective-permute-done | bytes 307232 | tf_op jit(solution)/shard_map/ppermute | solution.py:256
  29.9 0.7 copy-done.36
  30.6 1.0 pad_maximum_fusion
  31.7 1.5 collective-permute-start.5
  33.2 0.5 collective-permute-start.7
  33.7 0.5 collective-permute-start.8
  34.2 2.4 %collective-permute-start.6 = (bf16[32,9600]{1,0:T(8,128)(2,1)S(1)}, bf16[32,9600]{1,0:T(8,128)(2,1)}, u32[]{:S(2)}, u32[]{:S(2)}) collective-permute-start(bf16[32,9600]{1,0:T(8,128)(2,1)S(1)} %copy-done.7), channel_id=1, source_target_pairs={{0,3},{1,2},{2,1},{3,0},{4,7},{5,6},{6,5},{7,4},{8,11},{9,10},{10,... | collective-permute-start | bytes 1843208 | tf_op jit(solution)/shard_map/ppermute | solution.py:253
  36.7 2.4 %collective-permute-start.4 = (bf16[32,4800]{1,0:T(8,128)(2,1)}, bf16[32,4800]{1,0:T(8,128)(2,1)S(1)}, u32[]{:S(2)}, u32[]{:S(2)}) collective-permute-start(bf16[32,4800]{1,0:T(8,128)(2,1)} %get-tuple-element.145.refs_0_), channel_id=1, source_target_pairs={{0,16},{4,20},{8,24},{12,28},{16,0},{20,4},{24,8},{28,12},{1,17},{... | collective-permute-start | bytes 921608 | tf_op jit(solution)/shard_map/ppermute | solution.py:256
  39.0 13.5 %collective-permute-done.4.refs_2_ = bf16[32,4800]{1,0:T(8,128)(2,1)S(1)} collective-permute-done((bf16[32,4800]{1,0:T(8,128)(2,1)}, bf16[32,4800]{1,0:T(8,128)(2,1)S(1)}, u32[]{:S(2)}, u32[]{:S(2)}) %collective-permute-start.4) | collective-permute-done | bytes 307232 | tf_op jit(solution)/shard_map/ppermute | solution.py:256
  52.5 0.6 collective-permute-done.5.refs_3_.refs_1_
  53.2 8.0 %collective-permute-done.8.refs_2_ = bf16[32,9600]{1,0:T(8,128)(2,1)S(1)} collective-permute-done((bf16[32,9600]{1,0:T(8,128)(2,1)S(1)}, bf16[32,9600]{1,0:T(8,128)(2,1)S(1)}, u32[]{:S(2)}, u32[]{:S(2)}) %collective-permute-start.8) | collective-permute-done | bytes 614432 | tf_op jit(solution)/shard_map/ppermute | solution.py:253
  61.2 0.8 copy-done.5
  62.0 1.8 pad_maximum_fusion.1
  64.2 0.6 broadcast_xor_fusion
  64.8 2.5 %route.4 = (bf16[32,4800]{1,0:T(8,128)(2,1)}, bf16[32,4800]{1,0:T(8,128)(2,1)}, bf16[32,4800]{1,0:T(8,128)(2,1)}, bf16[32,4800]{1,0:T(8,128)(2,1)}) custom-call(s32[4]{0:T(128)} %get-tuple-element.215.place_ref, bf16[32,4800]{1,0:T(8,128)(2,1)} %get-tuple-element.126.refs_0_, bf16[32,4800]{1,0:T(8,128)(2,1)} %copy-done.36, bf16[32,4800]{1,0:T(8,128)(2,1)} %copy-done.12, ...), custom_call_target="tpu_custom_call" | custom-call | tf_op jit(solution)/shard_map/route/pallas_call | solution.py:123
  67.3 1.5 collective-permute-start.11
  68.8 0.5 collective-permute-start.12
  69.3 1.5 collective-permute-start.13
  70.8 3.3 %collective-permute-start.9 = (bf16[32,4800]{1,0:T(8,128)(2,1)S(1)}, bf16[32,4800]{1,0:T(8,128)(2,1)S(1)}, u32[]{:S(2)}, u32[]{:S(2)}) collective-permute-start(bf16[32,4800]{1,0:T(8,128)(2,1)S(1)} %copy-done.9), channel_id=1, source_target_pairs={{0,16},{4,20},{8,24},{12,28},{16,0},{20,4},{24,8},{28,12},{1,17},{... | collective-permute-start | bytes 921608 | tf_op jit(solution)/shard_map/ppermute | solution.py:256
  74.1 2.6 %collective-permute-done.11.refs_5_ = bf16[32,4800]{1,0:T(8,128)(2,1)S(1)} collective-permute-done((bf16[32,4800]{1,0:T(8,128)(2,1)}, bf16[32,4800]{1,0:T(8,128)(2,1)S(1)}, u32[]{:S(2)}, u32[]{:S(2)}) %collective-permute-start.11) | collective-permute-done | bytes 307232 | tf_op jit(solution)/shard_map/ppermute | solution.py:253
  76.7 5.0 %collective-permute-done.12.refs_6_ = bf16[32,4800]{1,0:T(8,128)(2,1)S(1)} collective-permute-done((bf16[32,4800]{1,0:T(8,128)(2,1)}, bf16[32,4800]{1,0:T(8,128)(2,1)S(1)}, u32[]{:S(2)}, u32[]{:S(2)}) %collective-permute-start.12) | collective-permute-done | bytes 307232 | tf_op jit(solution)/shard_map/ppermute | solution.py:253
  81.7 1.9 collective-permute-done.10.refs_3_.refs_1_
  83.6 0.5 collective-permute-start.20
  84.1 0.5 collective-permute-start.22
  84.7 4.4 %collective-permute-start.15 = (bf16[64,4800]{1,0:T(8,128)(2,1)S(1)}, bf16[64,4800]{1,0:T(8,128)(2,1)S(1)}, u32[]{:S(2)}, u32[]{:S(2)}) collective-permute-start(bf16[64,4800]{1,0:T(8,128)(2,1)S(1)} %pad_maximum_fusion.2), channel_id=1, source_target_pairs={{0,8},{4,12},{8,0},{12,4},{16,24},{20,28},{24,16},{28,20},{1,9},{5... | collective-permute-start | bytes 1843208 | tf_op jit(solution)/shard_map/ppermute | solution.py:256
  89.0 2.7 %route.5 = (bf16[32,4800]{1,0:T(8,128)(2,1)}, bf16[32,4800]{1,0:T(8,128)(2,1)}, bf16[32,4800]{1,0:T(8,128)(2,1)}, bf16[32,4800]{1,0:T(8,128)(2,1)}) custom-call(s32[4]{0:T(128)} %get-tuple-element.215.place_ref, bf16[32,4800]{1,0:T(8,128)(2,1)} %get-tuple-element.145.refs_0_, bf16[64,4800]{1,0:T(8,128)(2,1)} %copy-done.2, bf16[32,4800]{1,0:T(8,128)(2,1)} %copy-done.11, ...), custom_call_target="tpu_custom_call" | custom-call | tf_op jit(solution)/shard_map/route/pallas_call | solution.py:123
  91.7 0.6 collective-permute-start.16
  92.4 1.5 collective-permute-start.17
  93.9 1.4 collective-permute-start.18
  95.4 0.7 copy-done.44
  96.1 1.5 collective-permute-start.14
  97.6 0.6 concatenate.13.place_ref
  98.2 19.5 %correlate.4.refs_12_ = f32[41,128,256]{2,1,0:T(8,128)} custom-call(s32[12]{0:T(128)} %concatenate.13.place_ref, bf16[32,9600]{1,0:T(8,128)(2,1)} %get-tuple-element.169.refs_0_, bf16[32,9600]{1,0:T(8,128)(2,1)} %collective-permute-done.2.refs_1_, bf16[32,9600]{1,0:T(8,128)(2,1)} %collective-permute-done.3.refs_2_, ...), custom_call_target="tpu_custom_call" | custom-call | tf_op jit(solution)/shard_map/correlate/pallas_call | solution.py:226
  117.9 0.5 collective-permute-start.29
  118.5 0.4 collective-permute-start.31
  118.9 1.5 collective-permute-start.27
  120.4 2.5 %route.6 = (bf16[32,4800]{1,0:T(8,128)(2,1)}, bf16[32,4800]{1,0:T(8,128)(2,1)}, bf16[32,4800]{1,0:T(8,128)(2,1)}, bf16[32,4800]{1,0:T(8,128)(2,1)}) custom-call(s32[4]{0:T(128)} %get-tuple-element.215.place_ref, bf16[32,4800]{1,0:T(8,128)(2,1)} %get-tuple-element.167.refs_0_, bf16[64,4800]{1,0:T(8,128)(2,1)} %copy-done, bf16[32,4800]{1,0:T(8,128)(2,1)} %copy-done.10, ...), custom_call_target="tpu_custom_call" | custom-call | tf_op jit(solution)/shard_map/route/pallas_call | solution.py:123
  122.9 1.5 collective-permute-start.24
  124.4 0.5 collective-permute-start.25
  125.0 1.5 collective-permute-start.26
  126.6 0.7 copy-done.27
  127.2 19.9 %correlate.5.refs_12_ = f32[41,128,256]{2,1,0:T(8,128)} custom-call(s32[12]{0:T(128)} %concatenate.13.place_ref, bf16[32,9600]{1,0:T(8,128)(2,1)} %get-tuple-element.169.refs_0_, bf16[32,9600]{1,0:T(8,128)(2,1)} %collective-permute-done.2.refs_1_, bf16[32,9600]{1,0:T(8,128)(2,1)} %collective-permute-done.3.refs_2_, ...), custom_call_target="tpu_custom_call", output_to_operand_aliasing={{}: (13, {})} | custom-call | tf_op jit(solution)/shard_map/correlate/pallas_call | solution.py:226
  147.2 1.9 collective-permute-done.26.refs_7_
  149.1 0.5 collective-permute-start.36
  150.2 2.7 %route.7 = (bf16[32,4800]{1,0:T(8,128)(2,1)}, bf16[32,4800]{1,0:T(8,128)(2,1)}, bf16[32,4800]{1,0:T(8,128)(2,1)}, bf16[32,4800]{1,0:T(8,128)(2,1)}) custom-call(s32[4]{0:T(128)} %get-tuple-element.215.place_ref, bf16[32,4800]{1,0:T(8,128)(2,1)} %get-tuple-element.189.refs_0_, bf16[64,4800]{1,0:T(8,128)(2,1)} %copy-done.1, ...), custom_call_target="tpu_custom_call" | custom-call | tf_op jit(solution)/shard_map/route/pallas_call | solution.py:123
  152.9 0.7 collective-permute-start.32
  153.6 1.4 collective-permute-start.33
  155.0 1.4 collective-permute-start.34
  156.5 0.6 copy-done.30
  157.1 0.7 copy-done.31
  157.8 19.9 %correlate.6.refs_12_ = f32[41,128,256]{2,1,0:T(8,128)} custom-call(s32[12]{0:T(128)} %concatenate.13.place_ref, bf16[32,9600]{1,0:T(8,128)(2,1)} %get-tuple-element.206.refs_0_, bf16[32,9600]{1,0:T(8,128)(2,1)} %copy-done.4, bf16[32,9600]{1,0:T(8,128)(2,1)} %copy-done.5, bf16[32,9600]{1,0:T(8,128)(2,1)} %copy-done.6, ...), custom_call_target="tpu_custom_call", output_to_operand_aliasing={{}: (13, {})} | custom-call | tf_op jit(solution)/shard_map/correlate/pallas_call | solution.py:226
  177.9 0.5 collective-permute-start.40
  178.5 0.4 collective-permute-start.42
  178.9 0.6 collective-permute-done.39.refs_8_
  179.5 0.4 collective-permute-done.40.refs_9_
  179.9 0.4 collective-permute-done.41.refs_10_
  180.4 0.4 collective-permute-done.42.refs_11_
  181.1 0.7 copy-done.35
  181.8 20.1 %correlate.7 = f32[41,128,256]{2,1,0:T(8,128)} custom-call(s32[12]{0:T(128)} %concatenate.13.place_ref, bf16[32,9600]{1,0:T(8,128)(2,1)} %get-tuple-element.206.refs_0_, bf16[32,9600]{1,0:T(8,128)(2,1)} %copy-done.4, bf16[32,9600]{1,0:T(8,128)(2,1)} %copy-done.5, bf16[32,9600]{1,0:T(8,128)(2,1)} %copy-done.6, ...), custom_call_target="tpu_custom_call", output_to_operand_aliasing={{}: (13, {})} | custom-call | tf_op jit(solution)/shard_map/correlate/pallas_call | solution.py:226
  (127 shorter events, 2.0 us)
Async XLA Ops:
  8.7 24.4 %copy-start.3 = (bf16[32,9600]{1,0:T(8,128)(2,1)S(1)}, bf16[32,9600]{1,0:T(8,128)(2,1)}, u32[]{:S(2)}) copy-start(bf16[32,9600]{1,0:T(8,128)(2,1)} %get-tuple-element.206.refs_0_) | copy-start | bytes 1843204
  8.8 25.5 %copy-start.7 = (bf16[32,9600]{1,0:T(8,128)(2,1)S(1)}, bf16[32,9600]{1,0:T(8,128)(2,1)}, u32[]{:S(2)}) copy-start(bf16[32,9600]{1,0:T(8,128)(2,1)} %get-tuple-element.169.refs_0_) | copy-start | bytes 1843204
  8.8 21.1 %collective-permute-start.2 = (bf16[32,9600]{1,0:T(8,128)(2,1)}, bf16[32,9600]{1,0:T(8,128)(2,1)}, u32[]{:S(2)}, u32[]{:S(2)}) collective-permute-start(bf16[32,9600]{1,0:T(8,128)(2,1)} %get-tuple-element.169.refs_0_), channel_id=1, source_target_pairs={{0,1},{1,0},{2,3},{3,2},{4,5},{5,4},{6,7},{7,6},{8,9},{9,8},{10,11... | collective-permute-start | bytes 1843208 | tf_op jit(solution)/shard_map/ppermute | solution.py:253
  11.8 18.1 %collective-permute-start.3 = (bf16[32,9600]{1,0:T(8,128)(2,1)}, bf16[32,9600]{1,0:T(8,128)(2,1)}, u32[]{:S(2)}, u32[]{:S(2)}) collective-permute-start(bf16[32,9600]{1,0:T(8,128)(2,1)} %get-tuple-element.169.refs_0_), channel_id=1, source_target_pairs={{0,2},{1,3},{2,0},{3,1},{4,6},{5,7},{6,4},{7,5},{8,10},{9,11},{10,... | collective-permute-start | bytes 1843208 | tf_op jit(solution)/shard_map/ppermute | solution.py:253
  13.3 16.4 %collective-permute-start = (bf16[32,4800]{1,0:T(8,128)(2,1)}, bf16[32,4800]{1,0:T(8,128)(2,1)S(1)}, u32[]{:S(2)}, u32[]{:S(2)}) collective-permute-start(bf16[32,4800]{1,0:T(8,128)(2,1)} %get-tuple-element.126.refs_0_), channel_id=1, source_target_pairs={{0,16},{4,20},{8,24},{12,28},{16,0},{20,4},{24,8},{28,12},{1,17},{... | collective-permute-start | bytes 921608 | tf_op jit(solution)/shard_map/ppermute | solution.py:256
  15.9 14.0 %collective-permute-start.1 = (bf16[32,4800]{1,0:T(8,128)(2,1)}, bf16[32,4800]{1,0:T(8,128)(2,1)S(1)}, u32[]{:S(2)}, u32[]{:S(2)}) collective-permute-start(bf16[32,4800]{1,0:T(8,128)(2,1)} %get-tuple-element.126.refs_0_), channel_id=1, source_target_pairs={{0,8},{4,12},{8,0},{12,4},{16,24},{20,28},{24,16},{28,20},{1,9},{5... | collective-permute-start | bytes 921608 | tf_op jit(solution)/shard_map/ppermute | solution.py:256
  29.7 34.1 %copy-start.12 = (bf16[32,4800]{1,0:T(8,128)(2,1)}, bf16[32,4800]{1,0:T(8,128)(2,1)S(1)}, u32[]{:S(2)}) copy-start(bf16[32,4800]{1,0:T(8,128)(2,1)S(1)} %collective-permute-done.refs_2_) | copy-start | bytes 921604
  31.7 39.2 %copy-start.9 = (bf16[32,4800]{1,0:T(8,128)(2,1)S(1)}, bf16[32,4800]{1,0:T(8,128)(2,1)}, u32[]{:S(2)}) copy-start(bf16[32,4800]{1,0:T(8,128)(2,1)} %get-tuple-element.167.refs_0_) | copy-start | bytes 921604
  31.7 52.9 %copy-start.8 = (bf16[32,4800]{1,0:T(8,128)(2,1)S(1)}, bf16[32,4800]{1,0:T(8,128)(2,1)}, u32[]{:S(2)}) copy-start(bf16[32,4800]{1,0:T(8,128)(2,1)} %get-tuple-element.189.refs_0_) | copy-start | bytes 921604
  31.7 21.5 %collective-permute-start.5 = (bf16[64,4800]{1,0:T(8,128)(2,1)S(1)}, bf16[64,4800]{1,0:T(8,128)(2,1)S(1)}, u32[]{:S(2)}, u32[]{:S(2)}) collective-permute-start(bf16[64,4800]{1,0:T(8,128)(2,1)S(1)} %pad_maximum_fusion), channel_id=1, source_target_pairs={{0,8},{4,12},{8,0},{12,4},{16,24},{20,28},{24,16},{28,20},{1,9},{5... | collective-permute-start | bytes 1843208 | tf_op jit(solution)/shard_map/ppermute | solution.py:256
  33.2 20.0 %collective-permute-start.7 = (bf16[32,9600]{1,0:T(8,128)(2,1)S(1)}, bf16[32,9600]{1,0:T(8,128)(2,1)S(1)}, u32[]{:S(2)}, u32[]{:S(2)}) collective-permute-start(bf16[32,9600]{1,0:T(8,128)(2,1)S(1)} %copy-done.3), channel_id=1, source_target_pairs={{0,1},{1,0},{2,3},{3,2},{4,5},{5,4},{6,7},{7,6},{8,9},{9,8},{10,11... | collective-permute-start | bytes 1843208 | tf_op jit(solution)/shard_map/ppermute | solution.py:253
  33.7 27.5 %collective-permute-start.8 = (bf16[32,9600]{1,0:T(8,128)(2,1)S(1)}, bf16[32,9600]{1,0:T(8,128)(2,1)S(1)}, u32[]{:S(2)}, u32[]{:S(2)}) collective-permute-start(bf16[32,9600]{1,0:T(8,128)(2,1)S(1)} %copy-done.3), channel_id=1, source_target_pairs={{0,2},{1,3},{2,0},{3,1},{4,6},{5,7},{6,4},{7,5},{8,10},{9,11},{10,... | collective-permute-start | bytes 1843208 | tf_op jit(solution)/shard_map/ppermute | solution.py:253
  34.2 27.8 %collective-permute-start.6 = (bf16[32,9600]{1,0:T(8,128)(2,1)S(1)}, bf16[32,9600]{1,0:T(8,128)(2,1)}, u32[]{:S(2)}, u32[]{:S(2)}) collective-permute-start(bf16[32,9600]{1,0:T(8,128)(2,1)S(1)} %copy-done.7), channel_id=1, source_target_pairs={{0,3},{1,2},{2,1},{3,0},{4,7},{5,6},{6,5},{7,4},{8,11},{9,10},{10,... | collective-permute-start | bytes 1843208 | tf_op jit(solution)/shard_map/ppermute | solution.py:253
  36.7 15.8 %collective-permute-start.4 = (bf16[32,4800]{1,0:T(8,128)(2,1)}, bf16[32,4800]{1,0:T(8,128)(2,1)S(1)}, u32[]{:S(2)}, u32[]{:S(2)}) collective-permute-start(bf16[32,4800]{1,0:T(8,128)(2,1)} %get-tuple-element.145.refs_0_), channel_id=1, source_target_pairs={{0,16},{4,20},{8,24},{12,28},{16,0},{20,4},{24,8},{28,12},{1,17},{... | collective-permute-start | bytes 921608 | tf_op jit(solution)/shard_map/ppermute | solution.py:256
  52.5 32.1 %copy-start.11 = (bf16[32,4800]{1,0:T(8,128)(2,1)}, bf16[32,4800]{1,0:T(8,128)(2,1)S(1)}, u32[]{:S(2)}) copy-start(bf16[32,4800]{1,0:T(8,128)(2,1)S(1)} %collective-permute-done.4.refs_2_) | copy-start | bytes 921604
  53.1 11.7 %copy-start.2 = (bf16[64,4800]{1,0:T(8,128)(2,1)}, bf16[64,4800]{1,0:T(8,128)(2,1)S(1)}, u32[]{:S(2)}) copy-start(bf16[64,4800]{1,0:T(8,128)(2,1)S(1)} %collective-permute-done.5.refs_3_.refs_1_) | copy-start | bytes 1843204
  53.2 14.2 %copy-start.4 = (bf16[32,9600]{1,0:T(8,128)(2,1)}, bf16[32,9600]{1,0:T(8,128)(2,1)S(1)}, u32[]{:S(2)}) copy-start(bf16[32,9600]{1,0:T(8,128)(2,1)S(1)} %collective-permute-done.7.refs_1_) | copy-start | bytes 1843204
  63.8 19.7 %collective-permute-start.10 = (bf16[64,4800]{1,0:T(8,128)(2,1)}, bf16[64,4800]{1,0:T(8,128)(2,1)S(1)}, u32[]{:S(2)}, u32[]{:S(2)}) collective-permute-start(bf16[64,4800]{1,0:T(8,128)(2,1)} %pad_maximum_fusion.1), channel_id=1, source_target_pairs={{0,8},{4,12},{8,0},{12,4},{16,24},{20,28},{24,16},{28,20},{1,9},{5... | collective-permute-start | bytes 1843208 | tf_op jit(solution)/shard_map/ppermute | solution.py:256
  67.3 9.4 %collective-permute-start.11 = (bf16[32,4800]{1,0:T(8,128)(2,1)}, bf16[32,4800]{1,0:T(8,128)(2,1)S(1)}, u32[]{:S(2)}, u32[]{:S(2)}) collective-permute-start(bf16[32,4800]{1,0:T(8,128)(2,1)} %get-tuple-element.142), channel_id=1, source_target_pairs={{0,1},{1,0},{2,3},{3,2},{4,5},{5,4},{6,7},{7,6},{8,9},{9,8},{10,11... | collective-permute-start | bytes 921608 | tf_op jit(solution)/shard_map/ppermute | solution.py:253
  68.8 12.9 %collective-permute-start.12 = (bf16[32,4800]{1,0:T(8,128)(2,1)}, bf16[32,4800]{1,0:T(8,128)(2,1)S(1)}, u32[]{:S(2)}, u32[]{:S(2)}) collective-permute-start(bf16[32,4800]{1,0:T(8,128)(2,1)} %get-tuple-element.143), channel_id=1, source_target_pairs={{0,2},{1,3},{2,0},{3,1},{4,6},{5,7},{6,4},{7,5},{8,10},{9,11},{10,... | collective-permute-start | bytes 921608 | tf_op jit(solution)/shard_map/ppermute | solution.py:253
  69.3 12.4 %collective-permute-start.13 = (bf16[32,4800]{1,0:T(8,128)(2,1)}, bf16[32,4800]{1,0:T(8,128)(2,1)S(1)}, u32[]{:S(2)}, u32[]{:S(2)}) collective-permute-start(bf16[32,4800]{1,0:T(8,128)(2,1)} %get-tuple-element.144), channel_id=1, source_target_pairs={{0,3},{1,2},{2,1},{3,0},{4,7},{5,6},{6,5},{7,4},{8,11},{9,10},{10,... | collective-permute-start | bytes 921608 | tf_op jit(solution)/shard_map/ppermute | solution.py:253
  70.8 10.9 %collective-permute-start.9 = (bf16[32,4800]{1,0:T(8,128)(2,1)S(1)}, bf16[32,4800]{1,0:T(8,128)(2,1)S(1)}, u32[]{:S(2)}, u32[]{:S(2)}) collective-permute-start(bf16[32,4800]{1,0:T(8,128)(2,1)S(1)} %copy-done.9), channel_id=1, source_target_pairs={{0,16},{4,20},{8,24},{12,28},{16,0},{20,4},{24,8},{28,12},{1,17},{... | collective-permute-start | bytes 921608 | tf_op jit(solution)/shard_map/ppermute | solution.py:256
  76.7 15.0 %copy-start.38 = (bf16[32,4800]{1,0:T(8,128)(2,1)}, bf16[32,4800]{1,0:T(8,128)(2,1)S(1)}, u32[]{:S(2)}) copy-start(bf16[32,4800]{1,0:T(8,128)(2,1)S(1)} %collective-permute-done.11.refs_5_) | copy-start | bytes 921604
  81.7 13.6 %copy-start.39 = (bf16[32,4800]{1,0:T(8,128)(2,1)}, bf16[32,4800]{1,0:T(8,128)(2,1)S(1)}, u32[]{:S(2)}) copy-start(bf16[32,4800]{1,0:T(8,128)(2,1)S(1)} %collective-permute-done.12.refs_6_) | copy-start | bytes 921604
  81.7 13.6 %copy-start.40 = (bf16[32,4800]{1,0:T(8,128)(2,1)}, bf16[32,4800]{1,0:T(8,128)(2,1)S(1)}, u32[]{:S(2)}) copy-start(bf16[32,4800]{1,0:T(8,128)(2,1)S(1)} %collective-permute-done.13.refs_7_) | copy-start | bytes 921604
  81.7 10.0 %copy-start.10 = (bf16[32,4800]{1,0:T(8,128)(2,1)}, bf16[32,4800]{1,0:T(8,128)(2,1)S(1)}, u32[]{:S(2)}) copy-start(bf16[32,4800]{1,0:T(8,128)(2,1)S(1)} %collective-permute-done.9.refs_2_) | copy-start | bytes 921604
  83.6 8.2 %collective-permute-start.19 = (bf16[32,4800]{1,0:T(8,128)(2,1)}, bf16[32,4800]{1,0:T(8,128)(2,1)S(1)}, u32[]{:S(2)}, u32[]{:S(2)}) collective-permute-start(bf16[32,4800]{1,0:T(8,128)(2,1)} %get-tuple-element.163.refs_4_), channel_id=1, source_target_pairs={{0,4},{4,0},{8,12},{12,8},{16,20},{20,16},{24,28},{28,24},{1,5},{5... | collective-permute-start | bytes 921608 | tf_op jit(solution)/shard_map/ppermute | solution.py:259
  83.6 8.8 %collective-permute-start.20 = (bf16[32,4800]{1,0:T(8,128)(2,1)S(1)}, bf16[32,4800]{1,0:T(8,128)(2,1)S(1)}, u32[]{:S(2)}, u32[]{:S(2)}) collective-permute-start(bf16[32,4800]{1,0:T(8,128)(2,1)S(1)} %collective-permute-done.11.refs_5_), channel_id=1, source_target_pairs={{0,4},{4,0},{8,12},{12,8},{16,20},{20,16},{24,28},{28,24},{1,5},{5... | collective-permute-start | bytes 921608 | tf_op jit(solution)/shard_map/ppermute | solution.py:259
  84.1 9.8 %collective-permute-start.21 = (bf16[32,4800]{1,0:T(8,128)(2,1)S(1)}, bf16[32,4800]{1,0:T(8,128)(2,1)S(1)}, u32[]{:S(2)}, u32[]{:S(2)}) collective-permute-start(bf16[32,4800]{1,0:T(8,128)(2,1)S(1)} %collective-permute-done.12.refs_6_), channel_id=1, source_target_pairs={{0,4},{4,0},{8,12},{12,8},{16,20},{20,16},{24,28},{28,24},{1,5},{5... | collective-permute-start | bytes 921608 | tf_op jit(solution)/shard_map/ppermute | solution.py:259
  84.1 11.2 %collective-permute-start.22 = (bf16[32,4800]{1,0:T(8,128)(2,1)S(1)}, bf16[32,4800]{1,0:T(8,128)(2,1)S(1)}, u32[]{:S(2)}, u32[]{:S(2)}) collective-permute-start(bf16[32,4800]{1,0:T(8,128)(2,1)S(1)} %collective-permute-done.13.refs_7_), channel_id=1, source_target_pairs={{0,4},{4,0},{8,12},{12,8},{16,20},{20,16},{24,28},{28,24},{1,5},{5... | collective-permute-start | bytes 921608 | tf_op jit(solution)/shard_map/ppermute | solution.py:259
  84.7 33.1 %collective-permute-start.15 = (bf16[64,4800]{1,0:T(8,128)(2,1)S(1)}, bf16[64,4800]{1,0:T(8,128)(2,1)S(1)}, u32[]{:S(2)}, u32[]{:S(2)}) collective-permute-start(bf16[64,4800]{1,0:T(8,128)(2,1)S(1)} %pad_maximum_fusion.2), channel_id=1, source_target_pairs={{0,8},{4,12},{8,0},{12,4},{16,24},{20,28},{24,16},{28,20},{1,9},{5... | collective-permute-start | bytes 1843208 | tf_op jit(solution)/shard_map/ppermute | solution.py:256
  91.7 26.0 %collective-permute-start.16 = (bf16[32,4800]{1,0:T(8,128)(2,1)}, bf16[32,4800]{1,0:T(8,128)(2,1)S(1)}, u32[]{:S(2)}, u32[]{:S(2)}) collective-permute-start(bf16[32,4800]{1,0:T(8,128)(2,1)} %get-tuple-element.160), channel_id=1, source_target_pairs={{0,1},{1,0},{2,3},{3,2},{4,5},{5,4},{6,7},{7,6},{8,9},{9,8},{10,11... | collective-permute-start | bytes 921608 | tf_op jit(solution)/shard_map/ppermute | solution.py:253
  92.4 25.4 %collective-permute-start.17 = (bf16[32,4800]{1,0:T(8,128)(2,1)}, bf16[32,4800]{1,0:T(8,128)(2,1)S(1)}, u32[]{:S(2)}, u32[]{:S(2)}) collective-permute-start(bf16[32,4800]{1,0:T(8,128)(2,1)} %get-tuple-element.161), channel_id=1, source_target_pairs={{0,2},{1,3},{2,0},{3,1},{4,6},{5,7},{6,4},{7,5},{8,10},{9,11},{10,... | collective-permute-start | bytes 921608 | tf_op jit(solution)/shard_map/ppermute | solution.py:253
  93.9 23.9 %collective-permute-start.18 = (bf16[32,4800]{1,0:T(8,128)(2,1)}, bf16[32,4800]{1,0:T(8,128)(2,1)}, u32[]{:S(2)}, u32[]{:S(2)}) collective-permute-start(bf16[32,4800]{1,0:T(8,128)(2,1)} %get-tuple-element.162), channel_id=1, source_target_pairs={{0,3},{1,2},{2,1},{3,0},{4,7},{5,6},{6,5},{7,4},{8,11},{9,10},{10,... | collective-permute-start | bytes 921608 | tf_op jit(solution)/shard_map/ppermute | solution.py:253
  96.1 21.7 %collective-permute-start.14 = (bf16[32,4800]{1,0:T(8,128)(2,1)S(1)}, bf16[32,4800]{1,0:T(8,128)(2,1)}, u32[]{:S(2)}, u32[]{:S(2)}) collective-permute-start(bf16[32,4800]{1,0:T(8,128)(2,1)S(1)} %copy-done.8), channel_id=1, source_target_pairs={{0,16},{4,20},{8,24},{12,28},{16,0},{20,4},{24,8},{28,12},{1,17},{... | collective-permute-start | bytes 921608 | tf_op jit(solution)/shard_map/ppermute | solution.py:256
  98.2 19.6 %copy-start.13 = (bf16[32,4800]{1,0:T(8,128)(2,1)S(1)}, bf16[32,4800]{1,0:T(8,128)(2,1)}, u32[]{:S(2)}) copy-start(bf16[32,4800]{1,0:T(8,128)(2,1)} %get-tuple-element.184.refs_4_) | copy-start | bytes 921604
  117.7 8.8 %copy-start.14 = (bf16[32,4800]{1,0:T(8,128)(2,1)}, bf16[32,4800]{1,0:T(8,128)(2,1)S(1)}, u32[]{:S(2)}) copy-start(bf16[32,4800]{1,0:T(8,128)(2,1)S(1)} %collective-permute-done.16.refs_5_) | copy-start | bytes 921604
  117.8 8.8 %copy-start.15 = (bf16[32,4800]{1,0:T(8,128)(2,1)}, bf16[32,4800]{1,0:T(8,128)(2,1)S(1)}, u32[]{:S(2)}) copy-start(bf16[32,4800]{1,0:T(8,128)(2,1)S(1)} %collective-permute-done.17.refs_6_) | copy-start | bytes 921604
  117.8 5.1 %collective-permute-start.28 = (bf16[32,4800]{1,0:T(8,128)(2,1)S(1)}, bf16[32,4800]{1,0:T(8,128)(2,1)S(1)}, u32[]{:S(2)}, u32[]{:S(2)}) collective-permute-start(bf16[32,4800]{1,0:T(8,128)(2,1)S(1)} %copy-done.13), channel_id=1, source_target_pairs={{0,4},{4,0},{8,12},{12,8},{16,20},{20,16},{24,28},{28,24},{1,5},{5... | collective-permute-start | bytes 921608 | tf_op jit(solution)/shard_map/ppermute | solution.py:259
  117.9 6.5 %collective-permute-start.29 = (bf16[32,4800]{1,0:T(8,128)(2,1)S(1)}, bf16[32,4800]{1,0:T(8,128)(2,1)S(1)}, u32[]{:S(2)}, u32[]{:S(2)}) collective-permute-start(bf16[32,4800]{1,0:T(8,128)(2,1)S(1)} %collective-permute-done.16.refs_5_), channel_id=1, source_target_pairs={{0,4},{4,0},{8,12},{12,8},{16,20},{20,16},{24,28},{28,24},{1,5},{5... | collective-permute-start | bytes 921608 | tf_op jit(solution)/shard_map/ppermute | solution.py:259
  118.4 6.6 %collective-permute-start.30 = (bf16[32,4800]{1,0:T(8,128)(2,1)S(1)}, bf16[32,4800]{1,0:T(8,128)(2,1)S(1)}, u32[]{:S(2)}, u32[]{:S(2)}) collective-permute-start(bf16[32,4800]{1,0:T(8,128)(2,1)S(1)} %collective-permute-done.17.refs_6_), channel_id=1, source_target_pairs={{0,4},{4,0},{8,12},{12,8},{16,20},{20,16},{24,28},{28,24},{1,5},{5... | collective-permute-start | bytes 921608 | tf_op jit(solution)/shard_map/ppermute | solution.py:259
  118.5 8.0 %collective-permute-start.31 = (bf16[32,4800]{1,0:T(8,128)(2,1)}, bf16[32,4800]{1,0:T(8,128)(2,1)S(1)}, u32[]{:S(2)}, u32[]{:S(2)}) collective-permute-start(bf16[32,4800]{1,0:T(8,128)(2,1)} %collective-permute-done.18.refs_7_), channel_id=1, source_target_pairs={{0,4},{4,0},{8,12},{12,8},{16,20},{20,16},{24,28},{28,24},{1,5},{5... | collective-permute-start | bytes 921608 | tf_op jit(solution)/shard_map/ppermute | solution.py:259
  118.9 30.1 %collective-permute-start.27 = (bf16[32,9600]{1,0:T(8,128)(2,1)S(1)}, bf16[32,9600]{1,0:T(8,128)(2,1)S(1)}, u32[]{:S(2)}, u32[]{:S(2)}) collective-permute-start(bf16[32,9600]{1,0:T(8,128)(2,1)S(1)} %copy-done.3), channel_id=1, source_target_pairs={{0,3},{1,2},{2,1},{3,0},{4,7},{5,6},{6,5},{7,4},{8,11},{9,10},{10,... | collective-permute-start | bytes 1843208 | tf_op jit(solution)/shard_map/ppermute | solution.py:253
  122.9 24.2 %collective-permute-start.24 = (bf16[32,4800]{1,0:T(8,128)(2,1)}, bf16[32,4800]{1,0:T(8,128)(2,1)S(1)}, u32[]{:S(2)}, u32[]{:S(2)}) collective-permute-start(bf16[32,4800]{1,0:T(8,128)(2,1)} %get-tuple-element.181), channel_id=1, source_target_pairs={{0,1},{1,0},{2,3},{3,2},{4,5},{5,4},{6,7},{7,6},{8,9},{9,8},{10,11... | collective-permute-start | bytes 921608 | tf_op jit(solution)/shard_map/ppermute | solution.py:253
  124.4 22.7 %collective-permute-start.25 = (bf16[32,4800]{1,0:T(8,128)(2,1)}, bf16[32,4800]{1,0:T(8,128)(2,1)S(1)}, u32[]{:S(2)}, u32[]{:S(2)}) collective-permute-start(bf16[32,4800]{1,0:T(8,128)(2,1)} %get-tuple-element.182), channel_id=1, source_target_pairs={{0,2},{1,3},{2,0},{3,1},{4,6},{5,7},{6,4},{7,5},{8,10},{9,11},{10,... | collective-permute-start | bytes 921608 | tf_op jit(solution)/shard_map/ppermute | solution.py:253
  125.0 24.1 %copy-start.16 = (bf16[32,4800]{1,0:T(8,128)(2,1)S(1)}, bf16[32,4800]{1,0:T(8,128)(2,1)}, u32[]{:S(2)}) copy-start(bf16[32,4800]{1,0:T(8,128)(2,1)} %get-tuple-element.201.refs_4_) | copy-start | bytes 921604
  125.0 24.0 %collective-permute-start.26 = (bf16[32,4800]{1,0:T(8,128)(2,1)}, bf16[32,4800]{1,0:T(8,128)(2,1)S(1)}, u32[]{:S(2)}, u32[]{:S(2)}) collective-permute-start(bf16[32,4800]{1,0:T(8,128)(2,1)} %get-tuple-element.183), channel_id=1, source_target_pairs={{0,3},{1,2},{2,1},{3,0},{4,7},{5,6},{6,5},{7,4},{8,11},{9,10},{10,... | collective-permute-start | bytes 921608 | tf_op jit(solution)/shard_map/ppermute | solution.py:253
  126.5 22.5 %collective-permute-start.23 = (bf16[32,4800]{1,0:T(8,128)(2,1)}, bf16[32,4800]{1,0:T(8,128)(2,1)S(1)}, u32[]{:S(2)}, u32[]{:S(2)}) collective-permute-start(bf16[32,4800]{1,0:T(8,128)(2,1)} %collective-permute-done.14.refs_2_), channel_id=1, source_target_pairs={{0,8},{4,12},{8,0},{12,4},{16,24},{20,28},{24,16},{28,20},{1,9},{5... | collective-permute-start | bytes 921608 | tf_op jit(solution)/shard_map/ppermute | solution.py:256
  147.1 9.3 %copy-start.17 = (bf16[32,4800]{1,0:T(8,128)(2,1)}, bf16[32,4800]{1,0:T(8,128)(2,1)S(1)}, u32[]{:S(2)}) copy-start(bf16[32,4800]{1,0:T(8,128)(2,1)S(1)} %collective-permute-done.24.refs_5_) | copy-start | bytes 921604
  147.2 9.3 %copy-start.18 = (bf16[32,4800]{1,0:T(8,128)(2,1)}, bf16[32,4800]{1,0:T(8,128)(2,1)S(1)}, u32[]{:S(2)}) copy-start(bf16[32,4800]{1,0:T(8,128)(2,1)S(1)} %collective-permute-done.25.refs_6_) | copy-start | bytes 921604
  149.0 7.4 %copy-start.19 = (bf16[32,4800]{1,0:T(8,128)(2,1)}, bf16[32,4800]{1,0:T(8,128)(2,1)S(1)}, u32[]{:S(2)}) copy-start(bf16[32,4800]{1,0:T(8,128)(2,1)S(1)} %collective-permute-done.26.refs_7_) | copy-start | bytes 921604
  149.0 7.4 %copy-start.6 = (bf16[32,9600]{1,0:T(8,128)(2,1)}, bf16[32,9600]{1,0:T(8,128)(2,1)S(1)}, u32[]{:S(2)}) copy-start(bf16[32,9600]{1,0:T(8,128)(2,1)S(1)} %collective-permute-done.27.refs_3_) | copy-start | bytes 1843204
  149.1 4.5 %collective-permute-start.35 = (bf16[32,4800]{1,0:T(8,128)(2,1)S(1)}, bf16[32,4800]{1,0:T(8,128)(2,1)S(1)}, u32[]{:S(2)}, u32[]{:S(2)}) collective-permute-start(bf16[32,4800]{1,0:T(8,128)(2,1)S(1)} %copy-done.16), channel_id=1, source_target_pairs={{0,4},{4,0},{8,12},{12,8},{16,20},{20,16},{24,28},{28,24},{1,5},{5... | collective-permute-start | bytes 921608 | tf_op jit(solution)/shard_map/ppermute | solution.py:259
  149.1 5.8 %collective-permute-start.36 = (bf16[32,4800]{1,0:T(8,128)(2,1)S(1)}, bf16[32,4800]{1,0:T(8,128)(2,1)S(1)}, u32[]{:S(2)}, u32[]{:S(2)}) collective-permute-start(bf16[32,4800]{1,0:T(8,128)(2,1)S(1)} %collective-permute-done.24.refs_5_), channel_id=1, source_target_pairs={{0,4},{4,0},{8,12},{12,8},{16,20},{20,16},{24,28},{28,24},{1,5},{5... | collective-permute-start | bytes 921608 | tf_op jit(solution)/shard_map/ppermute | solution.py:259
  149.6 6.8 %collective-permute-start.37 = (bf16[32,4800]{1,0:T(8,128)(2,1)S(1)}, bf16[32,4800]{1,0:T(8,128)(2,1)S(1)}, u32[]{:S(2)}, u32[]{:S(2)}) collective-permute-start(bf16[32,4800]{1,0:T(8,128)(2,1)S(1)} %collective-permute-done.25.refs_6_), channel_id=1, source_target_pairs={{0,4},{4,0},{8,12},{12,8},{16,20},{20,16},{24,28},{28,24},{1,5},{5... | collective-permute-start | bytes 921608 | tf_op jit(solution)/shard_map/ppermute | solution.py:259
  149.7 6.7 %collective-permute-start.38 = (bf16[32,4800]{1,0:T(8,128)(2,1)S(1)}, bf16[32,4800]{1,0:T(8,128)(2,1)S(1)}, u32[]{:S(2)}, u32[]{:S(2)}) collective-permute-start(bf16[32,4800]{1,0:T(8,128)(2,1)S(1)} %collective-permute-done.26.refs_7_), channel_id=1, source_target_pairs={{0,4},{4,0},{8,12},{12,8},{16,20},{20,16},{24,28},{28,24},{1,5},{5... | collective-permute-start | bytes 921608 | tf_op jit(solution)/shard_map/ppermute | solution.py:259
  152.9 24.8 %collective-permute-start.32 = (bf16[32,4800]{1,0:T(8,128)(2,1)}, bf16[32,4800]{1,0:T(8,128)(2,1)S(1)}, u32[]{:S(2)}, u32[]{:S(2)}) collective-permute-start(bf16[32,4800]{1,0:T(8,128)(2,1)} %get-tuple-element.198), channel_id=1, source_target_pairs={{0,1},{1,0},{2,3},{3,2},{4,5},{5,4},{6,7},{7,6},{8,9},{9,8},{10,11... | collective-permute-start | bytes 921608 | tf_op jit(solution)/shard_map/ppermute | solution.py:253
  153.6 24.2 %collective-permute-start.33 = (bf16[32,4800]{1,0:T(8,128)(2,1)}, bf16[32,4800]{1,0:T(8,128)(2,1)S(1)}, u32[]{:S(2)}, u32[]{:S(2)}) collective-permute-start(bf16[32,4800]{1,0:T(8,128)(2,1)} %get-tuple-element.199), channel_id=1, source_target_pairs={{0,2},{1,3},{2,0},{3,1},{4,6},{5,7},{6,4},{7,5},{8,10},{9,11},{10,... | collective-permute-start | bytes 921608 | tf_op jit(solution)/shard_map/ppermute | solution.py:253
  155.0 22.8 %copy-start.20 = (bf16[32,4800]{1,0:T(8,128)(2,1)S(1)}, bf16[32,4800]{1,0:T(8,128)(2,1)}, u32[]{:S(2)}) copy-start(bf16[32,4800]{1,0:T(8,128)(2,1)} %get-tuple-element.210.refs_4_) | copy-start | bytes 921604
  155.0 22.8 %collective-permute-start.34 = (bf16[32,4800]{1,0:T(8,128)(2,1)}, bf16[32,4800]{1,0:T(8,128)(2,1)S(1)}, u32[]{:S(2)}, u32[]{:S(2)}) collective-permute-start(bf16[32,4800]{1,0:T(8,128)(2,1)} %get-tuple-element.200), channel_id=1, source_target_pairs={{0,3},{1,2},{2,1},{3,0},{4,7},{5,6},{6,5},{7,4},{8,11},{9,10},{10,... | collective-permute-start | bytes 921608 | tf_op jit(solution)/shard_map/ppermute | solution.py:253
  177.8 1.7 collective-permute-start.39
  177.9 2.0 %collective-permute-start.40 = (bf16[32,4800]{1,0:T(8,128)(2,1)S(1)}, bf16[32,4800]{1,0:T(8,128)(2,1)S(1)}, u32[]{:S(2)}, u32[]{:S(2)}) collective-permute-start(bf16[32,4800]{1,0:T(8,128)(2,1)S(1)} %collective-permute-done.32.refs_5_), channel_id=1, source_target_pairs={{0,4},{4,0},{8,12},{12,8},{16,20},{20,16},{24,28},{28,24},{1,5},{5... | collective-permute-start | bytes 921608 | tf_op jit(solution)/shard_map/ppermute | solution.py:259
  178.4 2.0 collective-permute-start.41
  178.5 2.4 %collective-permute-start.42 = (bf16[32,4800]{1,0:T(8,128)(2,1)S(1)}, bf16[32,4800]{1,0:T(8,128)(2,1)S(1)}, u32[]{:S(2)}, u32[]{:S(2)}) collective-permute-start(bf16[32,4800]{1,0:T(8,128)(2,1)S(1)} %collective-permute-done.34.refs_7_), channel_id=1, source_target_pairs={{0,4},{4,0},{8,12},{12,8},{16,20},{20,16},{24,28},{28,24},{1,5},{5... | collective-permute-start | bytes 921608 | tf_op jit(solution)/shard_map/ppermute | solution.py:259
  (24 other events, 46.1 us)

commit v3 on v2

--- a/solution.py
+++ b/solution.py
@@ -32,16 +32,16 @@
     return jnp.dot(left, right, preferred_element_type=jnp.float32)
 
 
-def whiten_kernel(starts, taps_ref, traces_ref, flags_ref, *out_refs):
-    rows, record_len = traces_ref.shape
-    blocks = record_len // LANES
-    traces = traces_ref[...]
-    stacked = jnp.concatenate(
-        [jnp.zeros((rows, LANES), jnp.float32)]
-        + [traces[:, j * LANES : (j + 1) * LANES] for j in range(blocks)]
-        + [jnp.zeros((2 * rows, LANES), jnp.float32)],
-        axis=0,
-    )
+def whiten_kernel(record_tiles, first, starts, taps_ref, traces_ref, flags_ref, *out_refs):
+    rows = traces_ref.shape[0]
+    blocks = max(start + out.shape[1] for start, out in zip(starts, out_refs)) // LANES - first
+
+    def tile(j):
+        if j < 0 or j >= record_tiles:
+            return jnp.zeros((rows, LANES), jnp.float32)
+        return traces_ref[:, j * LANES : (j + 1) * LANES]
+
+    stacked = jnp.concatenate([tile(first + j - 1) for j in range(blocks + 3)], axis=0)
 
     def windows(value):
         return jnp.concatenate([value[:-rows], value[rows:]], axis=1)
@@ -62,17 +62,17 @@
 
     magnitude = jnp.abs(both[:, :LANES])
     lane = lax.broadcasted_iota(jnp.int32, (rows, LANES), 1)
-    magnitude = jnp.concatenate(
-        [
-            jnp.where(lane >= LANES - HALF_TAPS, magnitude[:rows], 0.0),
-            magnitude[rows : blocks * rows],
-            jnp.where(
-                lane < LANES - HALF_TAPS, magnitude[blocks * rows : (blocks + 1) * rows], 0.0
-            ),
-            jnp.zeros((rows, LANES), jnp.float32),
-        ],
-        axis=0,
-    )
+    last = record_tiles - first
+
+    def inside_record(j):
+        value = magnitude[j * rows : (j + 1) * rows]
+        if first + j == 0:
+            return jnp.where(lane >= LANES - HALF_TAPS, value, 0.0)
+        if j >= last:
+            return jnp.where(lane < LANES - HALF_TAPS, value, 0.0) if j == last else jnp.zeros_like(value)
+        return value
+
+    magnitude = jnp.concatenate([inside_record(j) for j in range(blocks + 2)], axis=0)
     ones = jnp.where((offset >= 0) & (offset <= 2 * RADIUS), 1.0, 0.0).astype(jnp.bfloat16)
     high, low = split_bf16(magnitude)
     level = (dot_f32(windows(high), ones) + dot_f32(windows(low), ones)) * (1.0 / (2 * RADIUS + 1))
@@ -86,22 +86,31 @@
     flat = jnp.concatenate([aligned[j * rows : (j + 1) * rows] for j in range(blocks)], axis=1)
 
     segments = flags_ref.shape[1]
-    first = SAMP * lax.broadcasted_iota(jnp.int32, (segments, record_len), 0)
-    sample = lax.broadcasted_iota(jnp.int32, (segments, record_len), 1)
-    inside = jnp.where((sample >= first) & (sample < first + SAMP), 1.0, 0.0).astype(jnp.bfloat16)
+    at = lax.broadcasted_iota(jnp.int32, (segments, blocks * LANES), 1) + first * LANES
+    at -= SAMP * lax.broadcasted_iota(jnp.int32, (segments, blocks * LANES), 0)
+    inside = jnp.where((at >= 0) & (at < SAMP), 1.0, 0.0).astype(jnp.bfloat16)
     kept = dot_f32(flags_ref[...].astype(jnp.float32).astype(jnp.bfloat16), inside)
     flat = (flat * kept).astype(jnp.bfloat16)
     for start, out_ref in zip(starts, out_refs):
+        start -= first * LANES
         out_ref[...] = flat[:, start : start + out_ref.shape[1]]
 
 
 def whiten(traces, fir_taps, seg_flags, spans):
+    rows, record_len = traces.shape
     vmem = pl.BlockSpec(memory_space=pltpu.VMEM)
+    first = min(start for start, _ in spans) // LANES
+    reach = min(max(start + length for start, length in spans) + 2 * LANES, record_len)
     return pl.pallas_call(
-        functools.partial(whiten_kernel, [start for start, _ in spans]),
-        in_specs=[pl.BlockSpec(memory_space=pltpu.SMEM), vmem, vmem],
+        functools.partial(whiten_kernel, record_len // LANES, first, [start for start, _ in spans]),
+        grid=(1,),
+        in_specs=[
+            pl.BlockSpec(memory_space=pltpu.SMEM),
+            pl.BlockSpec((rows, reach), lambda step: (0, 0)),
+            vmem,
+        ],
         out_specs=[vmem] * len(spans),
-        out_shape=[jax.ShapeDtypeStruct((traces.shape[0], length), jnp.bfloat16) for _, length in spans],
+        out_shape=[jax.ShapeDtypeStruct((rows, length), jnp.bfloat16) for _, length in spans],
         compiler_params=pltpu.CompilerParams(vmem_limit_bytes=vmem_bytes),
         name="whiten",
     )(fir_taps, traces, seg_flags)
@@ -132,47 +141,44 @@
     )(place, *[array for array, _ in parts])
 
 
-def correlate_kernel(start, left_count, has_total, last, scale, place_ref, *refs):
+def correlate_kernel(offset, begins, left_count, has_total, last, scale, place_ref, *refs):
     lefts, refs = refs[:left_count], list(refs[left_count:])
-    piece_rows, chunk_len = refs[0].shape
+    piece_rows, padded_len = refs[0].shape
     staged = refs.pop() if piece_rows % 16 else None
     *refs, out_ref, moved, columns, shifted, sems = refs
-    staged = columns if staged is None else staged
     mask_ref = refs.pop() if last else None
     total_ref = refs.pop() if has_total else None
-    row_count, padded_len = moved.shape
+    row_count = moved.shape[0]
     step = pl.program_id(0)
-    begin = start // LANES * LANES
 
     @pl.when(step == 0)
     def _():
-        copies = [
-            pltpu.make_async_copy(
-                left.at[:, pl.ds(begin, padded_len)],
-                moved.at[pl.ds(index * left.shape[0], left.shape[0])],
-                sems.at[index],
-            )
-            for index, left in enumerate(lefts)
-        ]
-        for copy in copies:
-            copy.start()
-        edge = chunk_len // LANES * LANES
-        if padded_len > chunk_len:
-            columns[:, edge:] = jnp.zeros((columns.shape[0], padded_len - edge), columns.dtype)
+        copies = []
+
+        def copy(source, target):
+            copies.append(pltpu.make_async_copy(source, target, sems.at[len(copies)]))
+            copies[-1].start()
+
+        for index, left in enumerate(lefts):
+            rows = left.shape[0]
+            copy(left.at[:, pl.ds(begins[index], padded_len)], moved.at[pl.ds(index * rows, rows)])
         for index, piece in enumerate(refs):
-            at = pl.multiple_of(place_ref[index] * piece_rows, piece_rows)
-            staged[pl.ds(at, piece_rows), :chunk_len] = piece[...].astype(staged.dtype)
-        if staged is not columns:
-            columns[:, :chunk_len] = staged[:, :chunk_len].astype(columns.dtype)
-        for copy in copies:
-            copy.wait()
-        moved[...] = pltpu.roll(moved[...], padded_len - HALF_LAG - (start - begin), 1)
-
-    sample = lax.broadcasted_iota(jnp.int32, (16, padded_len), 1)
-    phase = sample
-    for segment in range(1, chunk_len // SAMP):
+            at = pl.ds(pl.multiple_of(place_ref[index] * piece_rows, piece_rows), piece_rows)
+            if staged is None:
+                copy(piece, columns.at[at])
+            else:
+                staged[at, :] = piece[...].astype(staged.dtype)
+        if staged is not None:
+            columns[...] = staged[...].astype(columns.dtype)
+        for started in copies:
+            started.wait()
+        moved[...] = pltpu.roll(moved[...], padded_len - HALF_LAG, 1)
+
+    sample = lax.broadcasted_iota(jnp.int32, (16, padded_len), 1) - offset
+    phase = jnp.where(sample < 0, -SAMP, sample)
+    for segment in range(1, chunk_segs):
         phase = jnp.where(sample >= segment * SAMP, sample - segment * SAMP, phase)
-    phase = jnp.where(sample >= chunk_len, -SAMP, phase)
+    phase = jnp.where(sample >= chunk_segs * SAMP, -SAMP, phase)
     base = moved[...]
     for index in range(lag_group):
         lag = step * lag_group + index - HALF_LAG
@@ -197,15 +203,15 @@
         out_ref[:, at, :] = product[:, index * rows : (index + 1) * rows] * weight[None]
 
 
-def correlate(place, lefts, start, right, total, mask, last, scale):
+def correlate(place, lefts, begins, offset, right, total, mask, last, scale):
     rows = sum(left.shape[0] for left in lefts)
-    piece_rows, chunk_len = right[0].shape
+    piece_rows, padded_len = right[0].shape
     cols = len(right) * piece_rows
-    padded_len = pl.cdiv(chunk_len, LANES) * LANES
-    whole = pl.BlockSpec((piece_rows, chunk_len), lambda step: (0, 0))
+    any_space = pl.BlockSpec(memory_space=pl.ANY)
+    whole = pl.BlockSpec((piece_rows, padded_len), lambda step: (0, 0)) if piece_rows % 16 else any_space
     block = pl.BlockSpec((lag_group, rows, cols), lambda step: (step, 0, 0))
     operands = [place, *lefts, *right]
-    specs = [pl.BlockSpec(memory_space=pltpu.SMEM)] + [pl.BlockSpec(memory_space=pl.ANY)] * len(lefts)
+    specs = [pl.BlockSpec(memory_space=pltpu.SMEM)] + [any_space] * len(lefts)
     specs += [whole] * len(right)
     aliases = {}
     if total is not None:
@@ -219,12 +225,12 @@
         pltpu.VMEM((rows, padded_len), jnp.bfloat16),
         pltpu.VMEM((cols, padded_len), jnp.bfloat16),
         pltpu.VMEM((lag_group * rows, padded_len), jnp.bfloat16),
-        pltpu.SemaphoreType.DMA((len(lefts),)),
+        pltpu.SemaphoreType.DMA((len(lefts) + len(right),)),
     ]
     if piece_rows % 16:
         scratch.append(pltpu.VMEM((cols, padded_len), jnp.float32))
     return pl.pallas_call(
-        functools.partial(correlate_kernel, start, len(lefts), total is not None, last, scale),
+        functools.partial(correlate_kernel, offset, begins, len(lefts), total is not None, last, scale),
         grid=(pl.cdiv(LAGS, lag_group),),
         in_specs=specs,
         out_specs=block,
@@ -259,10 +265,16 @@
         return lax.ppermute(value, "stn", [(i, i ^ j) for i in range(stn_count)])
 
     length = chunk_segs * SAMP
-    record_len = traces.shape[1]
-    half_len = record_len // 2
-    spans = [(u * length, length) for u in range(count)] + [(0, half_len), (half_len, half_len)]
-    *units, early, late = whiten(traces, fir_taps, seg_flags, spans)
+    window = pl.cdiv(length, LANES) * LANES
+    begins = [u * length // LANES * LANES for u in range(count)]
+    half = count // 2
+    middle = begins[1], pl.cdiv((half + 1) * length, LANES) * LANES - begins[1]
+    late = begins[half], traces.shape[1] - begins[half]
+    units = list(whiten(traces, fir_taps, seg_flags, [(begins[0], window)]))
+    spans = [(begin, window) for begin in begins[1:]] + [middle, late]
+    *rest, middle, late = whiten(traces, fir_taps, seg_flags, spans)
+    units += rest
+
     direct = [k for k in range(1, seg_count) if k & (k - 1) == 0][::-1]
     passed = [k for k in range(1, seg_count) if k & (k - 1)]
     gathered = rows % 16 > 0
@@ -270,7 +282,7 @@
     place = jnp.concatenate(place).astype(jnp.int32)
 
     state = {("unit", u): unit for u, unit in enumerate(units)}
-    state["early", 0], state["late", 0] = early, late
+    state["middle"], state["late"] = middle, late
     lines = [{0: (("unit", u), 0)} for u in range(count)]
 
     def fence():
@@ -306,35 +318,57 @@
         for k, piece in enumerate(route(route_place, parts, rows)):
             state["own", u, k] = to_seg(piece, k) if k else piece
 
-    def row_hops(name, which):
-        if not gathered:
-            for k in which:
-                state[name, k] = to_seg(state[name, 0], k)
-        elif which:
-            state[name, 0] = lax.all_gather(state[name, 0], "seg", axis=0, tiled=True)
+    rows_of = [{0: (("unit", u), 0)} for u in range(count)]
+
+    def row_hop(k, source, covered):
+        name = ("row", k, source)
+        state[name] = to_seg(state[source], k)
+        for u in covered:
+            rows_of[u][k] = name, 0 if source == ("unit", u) else begins[u] - begins[covered[0]]
+
+    def gather_rows(source, covered):
+        name = ("rows", source)
+        state[name] = lax.all_gather(state[source], "seg", axis=0, tiled=True)
+        for u in covered:
+            rows_of[u] = {0: (name, begins[u] - begins[covered[0]])}
 
     def products(u):
-        name, start = ("early", u * length) if u < count // 2 else ("late", u * length - half_len)
-        lefts = [state[name, k] for k in range(1 if gathered else seg_count)]
+        parts = [rows_of[u][k] for k in sorted(rows_of[u])]
         own = [state.pop(("own", u, k)) for k in range(seg_count)]
         right = own + [to_side(v, j) for j in range(1, sides) for v in own]
         state["total"] = correlate(
-            place, lefts, start, right, state.pop("total", None), pair_mask, u == count - 1, scale
+            place,
+            [state[name] for name, _ in parts],
+            [begin for _, begin in parts],
+            u * length - begins[u],
+            right,
+            state.pop("total", None),
+            pair_mask,
+            u == count - 1,
+            scale,
         )
 
-    near, far = list(range(1, seg_count - 1)), [seg_count - 1]
+    hops = list(range(1, seg_count))
+    row_plan = {
+        -1: [(k, ("unit", 0), [0]) for k in hops],
+        0: [(k, "middle", range(1, half + 1)) for k in hops[:-1]] + [(hops[-1], ("unit", 1), [1])],
+        half + 1: [(hops[-1], "late", range(half, count))],
+    }
+    for v in range(half + 1, count):
+        row_plan[v + 1] = row_plan.get(v + 1, []) + [(k, ("unit", v), [v]) for k in hops[:-1]]
     plane_hops(-1)
-    row_hops("early", near)
-    for u in range(count + 2):
-        fence()
-        plane_hops(u)
+    if gathered:
+        for source, covered in ((("unit", 0), [0]), ("middle", range(1, half)), ("late", range(half, count))):
+            gather_rows(source, list(covered))
+        row_plan = {}
+    for u in range(-1, count + 2):
+        if u >= 0:
+            fence()
+            plane_hops(u)
         if 1 <= u <= count:
             columns(u - 1)
-        if u == 0:
-            row_hops("early", [] if gathered else far)
-            row_hops("late", near)
-        if u == count // 2 + 1:
-            row_hops("late", [] if gathered else far)
+        for k, source, covered in row_plan.get(u, []):
+            row_hop(k, source, list(covered))
         if 2 <= u <= count:
             products(u - 2)
     products(count - 1)

time: 203 us -> 191 us (0.941)
  waiting for transfers between devices: 47.9 us -> 35.6 us
  Pallas kernels: 98.6 us -> 101 us
  local copies, waits for them, and re-layouts: 6.01 us -> 3.91 us
    ppermute x9, waiting for transfers between devices: 28.4 us -> 15.9 us  [to_plane(): lax.ppermute(value, 'stn', [(i, i ^ k * sides) for i in range(stn_count)])]
    pallas_call x5 -> x6, Pallas kernels: 88.2 us -> 90.4 us  [the longest x4 79.4 us: correlate(): pl.pallas_call(functools.partial(correlate_kernel, offset, begins, len(le...]
    unnamed x90 -> x108, local copies, waits for them, and re-layouts: 5.41 us -> 3.28 us
    ppermute x18 -> x21, starting transfers between devices: 23.6 us -> 25 us  [to_seg(): return lax.ppermute(value, 'seg', [(i, i ^ k) for i in range(seg_count)])]
    ppermute x18 -> x21, waiting for transfers between devices: 17.5 us -> 17.8 us  [to_seg(): return lax.ppermute(value, 'seg', [(i, i ^ k) for i in range(seg_count)])]
  transfers between devices with their start and end apart: 43 -> 46, of which waited for: 13 -> 13; matrix products, arithmetic and copies ran while one was open for 1% -> 1% of each run, Pallas kernels for 35% -> 41%
where the time goes in v3:
time: 191 us; the launch traced here: 190 us
  Pallas kernels  101 us (53%)
  starting transfers between devices  46.4 us (24%)
  waiting for transfers between devices  35.6 us (19%)
  local copies, waits for them, and re-layouts  3.91 us (2%)
  other arithmetic  2.62 us (1%)
    pallas_call x4, Pallas kernels, correlate(): pl.pallas_call(functools.partial(correlate_kernel, offset, begins, len(le...  79.4 us
    ppermute x21, starting transfers between devices, to_seg(): return lax.ppermute(value, 'seg', [(i, i ^ k) for i in range(seg_count)])  25 us
    ppermute x21, waiting for transfers between devices, to_seg(): return lax.ppermute(value, 'seg', [(i, i ^ k) for i in range(seg_count)])  17.8 us
    ppermute x9, starting transfers between devices, to_plane(): lax.ppermute(value, 'stn', [(i, i ^ k * sides) for i in range(stn_count)])  17.1 us
    ppermute x9, waiting for transfers between devices, to_plane(): lax.ppermute(value, 'stn', [(i, i ^ k * sides) for i in range(stn_count)])  15.9 us
    pallas_call x2, Pallas kernels, whiten(): pl.pallas_call(functools.partial(whiten_kernel, record_len // LANES, firs...  11.1 us
    pallas_call x4, Pallas kernels, route(): pl.pallas_call(route_kernel, grid=(1,), in_specs=[pl.BlockSpec(memory_spa...  10.5 us
    ppermute x16, starting transfers between devices, to_side(): return lax.ppermute(value, 'stn', [(i, i ^ j) for i in range(stn_count)])  4.31 us
  transfers between devices with their start and end apart: 46, of which 13 were waited for; matrix products, arithmetic and copies ran while one was open for 1% of the time, Pallas kernels for 41%

profile of v3, /device:TPU:0, one launch (start us, length us, event | category | flops | bytes accessed | tf_op | source)
XLA Modules:
  0.0 190.2 jit_solution(16780303081797319516)
XLA Ops:
  0.0 3.6 %whiten.2.refs_0_ = bf16[32,4864]{1,0:T(8,128)(2,1)} custom-call(f32[31]{0:T(128)} %taps_ref.3, f32[32,19200]{1,0:T(8,128)} %traces_ref.3, s32[32,32]{1,0:T(8,128)} %flags_ref.3), custom_call_target="tpu_custom_call" | custom-call | tf_op jit(solution)/shard_map/whiten/pallas_call | solution.py:104
  3.6 4.0 %collective-permute-start = (bf16[32,4864]{1,0:T(8,128)(2,1)}, bf16[32,4864]{1,0:T(8,128)(2,1)S(1)}, u32[]{:S(2)}, u32[]{:S(2)}) collective-permute-start(bf16[32,4864]{1,0:T(8,128)(2,1)} %whiten.2.refs_0_), channel_id=1, source_target_pairs={{0,16},{4,20},{8,24},{12,28},{16,0},{20,4},{24,8},{28,12},{1,17},{... | collective-permute-start | bytes 933896 | tf_op jit(solution)/shard_map/ppermute | solution.py:262
  7.7 1.6 collective-permute-start.1
  9.2 1.5 collective-permute-start.2
  10.7 1.5 collective-permute-start.3
  12.3 0.5 collective-permute-start.4
  12.7 7.4 %whiten.3 = (bf16[32,4864]{1,0:T(8,128)(2,1)}, bf16[32,4864]{1,0:T(8,128)(2,1)}, bf16[32,4864]{1,0:T(8,128)(2,1)}, bf16[32,9728]{1,0:T(8,128)(2,1)}, bf16[32,9600]{1,0:T(8,128)(2,1)}) custom-call(f32[31]{0:T(128)} %taps_ref.3, f32[32,19200]{1,0:T(8,128)} %traces_ref.3, s32[32,32]{1,0:T(8,128)} %flags_ref.3), custom_call_target="tpu_custom_call" | custom-call | tf_op jit(solution)/shard_map/whiten/pallas_call | solution.py:104
  20.2 1.8 collective-permute-done.refs_2_
  22.2 3.7 %collective-permute-done.3.refs_2_ = bf16[32,4864]{1,0:T(8,128)(2,1)S(1)} collective-permute-done((bf16[32,4864]{1,0:T(8,128)(2,1)}, bf16[32,4864]{1,0:T(8,128)(2,1)S(1)}, u32[]{:S(2)}, u32[]{:S(2)}) %collective-permute-start.3) | collective-permute-done | bytes 311328 | tf_op jit(solution)/shard_map/ppermute | solution.py:259
  25.9 0.7 copy-done.14
  26.6 1.0 pad_maximum_fusion
  27.6 0.5 collective-permute-start.6
  28.1 0.6 collective-permute-start.7
  28.8 1.4 collective-permute-start.8
  30.2 0.8 collective-permute-start.5
  31.0 1.0 collective-permute-start.9
  32.0 13.8 %collective-permute-done.5.refs_2_ = bf16[32,4864]{1,0:T(8,128)(2,1)S(1)} collective-permute-done((bf16[32,4864]{1,0:T(8,128)(2,1)S(1)}, bf16[32,4864]{1,0:T(8,128)(2,1)S(1)}, u32[]{:S(2)}, u32[]{:S(2)}) %collective-permute-start.5) | collective-permute-done | bytes 311328 | tf_op jit(solution)/shard_map/ppermute | solution.py:262
  45.8 2.3 %collective-permute-done.9.refs_3_ = bf16[32,4864]{1,0:T(8,128)(2,1)S(1)} collective-permute-done((bf16[32,4864]{1,0:T(8,128)(2,1)S(1)}, bf16[32,4864]{1,0:T(8,128)(2,1)S(1)}, u32[]{:S(2)}, u32[]{:S(2)}) %collective-permute-start.9) | collective-permute-done | bytes 311328 | tf_op jit(solution)/shard_map/ppermute | solution.py:259
  48.1 1.0 collective-permute-done.8.refs_2_
  49.2 0.9 pad_maximum_fusion.1
  50.1 1.6 collective-permute-start.11
  51.7 0.6 broadcast_xor_fusion
  52.4 2.6 %route.4 = (bf16[32,4864]{1,0:T(8,128)(2,1)}, bf16[32,4864]{1,0:T(8,128)(2,1)}, bf16[32,4864]{1,0:T(8,128)(2,1)}, bf16[32,4864]{1,0:T(8,128)(2,1)}) custom-call(s32[4]{0:T(128)} %get-tuple-element.213.place_ref, bf16[32,4864]{1,0:T(8,128)(2,1)} %whiten.2.refs_0_, bf16[32,4864]{1,0:T(8,128)(2,1)} %copy-done.24, bf16[32,4864]{1,0:T(8,128)(2,1)} %copy-done.12, ...), custom_call_target="tpu_custom_call" | custom-call | tf_op jit(solution)/shard_map/route/pallas_call | solution.py:132
  54.9 1.2 collective-permute-start.12
  56.1 1.4 collective-permute-start.13
  57.5 1.0 collective-permute-start.14
  58.5 1.7 collective-permute-start.10
  60.2 4.2 %collective-permute-done.12.refs_5_ = bf16[32,4864]{1,0:T(8,128)(2,1)S(1)} collective-permute-done((bf16[32,4864]{1,0:T(8,128)(2,1)}, bf16[32,4864]{1,0:T(8,128)(2,1)S(1)}, u32[]{:S(2)}, u32[]{:S(2)}) %collective-permute-start.12) | collective-permute-done | bytes 311328 | tf_op jit(solution)/shard_map/ppermute | solution.py:259
  64.4 4.7 %collective-permute-done.13.refs_6_ = bf16[32,4864]{1,0:T(8,128)(2,1)S(1)} collective-permute-done((bf16[32,4864]{1,0:T(8,128)(2,1)}, bf16[32,4864]{1,0:T(8,128)(2,1)S(1)}, u32[]{:S(2)}, u32[]{:S(2)}) %collective-permute-start.13) | collective-permute-done | bytes 311328 | tf_op jit(solution)/shard_map/ppermute | solution.py:259
  69.3 0.5 collective-permute-start.21
  69.9 0.4 collective-permute-start.23
  70.4 5.0 %collective-permute-start.16 = (bf16[64,4864]{1,0:T(8,128)(2,1)S(1)}, bf16[64,4864]{1,0:T(8,128)(2,1)S(1)}, u32[]{:S(2)}, u32[]{:S(2)}) collective-permute-start(bf16[64,4864]{1,0:T(8,128)(2,1)S(1)} %pad_maximum_fusion.2), channel_id=1, source_target_pairs={{0,8},{4,12},{8,0},{12,4},{16,24},{20,28},{24,16},{28,20},{1,9},{5... | collective-permute-start | bytes 1867784 | tf_op jit(solution)/shard_map/ppermute | solution.py:262
  75.3 2.7 %route.5 = (bf16[32,4864]{1,0:T(8,128)(2,1)}, bf16[32,4864]{1,0:T(8,128)(2,1)}, bf16[32,4864]{1,0:T(8,128)(2,1)}, bf16[32,4864]{1,0:T(8,128)(2,1)}) custom-call(s32[4]{0:T(128)} %get-tuple-element.213.place_ref, bf16[32,4864]{1,0:T(8,128)(2,1)} %get-tuple-element.167.refs_0_, bf16[64,4864]{1,0:T(8,128)(2,1)} %copy-done.8, bf16[32,4864]{1,0:T(8,128)(2,1)} %copy-done.11, ...), custom_call_target="tpu_custom_call" | custom-call | tf_op jit(solution)/shard_map/route/pallas_call | solution.py:132
  78.1 2.0 %collective-permute-start.17 = (bf16[32,4864]{1,0:T(8,128)(2,1)}, bf16[32,4864]{1,0:T(8,128)(2,1)S(1)}, u32[]{:S(2)}, u32[]{:S(2)}) collective-permute-start(bf16[32,4864]{1,0:T(8,128)(2,1)} %get-tuple-element.160), channel_id=1, source_target_pairs={{0,1},{1,0},{2,3},{3,2},{4,5},{5,4},{6,7},{7,6},{8,9},{9,8},{10,11... | collective-permute-start | bytes 933896 | tf_op jit(solution)/shard_map/ppermute | solution.py:259
  80.2 0.6 collective-permute-start.18
  80.7 1.0 collective-permute-start.19
  81.7 0.7 copy-done.22
  82.5 1.9 collective-permute-start.15
  84.4 0.6 concatenate.13.place_ref
  85.0 19.4 %correlate.4.refs_12_ = f32[41,128,256]{2,1,0:T(8,128)} custom-call(s32[12]{0:T(128)} %concatenate.13.place_ref, bf16[32,4864]{1,0:T(8,128)(2,1)} %whiten.2.refs_0_, bf16[32,4864]{1,0:T(8,128)(2,1)} %copy-done.13, bf16[32,4864]{1,0:T(8,128)(2,1)} %copy-done.14, bf16[32,4864]{1,0:T(8,128)(2,1)} %copy-done.15, bf16[32,4864]{1,0:T(8,128)(2,1)} %get-tuple-element.163.refs_4_, ...), custom_call_target="tpu_custom_call" | custom-call | tf_op jit(solution)/shard_map/correlate/pallas_call | solution.py:232
  104.6 0.5 collective-permute-start.30
  105.2 0.4 collective-permute-start.32
  105.6 1.8 collective-permute-start.28
  107.4 2.5 %route.6 = (bf16[32,4864]{1,0:T(8,128)(2,1)}, bf16[32,4864]{1,0:T(8,128)(2,1)}, bf16[32,4864]{1,0:T(8,128)(2,1)}, bf16[32,4864]{1,0:T(8,128)(2,1)}) custom-call(s32[4]{0:T(128)} %get-tuple-element.213.place_ref, bf16[32,4864]{1,0:T(8,128)(2,1)} %get-tuple-element.187.refs_0_, bf16[64,4864]{1,0:T(8,128)(2,1)} %copy-done.6, bf16[32,4864]{1,0:T(8,128)(2,1)} %copy-done.10, ...), custom_call_target="tpu_custom_call" | custom-call | tf_op jit(solution)/shard_map/route/pallas_call | solution.py:132
  109.9 0.7 collective-permute-start.25
  110.7 1.0 collective-permute-start.26
  111.7 1.8 collective-permute-start.27
  113.6 0.7 copy-done.48
  114.2 19.9 %correlate.5.refs_12_ = f32[41,128,256]{2,1,0:T(8,128)} custom-call(s32[12]{0:T(128)} %concatenate.13.place_ref, bf16[32,4864]{1,0:T(8,128)(2,1)} %get-tuple-element.167.refs_0_, bf16[32,9728]{1,0:T(8,128)(2,1)} %copy-done.4, bf16[32,9728]{1,0:T(8,128)(2,1)} %copy-done.5, bf16[32,4864]{1,0:T(8,128)(2,1)} %copy-done.26, ...), custom_call_target="tpu_custom_call", output_to_operand_aliasing={{}: (13, {})} | custom-call | tf_op jit(solution)/shard_map/correlate/pallas_call | solution.py:232
  134.2 1.7 collective-permute-done.27.refs_7_
  136.1 0.5 collective-permute-start.39
  137.1 1.8 collective-permute-start.36
  138.8 2.7 %route.7 = (bf16[32,4864]{1,0:T(8,128)(2,1)}, bf16[32,4864]{1,0:T(8,128)(2,1)}, bf16[32,4864]{1,0:T(8,128)(2,1)}, bf16[32,4864]{1,0:T(8,128)(2,1)}) custom-call(s32[4]{0:T(128)} %get-tuple-element.213.place_ref, bf16[32,4864]{1,0:T(8,128)(2,1)} %get-tuple-element.204.refs_0_, bf16[64,4864]{1,0:T(8,128)(2,1)} %copy-done.7, bf16[32,4864]{1,0:T(8,128)(2,1)} %copy-done.23, ...), custom_call_target="tpu_custom_call" | custom-call | tf_op jit(solution)/shard_map/route/pallas_call | solution.py:132
  141.9 1.0 collective-permute-start.34
  142.9 2.2 %collective-permute-start.35 = (bf16[32,4864]{1,0:T(8,128)(2,1)}, bf16[32,4864]{1,0:T(8,128)(2,1)S(1)}, u32[]{:S(2)}, u32[]{:S(2)}) collective-permute-start(bf16[32,4864]{1,0:T(8,128)(2,1)} %get-tuple-element.198), channel_id=1, source_target_pairs={{0,3},{1,2},{2,1},{3,0},{4,7},{5,6},{6,5},{7,4},{8,11},{9,10},{10,... | collective-permute-start | bytes 933896 | tf_op jit(solution)/shard_map/ppermute | solution.py:259
  145.1 0.7 collective-permute-start.37
  145.9 19.9 %correlate.6.refs_12_ = f32[41,128,256]{2,1,0:T(8,128)} custom-call(s32[12]{0:T(128)} %concatenate.13.place_ref, bf16[32,4864]{1,0:T(8,128)(2,1)} %get-tuple-element.187.refs_0_, bf16[32,9728]{1,0:T(8,128)(2,1)} %copy-done.4, bf16[32,9728]{1,0:T(8,128)(2,1)} %copy-done.5, bf16[32,9600]{1,0:T(8,128)(2,1)} %copy-done.9, ...), custom_call_target="tpu_custom_call", output_to_operand_aliasing={{}: (13, {})} | custom-call | tf_op jit(solution)/shard_map/correlate/pallas_call | solution.py:232
  166.0 0.5 collective-permute-start.43
  167.0 0.6 collective-permute-done.42.refs_8_
  167.6 0.4 collective-permute-done.43.refs_9_
  168.0 0.4 collective-permute-done.44.refs_10_
  168.5 0.4 collective-permute-done.45.refs_11_
  169.2 0.7 copy-done.52
  169.9 20.1 %correlate.7 = f32[41,128,256]{2,1,0:T(8,128)} custom-call(s32[12]{0:T(128)} %concatenate.13.place_ref, bf16[32,4864]{1,0:T(8,128)(2,1)} %get-tuple-element.204.refs_0_, bf16[32,4864]{1,0:T(8,128)(2,1)} %copy-done.35, bf16[32,4864]{1,0:T(8,128)(2,1)} %copy-done.40, bf16[32,9600]{1,0:T(8,128)(2,1)} %copy-done.9, ...), custom_call_target="tpu_custom_call", output_to_operand_aliasing={{}: (13, {})} | custom-call | tf_op jit(solution)/shard_map/correlate/pallas_call | solution.py:232
  (152 shorter events, 2.6 us)
Async XLA Ops:
  3.6 18.4 %collective-permute-start = (bf16[32,4864]{1,0:T(8,128)(2,1)}, bf16[32,4864]{1,0:T(8,128)(2,1)S(1)}, u32[]{:S(2)}, u32[]{:S(2)}) collective-permute-start(bf16[32,4864]{1,0:T(8,128)(2,1)} %whiten.2.refs_0_), channel_id=1, source_target_pairs={{0,16},{4,20},{8,24},{12,28},{16,0},{20,4},{24,8},{28,12},{1,17},{... | collective-permute-start | bytes 933896 | tf_op jit(solution)/shard_map/ppermute | solution.py:262
  7.7 14.5 %collective-permute-start.1 = (bf16[32,4864]{1,0:T(8,128)(2,1)}, bf16[32,4864]{1,0:T(8,128)(2,1)S(1)}, u32[]{:S(2)}, u32[]{:S(2)}) collective-permute-start(bf16[32,4864]{1,0:T(8,128)(2,1)} %whiten.2.refs_0_), channel_id=1, source_target_pairs={{0,8},{4,12},{8,0},{12,4},{16,24},{20,28},{24,16},{28,20},{1,9},{5... | collective-permute-start | bytes 933896 | tf_op jit(solution)/shard_map/ppermute | solution.py:262
  9.2 13.0 %collective-permute-start.2 = (bf16[32,4864]{1,0:T(8,128)(2,1)}, bf16[32,4864]{1,0:T(8,128)(2,1)S(1)}, u32[]{:S(2)}, u32[]{:S(2)}) collective-permute-start(bf16[32,4864]{1,0:T(8,128)(2,1)} %whiten.2.refs_0_), channel_id=1, source_target_pairs={{0,1},{1,0},{2,3},{3,2},{4,5},{5,4},{6,7},{7,6},{8,9},{9,8},{10,11... | collective-permute-start | bytes 933896 | tf_op jit(solution)/shard_map/ppermute | solution.py:259
  10.7 15.1 %collective-permute-start.3 = (bf16[32,4864]{1,0:T(8,128)(2,1)}, bf16[32,4864]{1,0:T(8,128)(2,1)S(1)}, u32[]{:S(2)}, u32[]{:S(2)}) collective-permute-start(bf16[32,4864]{1,0:T(8,128)(2,1)} %whiten.2.refs_0_), channel_id=1, source_target_pairs={{0,2},{1,3},{2,0},{3,1},{4,6},{5,7},{6,4},{7,5},{8,10},{9,11},{10,... | collective-permute-start | bytes 933896 | tf_op jit(solution)/shard_map/ppermute | solution.py:259
  12.3 13.6 %collective-permute-start.4 = (bf16[32,4864]{1,0:T(8,128)(2,1)}, bf16[32,4864]{1,0:T(8,128)(2,1)S(1)}, u32[]{:S(2)}, u32[]{:S(2)}) collective-permute-start(bf16[32,4864]{1,0:T(8,128)(2,1)} %whiten.2.refs_0_), channel_id=1, source_target_pairs={{0,3},{1,2},{2,1},{3,0},{4,7},{5,6},{6,5},{7,4},{8,11},{9,10},{10,... | collective-permute-start | bytes 933896 | tf_op jit(solution)/shard_map/ppermute | solution.py:259
  20.2 10.0 %copy-start.3 = (bf16[32,4864]{1,0:T(8,128)(2,1)S(1)}, bf16[32,4864]{1,0:T(8,128)(2,1)}, u32[]{:S(2)}) copy-start(bf16[32,4864]{1,0:T(8,128)(2,1)} %get-tuple-element.167.refs_0_) | copy-start | bytes 933892
  20.2 29.0 %copy-start.2 = (bf16[32,4864]{1,0:T(8,128)(2,1)S(1)}, bf16[32,4864]{1,0:T(8,128)(2,1)}, u32[]{:S(2)}) copy-start(bf16[32,4864]{1,0:T(8,128)(2,1)} %get-tuple-element.187.refs_0_) | copy-start | bytes 933892
  22.0 28.1 %copy-start.12 = (bf16[32,4864]{1,0:T(8,128)(2,1)}, bf16[32,4864]{1,0:T(8,128)(2,1)S(1)}, u32[]{:S(2)}) copy-start(bf16[32,4864]{1,0:T(8,128)(2,1)S(1)} %collective-permute-done.refs_2_) | copy-start | bytes 933892
  22.2 29.5 %copy-start.24 = (bf16[32,4864]{1,0:T(8,128)(2,1)}, bf16[32,4864]{1,0:T(8,128)(2,1)S(1)}, u32[]{:S(2)}) copy-start(bf16[32,4864]{1,0:T(8,128)(2,1)S(1)} %collective-permute-done.1.refs_1_) | copy-start | bytes 933892
  25.9 24.2 %copy-start.15 = (bf16[32,4864]{1,0:T(8,128)(2,1)}, bf16[32,4864]{1,0:T(8,128)(2,1)S(1)}, u32[]{:S(2)}) copy-start(bf16[32,4864]{1,0:T(8,128)(2,1)S(1)} %collective-permute-done.4.refs_3_) | copy-start | bytes 933892
  27.6 42.7 %copy-start = (bf16[32,4864]{1,0:T(8,128)(2,1)S(1)}, bf16[32,4864]{1,0:T(8,128)(2,1)}, u32[]{:S(2)}) copy-start(bf16[32,4864]{1,0:T(8,128)(2,1)} %get-tuple-element.204.refs_0_) | copy-start | bytes 933892
  27.6 20.5 %collective-permute-start.6 = (bf16[64,4864]{1,0:T(8,128)(2,1)S(1)}, bf16[64,4864]{1,0:T(8,128)(2,1)S(1)}, u32[]{:S(2)}, u32[]{:S(2)}) collective-permute-start(bf16[64,4864]{1,0:T(8,128)(2,1)S(1)} %pad_maximum_fusion), channel_id=1, source_target_pairs={{0,8},{4,12},{8,0},{12,4},{16,24},{20,28},{24,16},{28,20},{1,9},{5... | collective-permute-start | bytes 1867784 | tf_op jit(solution)/shard_map/ppermute | solution.py:262
  28.1 20.0 %collective-permute-start.7 = (bf16[32,9728]{1,0:T(8,128)(2,1)S(1)}, bf16[32,9728]{1,0:T(8,128)(2,1)S(1)}, u32[]{:S(2)}, u32[]{:S(2)}) collective-permute-start(bf16[32,9728]{1,0:T(8,128)(2,1)S(1)} %copy-done.53), channel_id=1, source_target_pairs={{0,1},{1,0},{2,3},{3,2},{4,5},{5,4},{6,7},{7,6},{8,9},{9,8},{10,11... | collective-permute-start | bytes 1867784 | tf_op jit(solution)/shard_map/ppermute | solution.py:259
  28.8 20.4 %collective-permute-start.8 = (bf16[32,9728]{1,0:T(8,128)(2,1)S(1)}, bf16[32,9728]{1,0:T(8,128)(2,1)S(1)}, u32[]{:S(2)}, u32[]{:S(2)}) collective-permute-start(bf16[32,9728]{1,0:T(8,128)(2,1)S(1)} %copy-done.53), channel_id=1, source_target_pairs={{0,2},{1,3},{2,0},{3,1},{4,6},{5,7},{6,4},{7,5},{8,10},{9,11},{10,... | collective-permute-start | bytes 1867784 | tf_op jit(solution)/shard_map/ppermute | solution.py:259
  30.2 15.6 %collective-permute-start.5 = (bf16[32,4864]{1,0:T(8,128)(2,1)S(1)}, bf16[32,4864]{1,0:T(8,128)(2,1)S(1)}, u32[]{:S(2)}, u32[]{:S(2)}) collective-permute-start(bf16[32,4864]{1,0:T(8,128)(2,1)S(1)} %copy-done.3), channel_id=1, source_target_pairs={{0,16},{4,20},{8,24},{12,28},{16,0},{20,4},{24,8},{28,12},{1,17},{... | collective-permute-start | bytes 933896 | tf_op jit(solution)/shard_map/ppermute | solution.py:262
  31.0 17.1 %collective-permute-start.9 = (bf16[32,4864]{1,0:T(8,128)(2,1)S(1)}, bf16[32,4864]{1,0:T(8,128)(2,1)S(1)}, u32[]{:S(2)}, u32[]{:S(2)}) collective-permute-start(bf16[32,4864]{1,0:T(8,128)(2,1)S(1)} %copy-done.3), channel_id=1, source_target_pairs={{0,3},{1,2},{2,1},{3,0},{4,7},{5,6},{6,5},{7,4},{8,11},{9,10},{10,... | collective-permute-start | bytes 933896 | tf_op jit(solution)/shard_map/ppermute | solution.py:259
  50.1 19.1 %collective-permute-start.11 = (bf16[64,4864]{1,0:T(8,128)(2,1)}, bf16[64,4864]{1,0:T(8,128)(2,1)S(1)}, u32[]{:S(2)}, u32[]{:S(2)}) collective-permute-start(bf16[64,4864]{1,0:T(8,128)(2,1)} %pad_maximum_fusion.1), channel_id=1, source_target_pairs={{0,8},{4,12},{8,0},{12,4},{16,24},{20,28},{24,16},{28,20},{1,9},{5... | collective-permute-start | bytes 1867784 | tf_op jit(solution)/shard_map/ppermute | solution.py:262
  54.9 9.5 %collective-permute-start.12 = (bf16[32,4864]{1,0:T(8,128)(2,1)}, bf16[32,4864]{1,0:T(8,128)(2,1)S(1)}, u32[]{:S(2)}, u32[]{:S(2)}) collective-permute-start(bf16[32,4864]{1,0:T(8,128)(2,1)} %get-tuple-element.141), channel_id=1, source_target_pairs={{0,1},{1,0},{2,3},{3,2},{4,5},{5,4},{6,7},{7,6},{8,9},{9,8},{10,11... | collective-permute-start | bytes 933896 | tf_op jit(solution)/shard_map/ppermute | solution.py:259
  56.1 13.1 %collective-permute-start.13 = (bf16[32,4864]{1,0:T(8,128)(2,1)}, bf16[32,4864]{1,0:T(8,128)(2,1)S(1)}, u32[]{:S(2)}, u32[]{:S(2)}) collective-permute-start(bf16[32,4864]{1,0:T(8,128)(2,1)} %get-tuple-element.142), channel_id=1, source_target_pairs={{0,2},{1,3},{2,0},{3,1},{4,6},{5,7},{6,4},{7,5},{8,10},{9,11},{10,... | collective-permute-start | bytes 933896 | tf_op jit(solution)/shard_map/ppermute | solution.py:259
  57.5 11.7 %collective-permute-start.14 = (bf16[32,4864]{1,0:T(8,128)(2,1)}, bf16[32,4864]{1,0:T(8,128)(2,1)S(1)}, u32[]{:S(2)}, u32[]{:S(2)}) collective-permute-start(bf16[32,4864]{1,0:T(8,128)(2,1)} %get-tuple-element.143), channel_id=1, source_target_pairs={{0,3},{1,2},{2,1},{3,0},{4,7},{5,6},{6,5},{7,4},{8,11},{9,10},{10,... | collective-permute-start | bytes 933896 | tf_op jit(solution)/shard_map/ppermute | solution.py:259
  58.5 10.7 %collective-permute-start.10 = (bf16[32,4864]{1,0:T(8,128)(2,1)S(1)}, bf16[32,4864]{1,0:T(8,128)(2,1)S(1)}, u32[]{:S(2)}, u32[]{:S(2)}) collective-permute-start(bf16[32,4864]{1,0:T(8,128)(2,1)S(1)} %copy-done.2), channel_id=1, source_target_pairs={{0,16},{4,20},{8,24},{12,28},{16,0},{20,4},{24,8},{28,12},{1,17},{... | collective-permute-start | bytes 933896 | tf_op jit(solution)/shard_map/ppermute | solution.py:262
  64.4 13.6 %copy-start.16 = (bf16[32,4864]{1,0:T(8,128)(2,1)}, bf16[32,4864]{1,0:T(8,128)(2,1)S(1)}, u32[]{:S(2)}) copy-start(bf16[32,4864]{1,0:T(8,128)(2,1)S(1)} %collective-permute-done.12.refs_5_) | copy-start | bytes 933892
  69.2 15.8 %copy-start.17 = (bf16[32,4864]{1,0:T(8,128)(2,1)}, bf16[32,4864]{1,0:T(8,128)(2,1)S(1)}, u32[]{:S(2)}) copy-start(bf16[32,4864]{1,0:T(8,128)(2,1)S(1)} %collective-permute-done.13.refs_6_) | copy-start | bytes 933892
  69.2 15.8 %copy-start.18 = (bf16[32,4864]{1,0:T(8,128)(2,1)}, bf16[32,4864]{1,0:T(8,128)(2,1)S(1)}, u32[]{:S(2)}) copy-start(bf16[32,4864]{1,0:T(8,128)(2,1)S(1)} %collective-permute-done.14.refs_7_) | copy-start | bytes 933892
  69.2 8.9 %collective-permute-start.20 = (bf16[32,4864]{1,0:T(8,128)(2,1)}, bf16[32,4864]{1,0:T(8,128)(2,1)S(1)}, u32[]{:S(2)}, u32[]{:S(2)}) collective-permute-start(bf16[32,4864]{1,0:T(8,128)(2,1)} %get-tuple-element.163.refs_4_), channel_id=1, source_target_pairs={{0,4},{4,0},{8,12},{12,8},{16,20},{20,16},{24,28},{28,24},{1,5},{5... | collective-permute-start | bytes 933896 | tf_op jit(solution)/shard_map/ppermute | solution.py:265
  69.3 10.8 %collective-permute-start.21 = (bf16[32,4864]{1,0:T(8,128)(2,1)S(1)}, bf16[32,4864]{1,0:T(8,128)(2,1)S(1)}, u32[]{:S(2)}, u32[]{:S(2)}) collective-permute-start(bf16[32,4864]{1,0:T(8,128)(2,1)S(1)} %collective-permute-done.12.refs_5_), channel_id=1, source_target_pairs={{0,4},{4,0},{8,12},{12,8},{16,20},{20,16},{24,28},{28,24},{1,5},{5... | collective-permute-start | bytes 933896 | tf_op jit(solution)/shard_map/ppermute | solution.py:265
  69.8 10.9 %collective-permute-start.22 = (bf16[32,4864]{1,0:T(8,128)(2,1)S(1)}, bf16[32,4864]{1,0:T(8,128)(2,1)S(1)}, u32[]{:S(2)}, u32[]{:S(2)}) collective-permute-start(bf16[32,4864]{1,0:T(8,128)(2,1)S(1)} %collective-permute-done.13.refs_6_), channel_id=1, source_target_pairs={{0,4},{4,0},{8,12},{12,8},{16,20},{20,16},{24,28},{28,24},{1,5},{5... | collective-permute-start | bytes 933896 | tf_op jit(solution)/shard_map/ppermute | solution.py:265
  69.9 11.8 %collective-permute-start.23 = (bf16[32,4864]{1,0:T(8,128)(2,1)S(1)}, bf16[32,4864]{1,0:T(8,128)(2,1)S(1)}, u32[]{:S(2)}, u32[]{:S(2)}) collective-permute-start(bf16[32,4864]{1,0:T(8,128)(2,1)S(1)} %collective-permute-done.14.refs_7_), channel_id=1, source_target_pairs={{0,4},{4,0},{8,12},{12,8},{16,20},{20,16},{24,28},{28,24},{1,5},{5... | collective-permute-start | bytes 933896 | tf_op jit(solution)/shard_map/ppermute | solution.py:265
  70.4 34.1 %collective-permute-start.16 = (bf16[64,4864]{1,0:T(8,128)(2,1)S(1)}, bf16[64,4864]{1,0:T(8,128)(2,1)S(1)}, u32[]{:S(2)}, u32[]{:S(2)}) collective-permute-start(bf16[64,4864]{1,0:T(8,128)(2,1)S(1)} %pad_maximum_fusion.2), channel_id=1, source_target_pairs={{0,8},{4,12},{8,0},{12,4},{16,24},{20,28},{24,16},{28,20},{1,9},{5... | collective-permute-start | bytes 1867784 | tf_op jit(solution)/shard_map/ppermute | solution.py:262
  78.1 26.3 %collective-permute-start.17 = (bf16[32,4864]{1,0:T(8,128)(2,1)}, bf16[32,4864]{1,0:T(8,128)(2,1)S(1)}, u32[]{:S(2)}, u32[]{:S(2)}) collective-permute-start(bf16[32,4864]{1,0:T(8,128)(2,1)} %get-tuple-element.160), channel_id=1, source_target_pairs={{0,1},{1,0},{2,3},{3,2},{4,5},{5,4},{6,7},{7,6},{8,9},{9,8},{10,11... | collective-permute-start | bytes 933896 | tf_op jit(solution)/shard_map/ppermute | solution.py:259
  80.2 24.3 %collective-permute-start.18 = (bf16[32,4864]{1,0:T(8,128)(2,1)}, bf16[32,4864]{1,0:T(8,128)(2,1)S(1)}, u32[]{:S(2)}, u32[]{:S(2)}) collective-permute-start(bf16[32,4864]{1,0:T(8,128)(2,1)} %get-tuple-element.161), channel_id=1, source_target_pairs={{0,2},{1,3},{2,0},{3,1},{4,6},{5,7},{6,4},{7,5},{8,10},{9,11},{10,... | collective-permute-start | bytes 933896 | tf_op jit(solution)/shard_map/ppermute | solution.py:259
  80.7 23.7 %collective-permute-start.19 = (bf16[32,4864]{1,0:T(8,128)(2,1)}, bf16[32,4864]{1,0:T(8,128)(2,1)S(1)}, u32[]{:S(2)}, u32[]{:S(2)}) collective-permute-start(bf16[32,4864]{1,0:T(8,128)(2,1)} %get-tuple-element.162), channel_id=1, source_target_pairs={{0,3},{1,2},{2,1},{3,0},{4,7},{5,6},{6,5},{7,4},{8,11},{9,10},{10,... | collective-permute-start | bytes 933896 | tf_op jit(solution)/shard_map/ppermute | solution.py:259
  82.5 22.0 %collective-permute-start.15 = (bf16[32,4864]{1,0:T(8,128)(2,1)S(1)}, bf16[32,4864]{1,0:T(8,128)(2,1)S(1)}, u32[]{:S(2)}, u32[]{:S(2)}) collective-permute-start(bf16[32,4864]{1,0:T(8,128)(2,1)S(1)} %copy-done), channel_id=1, source_target_pairs={{0,16},{4,20},{8,24},{12,28},{16,0},{20,4},{24,8},{28,12},{1,17},{... | collective-permute-start | bytes 933896 | tf_op jit(solution)/shard_map/ppermute | solution.py:262
  85.0 19.5 %copy-start.27 = (bf16[32,4864]{1,0:T(8,128)(2,1)S(1)}, bf16[32,4864]{1,0:T(8,128)(2,1)}, u32[]{:S(2)}) copy-start(bf16[32,4864]{1,0:T(8,128)(2,1)} %get-tuple-element.182.refs_4_) | copy-start | bytes 933892
  104.5 29.7 %copy-start.23 = (bf16[32,4864]{1,0:T(8,128)(2,1)}, bf16[32,4864]{1,0:T(8,128)(2,1)S(1)}, u32[]{:S(2)}) copy-start(bf16[32,4864]{1,0:T(8,128)(2,1)S(1)} %collective-permute-done.15.refs_2_) | copy-start | bytes 933892
  104.5 5.4 %collective-permute-start.29 = (bf16[32,4864]{1,0:T(8,128)(2,1)S(1)}, bf16[32,4864]{1,0:T(8,128)(2,1)S(1)}, u32[]{:S(2)}, u32[]{:S(2)}) collective-permute-start(bf16[32,4864]{1,0:T(8,128)(2,1)S(1)} %copy-done.27), channel_id=1, source_target_pairs={{0,4},{4,0},{8,12},{12,8},{16,20},{20,16},{24,28},{28,24},{1,5},{5... | collective-permute-start | bytes 933896 | tf_op jit(solution)/shard_map/ppermute | solution.py:265
  104.6 6.0 %collective-permute-start.30 = (bf16[32,4864]{1,0:T(8,128)(2,1)S(1)}, bf16[32,4864]{1,0:T(8,128)(2,1)S(1)}, u32[]{:S(2)}, u32[]{:S(2)}) collective-permute-start(bf16[32,4864]{1,0:T(8,128)(2,1)S(1)} %collective-permute-done.17.refs_5_), channel_id=1, source_target_pairs={{0,4},{4,0},{8,12},{12,8},{16,20},{20,16},{24,28},{28,24},{1,5},{5... | collective-permute-start | bytes 933896 | tf_op jit(solution)/shard_map/ppermute | solution.py:265
  105.1 6.6 %collective-permute-start.31 = (bf16[32,4864]{1,0:T(8,128)(2,1)S(1)}, bf16[32,4864]{1,0:T(8,128)(2,1)S(1)}, u32[]{:S(2)}, u32[]{:S(2)}) collective-permute-start(bf16[32,4864]{1,0:T(8,128)(2,1)S(1)} %collective-permute-done.18.refs_6_), channel_id=1, source_target_pairs={{0,4},{4,0},{8,12},{12,8},{16,20},{20,16},{24,28},{28,24},{1,5},{5... | collective-permute-start | bytes 933896 | tf_op jit(solution)/shard_map/ppermute | solution.py:265
  105.2 8.3 %collective-permute-start.32 = (bf16[32,4864]{1,0:T(8,128)(2,1)S(1)}, bf16[32,4864]{1,0:T(8,128)(2,1)S(1)}, u32[]{:S(2)}, u32[]{:S(2)}) collective-permute-start(bf16[32,4864]{1,0:T(8,128)(2,1)S(1)} %collective-permute-done.19.refs_7_), channel_id=1, source_target_pairs={{0,4},{4,0},{8,12},{12,8},{16,20},{20,16},{24,28},{28,24},{1,5},{5... | collective-permute-start | bytes 933896 | tf_op jit(solution)/shard_map/ppermute | solution.py:265
  105.6 30.3 %collective-permute-start.28 = (bf16[32,9600]{1,0:T(8,128)(2,1)}, bf16[32,9600]{1,0:T(8,128)(2,1)S(1)}, u32[]{:S(2)}, u32[]{:S(2)}) collective-permute-start(bf16[32,9600]{1,0:T(8,128)(2,1)} %get-tuple-element.170), channel_id=1, source_target_pairs={{0,3},{1,2},{2,1},{3,0},{4,7},{5,6},{6,5},{7,4},{8,11},{9,10},{10,... | collective-permute-start | bytes 1843208 | tf_op jit(solution)/shard_map/ppermute | solution.py:259
  109.9 24.2 %collective-permute-start.25 = (bf16[32,4864]{1,0:T(8,128)(2,1)}, bf16[32,4864]{1,0:T(8,128)(2,1)S(1)}, u32[]{:S(2)}, u32[]{:S(2)}) collective-permute-start(bf16[32,4864]{1,0:T(8,128)(2,1)} %get-tuple-element.179), channel_id=1, source_target_pairs={{0,1},{1,0},{2,3},{3,2},{4,5},{5,4},{6,7},{7,6},{8,9},{9,8},{10,11... | collective-permute-start | bytes 933896 | tf_op jit(solution)/shard_map/ppermute | solution.py:259
  110.7 23.5 %collective-permute-start.26 = (bf16[32,4864]{1,0:T(8,128)(2,1)}, bf16[32,4864]{1,0:T(8,128)(2,1)S(1)}, u32[]{:S(2)}, u32[]{:S(2)}) collective-permute-start(bf16[32,4864]{1,0:T(8,128)(2,1)} %get-tuple-element.180), channel_id=1, source_target_pairs={{0,2},{1,3},{2,0},{3,1},{4,6},{5,7},{6,4},{7,5},{8,10},{9,11},{10,... | collective-permute-start | bytes 933896 | tf_op jit(solution)/shard_map/ppermute | solution.py:259
  111.7 24.3 %copy-start.31 = (bf16[32,4864]{1,0:T(8,128)(2,1)S(1)}, bf16[32,4864]{1,0:T(8,128)(2,1)}, u32[]{:S(2)}) copy-start(bf16[32,4864]{1,0:T(8,128)(2,1)} %get-tuple-element.199.refs_4_) | copy-start | bytes 933892
  111.7 24.3 %collective-permute-start.27 = (bf16[32,4864]{1,0:T(8,128)(2,1)}, bf16[32,4864]{1,0:T(8,128)(2,1)S(1)}, u32[]{:S(2)}, u32[]{:S(2)}) collective-permute-start(bf16[32,4864]{1,0:T(8,128)(2,1)} %get-tuple-element.181), channel_id=1, source_target_pairs={{0,3},{1,2},{2,1},{3,0},{4,7},{5,6},{6,5},{7,4},{8,11},{9,10},{10,... | collective-permute-start | bytes 933896 | tf_op jit(solution)/shard_map/ppermute | solution.py:259
  113.5 22.4 %collective-permute-start.24 = (bf16[32,4864]{1,0:T(8,128)(2,1)S(1)}, bf16[32,4864]{1,0:T(8,128)(2,1)S(1)}, u32[]{:S(2)}, u32[]{:S(2)}) collective-permute-start(bf16[32,4864]{1,0:T(8,128)(2,1)S(1)} %collective-permute-done.15.refs_2_), channel_id=1, source_target_pairs={{0,8},{4,12},{8,0},{12,4},{16,24},{20,28},{24,16},{28,20},{1,9},{5... | collective-permute-start | bytes 933896 | tf_op jit(solution)/shard_map/ppermute | solution.py:262
  134.2 11.0 %copy-start.1 = (bf16[32,4864]{1,0:T(8,128)(2,1)S(1)}, bf16[32,4864]{1,0:T(8,128)(2,1)}, u32[]{:S(2)}) copy-start(bf16[32,4864]{1,0:T(8,128)(2,1)} %get-tuple-element.204.refs_0_) | copy-start | bytes 933892
  134.2 11.6 %copy-start.32 = (bf16[32,4864]{1,0:T(8,128)(2,1)}, bf16[32,4864]{1,0:T(8,128)(2,1)S(1)}, u32[]{:S(2)}) copy-start(bf16[32,4864]{1,0:T(8,128)(2,1)S(1)} %collective-permute-done.25.refs_5_) | copy-start | bytes 933892
  134.2 11.6 %copy-start.33 = (bf16[32,4864]{1,0:T(8,128)(2,1)}, bf16[32,4864]{1,0:T(8,128)(2,1)S(1)}, u32[]{:S(2)}) copy-start(bf16[32,4864]{1,0:T(8,128)(2,1)S(1)} %collective-permute-done.26.refs_6_) | copy-start | bytes 933892
  135.9 9.9 %copy-start.34 = (bf16[32,4864]{1,0:T(8,128)(2,1)}, bf16[32,4864]{1,0:T(8,128)(2,1)S(1)}, u32[]{:S(2)}) copy-start(bf16[32,4864]{1,0:T(8,128)(2,1)S(1)} %collective-permute-done.27.refs_7_) | copy-start | bytes 933892
  136.0 9.9 %copy-start.9 = (bf16[32,9600]{1,0:T(8,128)(2,1)}, bf16[32,9600]{1,0:T(8,128)(2,1)S(1)}, u32[]{:S(2)}) copy-start(bf16[32,9600]{1,0:T(8,128)(2,1)S(1)} %collective-permute-done.28.refs_3_) | copy-start | bytes 1843204
  136.0 5.6 %collective-permute-start.38 = (bf16[32,4864]{1,0:T(8,128)(2,1)S(1)}, bf16[32,4864]{1,0:T(8,128)(2,1)S(1)}, u32[]{:S(2)}, u32[]{:S(2)}) collective-permute-start(bf16[32,4864]{1,0:T(8,128)(2,1)S(1)} %copy-done.31), channel_id=1, source_target_pairs={{0,4},{4,0},{8,12},{12,8},{16,20},{20,16},{24,28},{28,24},{1,5},{5... | collective-permute-start | bytes 933896 | tf_op jit(solution)/shard_map/ppermute | solution.py:265
  136.1 5.8 %collective-permute-start.39 = (bf16[32,4864]{1,0:T(8,128)(2,1)S(1)}, bf16[32,4864]{1,0:T(8,128)(2,1)S(1)}, u32[]{:S(2)}, u32[]{:S(2)}) collective-permute-start(bf16[32,4864]{1,0:T(8,128)(2,1)S(1)} %collective-permute-done.25.refs_5_), channel_id=1, source_target_pairs={{0,4},{4,0},{8,12},{12,8},{16,20},{20,16},{24,28},{28,24},{1,5},{5... | collective-permute-start | bytes 933896 | tf_op jit(solution)/shard_map/ppermute | solution.py:265
  136.6 6.3 %collective-permute-start.40 = (bf16[32,4864]{1,0:T(8,128)(2,1)S(1)}, bf16[32,4864]{1,0:T(8,128)(2,1)S(1)}, u32[]{:S(2)}, u32[]{:S(2)}) collective-permute-start(bf16[32,4864]{1,0:T(8,128)(2,1)S(1)} %collective-permute-done.26.refs_6_), channel_id=1, source_target_pairs={{0,4},{4,0},{8,12},{12,8},{16,20},{20,16},{24,28},{28,24},{1,5},{5... | collective-permute-start | bytes 933896 | tf_op jit(solution)/shard_map/ppermute | solution.py:265
  136.6 8.5 %collective-permute-start.41 = (bf16[32,4864]{1,0:T(8,128)(2,1)S(1)}, bf16[32,4864]{1,0:T(8,128)(2,1)S(1)}, u32[]{:S(2)}, u32[]{:S(2)}) collective-permute-start(bf16[32,4864]{1,0:T(8,128)(2,1)S(1)} %collective-permute-done.27.refs_7_), channel_id=1, source_target_pairs={{0,4},{4,0},{8,12},{12,8},{16,20},{20,16},{24,28},{28,24},{1,5},{5... | collective-permute-start | bytes 933896 | tf_op jit(solution)/shard_map/ppermute | solution.py:265
  137.1 28.8 %collective-permute-start.36 = (bf16[32,4864]{1,0:T(8,128)(2,1)S(1)}, bf16[32,4864]{1,0:T(8,128)(2,1)S(1)}, u32[]{:S(2)}, u32[]{:S(2)}) collective-permute-start(bf16[32,4864]{1,0:T(8,128)(2,1)S(1)} %copy-done), channel_id=1, source_target_pairs={{0,1},{1,0},{2,3},{3,2},{4,5},{5,4},{6,7},{7,6},{8,9},{9,8},{10,11... | collective-permute-start | bytes 933896 | tf_op jit(solution)/shard_map/ppermute | solution.py:259
  141.6 24.2 %collective-permute-start.33 = (bf16[32,4864]{1,0:T(8,128)(2,1)}, bf16[32,4864]{1,0:T(8,128)(2,1)S(1)}, u32[]{:S(2)}, u32[]{:S(2)}) collective-permute-start(bf16[32,4864]{1,0:T(8,128)(2,1)} %get-tuple-element.196), channel_id=1, source_target_pairs={{0,1},{1,0},{2,3},{3,2},{4,5},{5,4},{6,7},{7,6},{8,9},{9,8},{10,11... | collective-permute-start | bytes 933896 | tf_op jit(solution)/shard_map/ppermute | solution.py:259
  141.9 23.9 %collective-permute-start.34 = (bf16[32,4864]{1,0:T(8,128)(2,1)}, bf16[32,4864]{1,0:T(8,128)(2,1)S(1)}, u32[]{:S(2)}, u32[]{:S(2)}) collective-permute-start(bf16[32,4864]{1,0:T(8,128)(2,1)} %get-tuple-element.197), channel_id=1, source_target_pairs={{0,2},{1,3},{2,0},{3,1},{4,6},{5,7},{6,4},{7,5},{8,10},{9,11},{10,... | collective-permute-start | bytes 933896 | tf_op jit(solution)/shard_map/ppermute | solution.py:259
  142.9 23.0 %copy-start.36 = (bf16[32,4864]{1,0:T(8,128)(2,1)S(1)}, bf16[32,4864]{1,0:T(8,128)(2,1)}, u32[]{:S(2)}) copy-start(bf16[32,4864]{1,0:T(8,128)(2,1)} %get-tuple-element.208.refs_4_) | copy-start | bytes 933892
  142.9 22.9 %collective-permute-start.35 = (bf16[32,4864]{1,0:T(8,128)(2,1)}, bf16[32,4864]{1,0:T(8,128)(2,1)S(1)}, u32[]{:S(2)}, u32[]{:S(2)}) collective-permute-start(bf16[32,4864]{1,0:T(8,128)(2,1)} %get-tuple-element.198), channel_id=1, source_target_pairs={{0,3},{1,2},{2,1},{3,0},{4,7},{5,6},{6,5},{7,4},{8,11},{9,10},{10,... | collective-permute-start | bytes 933896 | tf_op jit(solution)/shard_map/ppermute | solution.py:259
  145.1 20.7 %collective-permute-start.37 = (bf16[32,4864]{1,0:T(8,128)(2,1)S(1)}, bf16[32,4864]{1,0:T(8,128)(2,1)S(1)}, u32[]{:S(2)}, u32[]{:S(2)}) collective-permute-start(bf16[32,4864]{1,0:T(8,128)(2,1)S(1)} %copy-done.1), channel_id=1, source_target_pairs={{0,2},{1,3},{2,0},{3,1},{4,6},{5,7},{6,4},{7,5},{8,10},{9,11},{10,... | collective-permute-start | bytes 933896 | tf_op jit(solution)/shard_map/ppermute | solution.py:259
  165.9 1.7 collective-permute-start.42
  166.0 2.0 %collective-permute-start.43 = (bf16[32,4864]{1,0:T(8,128)(2,1)S(1)}, bf16[32,4864]{1,0:T(8,128)(2,1)S(1)}, u32[]{:S(2)}, u32[]{:S(2)}) collective-permute-start(bf16[32,4864]{1,0:T(8,128)(2,1)S(1)} %collective-permute-done.33.refs_5_), channel_id=1, source_target_pairs={{0,4},{4,0},{8,12},{12,8},{16,20},{20,16},{24,28},{28,24},{1,5},{5... | collective-permute-start | bytes 933896 | tf_op jit(solution)/shard_map/ppermute | solution.py:265
  166.5 2.0 %collective-permute-start.44 = (bf16[32,4864]{1,0:T(8,128)(2,1)S(1)}, bf16[32,4864]{1,0:T(8,128)(2,1)S(1)}, u32[]{:S(2)}, u32[]{:S(2)}) collective-permute-start(bf16[32,4864]{1,0:T(8,128)(2,1)S(1)} %collective-permute-done.34.refs_6_), channel_id=1, source_target_pairs={{0,4},{4,0},{8,12},{12,8},{16,20},{20,16},{24,28},{28,24},{1,5},{5... | collective-permute-start | bytes 933896 | tf_op jit(solution)/shard_map/ppermute | solution.py:265
  166.6 2.4 %collective-permute-start.45 = (bf16[32,4864]{1,0:T(8,128)(2,1)S(1)}, bf16[32,4864]{1,0:T(8,128)(2,1)S(1)}, u32[]{:S(2)}, u32[]{:S(2)}) collective-permute-start(bf16[32,4864]{1,0:T(8,128)(2,1)S(1)} %collective-permute-done.35.refs_7_), channel_id=1, source_target_pairs={{0,4},{4,0},{8,12},{12,8},{16,20},{20,16},{24,28},{28,24},{1,5},{5... | collective-permute-start | bytes 933896 | tf_op jit(solution)/shard_map/ppermute | solution.py:265
  (36 other events, 128.7 us)

commit v4 on v3

v4 whole, which is shorter than its diff:
```python
import functools
import math

import jax
import jax.numpy as jnp
from jax import lax
from jax.experimental import pallas as pl
from jax.experimental.pallas import tpu as pltpu
from jax.sharding import PartitionSpec as P

SAMP = 600
LAGS = 41
TAPS = 31
RADIUS = 64
LANES = 128
HALF_LAG = (LAGS - 1) // 2
SHIFTS = HALF_LAG + 1
HALF_TAPS = (TAPS - 1) // 2

epsilon = 1e-06
chunk_segs = 8
shift_group = 7
vmem_bytes = 58 << 20


def split_bf16(value):
    high = value.astype(jnp.bfloat16)
    low = (value - high.astype(jnp.float32)).astype(jnp.bfloat16)
    return high, low


def dot_f32(left, right):
    return jnp.dot(left, right, preferred_element_type=jnp.float32)


def whiten_kernel(record_tiles, first, blocks, starts, taps_ref, traces_ref, flags_ref, *out_refs):
    rows = traces_ref.shape[0]

    def tile(j):
        if j < 0 or j >= record_tiles:
            return jnp.zeros((rows, LANES), jnp.float32)
        return traces_ref[:, j * LANES : (j + 1) * LANES]

    stacked = jnp.concatenate([tile(first + j - 1) for j in range(blocks + 3)], axis=0)

    def windows(value):
        return jnp.concatenate([value[:-rows], value[rows:]], axis=1)

    offset = lax.broadcasted_iota(jnp.int32, (2 * LANES, LANES), 0) - lax.broadcasted_iota(
        jnp.int32, (2 * LANES, LANES), 1
    )
    band = jnp.zeros((2 * LANES, LANES), jnp.float32)
    for tap_index in range(TAPS):
        band = jnp.where(offset == tap_index, taps_ref[tap_index], band)
    late_band = jnp.concatenate(
        [jnp.zeros((RADIUS, LANES), jnp.float32), band[: 2 * LANES - RADIUS]], axis=0
    )
    band_high, band_low = split_bf16(jnp.concatenate([band, late_band], axis=1))
    high, low = split_bf16(stacked)
    high, low = windows(high), windows(low)
    both = dot_f32(high, band_high) + dot_f32(low, band_high) + dot_f32(high, band_low)

    magnitude = jnp.abs(both[:, :LANES])
    lane = lax.broadcasted_iota(jnp.int32, (rows, LANES), 1)
    last = record_tiles - first

    def inside_record(j):
        value = magnitude[j * rows : (j + 1) * rows]
        if first + j == 0:
            return jnp.where(lane >= LANES - HALF_TAPS, value, 0.0)
        if j >= last:
            return jnp.where(lane < LANES - HALF_TAPS, value, 0.0) if j == last else jnp.zeros_like(value)
        return value

    magnitude = jnp.concatenate([inside_record(j) for j in range(blocks + 2)], axis=0)
    ones = jnp.where((offset >= 0) & (offset <= 2 * RADIUS), 1.0, 0.0).astype(jnp.bfloat16)
    high, low = split_bf16(magnitude)
    level = (dot_f32(windows(high), ones) + dot_f32(windows(low), ones)) * (1.0 / (2 * RADIUS + 1))
    filtered = both[: (blocks + 1) * rows, LANES:]
    whitened = filtered / (level + epsilon)

    shift = LANES - HALF_TAPS - RADIUS
    moved = pltpu.roll(whitened, LANES - shift, 1)
    lane = lax.broadcasted_iota(jnp.int32, (blocks * rows, LANES), 1)
    aligned = jnp.where(lane < LANES - shift, moved[: blocks * rows], moved[rows:])
    flat = jnp.concatenate([aligned[j * rows : (j + 1) * rows] for j in range(blocks)], axis=1)

    segments = flags_ref.shape[1]
    at = lax.broadcasted_iota(jnp.int32, (segments, blocks * LANES), 1) + first * LANES
    at -= SAMP * lax.broadcasted_iota(jnp.int32, (segments, blocks * LANES), 0)
    inside = jnp.where((at >= 0) & (at < SAMP), 1.0, 0.0).astype(jnp.bfloat16)
    kept = dot_f32(flags_ref[...].astype(jnp.float32).astype(jnp.bfloat16), inside)
    flat = (flat * kept).astype(jnp.bfloat16)

    source = lax.broadcasted_iota(jnp.int32, (2 * LANES, 2 * LANES), 0)
    target = lax.broadcasted_iota(jnp.int32, (2 * LANES, 2 * LANES), 1)
    wanted = jnp.where(target < LANES, 2 * target, 2 * target - 2 * LANES + 1)
    sort = jnp.where(source == wanted, 1.0, 0.0).astype(jnp.bfloat16)
    pairs = range(0, blocks * LANES, 2 * LANES)
    stacked = jnp.concatenate([flat[:, j : j + 2 * LANES] for j in pairs], axis=0)
    sorted_pairs = dot_f32(stacked, sort).astype(jnp.bfloat16)
    phases = [
        jnp.concatenate(
            [sorted_pairs[j * rows : (j + 1) * rows, at : at + LANES] for j in range(len(pairs))], axis=1
        )
        for at in (0, LANES)
    ]
    length = chunk_segs * SAMP // 2
    filling = jnp.zeros((rows, pl.cdiv(length, LANES) * LANES - length), jnp.bfloat16)
    for unit_starts, out_ref in zip(starts, out_refs):
        parts = []
        for start in unit_starts:
            at = (start - first * LANES) // 2
            for phase in phases:
                parts += [phase[:, at : at + length], filling]
        out_ref[...] = jnp.concatenate(parts, axis=1)


def whiten(traces, fir_taps, seg_flags, starts):
    rows, record_len = traces.shape
    vmem = pl.BlockSpec(memory_space=pltpu.VMEM)
    length = chunk_segs * SAMP
    window = 2 * pl.cdiv(length // 2, LANES) * LANES
    first = min(min(s) for s in starts) // LANES
    blocks = pl.cdiv(max(max(s) for s in starts) + length - first * LANES, 2 * LANES) * 2
    reach = min((first + blocks + 2) * LANES, record_len)
    return pl.pallas_call(
        functools.partial(whiten_kernel, record_len // LANES, first, blocks, starts),
        grid=(1,),
        in_specs=[
            pl.BlockSpec(memory_space=pltpu.SMEM),
            pl.BlockSpec((rows, reach), lambda step: (0, 0)),
            vmem,
        ],
        out_specs=[vmem] * len(starts),
        out_shape=[jax.ShapeDtypeStruct((rows, window * len(s)), jnp.bfloat16) for s in starts],
        compiler_params=pltpu.CompilerParams(vmem_limit_bytes=vmem_bytes),
        name="whiten",
    )(fir_taps, traces, seg_flags)


def route_kernel(count, place_ref, *refs):
    rows = refs[0].shape[0]
    outs = refs[-count:]
    for index, out_ref in enumerate(outs):
        for source_index, source in enumerate(refs[:count]):

            @pl.when(place_ref[index] == source_index)
            def _(source=source, out_ref=out_ref):
                out_ref[:rows, :] = source[...]

        if out_ref.shape[0] > rows:
            out_ref[rows:, :] = refs[count][...]


def route(place, parts, rows, extra):
    length = parts[0][0].shape[1]
    kind = parts[0][0].dtype

    def spec(count, at=0):
        return pl.BlockSpec((count, length), lambda step: (at, 0))

    counts = [rows] + [rows if extra is None else 2 * rows] * (len(parts) - 1)
    more = [] if extra is None else [extra]
    return pl.pallas_call(
        functools.partial(route_kernel, len(parts)),
        grid=(1,),
        in_specs=[pl.BlockSpec(memory_space=pltpu.SMEM)]
        + [spec(rows, at) for _, at in parts]
        + [spec(rows) for _ in more],
        out_specs=[spec(count) for count in counts],
        out_shape=[jax.ShapeDtypeStruct((count, length), kind) for count in counts],
        compiler_params=pltpu.CompilerParams(vmem_limit_bytes=24 << 20),
        name="route",
    )(place, *[array for array, _ in parts], *more)


def correlate_kernel(begins, left_rows, piece_rows, has_total, last, scale, place_ref, *refs):
    lefts, refs = refs[: len(begins)], list(refs[len(begins) :])
    staged = refs.pop() if piece_rows % 16 else None
    *refs, out_ref, even, odd, columns, both, shifted, edge, sems = refs
    mask_ref = refs.pop() if last else None
    total_ref = refs.pop() if has_total else None
    row_count, width = even.shape
    step = pl.program_id(0)
    lowest = SHIFTS // 2 + 1 - shift_group * (step + 1)

    @pl.when(step == 0)
    def _():
        copies = []

        def copy(source, target):
            copies.append(pltpu.make_async_copy(source, target, sems.at[len(copies)]))
            copies[-1].start()

        for index, (left, (row, begin)) in enumerate(zip(lefts, begins)):
            at, rows = pl.ds(index * left_rows, left_rows), pl.ds(row, left_rows)
            copy(left.at[rows, pl.ds(begin, width)], even.at[at])
            copy(left.at[rows, pl.ds(begin + width, width)], odd.at[at])
        for index, piece in enumerate(refs):
            at = pl.ds(pl.multiple_of(place_ref[index] * piece_rows, piece_rows), piece_rows)
            if staged is None:
                copy(piece.at[pl.ds(0, piece_rows)], columns.at[at])
            else:
                staged[at, :] = piece[...].astype(staged.dtype)
        if staged is not None:
            columns[...] = staged[...].astype(columns.dtype)
        for started in copies:
            started.wait()
        both[...] = columns[:, :width] + columns[:, width:]
        start = (SHIFTS // 2 + 1 - shift_group) % width
        even[...] = pltpu.roll(even[...], start, 1)
        odd[...] = pltpu.roll(odd[...], start, 1)
        edge[...] = jnp.zeros_like(edge)

    half = SAMP // 2
    sample = lax.broadcasted_iota(jnp.int32, (16, width), 1)
    phase = sample
    for segment in range(1, chunk_segs):
        phase = jnp.where(sample >= segment * half, sample - segment * half, phase)
    phase = jnp.where(sample >= chunk_segs * half, -SAMP, phase)

    def shift(base, index):
        move = lowest + index
        rolled = pltpu.roll(base, index, 1) if index else base
        keep = jnp.where((phase >= move) & (phase < half + move), 1.0, 0.0).astype(jnp.bfloat16)
        return rolled * jnp.concatenate([keep] * (row_count // 16), axis=0)

    base_even, base_odd = even[...], odd[...]
    for index in range(shift_group):
        rows = slice(index * row_count, (index + 1) * row_count)
        now = shift(base_even, index)
        shifted[0, rows, :] = now
        shifted[1, rows, :] = shift(base_odd, index)
        shifted[2, rows, :] = now + shift(base_odd, index + 1)
    even[...] = pltpu.roll(base_even, width - shift_group, 1)
    odd[...] = pltpu.roll(base_odd, width - shift_group, 1)
    rights = columns.at[:, :width], columns.at[:, width:], both
    products = []
    for index, right in enumerate(rights):
        value = lax.dot_general(
            shifted[index], right[...], (((1,), (1,)), ((), ())), preferred_element_type=jnp.float32
        ).reshape(shift_group, row_count, columns.shape[0])
        products.append(value + total_ref[index].astype(jnp.float32) if has_total else value)
    if not last:
        for index, value in enumerate(products):
            out_ref[index] = value.astype(out_ref.dtype)
        return
    zero, one, mixed = products
    higher = [one[index] for index in range(1, shift_group)] + [edge[...]]
    for index in range(len(lefts)):
        rows = slice(index * left_rows, (index + 1) * left_rows)
        at = pl.ds(pl.multiple_of(place_ref[len(refs) + index] * left_rows, left_rows), left_rows)
        weight = mask_ref[at, :].astype(jnp.float32) * scale
        for m in range(shift_group):
            out_ref[2 * m, at, :] = (zero[m, rows] + one[m, rows]) * weight
            out_ref[2 * m + 1, at, :] = (mixed[m, rows] - zero[m, rows] - higher[m][rows]) * weight
    edge[...] = one[0]


def correlate(place, lefts, begins, right, total, mask, last, scale):
    rows, cols = mask.shape
    left_rows, piece_rows = rows // len(lefts), cols // len(right)
    window = right[0].shape[1]
    width = window // 2
    steps = SHIFTS // shift_group
    any_space = pl.BlockSpec(memory_space=pl.ANY)
    whole = pl.BlockSpec((piece_rows, window), lambda step: (0, 0)) if piece_rows % 16 else any_space
    block = pl.BlockSpec((3, shift_group, rows, cols), lambda step: (0, steps - 1 - step, 0, 0))
    operands = [place, *lefts, *right]
    specs = [pl.BlockSpec(memory_space=pltpu.SMEM)] + [any_space] * len(lefts)
    specs += [whole] * len(right)
    aliases = {}
    if total is not None:
        if not last:
            aliases = {len(operands): 0}
        operands.append(total)
        specs.append(block)
    if last:
        operands.append(mask)
        specs.append(pl.BlockSpec((rows, cols), lambda step: (0, 0)))
        block = pl.BlockSpec((2 * shift_group, rows, cols), lambda step: (steps - 1 - step, 0, 0))
    scratch = [
        pltpu.VMEM((rows, width), jnp.bfloat16),
        pltpu.VMEM((rows, width), jnp.bfloat16),
        pltpu.VMEM((cols, window), jnp.bfloat16),
        pltpu.VMEM((cols, width), jnp.bfloat16),
        pltpu.VMEM((3, shift_group * rows, width), jnp.bfloat16),
        pltpu.VMEM((rows, cols), jnp.float32),
        pltpu.SemaphoreType.DMA((2 * len(lefts) + len(right),)),
    ]
    if piece_rows % 16:
        scratch.append(pltpu.VMEM((cols, window), jnp.float32))
    out_shape = (LAGS, rows, cols) if last else (3, SHIFTS, rows, cols)
    return pl.pallas_call(
        functools.partial(
            correlate_kernel, begins, left_rows, piece_rows, total is not None, last, scale
        ),
        grid=(steps,),
        in_specs=specs,
        out_specs=block,
        out_shape=jax.ShapeDtypeStruct(out_shape, jnp.float32 if last else jnp.bfloat16),
        input_output_aliases=aliases,
        scratch_shapes=scratch,
        compiler_params=pltpu.CompilerParams(vmem_limit_bytes=vmem_bytes if total is None else 34 << 20),
        name="correlate",
    )(*operands)


def body(traces, fir_taps, seg_flags, pair_mask):
    stn_count, seg_count = lax.axis_size("stn"), lax.axis_size("seg")
    sides = stn_count // seg_count
    stn, seg = lax.axis_index("stn"), lax.axis_index("seg")
    plane, side = stn // sides, stn % sides
    segments = seg_flags.shape[1]
    count = segments // chunk_segs
    scale = 1.0 / math.sqrt(SAMP * segments)
    partner = jnp.stack([seg ^ k for k in range(seg_count)]).astype(jnp.int32)
    route_place = plane ^ partner
    rows = traces.shape[0]
    place = [(side ^ j) * seg_count + partner for j in range(sides)]

    def to_seg(value, k):
        return lax.ppermute(value, "seg", [(i, i ^ k) for i in range(seg_count)])

    def to_plane(value, k):
        return lax.ppermute(value, "stn", [(i, i ^ (k * sides)) for i in range(stn_count)])

    def to_side(value, j):
        return lax.ppermute(value, "stn", [(i, i ^ j) for i in range(stn_count)])

    length = chunk_segs * SAMP
    half = count // 2
    starts = [u * length for u in range(count)]
    units = list(whiten(traces, fir_taps, seg_flags, [[0]]))
    several = [starts[1 : half + 1], starts[half:]]
    *rest, middle, late = whiten(traces, fir_taps, seg_flags, [[start] for start in starts[1:]] + several)
    units += rest
    window = units[0].shape[1]

    direct = [k for k in range(1, seg_count) if k & (k - 1) == 0][::-1]
    passed = [k for k in range(1, seg_count) if k & (k - 1)]
    gathered = rows % 16 > 0
    place.append(jnp.zeros((1,), jnp.int32) if gathered else partner)
    place = jnp.concatenate(place).astype(jnp.int32)

    state = {("unit", u): unit for u, unit in enumerate(units)}
    state["middle"], state["late"] = middle, late
    lines = [{0: (("unit", u), 0)} for u in range(count)]

    def fence():
        names = list(state)
        state.update(zip(names, lax.optimization_barrier([state[n] for n in names])))

    def value(u, k):
        name, at = lines[u][k]
        return state[name][at * rows : (at + 1) * rows] if at else state[name][:rows]

    def hop(k, *moves):
        sent = [value(u, slot ^ k) for u, slot in moves]
        name = ("line", *moves)
        state[name] = to_plane(jnp.concatenate(sent, axis=0) if len(sent) > 1 else sent[0], k)
        for at, (u, slot) in enumerate(moves):
            lines[u][slot] = name, at

    def plane_hops(u):
        ahead = u + 1 < count
        if len(passed) == 1 and u >= 0:
            if ahead:
                hop(direct[0], (u + 1, direct[0]))
            if u < count:
                hop(direct[1], *([(u, passed[0])] + ([(u + 1, direct[1])] if ahead else [])))
            return
        for k in passed if 0 <= u < count else []:
            hop(k & (k - 1), (u, k))
        for k in direct if ahead else []:
            hop(k, (u + 1, k))

    def columns(u, extra=None):
        parts = [(state[lines[u][k][0]], lines[u][k][1]) for k in range(seg_count)]
        more = None if extra is None else state["unit", extra]
        for k, piece in enumerate(route(route_place, parts, rows, more)):
            state["own", u, k] = to_seg(piece, k) if k else piece
            if k and extra is not None:
                rows_of[extra][k] = ("own", u, k), (rows, 0)

    rows_of = [{0: (("unit", u), (0, 0))} for u in range(count)]

    def row_hop(k, source, covered):
        name = ("row", k, source)
        state[name] = to_seg(state[source], k)
        for u in covered:
            rows_of[u][k] = name, (0, (u - covered[0]) * window)

    def gather_rows(source, covered):
        name = ("rows", source)
        state[name] = lax.all_gather(state[source], "seg", axis=0, tiled=True)
        for u in covered:
            rows_of[u] = {0: (name, (0, (u - covered[0]) * window))}

    def products(u):
        parts = [rows_of[u][k] for k in sorted(rows_of[u])]
        own = [state["own", u, k] for k in range(seg_count)]
        right = own + [to_side(v, j) for j in range(1, sides) for v in own]
        state["total"] = correlate(
            place,
            [state[name] for name, _ in parts],
            [begin for _, begin in parts],
            right,
            state.pop("total", None),
            pair_mask,
            u == count - 1,
            scale,
        )

    hops = list(range(1, seg_count))
    row_plan = {
        -1: [(k, ("unit", 0), [0]) for k in hops],
        0: [(k, "middle", range(1, half + 1)) for k in hops[:-1]] + [(hops[-1], ("unit", 1), [1])],
        half + 1: [(hops[-1], ("unit", half), [half])],
    }
    plane_hops(-1)
    if gathered:
        for source, covered in ((("unit", 0), [0]), ("middle", range(1, half)), ("late", range(half, count))):
            gather_rows(source, list(covered))
        row_plan = {}
    for u in range(-1, count + 2):
        if u >= 0:
            fence()
            plane_hops(u)
        if 1 <= u <= count:
            carried = u + 1 if half <= u < count - 1 and not gathered else None
            columns(u - 1, carried)
        for k, source, covered in row_plan.get(u, []):
            row_hop(k, source, list(covered))
        if 2 <= u <= count:
            products(u - 2)
    products(count - 1)
    return state["total"]


def solution(mesh):
    return jax.shard_map(
        body,
        mesh=mesh,
        in_specs=(P(("stn", "seg"), None), P(), P(("stn", "seg"), None), P("stn", "seg")),
        out_specs=P(None, "stn", "seg"),
        check_vma=False,
    )
```

time: 191 us -> 177 us (0.927)
  Pallas kernels: 101 us -> 79.7 us
  waiting for transfers between devices: 35.6 us -> 39.9 us
  local copies, waits for them, and re-layouts: 3.91 us -> 7.65 us
    pallas_call x8, Pallas kernels: 89.9 us -> 67.6 us  [the longest x4 62.1 us: correlate(): pl.pallas_call(functools.partial(correlate_kernel, begins, left_rows, pie...]
    ppermute x21 -> x19, starting transfers between devices: 25 us -> 21.1 us  [to_seg(): return lax.ppermute(value, 'seg', [(i, i ^ k) for i in range(seg_count)])]
    unnamed x108 -> x62, local copies, waits for them, and re-layouts: 3.28 us -> 7.08 us
    ppermute x9, starting transfers between devices: 17.1 us -> 20.6 us  [to_plane(): lax.ppermute(value, 'stn', [(i, i ^ k * sides) for i in range(stn_count)])]
    ppermute x9, waiting for transfers between devices: 15.9 us -> 18.4 us  [to_plane(): lax.ppermute(value, 'stn', [(i, i ^ k * sides) for i in range(stn_count)])]
    ppermute x21 -> x19, waiting for transfers between devices: 17.8 us -> 18 us  [to_seg(): return lax.ppermute(value, 'seg', [(i, i ^ k) for i in range(seg_count)])]
  transfers between devices with their start and end apart: 46 -> 44, of which waited for: 13 -> 16; matrix products, arithmetic and copies ran while one was open for 1% -> 1% of each run, Pallas kernels for 41% -> 34%
where the time goes in v4:
time: 177 us
  Pallas kernels  79.7 us (45%)
  starting transfers between devices  45.9 us (26%)
  waiting for transfers between devices  39.9 us (23%)
  local copies, waits for them, and re-layouts  7.65 us (4%)
  other arithmetic  3.08 us (2%)
    pallas_call x4, Pallas kernels, correlate(): pl.pallas_call(functools.partial(correlate_kernel, begins, left_rows, pie...  62.1 us
    ppermute x19, starting transfers between devices, to_seg(): return lax.ppermute(value, 'seg', [(i, i ^ k) for i in range(seg_count)])  21.1 us
    ppermute x9, starting transfers between devices, to_plane(): lax.ppermute(value, 'stn', [(i, i ^ k * sides) for i in range(stn_count)])  20.6 us
    ppermute x9, waiting for transfers between devices, to_plane(): lax.ppermute(value, 'stn', [(i, i ^ k * sides) for i in range(stn_count)])  18.4 us
    ppermute x19, waiting for transfers between devices, to_seg(): return lax.ppermute(value, 'seg', [(i, i ^ k) for i in range(seg_count)])  18 us
    pallas_call x2, Pallas kernels, whiten(): pl.pallas_call(functools.partial(whiten_kernel, record_len // LANES, firs...  12.1 us
    unnamed x62, local copies, waits for them, and re-layouts  7.08 us
    pallas_call x4, Pallas kernels, route(): pl.pallas_call(functools.partial(route_kernel, len(parts)), grid=(1,), in...  5.54 us
  transfers between devices with their start and end apart: 44, of which 16 were waited for; matrix products, arithmetic and copies ran while one was open for 1% of the time, Pallas kernels for 34%

profile of v4, /device:TPU:0, one launch (start us, length us, event | category | flops | bytes accessed | tf_op | source)
XLA Modules:
  0.0 176.8 jit_solution(6037824507918315138)
XLA Ops:
  0.0 3.9 %whiten.2.refs_0_ = bf16[32,4864]{1,0:T(8,128)(2,1)} custom-call(f32[31]{0:T(128)} %taps_ref.3, f32[32,19200]{1,0:T(8,128)} %traces_ref.3, s32[32,32]{1,0:T(8,128)} %flags_ref.3), custom_call_target="tpu_custom_call" | custom-call | tf_op jit(solution)/shard_map/whiten/pallas_call | solution.py:127
  3.9 4.0 %collective-permute-start = (bf16[32,4864]{1,0:T(8,128)(2,1)}, bf16[32,4864]{1,0:T(8,128)(2,1)S(1)}, u32[]{:S(2)}, u32[]{:S(2)}) collective-permute-start(bf16[32,4864]{1,0:T(8,128)(2,1)} %whiten.2.refs_0_), channel_id=1, source_target_pairs={{0,16},{4,20},{8,24},{12,28},{16,0},{20,4},{24,8},{28,12},{1,17},{... | collective-permute-start | bytes 933896 | tf_op jit(solution)/shard_map/ppermute | solution.py:327
  8.0 1.6 collective-permute-start.1
  9.6 1.5 collective-permute-start.2
  11.1 1.5 collective-permute-start.3
  12.6 0.5 collective-permute-start.4
  13.1 8.2 %whiten.3 = (bf16[32,4864]{1,0:T(8,128)(2,1)}, bf16[32,4864]{1,0:T(8,128)(2,1)}, bf16[32,4864]{1,0:T(8,128)(2,1)}, bf16[32,9728]{1,0:T(8,128)(2,1)}, bf16[32,9728]{1,0:T(8,128)(2,1)}) custom-call(f32[31]{0:T(128)} %taps_ref.3, f32[32,19200]{1,0:T(8,128)} %traces_ref.3, s32[32,32]{1,0:T(8,128)} %flags_ref.3), custom_call_target="tpu_custom_call" | custom-call | tf_op jit(solution)/shard_map/whiten/pallas_call | solution.py:127
  21.2 1.1 collective-permute-done.refs_2_
  22.5 0.7 copy-done.12
  23.3 2.9 %collective-permute-done.3.refs_2_ = bf16[32,4864]{1,0:T(8,128)(2,1)S(1)} collective-permute-done((bf16[32,4864]{1,0:T(8,128)(2,1)}, bf16[32,4864]{1,0:T(8,128)(2,1)S(1)}, u32[]{:S(2)}, u32[]{:S(2)}) %collective-permute-start.3) | collective-permute-done | bytes 311328 | tf_op jit(solution)/shard_map/ppermute | solution.py:324
  26.2 1.3 pad_maximum_fusion
  27.5 0.5 collective-permute-start.6
  28.0 1.1 collective-permute-start.7
  29.1 0.9 collective-permute-start.8
  30.0 1.4 collective-permute-start.5
  31.5 0.5 collective-permute-start.9
  32.0 14.2 %collective-permute-done.5.refs_2_ = bf16[32,4864]{1,0:T(8,128)(2,1)S(1)} collective-permute-done((bf16[32,4864]{1,0:T(8,128)(2,1)S(1)}, bf16[32,4864]{1,0:T(8,128)(2,1)S(1)}, u32[]{:S(2)}, u32[]{:S(2)}) %collective-permute-start.5) | collective-permute-done | bytes 311328 | tf_op jit(solution)/shard_map/ppermute | solution.py:327
  46.1 2.5 %collective-permute-done.9.refs_3_ = bf16[32,4864]{1,0:T(8,128)(2,1)S(1)} collective-permute-done((bf16[32,4864]{1,0:T(8,128)(2,1)S(1)}, bf16[32,4864]{1,0:T(8,128)(2,1)S(1)}, u32[]{:S(2)}, u32[]{:S(2)}) %collective-permute-start.9) | collective-permute-done | bytes 311328 | tf_op jit(solution)/shard_map/ppermute | solution.py:324
  48.6 0.7 copy-done.14
  49.3 0.9 copy-done.5
  50.2 0.8 copy-done.7
  51.0 0.9 pad_maximum_fusion.1
  51.9 1.4 collective-permute-start.11
  53.4 1.0 copy-done.13
  54.4 0.7 route.4
  55.1 1.6 collective-permute-start.12
  56.7 1.4 collective-permute-start.13
  58.0 0.6 collective-permute-start.14
  58.7 2.3 %collective-permute-start.10 = (bf16[32,4864]{1,0:T(8,128)(2,1)S(1)}, bf16[32,4864]{1,0:T(8,128)(2,1)S(1)}, u32[]{:S(2)}, u32[]{:S(2)}) collective-permute-start(bf16[32,4864]{1,0:T(8,128)(2,1)S(1)} %copy-done.2), channel_id=1, source_target_pairs={{0,16},{4,20},{8,24},{12,28},{16,0},{20,4},{24,8},{28,12},{1,17},{... | collective-permute-start | bytes 933896 | tf_op jit(solution)/shard_map/ppermute | solution.py:327
  61.0 4.0 %collective-permute-done.12.refs_5_ = bf16[32,4864]{1,0:T(8,128)(2,1)S(1)} collective-permute-done((bf16[32,4864]{1,0:T(8,128)(2,1)S(1)}, bf16[32,4864]{1,0:T(8,128)(2,1)S(1)}, u32[]{:S(2)}, u32[]{:S(2)}) %collective-permute-start.12) | collective-permute-done | bytes 311328 | tf_op jit(solution)/shard_map/ppermute | solution.py:324
  65.0 5.2 %collective-permute-done.13.refs_6_ = bf16[32,4864]{1,0:T(8,128)(2,1)S(1)} collective-permute-done((bf16[32,4864]{1,0:T(8,128)(2,1)S(1)}, bf16[32,4864]{1,0:T(8,128)(2,1)S(1)}, u32[]{:S(2)}, u32[]{:S(2)}) %collective-permute-start.13) | collective-permute-done | bytes 311328 | tf_op jit(solution)/shard_map/ppermute | solution.py:324
  70.2 0.9 collective-permute-done.10.refs_2_
  71.1 0.7 collective-permute-done.11.refs_3_.refs_1_
  71.8 0.5 collective-permute-start.21
  72.3 0.5 collective-permute-start.23
  72.8 2.2 %route.5 = (bf16[32,4864]{1,0:T(8,128)(2,1)S(1)}, bf16[64,4864]{1,0:T(8,128)(2,1)}, bf16[64,4864]{1,0:T(8,128)(2,1)}, bf16[64,4864]{1,0:T(8,128)(2,1)}) custom-call(s32[4]{0:T(128)S(1)} %get-tuple-element.209.place_ref, bf16[32,4864]{1,0:T(8,128)(2,1)S(1)} %copy-done.4, bf16[64,4864]{1,0:T(8,128)(2,1)S(1)} %collective-permute-done.6.refs_3_.refs_1_, ...), custom_call_target="tpu_custom_call" | custom-call | tf_op jit(solution)/shard_map/route/pallas_call | solution.py:165
  75.0 1.9 %collective-permute-start.17 = (bf16[64,4864]{1,0:T(8,128)(2,1)}, bf16[64,4864]{1,0:T(8,128)(2,1)S(1)}, u32[]{:S(2)}, u32[]{:S(2)}) collective-permute-start(bf16[64,4864]{1,0:T(8,128)(2,1)} %get-tuple-element.158), channel_id=1, source_target_pairs={{0,1},{1,0},{2,3},{3,2},{4,5},{5,4},{6,7},{7,6},{8,9},{9,8},{10,11... | collective-permute-start | bytes 1867784 | tf_op jit(solution)/shard_map/ppermute | solution.py:324
  76.9 0.9 pad_maximum_fusion.2
  77.8 2.2 %collective-permute-start.18 = (bf16[64,4864]{1,0:T(8,128)(2,1)}, bf16[64,4864]{1,0:T(8,128)(2,1)S(1)}, u32[]{:S(2)}, u32[]{:S(2)}) collective-permute-start(bf16[64,4864]{1,0:T(8,128)(2,1)} %get-tuple-element.159), channel_id=1, source_target_pairs={{0,2},{1,3},{2,0},{3,1},{4,6},{5,7},{6,4},{7,5},{8,10},{9,11},{10,... | collective-permute-start | bytes 1867784 | tf_op jit(solution)/shard_map/ppermute | solution.py:324
  80.1 4.5 %collective-permute-start.16 = (bf16[64,4864]{1,0:T(8,128)(2,1)}, bf16[64,4864]{1,0:T(8,128)(2,1)}, u32[]{:S(2)}, u32[]{:S(2)}) collective-permute-start(bf16[64,4864]{1,0:T(8,128)(2,1)} %pad_maximum_fusion.2), channel_id=1, source_target_pairs={{0,8},{4,12},{8,0},{12,4},{16,24},{20,28},{24,16},{28,20},{1,9},{5... | collective-permute-start | bytes 1867784 | tf_op jit(solution)/shard_map/ppermute | solution.py:327
  84.7 0.7 copy-done.29
  85.7 0.6 concatenate.13.place_ref
  86.3 16.4 %correlate.4.refs_12_ = bf16[3,21,128,256]{3,2,1,0:T(8,128)(2,1)} custom-call(s32[12]{0:T(128)} %concatenate.13.place_ref, bf16[32,4864]{1,0:T(8,128)(2,1)} %whiten.2.refs_0_, bf16[32,4864]{1,0:T(8,128)(2,1)} %copy-done.20, bf16[32,4864]{1,0:T(8,128)(2,1)} %copy-done.21, bf16[32,4864]{1,0:T(8,128)(2,1)} %copy-done.22, bf16[32,4864]{1,0:T(8,128)(2,1)} %copy-done.11, ...), custom_call_target="tpu_custom_call" | custom-call | tf_op jit(solution)/shard_map/correlate/pallas_call | solution.py:295
  102.8 1.4 collective-permute-done.15.refs_2_
  104.2 3.3 %collective-permute-done.18.refs_6_.refs_2_ = bf16[64,4864]{1,0:T(8,128)(2,1)S(1)} collective-permute-done((bf16[64,4864]{1,0:T(8,128)(2,1)}, bf16[64,4864]{1,0:T(8,128)(2,1)S(1)}, u32[]{:S(2)}, u32[]{:S(2)}) %collective-permute-start.18) | collective-permute-done | bytes 622624 | tf_op jit(solution)/shard_map/ppermute | solution.py:324
  107.5 0.5 collective-permute-start.31
  108.5 1.2 route.6
  109.7 0.5 collective-permute-start.25
  110.3 1.5 collective-permute-done.29.refs_8_
  111.8 1.7 collective-permute-start.26
  113.7 4.4 %collective-permute-start.24 = (bf16[32,4864]{1,0:T(8,128)(2,1)S(1)}, bf16[32,4864]{1,0:T(8,128)(2,1)S(1)}, u32[]{:S(2)}, u32[]{:S(2)}) collective-permute-start(bf16[32,4864]{1,0:T(8,128)(2,1)S(1)} %collective-permute-done.15.refs_2_), channel_id=1, source_target_pairs={{0,8},{4,12},{8,0},{12,4},{16,24},{20,28},{24,16},{28,20},{1,9},{5... | collective-permute-start | bytes 933896 | tf_op jit(solution)/shard_map/ppermute | solution.py:327
  118.2 1.4 collective-permute-start.28
  119.7 2.2 %copy-done = bf16[3,21,128,256]{3,2,1,0:T(8,128)(2,1)S(1)} copy-done((bf16[3,21,128,256]{3,2,1,0:T(8,128)(2,1)S(1)}, bf16[3,21,128,256]{3,2,1,0:T(8,128)(2,1)}, u32[]{:S(2)}) %copy-start) | copy-done | bytes 4128792
  121.8 14.7 %correlate.5.refs_12_ = bf16[3,21,128,256]{3,2,1,0:T(8,128)(2,1)S(1)} custom-call(s32[12]{0:T(128)S(1)} %copy-done.19, bf16[32,4864]{1,0:T(8,128)(2,1)S(1)} %copy-done.4, bf16[32,9728]{1,0:T(8,128)(2,1)S(1)} %copy-done.6, bf16[32,9728]{1,0:T(8,128)(2,1)S(1)} %copy-done.8, bf16[32,4864]{1,0:T(8,128)(2,1)S(1)} %copy-done.15, ...), custom_call_target="tpu_custom_call", output_to_operand_aliasing={{}: (13, {})} | custom-call | tf_op jit(solution)/shard_map/correlate/pallas_call | solution.py:295
  136.7 0.5 collective-permute-start.37
  137.7 1.4 route.7
  139.1 0.6 collective-permute-start.33
  139.7 1.5 collective-permute-start.34
  141.2 1.4 collective-permute-start.35
  142.6 14.7 %correlate.6.refs_12_ = bf16[3,21,128,256]{3,2,1,0:T(8,128)(2,1)S(1)} custom-call(s32[12]{0:T(128)S(1)} %copy-done.19, bf16[32,4864]{1,0:T(8,128)(2,1)S(1)} %copy-done.2, bf16[32,9728]{1,0:T(8,128)(2,1)S(1)} %copy-done.6, bf16[32,9728]{1,0:T(8,128)(2,1)S(1)} %copy-done.8, ...), custom_call_target="tpu_custom_call", output_to_operand_aliasing={{}: (13, {})} | custom-call | tf_op jit(solution)/shard_map/correlate/pallas_call | solution.py:295
  157.5 0.5 collective-permute-start.41
  158.5 0.6 collective-permute-done.40.refs_8_
  159.0 0.4 collective-permute-done.41.refs_9_
  160.4 16.2 %correlate.7 = f32[41,128,256]{2,1,0:T(8,128)} custom-call(s32[12]{0:T(128)S(1)} %copy-done.19, bf16[32,4864]{1,0:T(8,128)(2,1)S(1)} %copy-done.1, bf16[64,4864]{1,0:T(8,128)(2,1)S(1)} %collective-permute-done.17.refs_5_.refs_1_, bf16[64,4864]{1,0:T(8,128)(2,1)S(1)} %collective-permute-done.18.refs_6_.refs_2_, ...), custom_call_target="tpu_custom_call" | custom-call | tf_op jit(solution)/shard_map/correlate/pallas_call | solution.py:295
  (102 shorter events, 3.5 us)
Async XLA Ops:
  3.9 18.4 %collective-permute-start = (bf16[32,4864]{1,0:T(8,128)(2,1)}, bf16[32,4864]{1,0:T(8,128)(2,1)S(1)}, u32[]{:S(2)}, u32[]{:S(2)}) collective-permute-start(bf16[32,4864]{1,0:T(8,128)(2,1)} %whiten.2.refs_0_), channel_id=1, source_target_pairs={{0,16},{4,20},{8,24},{12,28},{16,0},{20,4},{24,8},{28,12},{1,17},{... | collective-permute-start | bytes 933896 | tf_op jit(solution)/shard_map/ppermute | solution.py:327
  8.0 14.5 %collective-permute-start.1 = (bf16[32,4864]{1,0:T(8,128)(2,1)}, bf16[32,4864]{1,0:T(8,128)(2,1)S(1)}, u32[]{:S(2)}, u32[]{:S(2)}) collective-permute-start(bf16[32,4864]{1,0:T(8,128)(2,1)} %whiten.2.refs_0_), channel_id=1, source_target_pairs={{0,8},{4,12},{8,0},{12,4},{16,24},{20,28},{24,16},{28,20},{1,9},{5... | collective-permute-start | bytes 933896 | tf_op jit(solution)/shard_map/ppermute | solution.py:327
  9.6 13.7 %collective-permute-start.2 = (bf16[32,4864]{1,0:T(8,128)(2,1)}, bf16[32,4864]{1,0:T(8,128)(2,1)S(1)}, u32[]{:S(2)}, u32[]{:S(2)}) collective-permute-start(bf16[32,4864]{1,0:T(8,128)(2,1)} %whiten.2.refs_0_), channel_id=1, source_target_pairs={{0,1},{1,0},{2,3},{3,2},{4,5},{5,4},{6,7},{7,6},{8,9},{9,8},{10,11... | collective-permute-start | bytes 933896 | tf_op jit(solution)/shard_map/ppermute | solution.py:324
  11.1 15.1 %collective-permute-start.3 = (bf16[32,4864]{1,0:T(8,128)(2,1)}, bf16[32,4864]{1,0:T(8,128)(2,1)S(1)}, u32[]{:S(2)}, u32[]{:S(2)}) collective-permute-start(bf16[32,4864]{1,0:T(8,128)(2,1)} %whiten.2.refs_0_), channel_id=1, source_target_pairs={{0,2},{1,3},{2,0},{3,1},{4,6},{5,7},{6,4},{7,5},{8,10},{9,11},{10,... | collective-permute-start | bytes 933896 | tf_op jit(solution)/shard_map/ppermute | solution.py:324
  12.6 13.6 %collective-permute-start.4 = (bf16[32,4864]{1,0:T(8,128)(2,1)}, bf16[32,4864]{1,0:T(8,128)(2,1)S(1)}, u32[]{:S(2)}, u32[]{:S(2)}) collective-permute-start(bf16[32,4864]{1,0:T(8,128)(2,1)} %whiten.2.refs_0_), channel_id=1, source_target_pairs={{0,3},{1,2},{2,1},{3,0},{4,7},{5,6},{6,5},{7,4},{8,11},{9,10},{10,... | collective-permute-start | bytes 933896 | tf_op jit(solution)/shard_map/ppermute | solution.py:324
  21.2 6.8 %copy-start.30 = (bf16[32,9728]{1,0:T(8,128)(2,1)S(1)}, bf16[32,9728]{1,0:T(8,128)(2,1)}, u32[]{:S(2)}) copy-start(bf16[32,9728]{1,0:T(8,128)(2,1)} %get-tuple-element.115) | copy-start | bytes 1867780
  21.2 8.8 %copy-start.4 = (bf16[32,4864]{1,0:T(8,128)(2,1)S(1)}, bf16[32,4864]{1,0:T(8,128)(2,1)}, u32[]{:S(2)}) copy-start(bf16[32,4864]{1,0:T(8,128)(2,1)} %get-tuple-element.161.refs_0_) | copy-start | bytes 933892
  21.2 29.8 %copy-start.2 = (bf16[32,4864]{1,0:T(8,128)(2,1)S(1)}, bf16[32,4864]{1,0:T(8,128)(2,1)}, u32[]{:S(2)}) copy-start(bf16[32,4864]{1,0:T(8,128)(2,1)} %get-tuple-element.180.refs_0_) | copy-start | bytes 933892
  23.2 28.7 %copy-start.20 = (bf16[32,4864]{1,0:T(8,128)(2,1)}, bf16[32,4864]{1,0:T(8,128)(2,1)S(1)}, u32[]{:S(2)}) copy-start(bf16[32,4864]{1,0:T(8,128)(2,1)S(1)} %collective-permute-done.2.refs_1_) | copy-start | bytes 933892
  26.2 25.7 %copy-start.21 = (bf16[32,4864]{1,0:T(8,128)(2,1)}, bf16[32,4864]{1,0:T(8,128)(2,1)S(1)}, u32[]{:S(2)}) copy-start(bf16[32,4864]{1,0:T(8,128)(2,1)S(1)} %collective-permute-done.3.refs_2_) | copy-start | bytes 933892
  26.2 25.7 %copy-start.22 = (bf16[32,4864]{1,0:T(8,128)(2,1)}, bf16[32,4864]{1,0:T(8,128)(2,1)S(1)}, u32[]{:S(2)}) copy-start(bf16[32,4864]{1,0:T(8,128)(2,1)S(1)} %collective-permute-done.4.refs_3_) | copy-start | bytes 933892
  26.2 27.2 %copy-start.3 = (bf16[32,4864]{1,0:T(8,128)(2,1)S(1)}, bf16[32,4864]{1,0:T(8,128)(2,1)}, u32[]{:S(2)}) copy-start(bf16[32,4864]{1,0:T(8,128)(2,1)} %whiten.2.refs_0_) | copy-start | bytes 933892
  27.5 45.3 %copy-start.1 = (bf16[32,4864]{1,0:T(8,128)(2,1)S(1)}, bf16[32,4864]{1,0:T(8,128)(2,1)}, u32[]{:S(2)}) copy-start(bf16[32,4864]{1,0:T(8,128)(2,1)} %get-tuple-element.200.refs_4_.refs_0_) | copy-start | bytes 933892
  27.5 21.9 %collective-permute-start.6 = (bf16[64,4864]{1,0:T(8,128)(2,1)S(1)}, bf16[64,4864]{1,0:T(8,128)(2,1)S(1)}, u32[]{:S(2)}, u32[]{:S(2)}) collective-permute-start(bf16[64,4864]{1,0:T(8,128)(2,1)S(1)} %pad_maximum_fusion), channel_id=1, source_target_pairs={{0,8},{4,12},{8,0},{12,4},{16,24},{20,28},{24,16},{28,20},{1,9},{5... | collective-permute-start | bytes 1867784 | tf_op jit(solution)/shard_map/ppermute | solution.py:327
  28.0 21.4 %collective-permute-start.7 = (bf16[32,9728]{1,0:T(8,128)(2,1)S(1)}, bf16[32,9728]{1,0:T(8,128)(2,1)S(1)}, u32[]{:S(2)}, u32[]{:S(2)}) collective-permute-start(bf16[32,9728]{1,0:T(8,128)(2,1)S(1)} %copy-done.30), channel_id=1, source_target_pairs={{0,1},{1,0},{2,3},{3,2},{4,5},{5,4},{6,7},{7,6},{8,9},{9,8},{10,11... | collective-permute-start | bytes 1867784 | tf_op jit(solution)/shard_map/ppermute | solution.py:324
  29.1 21.1 %collective-permute-start.8 = (bf16[32,9728]{1,0:T(8,128)(2,1)S(1)}, bf16[32,9728]{1,0:T(8,128)(2,1)S(1)}, u32[]{:S(2)}, u32[]{:S(2)}) collective-permute-start(bf16[32,9728]{1,0:T(8,128)(2,1)S(1)} %copy-done.30), channel_id=1, source_target_pairs={{0,2},{1,3},{2,0},{3,1},{4,6},{5,7},{6,4},{7,5},{8,10},{9,11},{10,... | collective-permute-start | bytes 1867784 | tf_op jit(solution)/shard_map/ppermute | solution.py:324
  30.0 16.1 %collective-permute-start.5 = (bf16[32,4864]{1,0:T(8,128)(2,1)S(1)}, bf16[32,4864]{1,0:T(8,128)(2,1)S(1)}, u32[]{:S(2)}, u32[]{:S(2)}) collective-permute-start(bf16[32,4864]{1,0:T(8,128)(2,1)S(1)} %copy-done.4), channel_id=1, source_target_pairs={{0,16},{4,20},{8,24},{12,28},{16,0},{20,4},{24,8},{28,12},{1,17},{... | collective-permute-start | bytes 933896 | tf_op jit(solution)/shard_map/ppermute | solution.py:327
  31.5 17.1 %collective-permute-start.9 = (bf16[32,4864]{1,0:T(8,128)(2,1)S(1)}, bf16[32,4864]{1,0:T(8,128)(2,1)S(1)}, u32[]{:S(2)}, u32[]{:S(2)}) collective-permute-start(bf16[32,4864]{1,0:T(8,128)(2,1)S(1)} %copy-done.4), channel_id=1, source_target_pairs={{0,3},{1,2},{2,1},{3,0},{4,7},{5,6},{6,5},{7,4},{8,11},{9,10},{10,... | collective-permute-start | bytes 933896 | tf_op jit(solution)/shard_map/ppermute | solution.py:324
  51.9 19.8 %collective-permute-start.11 = (bf16[64,4864]{1,0:T(8,128)(2,1)}, bf16[64,4864]{1,0:T(8,128)(2,1)S(1)}, u32[]{:S(2)}, u32[]{:S(2)}) collective-permute-start(bf16[64,4864]{1,0:T(8,128)(2,1)} %pad_maximum_fusion.1), channel_id=1, source_target_pairs={{0,8},{4,12},{8,0},{12,4},{16,24},{20,28},{24,16},{28,20},{1,9},{5... | collective-permute-start | bytes 1867784 | tf_op jit(solution)/shard_map/ppermute | solution.py:327
  55.1 22.7 %copy-start.11 = (bf16[32,4864]{1,0:T(8,128)(2,1)}, bf16[32,4864]{1,0:T(8,128)(2,1)S(1)}, u32[]{:S(2)}) copy-start(bf16[32,4864]{1,0:T(8,128)(2,1)S(1)} %get-tuple-element.153.refs_4_) | copy-start | bytes 933892
  55.1 9.9 %collective-permute-start.12 = (bf16[32,4864]{1,0:T(8,128)(2,1)S(1)}, bf16[32,4864]{1,0:T(8,128)(2,1)S(1)}, u32[]{:S(2)}, u32[]{:S(2)}) collective-permute-start(bf16[32,4864]{1,0:T(8,128)(2,1)S(1)} %get-tuple-element.136), channel_id=1, source_target_pairs={{0,1},{1,0},{2,3},{3,2},{4,5},{5,4},{6,7},{7,6},{8,9},{9,8},{10,11... | collective-permute-start | bytes 933896 | tf_op jit(solution)/shard_map/ppermute | solution.py:324
  56.7 13.5 %collective-permute-start.13 = (bf16[32,4864]{1,0:T(8,128)(2,1)S(1)}, bf16[32,4864]{1,0:T(8,128)(2,1)S(1)}, u32[]{:S(2)}, u32[]{:S(2)}) collective-permute-start(bf16[32,4864]{1,0:T(8,128)(2,1)S(1)} %get-tuple-element.137), channel_id=1, source_target_pairs={{0,2},{1,3},{2,0},{3,1},{4,6},{5,7},{6,4},{7,5},{8,10},{9,11},{10,... | collective-permute-start | bytes 933896 | tf_op jit(solution)/shard_map/ppermute | solution.py:324
  58.0 12.1 %collective-permute-start.14 = (bf16[32,4864]{1,0:T(8,128)(2,1)S(1)}, bf16[32,4864]{1,0:T(8,128)(2,1)S(1)}, u32[]{:S(2)}, u32[]{:S(2)}) collective-permute-start(bf16[32,4864]{1,0:T(8,128)(2,1)S(1)} %get-tuple-element.138), channel_id=1, source_target_pairs={{0,3},{1,2},{2,1},{3,0},{4,7},{5,6},{6,5},{7,4},{8,11},{9,10},{10,... | collective-permute-start | bytes 933896 | tf_op jit(solution)/shard_map/ppermute | solution.py:324
  58.7 12.4 %collective-permute-start.10 = (bf16[32,4864]{1,0:T(8,128)(2,1)S(1)}, bf16[32,4864]{1,0:T(8,128)(2,1)S(1)}, u32[]{:S(2)}, u32[]{:S(2)}) collective-permute-start(bf16[32,4864]{1,0:T(8,128)(2,1)S(1)} %copy-done.2), channel_id=1, source_target_pairs={{0,16},{4,20},{8,24},{12,28},{16,0},{20,4},{24,8},{28,12},{1,17},{... | collective-permute-start | bytes 933896 | tf_op jit(solution)/shard_map/ppermute | solution.py:327
  65.0 12.8 %copy-start.23 = (bf16[32,4864]{1,0:T(8,128)(2,1)}, bf16[32,4864]{1,0:T(8,128)(2,1)S(1)}, u32[]{:S(2)}) copy-start(bf16[32,4864]{1,0:T(8,128)(2,1)S(1)} %collective-permute-done.12.refs_5_) | copy-start | bytes 933892
  70.2 7.6 %copy-start.24 = (bf16[32,4864]{1,0:T(8,128)(2,1)}, bf16[32,4864]{1,0:T(8,128)(2,1)S(1)}, u32[]{:S(2)}) copy-start(bf16[32,4864]{1,0:T(8,128)(2,1)S(1)} %collective-permute-done.13.refs_6_) | copy-start | bytes 933892
  70.2 7.6 %copy-start.25 = (bf16[32,4864]{1,0:T(8,128)(2,1)}, bf16[32,4864]{1,0:T(8,128)(2,1)S(1)}, u32[]{:S(2)}) copy-start(bf16[32,4864]{1,0:T(8,128)(2,1)S(1)} %collective-permute-done.14.refs_7_) | copy-start | bytes 933892
  71.8 6.0 %collective-permute-start.20 = (bf16[32,4864]{1,0:T(8,128)(2,1)S(1)}, bf16[32,4864]{1,0:T(8,128)(2,1)S(1)}, u32[]{:S(2)}, u32[]{:S(2)}) collective-permute-start(bf16[32,4864]{1,0:T(8,128)(2,1)S(1)} %get-tuple-element.153.refs_4_), channel_id=1, source_target_pairs={{0,4},{4,0},{8,12},{12,8},{16,20},{20,16},{24,28},{28,24},{1,5},{5... | collective-permute-start | bytes 933896 | tf_op jit(solution)/shard_map/ppermute | solution.py:330
  71.8 8.3 %collective-permute-start.21 = (bf16[32,4864]{1,0:T(8,128)(2,1)S(1)}, bf16[32,4864]{1,0:T(8,128)(2,1)S(1)}, u32[]{:S(2)}, u32[]{:S(2)}) collective-permute-start(bf16[32,4864]{1,0:T(8,128)(2,1)S(1)} %collective-permute-done.12.refs_5_), channel_id=1, source_target_pairs={{0,4},{4,0},{8,12},{12,8},{16,20},{20,16},{24,28},{28,24},{1,5},{5... | collective-permute-start | bytes 933896 | tf_op jit(solution)/shard_map/ppermute | solution.py:330
  72.3 7.8 %collective-permute-start.22 = (bf16[32,4864]{1,0:T(8,128)(2,1)S(1)}, bf16[32,4864]{1,0:T(8,128)(2,1)S(1)}, u32[]{:S(2)}, u32[]{:S(2)}) collective-permute-start(bf16[32,4864]{1,0:T(8,128)(2,1)S(1)} %collective-permute-done.13.refs_6_), channel_id=1, source_target_pairs={{0,4},{4,0},{8,12},{12,8},{16,20},{20,16},{24,28},{28,24},{1,5},{5... | collective-permute-start | bytes 933896 | tf_op jit(solution)/shard_map/ppermute | solution.py:330
  72.3 12.4 %collective-permute-start.23 = (bf16[32,4864]{1,0:T(8,128)(2,1)S(1)}, bf16[32,4864]{1,0:T(8,128)(2,1)S(1)}, u32[]{:S(2)}, u32[]{:S(2)}) collective-permute-start(bf16[32,4864]{1,0:T(8,128)(2,1)S(1)} %collective-permute-done.14.refs_7_), channel_id=1, source_target_pairs={{0,4},{4,0},{8,12},{12,8},{16,20},{20,16},{24,28},{28,24},{1,5},{5... | collective-permute-start | bytes 933896 | tf_op jit(solution)/shard_map/ppermute | solution.py:330
  75.0 29.2 %collective-permute-start.17 = (bf16[64,4864]{1,0:T(8,128)(2,1)}, bf16[64,4864]{1,0:T(8,128)(2,1)S(1)}, u32[]{:S(2)}, u32[]{:S(2)}) collective-permute-start(bf16[64,4864]{1,0:T(8,128)(2,1)} %get-tuple-element.158), channel_id=1, source_target_pairs={{0,1},{1,0},{2,3},{3,2},{4,5},{5,4},{6,7},{7,6},{8,9},{9,8},{10,11... | collective-permute-start | bytes 1867784 | tf_op jit(solution)/shard_map/ppermute | solution.py:324
  77.8 6.8 %copy-start.26 = (bf16[32,4864]{1,0:T(8,128)(2,1)}, bf16[32,4864]{1,0:T(8,128)(2,1)S(1)}, u32[]{:S(2)}) copy-start(bf16[32,4864]{1,0:T(8,128)(2,1)S(1)} %collective-permute-done.20.refs_8_) | copy-start | bytes 933892
  77.8 29.7 %collective-permute-start.18 = (bf16[64,4864]{1,0:T(8,128)(2,1)}, bf16[64,4864]{1,0:T(8,128)(2,1)S(1)}, u32[]{:S(2)}, u32[]{:S(2)}) collective-permute-start(bf16[64,4864]{1,0:T(8,128)(2,1)} %get-tuple-element.159), channel_id=1, source_target_pairs={{0,2},{1,3},{2,0},{3,1},{4,6},{5,7},{6,4},{7,5},{8,10},{9,11},{10,... | collective-permute-start | bytes 1867784 | tf_op jit(solution)/shard_map/ppermute | solution.py:324
  80.0 27.5 %collective-permute-start.19 = (bf16[64,4864]{1,0:T(8,128)(2,1)}, bf16[64,4864]{1,0:T(8,128)(2,1)S(1)}, u32[]{:S(2)}, u32[]{:S(2)}) collective-permute-start(bf16[64,4864]{1,0:T(8,128)(2,1)} %get-tuple-element.160), channel_id=1, source_target_pairs={{0,3},{1,2},{2,1},{3,0},{4,7},{5,6},{6,5},{7,4},{8,11},{9,10},{10,... | collective-permute-start | bytes 1867784 | tf_op jit(solution)/shard_map/ppermute | solution.py:324
  80.1 27.4 %collective-permute-start.16 = (bf16[64,4864]{1,0:T(8,128)(2,1)}, bf16[64,4864]{1,0:T(8,128)(2,1)}, u32[]{:S(2)}, u32[]{:S(2)}) collective-permute-start(bf16[64,4864]{1,0:T(8,128)(2,1)} %pad_maximum_fusion.2), channel_id=1, source_target_pairs={{0,8},{4,12},{8,0},{12,4},{16,24},{20,28},{24,16},{28,20},{1,9},{5... | collective-permute-start | bytes 1867784 | tf_op jit(solution)/shard_map/ppermute | solution.py:327
  85.4 18.8 %collective-permute-start.15 = (bf16[32,4864]{1,0:T(8,128)(2,1)S(1)}, bf16[32,4864]{1,0:T(8,128)(2,1)S(1)}, u32[]{:S(2)}, u32[]{:S(2)}) collective-permute-start(bf16[32,4864]{1,0:T(8,128)(2,1)S(1)} %copy-done.1), channel_id=1, source_target_pairs={{0,16},{4,20},{8,24},{12,28},{16,0},{20,4},{24,8},{28,12},{1,17},{... | collective-permute-start | bytes 933896 | tf_op jit(solution)/shard_map/ppermute | solution.py:327
  86.3 21.8 %copy-start.17 = (bf16[32,4864]{1,0:T(8,128)(2,1)S(1)}, bf16[32,4864]{1,0:T(8,128)(2,1)}, u32[]{:S(2)}) copy-start(bf16[32,4864]{1,0:T(8,128)(2,1)} %copy-done.16) | copy-start | bytes 933892
  86.3 22.3 %copy-start.10 = (bf16[64,4864]{1,0:T(8,128)(2,1)S(1)}, bf16[64,4864]{1,0:T(8,128)(2,1)}, u32[]{:S(2)}) copy-start(bf16[64,4864]{1,0:T(8,128)(2,1)} %copy-done.9) | copy-start | bytes 1867780
  102.7 16.9 %copy-start.6 = (bf16[32,9728]{1,0:T(8,128)(2,1)S(1)}, bf16[32,9728]{1,0:T(8,128)(2,1)}, u32[]{:S(2)}) copy-start(bf16[32,9728]{1,0:T(8,128)(2,1)} %copy-done.5) | copy-start | bytes 1867780
  102.7 16.9 %copy-start.8 = (bf16[32,9728]{1,0:T(8,128)(2,1)S(1)}, bf16[32,9728]{1,0:T(8,128)(2,1)}, u32[]{:S(2)}) copy-start(bf16[32,9728]{1,0:T(8,128)(2,1)} %copy-done.7) | copy-start | bytes 1867780
  102.7 16.9 %copy-start.15 = (bf16[32,4864]{1,0:T(8,128)(2,1)S(1)}, bf16[32,4864]{1,0:T(8,128)(2,1)}, u32[]{:S(2)}) copy-start(bf16[32,4864]{1,0:T(8,128)(2,1)} %copy-done.14) | copy-start | bytes 933892
  102.7 16.9 %copy-start.19 = (s32[12]{0:T(128)S(1)}, s32[12]{0:T(128)}, u32[]{:S(2)}) copy-start(s32[12]{0:T(128)} %concatenate.13.place_ref) | copy-start | bytes 148
  107.5 6.0 %collective-permute-start.30 = (bf16[64,4864]{1,0:T(8,128)(2,1)S(1)}, bf16[64,4864]{1,0:T(8,128)(2,1)S(1)}, u32[]{:S(2)}, u32[]{:S(2)}) collective-permute-start(bf16[64,4864]{1,0:T(8,128)(2,1)S(1)} %collective-permute-done.17.refs_5_.refs_1_), channel_id=1, source_target_pairs={{0,4},{4,0},{8,12},{12,8},{16,20},{20,16},{24,28},{28,24},{1,5},{5... | collective-permute-start | bytes 1867784 | tf_op jit(solution)/shard_map/ppermute | solution.py:330
  107.5 6.2 %collective-permute-start.31 = (bf16[64,4864]{1,0:T(8,128)(2,1)S(1)}, bf16[64,4864]{1,0:T(8,128)(2,1)S(1)}, u32[]{:S(2)}, u32[]{:S(2)}) collective-permute-start(bf16[64,4864]{1,0:T(8,128)(2,1)S(1)} %collective-permute-done.18.refs_6_.refs_2_), channel_id=1, source_target_pairs={{0,4},{4,0},{8,12},{12,8},{16,20},{20,16},{24,28},{28,24},{1,5},{5... | collective-permute-start | bytes 1867784 | tf_op jit(solution)/shard_map/ppermute | solution.py:330
  108.0 10.2 %collective-permute-start.32 = (bf16[64,4864]{1,0:T(8,128)(2,1)S(1)}, bf16[64,4864]{1,0:T(8,128)(2,1)S(1)}, u32[]{:S(2)}, u32[]{:S(2)}) collective-permute-start(bf16[64,4864]{1,0:T(8,128)(2,1)S(1)} %collective-permute-done.19.refs_7_.refs_3_), channel_id=1, source_target_pairs={{0,4},{4,0},{8,12},{12,8},{16,20},{20,16},{24,28},{28,24},{1,5},{5... | collective-permute-start | bytes 1867784 | tf_op jit(solution)/shard_map/ppermute | solution.py:330
  108.1 3.7 %collective-permute-start.29 = (bf16[32,4864]{1,0:T(8,128)(2,1)S(1)}, bf16[32,4864]{1,0:T(8,128)(2,1)S(1)}, u32[]{:S(2)}, u32[]{:S(2)}) collective-permute-start(bf16[32,4864]{1,0:T(8,128)(2,1)S(1)} %copy-done.17), channel_id=1, source_target_pairs={{0,4},{4,0},{8,12},{12,8},{16,20},{20,16},{24,28},{28,24},{1,5},{5... | collective-permute-start | bytes 933896 | tf_op jit(solution)/shard_map/ppermute | solution.py:330
  109.7 26.8 %collective-permute-start.25 = (bf16[32,4864]{1,0:T(8,128)(2,1)S(1)}, bf16[32,4864]{1,0:T(8,128)(2,1)S(1)}, u32[]{:S(2)}, u32[]{:S(2)}) collective-permute-start(bf16[32,4864]{1,0:T(8,128)(2,1)S(1)} %get-tuple-element.176), channel_id=1, source_target_pairs={{0,1},{1,0},{2,3},{3,2},{4,5},{5,4},{6,7},{7,6},{8,9},{9,8},{10,11... | collective-permute-start | bytes 933896 | tf_op jit(solution)/shard_map/ppermute | solution.py:324
  111.8 24.7 %collective-permute-start.26 = (bf16[32,4864]{1,0:T(8,128)(2,1)S(1)}, bf16[32,4864]{1,0:T(8,128)(2,1)S(1)}, u32[]{:S(2)}, u32[]{:S(2)}) collective-permute-start(bf16[32,4864]{1,0:T(8,128)(2,1)S(1)} %get-tuple-element.177), channel_id=1, source_target_pairs={{0,2},{1,3},{2,0},{3,1},{4,6},{5,7},{6,4},{7,5},{8,10},{9,11},{10,... | collective-permute-start | bytes 933896 | tf_op jit(solution)/shard_map/ppermute | solution.py:324
  113.5 23.0 %collective-permute-start.27 = (bf16[32,4864]{1,0:T(8,128)(2,1)S(1)}, bf16[32,4864]{1,0:T(8,128)(2,1)S(1)}, u32[]{:S(2)}, u32[]{:S(2)}) collective-permute-start(bf16[32,4864]{1,0:T(8,128)(2,1)S(1)} %get-tuple-element.178), channel_id=1, source_target_pairs={{0,3},{1,2},{2,1},{3,0},{4,7},{5,6},{6,5},{7,4},{8,11},{9,10},{10,... | collective-permute-start | bytes 933896 | tf_op jit(solution)/shard_map/ppermute | solution.py:324
  113.7 22.8 %collective-permute-start.24 = (bf16[32,4864]{1,0:T(8,128)(2,1)S(1)}, bf16[32,4864]{1,0:T(8,128)(2,1)S(1)}, u32[]{:S(2)}, u32[]{:S(2)}) collective-permute-start(bf16[32,4864]{1,0:T(8,128)(2,1)S(1)} %collective-permute-done.15.refs_2_), channel_id=1, source_target_pairs={{0,8},{4,12},{8,0},{12,4},{16,24},{20,28},{24,16},{28,20},{1,9},{5... | collective-permute-start | bytes 933896 | tf_op jit(solution)/shard_map/ppermute | solution.py:327
  118.2 18.4 %collective-permute-start.28 = (bf16[32,4864]{1,0:T(8,128)(2,1)S(1)}, bf16[32,4864]{1,0:T(8,128)(2,1)S(1)}, u32[]{:S(2)}, u32[]{:S(2)}) collective-permute-start(bf16[32,4864]{1,0:T(8,128)(2,1)S(1)} %copy-done.2), channel_id=1, source_target_pairs={{0,3},{1,2},{2,1},{3,0},{4,7},{5,6},{6,5},{7,4},{8,11},{9,10},{10,... | collective-permute-start | bytes 933896 | tf_op jit(solution)/shard_map/ppermute | solution.py:324
  136.6 3.1 %collective-permute-start.36 = (bf16[32,4864]{1,0:T(8,128)(2,1)S(1)}, bf16[32,4864]{1,0:T(8,128)(2,1)S(1)}, u32[]{:S(2)}, u32[]{:S(2)}) collective-permute-start(bf16[32,4864]{1,0:T(8,128)(2,1)S(1)} %get-tuple-element.190.refs_4_), channel_id=1, source_target_pairs={{0,4},{4,0},{8,12},{12,8},{16,20},{20,16},{24,28},{28,24},{1,5},{5... | collective-permute-start | bytes 933896 | tf_op jit(solution)/shard_map/ppermute | solution.py:330
  136.7 4.5 %collective-permute-start.37 = (bf16[32,4864]{1,0:T(8,128)(2,1)S(1)}, bf16[32,4864]{1,0:T(8,128)(2,1)S(1)}, u32[]{:S(2)}, u32[]{:S(2)}) collective-permute-start(bf16[32,4864]{1,0:T(8,128)(2,1)S(1)} %collective-permute-done.25.refs_5_), channel_id=1, source_target_pairs={{0,4},{4,0},{8,12},{12,8},{16,20},{20,16},{24,28},{28,24},{1,5},{5... | collective-permute-start | bytes 933896 | tf_op jit(solution)/shard_map/ppermute | solution.py:330
  137.2 5.5 %collective-permute-start.38 = (bf16[32,4864]{1,0:T(8,128)(2,1)S(1)}, bf16[32,4864]{1,0:T(8,128)(2,1)S(1)}, u32[]{:S(2)}, u32[]{:S(2)}) collective-permute-start(bf16[32,4864]{1,0:T(8,128)(2,1)S(1)} %collective-permute-done.26.refs_6_), channel_id=1, source_target_pairs={{0,4},{4,0},{8,12},{12,8},{16,20},{20,16},{24,28},{28,24},{1,5},{5... | collective-permute-start | bytes 933896 | tf_op jit(solution)/shard_map/ppermute | solution.py:330
  137.2 5.4 %collective-permute-start.39 = (bf16[32,4864]{1,0:T(8,128)(2,1)S(1)}, bf16[32,4864]{1,0:T(8,128)(2,1)S(1)}, u32[]{:S(2)}, u32[]{:S(2)}) collective-permute-start(bf16[32,4864]{1,0:T(8,128)(2,1)S(1)} %collective-permute-done.27.refs_7_), channel_id=1, source_target_pairs={{0,4},{4,0},{8,12},{12,8},{16,20},{20,16},{24,28},{28,24},{1,5},{5... | collective-permute-start | bytes 933896 | tf_op jit(solution)/shard_map/ppermute | solution.py:330
  139.1 18.3 %collective-permute-start.33 = (bf16[32,4864]{1,0:T(8,128)(2,1)S(1)}, bf16[32,4864]{1,0:T(8,128)(2,1)S(1)}, u32[]{:S(2)}, u32[]{:S(2)}) collective-permute-start(bf16[32,4864]{1,0:T(8,128)(2,1)S(1)} %get-tuple-element.196), channel_id=1, source_target_pairs={{0,1},{1,0},{2,3},{3,2},{4,5},{5,4},{6,7},{7,6},{8,9},{9,8},{10,11... | collective-permute-start | bytes 933896 | tf_op jit(solution)/shard_map/ppermute | solution.py:324
  139.7 17.7 %collective-permute-start.34 = (bf16[32,4864]{1,0:T(8,128)(2,1)S(1)}, bf16[32,4864]{1,0:T(8,128)(2,1)S(1)}, u32[]{:S(2)}, u32[]{:S(2)}) collective-permute-start(bf16[32,4864]{1,0:T(8,128)(2,1)S(1)} %get-tuple-element.197), channel_id=1, source_target_pairs={{0,2},{1,3},{2,0},{3,1},{4,6},{5,7},{6,4},{7,5},{8,10},{9,11},{10,... | collective-permute-start | bytes 933896 | tf_op jit(solution)/shard_map/ppermute | solution.py:324
  141.2 19.2 %copy-start.18 = (s32[128,256]{1,0:T(8,128)S(1)}, s32[128,256]{1,0:T(8,128)}, u32[]{:S(2)}) copy-start(s32[128,256]{1,0:T(8,128)} %refs_13_.1) | copy-start | bytes 393220
  141.2 16.2 %collective-permute-start.35 = (bf16[32,4864]{1,0:T(8,128)(2,1)S(1)}, bf16[32,4864]{1,0:T(8,128)(2,1)S(1)}, u32[]{:S(2)}, u32[]{:S(2)}) collective-permute-start(bf16[32,4864]{1,0:T(8,128)(2,1)S(1)} %get-tuple-element.198), channel_id=1, source_target_pairs={{0,3},{1,2},{2,1},{3,0},{4,7},{5,6},{6,5},{7,4},{8,11},{9,10},{10,... | collective-permute-start | bytes 933896 | tf_op jit(solution)/shard_map/ppermute | solution.py:324
  157.4 1.7 collective-permute-start.40
  157.5 2.0 %collective-permute-start.41 = (bf16[32,4864]{1,0:T(8,128)(2,1)S(1)}, bf16[32,4864]{1,0:T(8,128)(2,1)S(1)}, u32[]{:S(2)}, u32[]{:S(2)}) collective-permute-start(bf16[32,4864]{1,0:T(8,128)(2,1)S(1)} %collective-permute-done.33.refs_5_), channel_id=1, source_target_pairs={{0,4},{4,0},{8,12},{12,8},{16,20},{20,16},{24,28},{28,24},{1,5},{5... | collective-permute-start | bytes 933896 | tf_op jit(solution)/shard_map/ppermute | solution.py:330
  158.0 2.0 %collective-permute-start.42 = (bf16[32,4864]{1,0:T(8,128)(2,1)S(1)}, bf16[32,4864]{1,0:T(8,128)(2,1)S(1)}, u32[]{:S(2)}, u32[]{:S(2)}) collective-permute-start(bf16[32,4864]{1,0:T(8,128)(2,1)S(1)} %collective-permute-done.34.refs_6_), channel_id=1, source_target_pairs={{0,4},{4,0},{8,12},{12,8},{16,20},{20,16},{24,28},{28,24},{1,5},{5... | collective-permute-start | bytes 933896 | tf_op jit(solution)/shard_map/ppermute | solution.py:330
  158.0 2.4 %collective-permute-start.43 = (bf16[32,4864]{1,0:T(8,128)(2,1)S(1)}, bf16[32,4864]{1,0:T(8,128)(2,1)S(1)}, u32[]{:S(2)}, u32[]{:S(2)}) collective-permute-start(bf16[32,4864]{1,0:T(8,128)(2,1)S(1)} %collective-permute-done.35.refs_7_), channel_id=1, source_target_pairs={{0,4},{4,0},{8,12},{12,8},{16,20},{20,16},{24,28},{28,24},{1,5},{5... | collective-permute-start | bytes 933896 | tf_op jit(solution)/shard_map/ppermute | solution.py:330
  (11 other events, 22.2 us)

commit v5 on v4

--- a/solution.py
+++ b/solution.py
@@ -153,15 +153,15 @@
             out_ref[rows:, :] = refs[count][...]
 
 
-def route(place, parts, rows, extra):
+def route(place, parts, rows, extra, longer):
     length = parts[0][0].shape[1]
     kind = parts[0][0].dtype
 
     def spec(count, at=0):
         return pl.BlockSpec((count, length), lambda step: (at, 0))
 
-    counts = [rows] + [rows if extra is None else 2 * rows] * (len(parts) - 1)
-    more = [] if extra is None else [extra]
+    counts = [2 * rows if k in longer else rows for k in range(len(parts))]
+    more = [extra] if longer else []
     return pl.pallas_call(
         functools.partial(route_kernel, len(parts)),
         grid=(1,),
@@ -205,13 +205,15 @@
                 staged[at, :] = piece[...].astype(staged.dtype)
         if staged is not None:
             columns[...] = staged[...].astype(columns.dtype)
-        for started in copies:
+        edge[...] = jnp.zeros_like(edge)
+        start = (SHIFTS // 2 + 1 - shift_group) % width
+        for started in copies[: 2 * len(lefts)]:
+            started.wait()
+        even[...] = pltpu.roll(even[...], start, 1)
+        odd[...] = pltpu.roll(odd[...], start, 1)
+        for started in copies[2 * len(lefts) :]:
             started.wait()
         both[...] = columns[:, :width] + columns[:, width:]
-        start = (SHIFTS // 2 + 1 - shift_group) % width
-        even[...] = pltpu.roll(even[...], start, 1)
-        odd[...] = pltpu.roll(odd[...], start, 1)
-        edge[...] = jnp.zeros_like(edge)
 
     half = SAMP // 2
     sample = lax.broadcasted_iota(jnp.int32, (16, width), 1)
@@ -302,7 +304,7 @@
         out_shape=jax.ShapeDtypeStruct(out_shape, jnp.float32 if last else jnp.bfloat16),
         input_output_aliases=aliases,
         scratch_shapes=scratch,
-        compiler_params=pltpu.CompilerParams(vmem_limit_bytes=vmem_bytes if total is None else 34 << 20),
+        compiler_params=pltpu.CompilerParams(vmem_limit_bytes=(58 if total is None else 51) << 20),
         name="correlate",
     )(*operands)
 
@@ -376,12 +378,12 @@
         for k in direct if ahead else []:
             hop(k, (u + 1, k))
 
-    def columns(u, extra=None):
+    def columns(u, extra, longer):
         parts = [(state[lines[u][k][0]], lines[u][k][1]) for k in range(seg_count)]
-        more = None if extra is None else state["unit", extra]
-        for k, piece in enumerate(route(route_place, parts, rows, more)):
+        more = state["unit", extra] if longer else None
+        for k, piece in enumerate(route(route_place, parts, rows, more, longer)):
             state["own", u, k] = to_seg(piece, k) if k else piece
-            if k and extra is not None:
+            if k in longer:
                 rows_of[extra][k] = ("own", u, k), (rows, 0)
 
     rows_of = [{0: (("unit", u), (0, 0))} for u in range(count)]
@@ -417,20 +419,22 @@
     row_plan = {
         -1: [(k, ("unit", 0), [0]) for k in hops],
         0: [(k, "middle", range(1, half + 1)) for k in hops[:-1]] + [(hops[-1], ("unit", 1), [1])],
-        half + 1: [(hops[-1], ("unit", half), [half])],
     }
+    carried = {0: (half, hops[-1:])}
+    for v in range(half + 1, count):
+        carried[v - 2] = v, hops[:-1]
+        carried[v - 1] = v, hops[-1:]
     plane_hops(-1)
     if gathered:
         for source, covered in ((("unit", 0), [0]), ("middle", range(1, half)), ("late", range(half, count))):
             gather_rows(source, list(covered))
-        row_plan = {}
+        row_plan, carried = {}, {}
     for u in range(-1, count + 2):
         if u >= 0:
             fence()
             plane_hops(u)
         if 1 <= u <= count:
-            carried = u + 1 if half <= u < count - 1 and not gathered else None
-            columns(u - 1, carried)
+            columns(u - 1, *carried.get(u - 1, (None, [])))
         for k, source, covered in row_plan.get(u, []):
             row_hop(k, source, list(covered))
         if 2 <= u <= count:

time: 177 us -> 173 us (0.977)
  starting transfers between devices: 45.9 us -> 39.9 us
  Pallas kernels: 79.7 us -> 83 us
  local copies, waits for them, and re-layouts: 7.65 us -> 4.8 us
    ppermute x9, starting transfers between devices: 20.6 us -> 14.9 us  [to_plane(): lax.ppermute(value, 'stn', [(i, i ^ k * sides) for i in range(stn_count)])]
    pallas_call x4, Pallas kernels: 62.1 us -> 65.9 us  [correlate(): pl.pallas_call(functools.partial(correlate_kernel, begins, left_rows, pie...]
    ppermute x19 -> x18, waiting for transfers between devices: 18 us -> 21 us  [to_seg(): return lax.ppermute(value, 'seg', [(i, i ^ k) for i in range(seg_count)])]
    unnamed x62 -> x50, local copies, waits for them, and re-layouts: 7.08 us -> 4.18 us
    ppermute x19 -> x18, starting transfers between devices: 21.1 us -> 20.8 us  [to_seg(): return lax.ppermute(value, 'seg', [(i, i ^ k) for i in range(seg_count)])]
  transfers between devices with their start and end apart: 44 -> 43, of which waited for: 16 -> 17; matrix products, arithmetic and copies ran while one was open for 1% -> 1% of each run, Pallas kernels for 34% -> 36%
where the time goes in v5:
time: 173 us
  Pallas kernels  83 us (48%)
  waiting for transfers between devices  41.5 us (24%)
  starting transfers between devices  39.9 us (23%)
  local copies, waits for them, and re-layouts  4.8 us (3%)
  other arithmetic  2.93 us (2%)
    pallas_call x4, Pallas kernels, correlate(): pl.pallas_call(functools.partial(correlate_kernel, begins, left_rows, pie...  65.9 us
    ppermute x18, waiting for transfers between devices, to_seg(): return lax.ppermute(value, 'seg', [(i, i ^ k) for i in range(seg_count)])  21 us
    ppermute x18, starting transfers between devices, to_seg(): return lax.ppermute(value, 'seg', [(i, i ^ k) for i in range(seg_count)])  20.8 us
    ppermute x9, waiting for transfers between devices, to_plane(): lax.ppermute(value, 'stn', [(i, i ^ k * sides) for i in range(stn_count)])  18.5 us
    ppermute x9, starting transfers between devices, to_plane(): lax.ppermute(value, 'stn', [(i, i ^ k * sides) for i in range(stn_count)])  14.9 us
    pallas_call x2, Pallas kernels, whiten(): pl.pallas_call(functools.partial(whiten_kernel, record_len // LANES, firs...  12.1 us
    pallas_call x4, Pallas kernels, route(): pl.pallas_call(functools.partial(route_kernel, len(parts)), grid=(1,), in...  4.97 us
    ppermute x16, starting transfers between devices, to_side(): return lax.ppermute(value, 'stn', [(i, i ^ j) for i in range(stn_count)])  4.2 us
  transfers between devices with their start and end apart: 43, of which 17 were waited for; matrix products, arithmetic and copies ran while one was open for 1% of the time, Pallas kernels for 36%

profile of v5, /device:TPU:0, one launch (start us, length us, event | category | flops | bytes accessed | tf_op | source)
XLA Modules:
  0.0 172.5 jit_solution(5872518538687750158)
XLA Ops:
  0.0 3.9 %whiten.2.refs_0_ = bf16[32,4864]{1,0:T(8,128)(2,1)} custom-call(f32[31]{0:T(128)} %taps_ref.3, f32[32,19200]{1,0:T(8,128)} %traces_ref.3, s32[32,32]{1,0:T(8,128)} %flags_ref.3), custom_call_target="tpu_custom_call" | custom-call | tf_op jit(solution)/shard_map/whiten/pallas_call | solution.py:127
  3.9 4.0 %collective-permute-start = (bf16[32,4864]{1,0:T(8,128)(2,1)}, bf16[32,4864]{1,0:T(8,128)(2,1)S(1)}, u32[]{:S(2)}, u32[]{:S(2)}) collective-permute-start(bf16[32,4864]{1,0:T(8,128)(2,1)} %whiten.2.refs_0_), channel_id=1, source_target_pairs={{0,16},{4,20},{8,24},{12,28},{16,0},{20,4},{24,8},{28,12},{1,17},{... | collective-permute-start | bytes 933896 | tf_op jit(solution)/shard_map/ppermute | solution.py:329
  8.0 1.6 collective-permute-start.1
  9.5 1.5 collective-permute-start.2
  11.0 1.5 collective-permute-start.3
  12.5 0.5 collective-permute-start.4
  13.0 8.2 %whiten.3 = (bf16[32,4864]{1,0:T(8,128)(2,1)}, bf16[32,4864]{1,0:T(8,128)(2,1)}, bf16[32,4864]{1,0:T(8,128)(2,1)}, bf16[32,9728]{1,0:T(8,128)(2,1)}, bf16[32,9728]{1,0:T(8,128)(2,1)}) custom-call(f32[31]{0:T(128)} %taps_ref.3, f32[32,19200]{1,0:T(8,128)} %traces_ref.3, s32[32,32]{1,0:T(8,128)} %flags_ref.3), custom_call_target="tpu_custom_call" | custom-call | tf_op jit(solution)/shard_map/whiten/pallas_call | solution.py:127
  21.2 1.1 collective-permute-done.refs_2_
  22.5 3.7 %collective-permute-done.3.refs_2_ = bf16[32,4864]{1,0:T(8,128)(2,1)S(1)} collective-permute-done((bf16[32,4864]{1,0:T(8,128)(2,1)}, bf16[32,4864]{1,0:T(8,128)(2,1)S(1)}, u32[]{:S(2)}, u32[]{:S(2)}) %collective-permute-start.3) | collective-permute-done | bytes 311328 | tf_op jit(solution)/shard_map/ppermute | solution.py:326
  26.2 0.7 copy-done.18
  27.0 1.9 %pad_maximum_fusion = bf16[64,4864]{1,0:T(8,128)(2,1)} fusion(bf16[32,4864]{1,0:T(8,128)(2,1)} %get-tuple-element.161.refs_0_, bf16[32,4864]{1,0:T(8,128)(2,1)S(1)} %collective-permute-done.refs_2_), kind=kLoop, calls=%fused_computation | loop fusion | flops 1245184 | bytes 1245184 | tf_op jit(solution)/shard_map/concatenate | solution.py:364
  28.9 0.4 collective-permute-start.6
  29.3 1.1 collective-permute-start.7
  30.5 0.9 collective-permute-start.8
  31.4 0.7 collective-permute-start.5
  32.1 1.0 collective-permute-start.9
  33.2 14.5 %collective-permute-done.5.refs_2_ = bf16[32,4864]{1,0:T(8,128)(2,1)S(1)} collective-permute-done((bf16[32,4864]{1,0:T(8,128)(2,1)S(1)}, bf16[32,4864]{1,0:T(8,128)(2,1)S(1)}, u32[]{:S(2)}, u32[]{:S(2)}) %collective-permute-start.5) | collective-permute-done | bytes 311328 | tf_op jit(solution)/shard_map/ppermute | solution.py:329
  47.7 2.2 %collective-permute-done.9.refs_3_ = bf16[32,4864]{1,0:T(8,128)(2,1)S(1)} collective-permute-done((bf16[32,4864]{1,0:T(8,128)(2,1)S(1)}, bf16[32,4864]{1,0:T(8,128)(2,1)S(1)}, u32[]{:S(2)}, u32[]{:S(2)}) %collective-permute-start.9) | collective-permute-done | bytes 311328 | tf_op jit(solution)/shard_map/ppermute | solution.py:326
  50.0 0.7 copy-done.4
  50.7 0.5 collective-permute-done.8.refs_2_
  51.2 0.8 route.4
  52.0 1.9 %collective-permute-start.14 = (bf16[64,4864]{1,0:T(8,128)(2,1)S(1)}, bf16[64,4864]{1,0:T(8,128)(2,1)S(1)}, u32[]{:S(2)}, u32[]{:S(2)}) collective-permute-start(bf16[64,4864]{1,0:T(8,128)(2,1)S(1)} %get-tuple-element.138), channel_id=1, source_target_pairs={{0,3},{1,2},{2,1},{3,0},{4,7},{5,6},{6,5},{7,4},{8,11},{9,10},{10,... | collective-permute-start | bytes 1867784 | tf_op jit(solution)/shard_map/ppermute | solution.py:326
  53.9 1.6 collective-permute-start.11
  55.5 0.7 collective-permute-start.12
  56.2 1.0 collective-permute-start.13
  57.2 1.0 collective-permute-start.10
  58.2 13.7 %collective-permute-done.12.refs_5_ = bf16[32,4864]{1,0:T(8,128)(2,1)S(1)} collective-permute-done((bf16[32,4864]{1,0:T(8,128)(2,1)S(1)}, bf16[32,4864]{1,0:T(8,128)(2,1)S(1)}, u32[]{:S(2)}, u32[]{:S(2)}) %collective-permute-start.12) | collective-permute-done | bytes 311328 | tf_op jit(solution)/shard_map/ppermute | solution.py:326
  71.9 0.6 collective-permute-done.10.refs_2_
  72.5 0.9 collective-permute-done.11.refs_3_.refs_1_
  73.4 0.5 collective-permute-start.20
  74.0 0.5 collective-permute-start.22
  74.5 2.1 %route.5 = (bf16[32,4864]{1,0:T(8,128)(2,1)S(1)}, bf16[64,4864]{1,0:T(8,128)(2,1)}, bf16[64,4864]{1,0:T(8,128)(2,1)}, bf16[32,4864]{1,0:T(8,128)(2,1)}) custom-call(s32[4]{0:T(128)S(1)} %get-tuple-element.209.place_ref, bf16[32,4864]{1,0:T(8,128)(2,1)S(1)} %copy-done.2, bf16[64,4864]{1,0:T(8,128)(2,1)S(1)} %collective-permute-done.6.refs_3_.refs_1_, ...), custom_call_target="tpu_custom_call" | custom-call | tf_op jit(solution)/shard_map/route/pallas_call | solution.py:165
  76.5 0.7 collective-permute-start.17
  77.3 0.9 pad_maximum_fusion.2
  78.2 1.0 collective-permute-start.18
  79.3 3.4 %collective-permute-start.16 = (bf16[64,4864]{1,0:T(8,128)(2,1)}, bf16[64,4864]{1,0:T(8,128)(2,1)S(1)}, u32[]{:S(2)}, u32[]{:S(2)}) collective-permute-start(bf16[64,4864]{1,0:T(8,128)(2,1)} %pad_maximum_fusion.2), channel_id=1, source_target_pairs={{0,8},{4,12},{8,0},{12,4},{16,24},{20,28},{24,16},{28,20},{1,9},{5... | collective-permute-start | bytes 1867784 | tf_op jit(solution)/shard_map/ppermute | solution.py:329
  82.7 1.7 %collective-permute-start.19 = (bf16[32,4864]{1,0:T(8,128)(2,1)}, bf16[32,4864]{1,0:T(8,128)(2,1)S(1)}, u32[]{:S(2)}, u32[]{:S(2)}) collective-permute-start(bf16[32,4864]{1,0:T(8,128)(2,1)} %get-tuple-element.160), channel_id=1, source_target_pairs={{0,3},{1,2},{2,1},{3,0},{4,7},{5,6},{6,5},{7,4},{8,11},{9,10},{10,... | collective-permute-start | bytes 933896 | tf_op jit(solution)/shard_map/ppermute | solution.py:326
  84.5 0.9 copy-done.13
  85.6 0.6 concatenate.13.place_ref
  86.2 16.1 %correlate.4.refs_12_ = bf16[3,21,128,256]{3,2,1,0:T(8,128)(2,1)} custom-call(s32[12]{0:T(128)} %concatenate.13.place_ref, bf16[32,4864]{1,0:T(8,128)(2,1)} %whiten.2.refs_0_, bf16[32,4864]{1,0:T(8,128)(2,1)} %copy-done.17, bf16[32,4864]{1,0:T(8,128)(2,1)} %copy-done.18, bf16[32,4864]{1,0:T(8,128)(2,1)} %copy-done.19, bf16[32,4864]{1,0:T(8,128)(2,1)} %copy-done.8, ...), custom_call_target="tpu_custom_call" | custom-call | tf_op jit(solution)/shard_map/correlate/pallas_call | solution.py:297
  102.3 0.5 collective-permute-done.15.refs_2_
  102.9 0.7 collective-permute-done.16.refs_3_.refs_1_
  103.6 0.5 collective-permute-start.30
  104.1 0.5 collective-permute-start.31
  104.6 0.8 route.6
  105.4 1.6 collective-permute-start.27
  107.0 1.3 collective-permute-start.25
  108.2 0.7 collective-permute-start.26
  108.9 1.8 %collective-permute-start.24 = (bf16[32,4864]{1,0:T(8,128)(2,1)}, bf16[32,4864]{1,0:T(8,128)(2,1)S(1)}, u32[]{:S(2)}, u32[]{:S(2)}) collective-permute-start(bf16[32,4864]{1,0:T(8,128)(2,1)} %collective-permute-done.15.refs_2_), channel_id=1, source_target_pairs={{0,8},{4,12},{8,0},{12,4},{16,24},{20,28},{24,16},{28,20},{1,9},{5... | collective-permute-start | bytes 933896 | tf_op jit(solution)/shard_map/ppermute | solution.py:329
  110.8 0.9 copy-done.16
  111.7 16.4 %correlate.5.refs_12_ = bf16[3,21,128,256]{3,2,1,0:T(8,128)(2,1)} custom-call(s32[12]{0:T(128)S(1)} %copy-done.10, bf16[32,4864]{1,0:T(8,128)(2,1)S(1)} %copy-done.2, bf16[32,9728]{1,0:T(8,128)(2,1)S(1)} %collective-permute-done.7.refs_1_, bf16[32,9728]{1,0:T(8,128)(2,1)} %collective-permute-done.8.refs_2_, ...), custom_call_target="tpu_custom_call", output_to_operand_aliasing={{}: (13, {})} | custom-call | tf_op jit(solution)/shard_map/correlate/pallas_call | solution.py:297
  128.1 0.8 collective-permute-done.26.refs_6_
  129.0 0.5 collective-permute-start.35
  130.0 1.4 route.7
  131.4 1.8 %collective-permute-start.32 = (bf16[32,4864]{1,0:T(8,128)(2,1)S(1)}, bf16[32,4864]{1,0:T(8,128)(2,1)S(1)}, u32[]{:S(2)}, u32[]{:S(2)}) collective-permute-start(bf16[32,4864]{1,0:T(8,128)(2,1)S(1)} %get-tuple-element.196), channel_id=1, source_target_pairs={{0,1},{1,0},{2,3},{3,2},{4,5},{5,4},{6,7},{7,6},{8,9},{9,8},{10,11... | collective-permute-start | bytes 933896 | tf_op jit(solution)/shard_map/ppermute | solution.py:326
  133.2 0.6 collective-permute-start.33
  133.8 1.2 collective-permute-start.34
  135.0 0.8 copy-done.14
  135.8 16.4 %correlate.6.refs_12_ = bf16[3,21,128,256]{3,2,1,0:T(8,128)(2,1)} custom-call(s32[12]{0:T(128)S(1)} %copy-done.10, bf16[32,4864]{1,0:T(8,128)(2,1)S(1)} %copy-done.1, bf16[32,9728]{1,0:T(8,128)(2,1)S(1)} %collective-permute-done.7.refs_1_, bf16[32,9728]{1,0:T(8,128)(2,1)} %collective-permute-done.8.refs_2_, ...), custom_call_target="tpu_custom_call", output_to_operand_aliasing={{}: (13, {})} | custom-call | tf_op jit(solution)/shard_map/correlate/pallas_call | solution.py:297
  152.4 0.5 collective-permute-start.40
  153.4 0.6 collective-permute-done.39.refs_8_
  154.0 0.4 collective-permute-done.40.refs_9_
  154.4 0.4 collective-permute-done.41.refs_10_
  155.3 17.0 %correlate.7 = f32[41,128,256]{2,1,0:T(8,128)} custom-call(s32[12]{0:T(128)S(1)} %copy-done.10, bf16[32,4864]{1,0:T(8,128)(2,1)S(1)} %copy-done, bf16[64,4864]{1,0:T(8,128)(2,1)} %collective-permute-done.17.refs_5_.refs_1_, bf16[64,4864]{1,0:T(8,128)(2,1)} %collective-permute-done.18.refs_6_.refs_2_, bf16[64,4864]{1,0:T(8,128)(2,1)} %copy-done.11, ...), custom_call_target="tpu_custom_call" | custom-call | tf_op jit(solution)/shard_map/correlate/pallas_call | solution.py:297
  (88 shorter events, 2.5 us)
Async XLA Ops:
  3.9 18.4 %collective-permute-start = (bf16[32,4864]{1,0:T(8,128)(2,1)}, bf16[32,4864]{1,0:T(8,128)(2,1)S(1)}, u32[]{:S(2)}, u32[]{:S(2)}) collective-permute-start(bf16[32,4864]{1,0:T(8,128)(2,1)} %whiten.2.refs_0_), channel_id=1, source_target_pairs={{0,16},{4,20},{8,24},{12,28},{16,0},{20,4},{24,8},{28,12},{1,17},{... | collective-permute-start | bytes 933896 | tf_op jit(solution)/shard_map/ppermute | solution.py:329
  8.0 14.5 %collective-permute-start.1 = (bf16[32,4864]{1,0:T(8,128)(2,1)}, bf16[32,4864]{1,0:T(8,128)(2,1)S(1)}, u32[]{:S(2)}, u32[]{:S(2)}) collective-permute-start(bf16[32,4864]{1,0:T(8,128)(2,1)} %whiten.2.refs_0_), channel_id=1, source_target_pairs={{0,8},{4,12},{8,0},{12,4},{16,24},{20,28},{24,16},{28,20},{1,9},{5... | collective-permute-start | bytes 933896 | tf_op jit(solution)/shard_map/ppermute | solution.py:329
  9.5 13.0 %collective-permute-start.2 = (bf16[32,4864]{1,0:T(8,128)(2,1)}, bf16[32,4864]{1,0:T(8,128)(2,1)S(1)}, u32[]{:S(2)}, u32[]{:S(2)}) collective-permute-start(bf16[32,4864]{1,0:T(8,128)(2,1)} %whiten.2.refs_0_), channel_id=1, source_target_pairs={{0,1},{1,0},{2,3},{3,2},{4,5},{5,4},{6,7},{7,6},{8,9},{9,8},{10,11... | collective-permute-start | bytes 933896 | tf_op jit(solution)/shard_map/ppermute | solution.py:326
  11.0 15.1 %collective-permute-start.3 = (bf16[32,4864]{1,0:T(8,128)(2,1)}, bf16[32,4864]{1,0:T(8,128)(2,1)S(1)}, u32[]{:S(2)}, u32[]{:S(2)}) collective-permute-start(bf16[32,4864]{1,0:T(8,128)(2,1)} %whiten.2.refs_0_), channel_id=1, source_target_pairs={{0,2},{1,3},{2,0},{3,1},{4,6},{5,7},{6,4},{7,5},{8,10},{9,11},{10,... | collective-permute-start | bytes 933896 | tf_op jit(solution)/shard_map/ppermute | solution.py:326
  12.5 13.6 %collective-permute-start.4 = (bf16[32,4864]{1,0:T(8,128)(2,1)}, bf16[32,4864]{1,0:T(8,128)(2,1)S(1)}, u32[]{:S(2)}, u32[]{:S(2)}) collective-permute-start(bf16[32,4864]{1,0:T(8,128)(2,1)} %whiten.2.refs_0_), channel_id=1, source_target_pairs={{0,3},{1,2},{2,1},{3,0},{4,7},{5,6},{6,5},{7,4},{8,11},{9,10},{10,... | collective-permute-start | bytes 933896 | tf_op jit(solution)/shard_map/ppermute | solution.py:326
  21.2 10.2 %copy-start.2 = (bf16[32,4864]{1,0:T(8,128)(2,1)S(1)}, bf16[32,4864]{1,0:T(8,128)(2,1)}, u32[]{:S(2)}) copy-start(bf16[32,4864]{1,0:T(8,128)(2,1)} %get-tuple-element.161.refs_0_) | copy-start | bytes 933892
  21.2 30.0 %copy-start.1 = (bf16[32,4864]{1,0:T(8,128)(2,1)S(1)}, bf16[32,4864]{1,0:T(8,128)(2,1)}, u32[]{:S(2)}) copy-start(bf16[32,4864]{1,0:T(8,128)(2,1)} %get-tuple-element.181.refs_4_.refs_0_) | copy-start | bytes 933892
  21.2 30.0 %copy-start.3 = (bf16[32,4864]{1,0:T(8,128)(2,1)S(1)}, bf16[32,4864]{1,0:T(8,128)(2,1)}, u32[]{:S(2)}) copy-start(bf16[32,4864]{1,0:T(8,128)(2,1)} %whiten.2.refs_0_) | copy-start | bytes 933892
  22.5 8.9 %copy-start.17 = (bf16[32,4864]{1,0:T(8,128)(2,1)}, bf16[32,4864]{1,0:T(8,128)(2,1)S(1)}, u32[]{:S(2)}) copy-start(bf16[32,4864]{1,0:T(8,128)(2,1)S(1)} %collective-permute-done.2.refs_1_) | copy-start | bytes 933892
  28.9 21.8 %collective-permute-start.6 = (bf16[64,4864]{1,0:T(8,128)(2,1)}, bf16[64,4864]{1,0:T(8,128)(2,1)S(1)}, u32[]{:S(2)}, u32[]{:S(2)}) collective-permute-start(bf16[64,4864]{1,0:T(8,128)(2,1)} %pad_maximum_fusion), channel_id=1, source_target_pairs={{0,8},{4,12},{8,0},{12,4},{16,24},{20,28},{24,16},{28,20},{1,9},{5... | collective-permute-start | bytes 1867784 | tf_op jit(solution)/shard_map/ppermute | solution.py:329
  29.3 21.4 %collective-permute-start.7 = (bf16[32,9728]{1,0:T(8,128)(2,1)}, bf16[32,9728]{1,0:T(8,128)(2,1)S(1)}, u32[]{:S(2)}, u32[]{:S(2)}) collective-permute-start(bf16[32,9728]{1,0:T(8,128)(2,1)} %get-tuple-element.115), channel_id=1, source_target_pairs={{0,1},{1,0},{2,3},{3,2},{4,5},{5,4},{6,7},{7,6},{8,9},{9,8},{10,11... | collective-permute-start | bytes 1867784 | tf_op jit(solution)/shard_map/ppermute | solution.py:326
  30.5 20.7 %collective-permute-start.8 = (bf16[32,9728]{1,0:T(8,128)(2,1)}, bf16[32,9728]{1,0:T(8,128)(2,1)}, u32[]{:S(2)}, u32[]{:S(2)}) collective-permute-start(bf16[32,9728]{1,0:T(8,128)(2,1)} %get-tuple-element.115), channel_id=1, source_target_pairs={{0,2},{1,3},{2,0},{3,1},{4,6},{5,7},{6,4},{7,5},{8,10},{9,11},{10,... | collective-permute-start | bytes 1867784 | tf_op jit(solution)/shard_map/ppermute | solution.py:326
  31.4 16.3 %collective-permute-start.5 = (bf16[32,4864]{1,0:T(8,128)(2,1)S(1)}, bf16[32,4864]{1,0:T(8,128)(2,1)S(1)}, u32[]{:S(2)}, u32[]{:S(2)}) collective-permute-start(bf16[32,4864]{1,0:T(8,128)(2,1)S(1)} %copy-done.2), channel_id=1, source_target_pairs={{0,16},{4,20},{8,24},{12,28},{16,0},{20,4},{24,8},{28,12},{1,17},{... | collective-permute-start | bytes 933896 | tf_op jit(solution)/shard_map/ppermute | solution.py:329
  32.1 17.8 %collective-permute-start.9 = (bf16[32,4864]{1,0:T(8,128)(2,1)S(1)}, bf16[32,4864]{1,0:T(8,128)(2,1)S(1)}, u32[]{:S(2)}, u32[]{:S(2)}) collective-permute-start(bf16[32,4864]{1,0:T(8,128)(2,1)S(1)} %copy-done.2), channel_id=1, source_target_pairs={{0,3},{1,2},{2,1},{3,0},{4,7},{5,6},{6,5},{7,4},{8,11},{9,10},{10,... | collective-permute-start | bytes 933896 | tf_op jit(solution)/shard_map/ppermute | solution.py:326
  51.2 23.3 %copy-start = (bf16[32,4864]{1,0:T(8,128)(2,1)S(1)}, bf16[32,4864]{1,0:T(8,128)(2,1)}, u32[]{:S(2)}) copy-start(bf16[32,4864]{1,0:T(8,128)(2,1)} %get-tuple-element.200.refs_4_.refs_0_) | copy-start | bytes 933892
  51.9 24.6 %copy-start.8 = (bf16[32,4864]{1,0:T(8,128)(2,1)}, bf16[32,4864]{1,0:T(8,128)(2,1)S(1)}, u32[]{:S(2)}) copy-start(bf16[32,4864]{1,0:T(8,128)(2,1)S(1)} %get-tuple-element.153.refs_4_) | copy-start | bytes 933892
  52.0 20.6 %collective-permute-start.14 = (bf16[64,4864]{1,0:T(8,128)(2,1)S(1)}, bf16[64,4864]{1,0:T(8,128)(2,1)S(1)}, u32[]{:S(2)}, u32[]{:S(2)}) collective-permute-start(bf16[64,4864]{1,0:T(8,128)(2,1)S(1)} %get-tuple-element.138), channel_id=1, source_target_pairs={{0,3},{1,2},{2,1},{3,0},{4,7},{5,6},{6,5},{7,4},{8,11},{9,10},{10,... | collective-permute-start | bytes 1867784 | tf_op jit(solution)/shard_map/ppermute | solution.py:326
  53.9 19.5 %collective-permute-start.11 = (bf16[64,4864]{1,0:T(8,128)(2,1)S(1)}, bf16[64,4864]{1,0:T(8,128)(2,1)S(1)}, u32[]{:S(2)}, u32[]{:S(2)}) collective-permute-start(bf16[64,4864]{1,0:T(8,128)(2,1)S(1)} %pad_maximum_fusion.1), channel_id=1, source_target_pairs={{0,8},{4,12},{8,0},{12,4},{16,24},{20,28},{24,16},{28,20},{1,9},{5... | collective-permute-start | bytes 1867784 | tf_op jit(solution)/shard_map/ppermute | solution.py:329
  55.5 16.4 %collective-permute-start.12 = (bf16[32,4864]{1,0:T(8,128)(2,1)S(1)}, bf16[32,4864]{1,0:T(8,128)(2,1)S(1)}, u32[]{:S(2)}, u32[]{:S(2)}) collective-permute-start(bf16[32,4864]{1,0:T(8,128)(2,1)S(1)} %get-tuple-element.136), channel_id=1, source_target_pairs={{0,1},{1,0},{2,3},{3,2},{4,5},{5,4},{6,7},{7,6},{8,9},{9,8},{10,11... | collective-permute-start | bytes 933896 | tf_op jit(solution)/shard_map/ppermute | solution.py:326
  56.2 15.7 %collective-permute-start.13 = (bf16[32,4864]{1,0:T(8,128)(2,1)S(1)}, bf16[32,4864]{1,0:T(8,128)(2,1)S(1)}, u32[]{:S(2)}, u32[]{:S(2)}) collective-permute-start(bf16[32,4864]{1,0:T(8,128)(2,1)S(1)} %get-tuple-element.137), channel_id=1, source_target_pairs={{0,2},{1,3},{2,0},{3,1},{4,6},{5,7},{6,4},{7,5},{8,10},{9,11},{10,... | collective-permute-start | bytes 933896 | tf_op jit(solution)/shard_map/ppermute | solution.py:326
  57.2 15.3 %collective-permute-start.10 = (bf16[32,4864]{1,0:T(8,128)(2,1)S(1)}, bf16[32,4864]{1,0:T(8,128)(2,1)S(1)}, u32[]{:S(2)}, u32[]{:S(2)}) collective-permute-start(bf16[32,4864]{1,0:T(8,128)(2,1)S(1)} %copy-done.1), channel_id=1, source_target_pairs={{0,16},{4,20},{8,24},{12,28},{16,0},{20,4},{24,8},{28,12},{1,17},{... | collective-permute-start | bytes 933896 | tf_op jit(solution)/shard_map/ppermute | solution.py:329
  71.9 6.3 %copy-start.20 = (bf16[32,4864]{1,0:T(8,128)(2,1)}, bf16[32,4864]{1,0:T(8,128)(2,1)S(1)}, u32[]{:S(2)}) copy-start(bf16[32,4864]{1,0:T(8,128)(2,1)S(1)} %collective-permute-done.12.refs_5_) | copy-start | bytes 933892
  71.9 6.3 %copy-start.21 = (bf16[32,4864]{1,0:T(8,128)(2,1)}, bf16[32,4864]{1,0:T(8,128)(2,1)S(1)}, u32[]{:S(2)}) copy-start(bf16[32,4864]{1,0:T(8,128)(2,1)S(1)} %collective-permute-done.13.refs_6_) | copy-start | bytes 933892
  72.5 5.7 %copy-start.12 = (bf16[64,4864]{1,0:T(8,128)(2,1)}, bf16[64,4864]{1,0:T(8,128)(2,1)S(1)}, u32[]{:S(2)}) copy-start(bf16[64,4864]{1,0:T(8,128)(2,1)S(1)} %collective-permute-done.14.refs_7_.refs_3_) | copy-start | bytes 1867780
  73.4 11.0 %collective-permute-start.23 = (bf16[64,4864]{1,0:T(8,128)(2,1)S(1)}, bf16[64,4864]{1,0:T(8,128)(2,1)S(1)}, u32[]{:S(2)}, u32[]{:S(2)}) collective-permute-start(bf16[64,4864]{1,0:T(8,128)(2,1)S(1)} %collective-permute-done.14.refs_7_.refs_3_), channel_id=1, source_target_pairs={{0,4},{4,0},{8,12},{12,8},{16,20},{20,16},{24,28},{28,24},{1,5},{5... | collective-permute-start | bytes 1867784 | tf_op jit(solution)/shard_map/ppermute | solution.py:332
  73.4 4.8 %collective-permute-start.20 = (bf16[32,4864]{1,0:T(8,128)(2,1)S(1)}, bf16[32,4864]{1,0:T(8,128)(2,1)S(1)}, u32[]{:S(2)}, u32[]{:S(2)}) collective-permute-start(bf16[32,4864]{1,0:T(8,128)(2,1)S(1)} %get-tuple-element.153.refs_4_), channel_id=1, source_target_pairs={{0,4},{4,0},{8,12},{12,8},{16,20},{20,16},{24,28},{28,24},{1,5},{5... | collective-permute-start | bytes 933896 | tf_op jit(solution)/shard_map/ppermute | solution.py:332
  74.0 5.3 %collective-permute-start.21 = (bf16[32,4864]{1,0:T(8,128)(2,1)S(1)}, bf16[32,4864]{1,0:T(8,128)(2,1)S(1)}, u32[]{:S(2)}, u32[]{:S(2)}) collective-permute-start(bf16[32,4864]{1,0:T(8,128)(2,1)S(1)} %collective-permute-done.12.refs_5_), channel_id=1, source_target_pairs={{0,4},{4,0},{8,12},{12,8},{16,20},{20,16},{24,28},{28,24},{1,5},{5... | collective-permute-start | bytes 933896 | tf_op jit(solution)/shard_map/ppermute | solution.py:332
  74.0 8.8 %collective-permute-start.22 = (bf16[32,4864]{1,0:T(8,128)(2,1)S(1)}, bf16[32,4864]{1,0:T(8,128)(2,1)S(1)}, u32[]{:S(2)}, u32[]{:S(2)}) collective-permute-start(bf16[32,4864]{1,0:T(8,128)(2,1)S(1)} %collective-permute-done.13.refs_6_), channel_id=1, source_target_pairs={{0,4},{4,0},{8,12},{12,8},{16,20},{20,16},{24,28},{28,24},{1,5},{5... | collective-permute-start | bytes 933896 | tf_op jit(solution)/shard_map/ppermute | solution.py:332
  76.5 7.9 %copy-start.6 = (bf16[32,4864]{1,0:T(8,128)(2,1)}, bf16[32,4864]{1,0:T(8,128)(2,1)S(1)}, u32[]{:S(2)}) copy-start(bf16[32,4864]{1,0:T(8,128)(2,1)S(1)} %get-tuple-element.172.refs_4_) | copy-start | bytes 933892
  76.5 26.3 %collective-permute-start.17 = (bf16[64,4864]{1,0:T(8,128)(2,1)}, bf16[64,4864]{1,0:T(8,128)(2,1)}, u32[]{:S(2)}, u32[]{:S(2)}) collective-permute-start(bf16[64,4864]{1,0:T(8,128)(2,1)} %get-tuple-element.158), channel_id=1, source_target_pairs={{0,1},{1,0},{2,3},{3,2},{4,5},{5,4},{6,7},{7,6},{8,9},{9,8},{10,11... | collective-permute-start | bytes 1867784 | tf_op jit(solution)/shard_map/ppermute | solution.py:326
  78.2 6.2 %copy-start.22 = (bf16[32,4864]{1,0:T(8,128)(2,1)}, bf16[32,4864]{1,0:T(8,128)(2,1)S(1)}, u32[]{:S(2)}) copy-start(bf16[32,4864]{1,0:T(8,128)(2,1)S(1)} %collective-permute-done.20.refs_8_) | copy-start | bytes 933892
  78.2 24.6 %collective-permute-start.18 = (bf16[64,4864]{1,0:T(8,128)(2,1)}, bf16[64,4864]{1,0:T(8,128)(2,1)}, u32[]{:S(2)}, u32[]{:S(2)}) collective-permute-start(bf16[64,4864]{1,0:T(8,128)(2,1)} %get-tuple-element.159), channel_id=1, source_target_pairs={{0,2},{1,3},{2,0},{3,1},{4,6},{5,7},{6,4},{7,5},{8,10},{9,11},{10,... | collective-permute-start | bytes 1867784 | tf_op jit(solution)/shard_map/ppermute | solution.py:326
  79.3 5.2 %copy-start.23 = (bf16[32,4864]{1,0:T(8,128)(2,1)}, bf16[32,4864]{1,0:T(8,128)(2,1)S(1)}, u32[]{:S(2)}) copy-start(bf16[32,4864]{1,0:T(8,128)(2,1)S(1)} %collective-permute-done.21.refs_9_) | copy-start | bytes 933892
  79.3 24.3 %collective-permute-start.16 = (bf16[64,4864]{1,0:T(8,128)(2,1)}, bf16[64,4864]{1,0:T(8,128)(2,1)S(1)}, u32[]{:S(2)}, u32[]{:S(2)}) collective-permute-start(bf16[64,4864]{1,0:T(8,128)(2,1)} %pad_maximum_fusion.2), channel_id=1, source_target_pairs={{0,8},{4,12},{8,0},{12,4},{16,24},{20,28},{24,16},{28,20},{1,9},{5... | collective-permute-start | bytes 1867784 | tf_op jit(solution)/shard_map/ppermute | solution.py:329
  82.7 1.8 %copy-start.24 = (bf16[32,4864]{1,0:T(8,128)(2,1)}, bf16[32,4864]{1,0:T(8,128)(2,1)S(1)}, u32[]{:S(2)}) copy-start(bf16[32,4864]{1,0:T(8,128)(2,1)S(1)} %collective-permute-done.22.refs_10_) | copy-start | bytes 933892
  82.7 19.6 %collective-permute-start.19 = (bf16[32,4864]{1,0:T(8,128)(2,1)}, bf16[32,4864]{1,0:T(8,128)(2,1)S(1)}, u32[]{:S(2)}, u32[]{:S(2)}) collective-permute-start(bf16[32,4864]{1,0:T(8,128)(2,1)} %get-tuple-element.160), channel_id=1, source_target_pairs={{0,3},{1,2},{2,1},{3,0},{4,7},{5,6},{6,5},{7,4},{8,11},{9,10},{10,... | collective-permute-start | bytes 933896 | tf_op jit(solution)/shard_map/ppermute | solution.py:326
  84.5 0.9 copy-start.13
  85.4 17.5 %collective-permute-start.15 = (bf16[32,4864]{1,0:T(8,128)(2,1)S(1)}, bf16[32,4864]{1,0:T(8,128)(2,1)}, u32[]{:S(2)}, u32[]{:S(2)}) collective-permute-start(bf16[32,4864]{1,0:T(8,128)(2,1)S(1)} %copy-done), channel_id=1, source_target_pairs={{0,16},{4,20},{8,24},{12,28},{16,0},{20,4},{24,8},{28,12},{1,17},{... | collective-permute-start | bytes 933896 | tf_op jit(solution)/shard_map/ppermute | solution.py:329
  86.2 17.9 %copy-start.7 = (bf16[32,4864]{1,0:T(8,128)(2,1)S(1)}, bf16[32,4864]{1,0:T(8,128)(2,1)}, u32[]{:S(2)}) copy-start(bf16[32,4864]{1,0:T(8,128)(2,1)} %copy-done.6) | copy-start | bytes 933892
  102.3 9.4 %copy-start.5 = (bf16[32,4864]{1,0:T(8,128)(2,1)S(1)}, bf16[32,4864]{1,0:T(8,128)(2,1)}, u32[]{:S(2)}) copy-start(bf16[32,4864]{1,0:T(8,128)(2,1)} %copy-done.4) | copy-start | bytes 933892
  102.3 9.4 %copy-start.10 = (s32[12]{0:T(128)S(1)}, s32[12]{0:T(128)}, u32[]{:S(2)}) copy-start(s32[12]{0:T(128)} %concatenate.13.place_ref) | copy-start | bytes 148
  103.6 5.3 %collective-permute-start.29 = (bf16[64,4864]{1,0:T(8,128)(2,1)}, bf16[64,4864]{1,0:T(8,128)(2,1)S(1)}, u32[]{:S(2)}, u32[]{:S(2)}) collective-permute-start(bf16[64,4864]{1,0:T(8,128)(2,1)} %collective-permute-done.17.refs_5_.refs_1_), channel_id=1, source_target_pairs={{0,4},{4,0},{8,12},{12,8},{16,20},{20,16},{24,28},{28,24},{1,5},{5... | collective-permute-start | bytes 1867784 | tf_op jit(solution)/shard_map/ppermute | solution.py:332
  103.6 7.2 %collective-permute-start.30 = (bf16[64,4864]{1,0:T(8,128)(2,1)}, bf16[64,4864]{1,0:T(8,128)(2,1)S(1)}, u32[]{:S(2)}, u32[]{:S(2)}) collective-permute-start(bf16[64,4864]{1,0:T(8,128)(2,1)} %collective-permute-done.18.refs_6_.refs_2_), channel_id=1, source_target_pairs={{0,4},{4,0},{8,12},{12,8},{16,20},{20,16},{24,28},{28,24},{1,5},{5... | collective-permute-start | bytes 1867784 | tf_op jit(solution)/shard_map/ppermute | solution.py:332
  104.1 2.8 %collective-permute-start.28 = (bf16[32,4864]{1,0:T(8,128)(2,1)S(1)}, bf16[32,4864]{1,0:T(8,128)(2,1)S(1)}, u32[]{:S(2)}, u32[]{:S(2)}) collective-permute-start(bf16[32,4864]{1,0:T(8,128)(2,1)S(1)} %copy-done.7), channel_id=1, source_target_pairs={{0,4},{4,0},{8,12},{12,8},{16,20},{20,16},{24,28},{28,24},{1,5},{5... | collective-permute-start | bytes 933896 | tf_op jit(solution)/shard_map/ppermute | solution.py:332
  104.1 4.1 %collective-permute-start.31 = (bf16[32,4864]{1,0:T(8,128)(2,1)S(1)}, bf16[32,4864]{1,0:T(8,128)(2,1)S(1)}, u32[]{:S(2)}, u32[]{:S(2)}) collective-permute-start(bf16[32,4864]{1,0:T(8,128)(2,1)S(1)} %collective-permute-done.19.refs_7_), channel_id=1, source_target_pairs={{0,4},{4,0},{8,12},{12,8},{16,20},{20,16},{24,28},{28,24},{1,5},{5... | collective-permute-start | bytes 933896 | tf_op jit(solution)/shard_map/ppermute | solution.py:332
  105.4 23.6 %collective-permute-start.27 = (bf16[64,4864]{1,0:T(8,128)(2,1)S(1)}, bf16[64,4864]{1,0:T(8,128)(2,1)S(1)}, u32[]{:S(2)}, u32[]{:S(2)}) collective-permute-start(bf16[64,4864]{1,0:T(8,128)(2,1)S(1)} %get-tuple-element.179), channel_id=1, source_target_pairs={{0,3},{1,2},{2,1},{3,0},{4,7},{5,6},{6,5},{7,4},{8,11},{9,10},{10,... | collective-permute-start | bytes 1867784 | tf_op jit(solution)/shard_map/ppermute | solution.py:326
  107.0 21.2 %collective-permute-start.25 = (bf16[32,4864]{1,0:T(8,128)(2,1)S(1)}, bf16[32,4864]{1,0:T(8,128)(2,1)S(1)}, u32[]{:S(2)}, u32[]{:S(2)}) collective-permute-start(bf16[32,4864]{1,0:T(8,128)(2,1)S(1)} %get-tuple-element.177), channel_id=1, source_target_pairs={{0,1},{1,0},{2,3},{3,2},{4,5},{5,4},{6,7},{7,6},{8,9},{9,8},{10,11... | collective-permute-start | bytes 933896 | tf_op jit(solution)/shard_map/ppermute | solution.py:326
  108.2 20.7 %collective-permute-start.26 = (bf16[32,4864]{1,0:T(8,128)(2,1)S(1)}, bf16[32,4864]{1,0:T(8,128)(2,1)S(1)}, u32[]{:S(2)}, u32[]{:S(2)}) collective-permute-start(bf16[32,4864]{1,0:T(8,128)(2,1)S(1)} %get-tuple-element.178), channel_id=1, source_target_pairs={{0,2},{1,3},{2,0},{3,1},{4,6},{5,7},{6,4},{7,5},{8,10},{9,11},{10,... | collective-permute-start | bytes 933896 | tf_op jit(solution)/shard_map/ppermute | solution.py:326
  108.9 1.8 %copy-start.15 = (bf16[64,4864]{1,0:T(8,128)(2,1)}, bf16[64,4864]{1,0:T(8,128)(2,1)S(1)}, u32[]{:S(2)}) copy-start(bf16[64,4864]{1,0:T(8,128)(2,1)S(1)} %collective-permute-done.29.refs_9_) | copy-start | bytes 1867780
  108.9 20.0 %collective-permute-start.24 = (bf16[32,4864]{1,0:T(8,128)(2,1)}, bf16[32,4864]{1,0:T(8,128)(2,1)S(1)}, u32[]{:S(2)}, u32[]{:S(2)}) collective-permute-start(bf16[32,4864]{1,0:T(8,128)(2,1)} %collective-permute-done.15.refs_2_), channel_id=1, source_target_pairs={{0,8},{4,12},{8,0},{12,4},{16,24},{20,28},{24,16},{28,20},{1,9},{5... | collective-permute-start | bytes 933896 | tf_op jit(solution)/shard_map/ppermute | solution.py:329
  110.8 0.9 copy-start.16
  129.0 6.1 %copy-start.11 = (bf16[64,4864]{1,0:T(8,128)(2,1)}, bf16[64,4864]{1,0:T(8,128)(2,1)S(1)}, u32[]{:S(2)}) copy-start(bf16[64,4864]{1,0:T(8,128)(2,1)S(1)} %collective-permute-done.27.refs_7_.refs_3_) | copy-start | bytes 1867780
  129.0 6.1 %collective-permute-start.38 = (bf16[64,4864]{1,0:T(8,128)(2,1)S(1)}, bf16[64,4864]{1,0:T(8,128)(2,1)S(1)}, u32[]{:S(2)}, u32[]{:S(2)}) collective-permute-start(bf16[64,4864]{1,0:T(8,128)(2,1)S(1)} %collective-permute-done.27.refs_7_.refs_3_), channel_id=1, source_target_pairs={{0,4},{4,0},{8,12},{12,8},{16,20},{20,16},{24,28},{28,24},{1,5},{5... | collective-permute-start | bytes 1867784 | tf_op jit(solution)/shard_map/ppermute | solution.py:332
  129.0 4.2 %collective-permute-start.35 = (bf16[32,4864]{1,0:T(8,128)(2,1)S(1)}, bf16[32,4864]{1,0:T(8,128)(2,1)S(1)}, u32[]{:S(2)}, u32[]{:S(2)}) collective-permute-start(bf16[32,4864]{1,0:T(8,128)(2,1)S(1)} %get-tuple-element.191.refs_4_), channel_id=1, source_target_pairs={{0,4},{4,0},{8,12},{12,8},{16,20},{20,16},{24,28},{28,24},{1,5},{5... | collective-permute-start | bytes 933896 | tf_op jit(solution)/shard_map/ppermute | solution.py:332
  129.5 4.3 %collective-permute-start.36 = (bf16[32,4864]{1,0:T(8,128)(2,1)S(1)}, bf16[32,4864]{1,0:T(8,128)(2,1)S(1)}, u32[]{:S(2)}, u32[]{:S(2)}) collective-permute-start(bf16[32,4864]{1,0:T(8,128)(2,1)S(1)} %collective-permute-done.25.refs_5_), channel_id=1, source_target_pairs={{0,4},{4,0},{8,12},{12,8},{16,20},{20,16},{24,28},{28,24},{1,5},{5... | collective-permute-start | bytes 933896 | tf_op jit(solution)/shard_map/ppermute | solution.py:332
  129.6 5.4 %collective-permute-start.37 = (bf16[32,4864]{1,0:T(8,128)(2,1)S(1)}, bf16[32,4864]{1,0:T(8,128)(2,1)S(1)}, u32[]{:S(2)}, u32[]{:S(2)}) collective-permute-start(bf16[32,4864]{1,0:T(8,128)(2,1)S(1)} %collective-permute-done.26.refs_6_), channel_id=1, source_target_pairs={{0,4},{4,0},{8,12},{12,8},{16,20},{20,16},{24,28},{28,24},{1,5},{5... | collective-permute-start | bytes 933896 | tf_op jit(solution)/shard_map/ppermute | solution.py:332
  131.4 20.9 %collective-permute-start.32 = (bf16[32,4864]{1,0:T(8,128)(2,1)S(1)}, bf16[32,4864]{1,0:T(8,128)(2,1)S(1)}, u32[]{:S(2)}, u32[]{:S(2)}) collective-permute-start(bf16[32,4864]{1,0:T(8,128)(2,1)S(1)} %get-tuple-element.196), channel_id=1, source_target_pairs={{0,1},{1,0},{2,3},{3,2},{4,5},{5,4},{6,7},{7,6},{8,9},{9,8},{10,11... | collective-permute-start | bytes 933896 | tf_op jit(solution)/shard_map/ppermute | solution.py:326
  133.2 19.1 %collective-permute-start.33 = (bf16[32,4864]{1,0:T(8,128)(2,1)S(1)}, bf16[32,4864]{1,0:T(8,128)(2,1)S(1)}, u32[]{:S(2)}, u32[]{:S(2)}) collective-permute-start(bf16[32,4864]{1,0:T(8,128)(2,1)S(1)} %get-tuple-element.197), channel_id=1, source_target_pairs={{0,2},{1,3},{2,0},{3,1},{4,6},{5,7},{6,4},{7,5},{8,10},{9,11},{10,... | collective-permute-start | bytes 933896 | tf_op jit(solution)/shard_map/ppermute | solution.py:326
  133.8 21.5 %copy-start.9 = (s32[128,256]{1,0:T(8,128)S(1)}, s32[128,256]{1,0:T(8,128)}, u32[]{:S(2)}) copy-start(s32[128,256]{1,0:T(8,128)} %refs_13_.1) | copy-start | bytes 393220
  133.8 18.5 %collective-permute-start.34 = (bf16[32,4864]{1,0:T(8,128)(2,1)S(1)}, bf16[32,4864]{1,0:T(8,128)(2,1)S(1)}, u32[]{:S(2)}, u32[]{:S(2)}) collective-permute-start(bf16[32,4864]{1,0:T(8,128)(2,1)S(1)} %get-tuple-element.198), channel_id=1, source_target_pairs={{0,3},{1,2},{2,1},{3,0},{4,7},{5,6},{6,5},{7,4},{8,11},{9,10},{10,... | collective-permute-start | bytes 933896 | tf_op jit(solution)/shard_map/ppermute | solution.py:326
  152.3 1.7 collective-permute-start.39
  152.4 2.0 %collective-permute-start.40 = (bf16[32,4864]{1,0:T(8,128)(2,1)S(1)}, bf16[32,4864]{1,0:T(8,128)(2,1)S(1)}, u32[]{:S(2)}, u32[]{:S(2)}) collective-permute-start(bf16[32,4864]{1,0:T(8,128)(2,1)S(1)} %collective-permute-done.32.refs_5_), channel_id=1, source_target_pairs={{0,4},{4,0},{8,12},{12,8},{16,20},{20,16},{24,28},{28,24},{1,5},{5... | collective-permute-start | bytes 933896 | tf_op jit(solution)/shard_map/ppermute | solution.py:332
  152.9 2.0 %collective-permute-start.41 = (bf16[32,4864]{1,0:T(8,128)(2,1)S(1)}, bf16[32,4864]{1,0:T(8,128)(2,1)S(1)}, u32[]{:S(2)}, u32[]{:S(2)}) collective-permute-start(bf16[32,4864]{1,0:T(8,128)(2,1)S(1)} %collective-permute-done.33.refs_6_), channel_id=1, source_target_pairs={{0,4},{4,0},{8,12},{12,8},{16,20},{20,16},{24,28},{28,24},{1,5},{5... | collective-permute-start | bytes 933896 | tf_op jit(solution)/shard_map/ppermute | solution.py:332
  153.0 2.4 %collective-permute-start.42 = (bf16[32,4864]{1,0:T(8,128)(2,1)S(1)}, bf16[32,4864]{1,0:T(8,128)(2,1)S(1)}, u32[]{:S(2)}, u32[]{:S(2)}) collective-permute-start(bf16[32,4864]{1,0:T(8,128)(2,1)S(1)} %collective-permute-done.34.refs_7_), channel_id=1, source_target_pairs={{0,4},{4,0},{8,12},{12,8},{16,20},{20,16},{24,28},{28,24},{1,5},{5... | collective-permute-start | bytes 933896 | tf_op jit(solution)/shard_map/ppermute | solution.py:332
  (4 other events, 3.1 us)

commit v6 on v5

--- a/solution.py
+++ b/solution.py
@@ -304,7 +304,7 @@
         out_shape=jax.ShapeDtypeStruct(out_shape, jnp.float32 if last else jnp.bfloat16),
         input_output_aliases=aliases,
         scratch_shapes=scratch,
-        compiler_params=pltpu.CompilerParams(vmem_limit_bytes=(58 if total is None else 51) << 20),
+        compiler_params=pltpu.CompilerParams(vmem_limit_bytes=(53 if total is None else 51) << 20),
         name="correlate",
     )(*operands)
 
@@ -348,6 +348,7 @@
 
     state = {("unit", u): unit for u, unit in enumerate(units)}
     state["middle"], state["late"] = middle, late
+    state["place"], state["route_place"] = place, route_place
     lines = [{0: (("unit", u), 0)} for u in range(count)]
 
     def fence():
@@ -381,7 +382,7 @@
     def columns(u, extra, longer):
         parts = [(state[lines[u][k][0]], lines[u][k][1]) for k in range(seg_count)]
         more = state["unit", extra] if longer else None
-        for k, piece in enumerate(route(route_place, parts, rows, more, longer)):
+        for k, piece in enumerate(route(state["route_place"], parts, rows, more, longer)):
             state["own", u, k] = to_seg(piece, k) if k else piece
             if k in longer:
                 rows_of[extra][k] = ("own", u, k), (rows, 0)
@@ -405,7 +406,7 @@
         own = [state["own", u, k] for k in range(seg_count)]
         right = own + [to_side(v, j) for j in range(1, sides) for v in own]
         state["total"] = correlate(
-            place,
+            state["place"],
             [state[name] for name, _ in parts],
             [begin for _, begin in parts],
             right,

time: 173 us -> 168 us (0.971)
  local copies, waits for them, and re-layouts: 4.8 us -> 1.91 us
  waiting for transfers between devices: 41.5 us -> 44.1 us
  Pallas kernels: 83 us -> 81.2 us
    unnamed x50 -> x42, local copies, waits for them, and re-layouts: 4.18 us -> 1.82 us
  transfers between devices with their start and end apart: 43 -> 43, of which waited for: 17 -> 19; matrix products, arithmetic and copies ran while one was open for 1% -> 0% of each run, Pallas kernels for 36% -> 35%
where the time goes in v6:
time: 168 us
  Pallas kernels  81.2 us (48%)
  waiting for transfers between devices  44.1 us (26%)
  starting transfers between devices  39.1 us (23%)
  local copies, waits for them, and re-layouts  1.91 us (1%)
    pallas_call x4, Pallas kernels, correlate(): pl.pallas_call(functools.partial(correlate_kernel, begins, left_rows, pie...  65.7 us
    ppermute x18, waiting for transfers between devices, to_seg(): return lax.ppermute(value, 'seg', [(i, i ^ k) for i in range(seg_count)])  22.3 us
    ppermute x18, starting transfers between devices, to_seg(): return lax.ppermute(value, 'seg', [(i, i ^ k) for i in range(seg_count)])  20.2 us
    ppermute x9, waiting for transfers between devices, to_plane(): lax.ppermute(value, 'stn', [(i, i ^ k * sides) for i in range(stn_count)])  19.5 us
    ppermute x9, starting transfers between devices, to_plane(): lax.ppermute(value, 'stn', [(i, i ^ k * sides) for i in range(stn_count)])  14.7 us
    pallas_call x2, Pallas kernels, whiten(): pl.pallas_call(functools.partial(whiten_kernel, record_len // LANES, firs...  12.1 us
    ppermute x16, starting transfers between devices, to_side(): return lax.ppermute(value, 'stn', [(i, i ^ j) for i in range(stn_count)])  4.2 us
    pallas_call x4, Pallas kernels, route(): pl.pallas_call(functools.partial(route_kernel, len(parts)), grid=(1,), in...  3.39 us
  transfers between devices with their start and end apart: 43, of which 19 were waited for; matrix products, arithmetic and copies ran while one was open for 0% of the time, Pallas kernels for 35%

profile of v6, /device:TPU:0, one launch (start us, length us, event | category | flops | bytes accessed | tf_op | source)
XLA Modules:
  0.0 168.0 jit_solution(11961253933908090366)
XLA Ops:
  0.0 3.9 %whiten.2.refs_0_ = bf16[32,4864]{1,0:T(8,128)(2,1)} custom-call(f32[31]{0:T(128)} %taps_ref.3, f32[32,19200]{1,0:T(8,128)} %traces_ref.3, s32[32,32]{1,0:T(8,128)} %flags_ref.3), custom_call_target="tpu_custom_call" | custom-call | tf_op jit(solution)/shard_map/whiten/pallas_call | solution.py:127
  3.9 4.0 %collective-permute-start = (bf16[32,4864]{1,0:T(8,128)(2,1)}, bf16[32,4864]{1,0:T(8,128)(2,1)S(1)}, u32[]{:S(2)}, u32[]{:S(2)}) collective-permute-start(bf16[32,4864]{1,0:T(8,128)(2,1)} %whiten.2.refs_0_), channel_id=1, source_target_pairs={{0,16},{4,20},{8,24},{12,28},{16,0},{20,4},{24,8},{28,12},{1,17},{... | collective-permute-start | bytes 933896 | tf_op jit(solution)/shard_map/ppermute | solution.py:329
  8.0 1.6 collective-permute-start.1
  9.6 1.5 collective-permute-start.2
  11.0 1.5 collective-permute-start.3
  12.6 0.5 collective-permute-start.4
  13.0 8.2 %whiten.3 = (bf16[32,4864]{1,0:T(8,128)(2,1)}, bf16[32,4864]{1,0:T(8,128)(2,1)}, bf16[32,4864]{1,0:T(8,128)(2,1)}, bf16[32,9728]{1,0:T(8,128)(2,1)}, bf16[32,9728]{1,0:T(8,128)(2,1)}) custom-call(f32[31]{0:T(128)} %taps_ref.3, f32[32,19200]{1,0:T(8,128)} %traces_ref.3, s32[32,32]{1,0:T(8,128)} %flags_ref.3), custom_call_target="tpu_custom_call" | custom-call | tf_op jit(solution)/shard_map/whiten/pallas_call | solution.py:127
  21.4 0.9 collective-permute-done.refs_2_
  22.5 3.7 %collective-permute-done.3.refs_2_ = bf16[32,4864]{1,0:T(8,128)(2,1)S(1)} collective-permute-done((bf16[32,4864]{1,0:T(8,128)(2,1)}, bf16[32,4864]{1,0:T(8,128)(2,1)S(1)}, u32[]{:S(2)}, u32[]{:S(2)}) %collective-permute-start.3) | collective-permute-done | bytes 311328 | tf_op jit(solution)/shard_map/ppermute | solution.py:326
  26.2 1.1 pad_maximum_fusion
  27.3 0.5 collective-permute-start.6
  27.8 1.2 collective-permute-start.7
  29.1 0.8 collective-permute-start.8
  29.9 0.7 collective-permute-start.5
  30.6 1.1 collective-permute-start.9
  31.7 14.4 %collective-permute-done.5.refs_2_ = bf16[32,4864]{1,0:T(8,128)(2,1)S(1)} collective-permute-done((bf16[32,4864]{1,0:T(8,128)(2,1)S(1)}, bf16[32,4864]{1,0:T(8,128)(2,1)S(1)}, u32[]{:S(2)}, u32[]{:S(2)}) %collective-permute-start.5) | collective-permute-done | bytes 311328 | tf_op jit(solution)/shard_map/ppermute | solution.py:329
  46.1 2.5 %collective-permute-done.9.refs_3_ = bf16[32,4864]{1,0:T(8,128)(2,1)S(1)} collective-permute-done((bf16[32,4864]{1,0:T(8,128)(2,1)S(1)}, bf16[32,4864]{1,0:T(8,128)(2,1)S(1)}, u32[]{:S(2)}, u32[]{:S(2)}) %collective-permute-start.9) | collective-permute-done | bytes 311328 | tf_op jit(solution)/shard_map/ppermute | solution.py:326
  48.6 1.1 collective-permute-done.8.refs_2_
  49.7 0.8 route.4
  50.5 1.3 collective-permute-start.14
  51.8 1.6 collective-permute-start.11
  53.4 0.8 collective-permute-start.12
  54.2 1.5 collective-permute-start.13
  55.7 0.4 collective-permute-start.10
  56.1 13.8 %collective-permute-done.12.refs_5_ = bf16[32,4864]{1,0:T(8,128)(2,1)S(1)} collective-permute-done((bf16[32,4864]{1,0:T(8,128)(2,1)S(1)}, bf16[32,4864]{1,0:T(8,128)(2,1)S(1)}, u32[]{:S(2)}, u32[]{:S(2)}) %collective-permute-start.12) | collective-permute-done | bytes 311328 | tf_op jit(solution)/shard_map/ppermute | solution.py:326
  70.0 0.5 collective-permute-done.10.refs_2_
  70.4 0.9 collective-permute-done.11.refs_3_.refs_1_
  71.3 0.5 collective-permute-start.20
  71.9 0.5 collective-permute-start.22
  72.4 0.9 route.5
  73.3 1.1 collective-permute-start.17
  74.5 0.7 collective-permute-start.18
  75.3 3.5 %collective-permute-start.16 = (bf16[64,4864]{1,0:T(8,128)(2,1)S(1)}, bf16[64,4864]{1,0:T(8,128)(2,1)S(1)}, u32[]{:S(2)}, u32[]{:S(2)}) collective-permute-start(bf16[64,4864]{1,0:T(8,128)(2,1)S(1)} %pad_maximum_fusion.2), channel_id=1, source_target_pairs={{0,8},{4,12},{8,0},{12,4},{16,24},{20,28},{24,16},{28,20},{1,9},{5... | collective-permute-start | bytes 1867784 | tf_op jit(solution)/shard_map/ppermute | solution.py:329
  78.8 1.4 collective-permute-start.19
  80.2 0.8 collective-permute-start.15
  81.0 15.8 %correlate.4.refs_12_ = bf16[3,21,128,256]{3,2,1,0:T(8,128)(2,1)} custom-call(s32[12]{0:T(128)S(1)} %concatenate.13.place_ref, bf16[32,4864]{1,0:T(8,128)(2,1)S(1)} %copy-done.3, bf16[32,4864]{1,0:T(8,128)(2,1)S(1)} %collective-permute-done.2.refs_1_, bf16[32,4864]{1,0:T(8,128)(2,1)S(1)} %collective-permute-done.3.refs_2_, bf16[32,4864]{1,0:T(8,128)(2,1)} %copy-done.15, ...), custom_call_target="tpu_custom_call" | custom-call | tf_op jit(solution)/shard_map/correlate/pallas_call | solution.py:297
  96.9 1.9 %collective-permute-done.15.refs_2_ = bf16[32,4864]{1,0:T(8,128)(2,1)S(1)} collective-permute-done((bf16[32,4864]{1,0:T(8,128)(2,1)S(1)}, bf16[32,4864]{1,0:T(8,128)(2,1)S(1)}, u32[]{:S(2)}, u32[]{:S(2)}) %collective-permute-start.15) | collective-permute-done | bytes 311328 | tf_op jit(solution)/shard_map/ppermute | solution.py:329
  98.8 0.7 collective-permute-done.16.refs_3_.refs_1_
  99.5 0.5 collective-permute-start.30
  100.0 0.5 collective-permute-start.31
  100.5 0.8 route.6
  101.3 1.3 collective-permute-start.27
  102.9 1.4 collective-permute-start.25
  104.3 0.6 collective-permute-start.26
  104.9 1.5 collective-permute-start.24
  106.4 0.8 copy-done.14
  107.3 16.4 %correlate.5.refs_12_ = bf16[3,21,128,256]{3,2,1,0:T(8,128)(2,1)} custom-call(s32[12]{0:T(128)S(1)} %concatenate.13.place_ref, bf16[32,4864]{1,0:T(8,128)(2,1)S(1)} %copy-done.2, bf16[32,9728]{1,0:T(8,128)(2,1)S(1)} %collective-permute-done.7.refs_1_, bf16[32,9728]{1,0:T(8,128)(2,1)} %copy-done.10, ...), custom_call_target="tpu_custom_call", output_to_operand_aliasing={{}: (13, {})} | custom-call | tf_op jit(solution)/shard_map/correlate/pallas_call | solution.py:297
  123.7 0.5 collective-permute-done.25.refs_5_
  124.2 0.7 collective-permute-done.26.refs_6_
  125.0 0.5 collective-permute-start.35
  125.5 0.4 collective-permute-start.37
  126.0 1.0 route.7
  126.9 1.5 collective-permute-start.32
  128.4 0.6 collective-permute-start.33
  129.0 1.5 collective-permute-start.34
  130.5 0.8 copy-done.12
  131.3 16.4 %correlate.6.refs_12_ = bf16[3,21,128,256]{3,2,1,0:T(8,128)(2,1)} custom-call(s32[12]{0:T(128)S(1)} %concatenate.13.place_ref, bf16[32,4864]{1,0:T(8,128)(2,1)S(1)} %copy-done.1, bf16[32,9728]{1,0:T(8,128)(2,1)S(1)} %collective-permute-done.7.refs_1_, bf16[32,9728]{1,0:T(8,128)(2,1)} %copy-done.10, ...), custom_call_target="tpu_custom_call", output_to_operand_aliasing={{}: (13, {})} | custom-call | tf_op jit(solution)/shard_map/correlate/pallas_call | solution.py:297
  147.9 0.5 collective-permute-start.40
  148.5 0.4 collective-permute-start.42
  148.9 0.6 collective-permute-done.39.refs_8_
  149.5 0.4 collective-permute-done.40.refs_9_
  149.9 0.4 collective-permute-done.41.refs_10_
  150.4 0.4 collective-permute-done.42.refs_11_
  150.8 17.0 %correlate.7 = f32[41,128,256]{2,1,0:T(8,128)} custom-call(s32[12]{0:T(128)S(1)} %concatenate.13.place_ref, bf16[32,4864]{1,0:T(8,128)(2,1)S(1)} %copy-done, bf16[64,4864]{1,0:T(8,128)(2,1)} %copy-done.6, bf16[64,4864]{1,0:T(8,128)(2,1)} %copy-done.7, bf16[64,4864]{1,0:T(8,128)(2,1)} %copy-done.8, bf16[32,4864]{1,0:T(8,128)(2,1)S(1)} %get-tuple-element.226.refs_4_, ...), custom_call_target="tpu_custom_call" | custom-call | tf_op jit(solution)/shard_map/correlate/pallas_call | solution.py:297
  (80 shorter events, 1.4 us)
Async XLA Ops:
  3.9 18.4 %collective-permute-start = (bf16[32,4864]{1,0:T(8,128)(2,1)}, bf16[32,4864]{1,0:T(8,128)(2,1)S(1)}, u32[]{:S(2)}, u32[]{:S(2)}) collective-permute-start(bf16[32,4864]{1,0:T(8,128)(2,1)} %whiten.2.refs_0_), channel_id=1, source_target_pairs={{0,16},{4,20},{8,24},{12,28},{16,0},{20,4},{24,8},{28,12},{1,17},{... | collective-permute-start | bytes 933896 | tf_op jit(solution)/shard_map/ppermute | solution.py:329
  8.0 14.5 %collective-permute-start.1 = (bf16[32,4864]{1,0:T(8,128)(2,1)}, bf16[32,4864]{1,0:T(8,128)(2,1)S(1)}, u32[]{:S(2)}, u32[]{:S(2)}) collective-permute-start(bf16[32,4864]{1,0:T(8,128)(2,1)} %whiten.2.refs_0_), channel_id=1, source_target_pairs={{0,8},{4,12},{8,0},{12,4},{16,24},{20,28},{24,16},{28,20},{1,9},{5... | collective-permute-start | bytes 933896 | tf_op jit(solution)/shard_map/ppermute | solution.py:329
  9.6 13.0 %collective-permute-start.2 = (bf16[32,4864]{1,0:T(8,128)(2,1)}, bf16[32,4864]{1,0:T(8,128)(2,1)S(1)}, u32[]{:S(2)}, u32[]{:S(2)}) collective-permute-start(bf16[32,4864]{1,0:T(8,128)(2,1)} %whiten.2.refs_0_), channel_id=1, source_target_pairs={{0,1},{1,0},{2,3},{3,2},{4,5},{5,4},{6,7},{7,6},{8,9},{9,8},{10,11... | collective-permute-start | bytes 933896 | tf_op jit(solution)/shard_map/ppermute | solution.py:326
  11.0 15.1 %collective-permute-start.3 = (bf16[32,4864]{1,0:T(8,128)(2,1)}, bf16[32,4864]{1,0:T(8,128)(2,1)S(1)}, u32[]{:S(2)}, u32[]{:S(2)}) collective-permute-start(bf16[32,4864]{1,0:T(8,128)(2,1)} %whiten.2.refs_0_), channel_id=1, source_target_pairs={{0,2},{1,3},{2,0},{3,1},{4,6},{5,7},{6,4},{7,5},{8,10},{9,11},{10,... | collective-permute-start | bytes 933896 | tf_op jit(solution)/shard_map/ppermute | solution.py:326
  12.6 13.6 %collective-permute-start.4 = (bf16[32,4864]{1,0:T(8,128)(2,1)}, bf16[32,4864]{1,0:T(8,128)(2,1)S(1)}, u32[]{:S(2)}, u32[]{:S(2)}) collective-permute-start(bf16[32,4864]{1,0:T(8,128)(2,1)} %whiten.2.refs_0_), channel_id=1, source_target_pairs={{0,3},{1,2},{2,1},{3,0},{4,7},{5,6},{6,5},{7,4},{8,11},{9,10},{10,... | collective-permute-start | bytes 933896 | tf_op jit(solution)/shard_map/ppermute | solution.py:326
  21.2 8.7 %copy-start.2 = (bf16[32,4864]{1,0:T(8,128)(2,1)S(1)}, bf16[32,4864]{1,0:T(8,128)(2,1)}, u32[]{:S(2)}) copy-start(bf16[32,4864]{1,0:T(8,128)(2,1)} %get-tuple-element.178.refs_0_) | copy-start | bytes 933892
  21.2 28.5 %copy-start.1 = (bf16[32,4864]{1,0:T(8,128)(2,1)S(1)}, bf16[32,4864]{1,0:T(8,128)(2,1)}, u32[]{:S(2)}) copy-start(bf16[32,4864]{1,0:T(8,128)(2,1)} %get-tuple-element.200.refs_4_.refs_0_) | copy-start | bytes 933892
  21.2 28.5 %copy-start.3 = (bf16[32,4864]{1,0:T(8,128)(2,1)S(1)}, bf16[32,4864]{1,0:T(8,128)(2,1)}, u32[]{:S(2)}) copy-start(bf16[32,4864]{1,0:T(8,128)(2,1)} %whiten.2.refs_0_) | copy-start | bytes 933892
  26.2 1.7 copy-start.15
  27.3 45.0 %copy-start = (bf16[32,4864]{1,0:T(8,128)(2,1)S(1)}, bf16[32,4864]{1,0:T(8,128)(2,1)}, u32[]{:S(2)}) copy-start(bf16[32,4864]{1,0:T(8,128)(2,1)} %get-tuple-element.222.refs_4_.refs_0_) | copy-start | bytes 933892
  27.3 21.2 %collective-permute-start.6 = (bf16[64,4864]{1,0:T(8,128)(2,1)S(1)}, bf16[64,4864]{1,0:T(8,128)(2,1)S(1)}, u32[]{:S(2)}, u32[]{:S(2)}) collective-permute-start(bf16[64,4864]{1,0:T(8,128)(2,1)S(1)} %pad_maximum_fusion), channel_id=1, source_target_pairs={{0,8},{4,12},{8,0},{12,4},{16,24},{20,28},{24,16},{28,20},{1,9},{5... | collective-permute-start | bytes 1867784 | tf_op jit(solution)/shard_map/ppermute | solution.py:329
  27.8 20.7 %collective-permute-start.7 = (bf16[32,9728]{1,0:T(8,128)(2,1)}, bf16[32,9728]{1,0:T(8,128)(2,1)S(1)}, u32[]{:S(2)}, u32[]{:S(2)}) collective-permute-start(bf16[32,9728]{1,0:T(8,128)(2,1)} %get-tuple-element.126), channel_id=1, source_target_pairs={{0,1},{1,0},{2,3},{3,2},{4,5},{5,4},{6,7},{7,6},{8,9},{9,8},{10,11... | collective-permute-start | bytes 1867784 | tf_op jit(solution)/shard_map/ppermute | solution.py:326
  29.1 20.6 %collective-permute-start.8 = (bf16[32,9728]{1,0:T(8,128)(2,1)}, bf16[32,9728]{1,0:T(8,128)(2,1)S(1)}, u32[]{:S(2)}, u32[]{:S(2)}) collective-permute-start(bf16[32,9728]{1,0:T(8,128)(2,1)} %get-tuple-element.126), channel_id=1, source_target_pairs={{0,2},{1,3},{2,0},{3,1},{4,6},{5,7},{6,4},{7,5},{8,10},{9,11},{10,... | collective-permute-start | bytes 1867784 | tf_op jit(solution)/shard_map/ppermute | solution.py:326
  29.9 16.2 %collective-permute-start.5 = (bf16[32,4864]{1,0:T(8,128)(2,1)S(1)}, bf16[32,4864]{1,0:T(8,128)(2,1)S(1)}, u32[]{:S(2)}, u32[]{:S(2)}) collective-permute-start(bf16[32,4864]{1,0:T(8,128)(2,1)S(1)} %copy-done.2), channel_id=1, source_target_pairs={{0,16},{4,20},{8,24},{12,28},{16,0},{20,4},{24,8},{28,12},{1,17},{... | collective-permute-start | bytes 933896 | tf_op jit(solution)/shard_map/ppermute | solution.py:329
  30.6 18.0 %collective-permute-start.9 = (bf16[32,4864]{1,0:T(8,128)(2,1)S(1)}, bf16[32,4864]{1,0:T(8,128)(2,1)S(1)}, u32[]{:S(2)}, u32[]{:S(2)}) collective-permute-start(bf16[32,4864]{1,0:T(8,128)(2,1)S(1)} %copy-done.2), channel_id=1, source_target_pairs={{0,3},{1,2},{2,1},{3,0},{4,7},{5,6},{6,5},{7,4},{8,11},{9,10},{10,... | collective-permute-start | bytes 933896 | tf_op jit(solution)/shard_map/ppermute | solution.py:326
  49.7 2.1 %copy-start.10 = (bf16[32,9728]{1,0:T(8,128)(2,1)}, bf16[32,9728]{1,0:T(8,128)(2,1)S(1)}, u32[]{:S(2)}) copy-start(bf16[32,9728]{1,0:T(8,128)(2,1)S(1)} %collective-permute-done.8.refs_2_) | copy-start | bytes 1867780
  50.5 22.9 %copy-start.4 = (bf16[32,4864]{1,0:T(8,128)(2,1)}, bf16[32,4864]{1,0:T(8,128)(2,1)S(1)}, u32[]{:S(2)}) copy-start(bf16[32,4864]{1,0:T(8,128)(2,1)S(1)} %get-tuple-element.170.refs_4_) | copy-start | bytes 933892
  50.5 20.0 %collective-permute-start.14 = (bf16[64,4864]{1,0:T(8,128)(2,1)S(1)}, bf16[64,4864]{1,0:T(8,128)(2,1)S(1)}, u32[]{:S(2)}, u32[]{:S(2)}) collective-permute-start(bf16[64,4864]{1,0:T(8,128)(2,1)S(1)} %get-tuple-element.153), channel_id=1, source_target_pairs={{0,3},{1,2},{2,1},{3,0},{4,7},{5,6},{6,5},{7,4},{8,11},{9,10},{10,... | collective-permute-start | bytes 1867784 | tf_op jit(solution)/shard_map/ppermute | solution.py:326
  51.8 19.5 %collective-permute-start.11 = (bf16[64,4864]{1,0:T(8,128)(2,1)S(1)}, bf16[64,4864]{1,0:T(8,128)(2,1)S(1)}, u32[]{:S(2)}, u32[]{:S(2)}) collective-permute-start(bf16[64,4864]{1,0:T(8,128)(2,1)S(1)} %pad_maximum_fusion.1), channel_id=1, source_target_pairs={{0,8},{4,12},{8,0},{12,4},{16,24},{20,28},{24,16},{28,20},{1,9},{5... | collective-permute-start | bytes 1867784 | tf_op jit(solution)/shard_map/ppermute | solution.py:329
  53.4 16.5 %collective-permute-start.12 = (bf16[32,4864]{1,0:T(8,128)(2,1)S(1)}, bf16[32,4864]{1,0:T(8,128)(2,1)S(1)}, u32[]{:S(2)}, u32[]{:S(2)}) collective-permute-start(bf16[32,4864]{1,0:T(8,128)(2,1)S(1)} %get-tuple-element.151), channel_id=1, source_target_pairs={{0,1},{1,0},{2,3},{3,2},{4,5},{5,4},{6,7},{7,6},{8,9},{9,8},{10,11... | collective-permute-start | bytes 933896 | tf_op jit(solution)/shard_map/ppermute | solution.py:326
  54.2 15.7 %collective-permute-start.13 = (bf16[32,4864]{1,0:T(8,128)(2,1)S(1)}, bf16[32,4864]{1,0:T(8,128)(2,1)S(1)}, u32[]{:S(2)}, u32[]{:S(2)}) collective-permute-start(bf16[32,4864]{1,0:T(8,128)(2,1)S(1)} %get-tuple-element.152), channel_id=1, source_target_pairs={{0,2},{1,3},{2,0},{3,1},{4,6},{5,7},{6,4},{7,5},{8,10},{9,11},{10,... | collective-permute-start | bytes 933896 | tf_op jit(solution)/shard_map/ppermute | solution.py:326
  55.7 14.7 %collective-permute-start.10 = (bf16[32,4864]{1,0:T(8,128)(2,1)S(1)}, bf16[32,4864]{1,0:T(8,128)(2,1)S(1)}, u32[]{:S(2)}, u32[]{:S(2)}) collective-permute-start(bf16[32,4864]{1,0:T(8,128)(2,1)S(1)} %copy-done.1), channel_id=1, source_target_pairs={{0,16},{4,20},{8,24},{12,28},{16,0},{20,4},{24,8},{28,12},{1,17},{... | collective-permute-start | bytes 933896 | tf_op jit(solution)/shard_map/ppermute | solution.py:329
  69.9 4.6 %copy-start.16 = (bf16[32,4864]{1,0:T(8,128)(2,1)}, bf16[32,4864]{1,0:T(8,128)(2,1)S(1)}, u32[]{:S(2)}) copy-start(bf16[32,4864]{1,0:T(8,128)(2,1)S(1)} %collective-permute-done.12.refs_5_) | copy-start | bytes 933892
  70.0 4.5 %copy-start.17 = (bf16[32,4864]{1,0:T(8,128)(2,1)}, bf16[32,4864]{1,0:T(8,128)(2,1)S(1)}, u32[]{:S(2)}) copy-start(bf16[32,4864]{1,0:T(8,128)(2,1)S(1)} %collective-permute-done.13.refs_6_) | copy-start | bytes 933892
  70.4 4.1 %copy-start.9 = (bf16[64,4864]{1,0:T(8,128)(2,1)}, bf16[64,4864]{1,0:T(8,128)(2,1)S(1)}, u32[]{:S(2)}) copy-start(bf16[64,4864]{1,0:T(8,128)(2,1)S(1)} %collective-permute-done.14.refs_7_.refs_3_) | copy-start | bytes 1867780
  71.3 8.8 %collective-permute-start.23 = (bf16[64,4864]{1,0:T(8,128)(2,1)S(1)}, bf16[64,4864]{1,0:T(8,128)(2,1)S(1)}, u32[]{:S(2)}, u32[]{:S(2)}) collective-permute-start(bf16[64,4864]{1,0:T(8,128)(2,1)S(1)} %collective-permute-done.14.refs_7_.refs_3_), channel_id=1, source_target_pairs={{0,4},{4,0},{8,12},{12,8},{16,20},{20,16},{24,28},{28,24},{1,5},{5... | collective-permute-start | bytes 1867784 | tf_op jit(solution)/shard_map/ppermute | solution.py:332
  71.3 3.2 %collective-permute-start.20 = (bf16[32,4864]{1,0:T(8,128)(2,1)S(1)}, bf16[32,4864]{1,0:T(8,128)(2,1)S(1)}, u32[]{:S(2)}, u32[]{:S(2)}) collective-permute-start(bf16[32,4864]{1,0:T(8,128)(2,1)S(1)} %get-tuple-element.170.refs_4_), channel_id=1, source_target_pairs={{0,4},{4,0},{8,12},{12,8},{16,20},{20,16},{24,28},{28,24},{1,5},{5... | collective-permute-start | bytes 933896 | tf_op jit(solution)/shard_map/ppermute | solution.py:332
  71.9 3.4 %collective-permute-start.21 = (bf16[32,4864]{1,0:T(8,128)(2,1)S(1)}, bf16[32,4864]{1,0:T(8,128)(2,1)S(1)}, u32[]{:S(2)}, u32[]{:S(2)}) collective-permute-start(bf16[32,4864]{1,0:T(8,128)(2,1)S(1)} %collective-permute-done.12.refs_5_), channel_id=1, source_target_pairs={{0,4},{4,0},{8,12},{12,8},{16,20},{20,16},{24,28},{28,24},{1,5},{5... | collective-permute-start | bytes 933896 | tf_op jit(solution)/shard_map/ppermute | solution.py:332
  71.9 6.9 %collective-permute-start.22 = (bf16[32,4864]{1,0:T(8,128)(2,1)S(1)}, bf16[32,4864]{1,0:T(8,128)(2,1)S(1)}, u32[]{:S(2)}, u32[]{:S(2)}) collective-permute-start(bf16[32,4864]{1,0:T(8,128)(2,1)S(1)} %collective-permute-done.13.refs_6_), channel_id=1, source_target_pairs={{0,4},{4,0},{8,12},{12,8},{16,20},{20,16},{24,28},{28,24},{1,5},{5... | collective-permute-start | bytes 933896 | tf_op jit(solution)/shard_map/ppermute | solution.py:332
  73.3 25.4 %collective-permute-start.17 = (bf16[64,4864]{1,0:T(8,128)(2,1)S(1)}, bf16[64,4864]{1,0:T(8,128)(2,1)S(1)}, u32[]{:S(2)}, u32[]{:S(2)}) collective-permute-start(bf16[64,4864]{1,0:T(8,128)(2,1)S(1)} %get-tuple-element.175), channel_id=1, source_target_pairs={{0,1},{1,0},{2,3},{3,2},{4,5},{5,4},{6,7},{7,6},{8,9},{9,8},{10,11... | collective-permute-start | bytes 1867784 | tf_op jit(solution)/shard_map/ppermute | solution.py:326
  74.5 6.4 %copy-start.18 = (bf16[32,4864]{1,0:T(8,128)(2,1)}, bf16[32,4864]{1,0:T(8,128)(2,1)S(1)}, u32[]{:S(2)}) copy-start(bf16[32,4864]{1,0:T(8,128)(2,1)S(1)} %collective-permute-done.20.refs_8_) | copy-start | bytes 933892
  74.5 24.2 %collective-permute-start.18 = (bf16[64,4864]{1,0:T(8,128)(2,1)S(1)}, bf16[64,4864]{1,0:T(8,128)(2,1)S(1)}, u32[]{:S(2)}, u32[]{:S(2)}) collective-permute-start(bf16[64,4864]{1,0:T(8,128)(2,1)S(1)} %get-tuple-element.176), channel_id=1, source_target_pairs={{0,2},{1,3},{2,0},{3,1},{4,6},{5,7},{6,4},{7,5},{8,10},{9,11},{10,... | collective-permute-start | bytes 1867784 | tf_op jit(solution)/shard_map/ppermute | solution.py:326
  75.3 3.5 %copy-start.19 = (bf16[32,4864]{1,0:T(8,128)(2,1)}, bf16[32,4864]{1,0:T(8,128)(2,1)S(1)}, u32[]{:S(2)}) copy-start(bf16[32,4864]{1,0:T(8,128)(2,1)S(1)} %collective-permute-done.21.refs_9_) | copy-start | bytes 933892
  75.3 24.2 %collective-permute-start.16 = (bf16[64,4864]{1,0:T(8,128)(2,1)S(1)}, bf16[64,4864]{1,0:T(8,128)(2,1)S(1)}, u32[]{:S(2)}, u32[]{:S(2)}) collective-permute-start(bf16[64,4864]{1,0:T(8,128)(2,1)S(1)} %pad_maximum_fusion.2), channel_id=1, source_target_pairs={{0,8},{4,12},{8,0},{12,4},{16,24},{20,28},{24,16},{28,20},{1,9},{5... | collective-permute-start | bytes 1867784 | tf_op jit(solution)/shard_map/ppermute | solution.py:329
  78.8 1.4 copy-start.20
  78.8 18.1 %collective-permute-start.19 = (bf16[32,4864]{1,0:T(8,128)(2,1)S(1)}, bf16[32,4864]{1,0:T(8,128)(2,1)S(1)}, u32[]{:S(2)}, u32[]{:S(2)}) collective-permute-start(bf16[32,4864]{1,0:T(8,128)(2,1)S(1)} %get-tuple-element.177), channel_id=1, source_target_pairs={{0,3},{1,2},{2,1},{3,0},{4,7},{5,6},{6,5},{7,4},{8,11},{9,10},{10,... | collective-permute-start | bytes 933896 | tf_op jit(solution)/shard_map/ppermute | solution.py:326
  80.2 0.8 copy-start.11
  80.2 18.6 %collective-permute-start.15 = (bf16[32,4864]{1,0:T(8,128)(2,1)S(1)}, bf16[32,4864]{1,0:T(8,128)(2,1)S(1)}, u32[]{:S(2)}, u32[]{:S(2)}) collective-permute-start(bf16[32,4864]{1,0:T(8,128)(2,1)S(1)} %copy-done), channel_id=1, source_target_pairs={{0,16},{4,20},{8,24},{12,28},{16,0},{20,4},{24,8},{28,12},{1,17},{... | collective-permute-start | bytes 933896 | tf_op jit(solution)/shard_map/ppermute | solution.py:329
  98.8 7.6 %copy-start.6 = (bf16[64,4864]{1,0:T(8,128)(2,1)}, bf16[64,4864]{1,0:T(8,128)(2,1)S(1)}, u32[]{:S(2)}) copy-start(bf16[64,4864]{1,0:T(8,128)(2,1)S(1)} %collective-permute-done.17.refs_5_.refs_1_) | copy-start | bytes 1867780
  98.8 7.6 %copy-start.7 = (bf16[64,4864]{1,0:T(8,128)(2,1)}, bf16[64,4864]{1,0:T(8,128)(2,1)S(1)}, u32[]{:S(2)}) copy-start(bf16[64,4864]{1,0:T(8,128)(2,1)S(1)} %collective-permute-done.18.refs_6_.refs_2_) | copy-start | bytes 1867780
  99.5 5.3 %collective-permute-start.29 = (bf16[64,4864]{1,0:T(8,128)(2,1)S(1)}, bf16[64,4864]{1,0:T(8,128)(2,1)S(1)}, u32[]{:S(2)}, u32[]{:S(2)}) collective-permute-start(bf16[64,4864]{1,0:T(8,128)(2,1)S(1)} %collective-permute-done.17.refs_5_.refs_1_), channel_id=1, source_target_pairs={{0,4},{4,0},{8,12},{12,8},{16,20},{20,16},{24,28},{28,24},{1,5},{5... | collective-permute-start | bytes 1867784 | tf_op jit(solution)/shard_map/ppermute | solution.py:332
  99.5 6.9 %collective-permute-start.30 = (bf16[64,4864]{1,0:T(8,128)(2,1)S(1)}, bf16[64,4864]{1,0:T(8,128)(2,1)S(1)}, u32[]{:S(2)}, u32[]{:S(2)}) collective-permute-start(bf16[64,4864]{1,0:T(8,128)(2,1)S(1)} %collective-permute-done.18.refs_6_.refs_2_), channel_id=1, source_target_pairs={{0,4},{4,0},{8,12},{12,8},{16,20},{20,16},{24,28},{28,24},{1,5},{5... | collective-permute-start | bytes 1867784 | tf_op jit(solution)/shard_map/ppermute | solution.py:332
  100.0 2.9 %collective-permute-start.28 = (bf16[32,4864]{1,0:T(8,128)(2,1)S(1)}, bf16[32,4864]{1,0:T(8,128)(2,1)S(1)}, u32[]{:S(2)}, u32[]{:S(2)}) collective-permute-start(bf16[32,4864]{1,0:T(8,128)(2,1)S(1)} %get-tuple-element.191.refs_4_), channel_id=1, source_target_pairs={{0,4},{4,0},{8,12},{12,8},{16,20},{20,16},{24,28},{28,24},{1,5},{5... | collective-permute-start | bytes 933896 | tf_op jit(solution)/shard_map/ppermute | solution.py:332
  100.0 4.3 %collective-permute-start.31 = (bf16[32,4864]{1,0:T(8,128)(2,1)S(1)}, bf16[32,4864]{1,0:T(8,128)(2,1)S(1)}, u32[]{:S(2)}, u32[]{:S(2)}) collective-permute-start(bf16[32,4864]{1,0:T(8,128)(2,1)S(1)} %collective-permute-done.19.refs_7_), channel_id=1, source_target_pairs={{0,4},{4,0},{8,12},{12,8},{16,20},{20,16},{24,28},{28,24},{1,5},{5... | collective-permute-start | bytes 933896 | tf_op jit(solution)/shard_map/ppermute | solution.py:332
  101.3 23.6 %collective-permute-start.27 = (bf16[64,4864]{1,0:T(8,128)(2,1)S(1)}, bf16[64,4864]{1,0:T(8,128)(2,1)S(1)}, u32[]{:S(2)}, u32[]{:S(2)}) collective-permute-start(bf16[64,4864]{1,0:T(8,128)(2,1)S(1)} %get-tuple-element.198), channel_id=1, source_target_pairs={{0,3},{1,2},{2,1},{3,0},{4,7},{5,6},{6,5},{7,4},{8,11},{9,10},{10,... | collective-permute-start | bytes 1867784 | tf_op jit(solution)/shard_map/ppermute | solution.py:326
  102.9 21.3 %collective-permute-start.25 = (bf16[32,4864]{1,0:T(8,128)(2,1)S(1)}, bf16[32,4864]{1,0:T(8,128)(2,1)S(1)}, u32[]{:S(2)}, u32[]{:S(2)}) collective-permute-start(bf16[32,4864]{1,0:T(8,128)(2,1)S(1)} %get-tuple-element.196), channel_id=1, source_target_pairs={{0,1},{1,0},{2,3},{3,2},{4,5},{5,4},{6,7},{7,6},{8,9},{9,8},{10,11... | collective-permute-start | bytes 933896 | tf_op jit(solution)/shard_map/ppermute | solution.py:326
  104.3 20.6 %collective-permute-start.26 = (bf16[32,4864]{1,0:T(8,128)(2,1)S(1)}, bf16[32,4864]{1,0:T(8,128)(2,1)S(1)}, u32[]{:S(2)}, u32[]{:S(2)}) collective-permute-start(bf16[32,4864]{1,0:T(8,128)(2,1)S(1)} %get-tuple-element.197), channel_id=1, source_target_pairs={{0,2},{1,3},{2,0},{3,1},{4,6},{5,7},{6,4},{7,5},{8,10},{9,11},{10,... | collective-permute-start | bytes 933896 | tf_op jit(solution)/shard_map/ppermute | solution.py:326
  104.9 1.5 copy-start.13
  104.9 20.0 %collective-permute-start.24 = (bf16[32,4864]{1,0:T(8,128)(2,1)S(1)}, bf16[32,4864]{1,0:T(8,128)(2,1)S(1)}, u32[]{:S(2)}, u32[]{:S(2)}) collective-permute-start(bf16[32,4864]{1,0:T(8,128)(2,1)S(1)} %collective-permute-done.15.refs_2_), channel_id=1, source_target_pairs={{0,8},{4,12},{8,0},{12,4},{16,24},{20,28},{24,16},{28,20},{1,9},{5... | collective-permute-start | bytes 933896 | tf_op jit(solution)/shard_map/ppermute | solution.py:329
  106.4 0.9 copy-start.14
  124.9 5.6 %copy-start.8 = (bf16[64,4864]{1,0:T(8,128)(2,1)}, bf16[64,4864]{1,0:T(8,128)(2,1)S(1)}, u32[]{:S(2)}) copy-start(bf16[64,4864]{1,0:T(8,128)(2,1)S(1)} %collective-permute-done.27.refs_7_.refs_3_) | copy-start | bytes 1867780
  124.9 5.6 %collective-permute-start.38 = (bf16[64,4864]{1,0:T(8,128)(2,1)S(1)}, bf16[64,4864]{1,0:T(8,128)(2,1)S(1)}, u32[]{:S(2)}, u32[]{:S(2)}) collective-permute-start(bf16[64,4864]{1,0:T(8,128)(2,1)S(1)} %collective-permute-done.27.refs_7_.refs_3_), channel_id=1, source_target_pairs={{0,4},{4,0},{8,12},{12,8},{16,20},{20,16},{24,28},{28,24},{1,5},{5... | collective-permute-start | bytes 1867784 | tf_op jit(solution)/shard_map/ppermute | solution.py:332
  125.0 3.4 %collective-permute-start.35 = (bf16[32,4864]{1,0:T(8,128)(2,1)S(1)}, bf16[32,4864]{1,0:T(8,128)(2,1)S(1)}, u32[]{:S(2)}, u32[]{:S(2)}) collective-permute-start(bf16[32,4864]{1,0:T(8,128)(2,1)S(1)} %get-tuple-element.212.refs_4_), channel_id=1, source_target_pairs={{0,4},{4,0},{8,12},{12,8},{16,20},{20,16},{24,28},{28,24},{1,5},{5... | collective-permute-start | bytes 933896 | tf_op jit(solution)/shard_map/ppermute | solution.py:332
  125.4 3.6 %collective-permute-start.36 = (bf16[32,4864]{1,0:T(8,128)(2,1)S(1)}, bf16[32,4864]{1,0:T(8,128)(2,1)S(1)}, u32[]{:S(2)}, u32[]{:S(2)}) collective-permute-start(bf16[32,4864]{1,0:T(8,128)(2,1)S(1)} %collective-permute-done.25.refs_5_), channel_id=1, source_target_pairs={{0,4},{4,0},{8,12},{12,8},{16,20},{20,16},{24,28},{28,24},{1,5},{5... | collective-permute-start | bytes 933896 | tf_op jit(solution)/shard_map/ppermute | solution.py:332
  125.5 5.0 %collective-permute-start.37 = (bf16[32,4864]{1,0:T(8,128)(2,1)S(1)}, bf16[32,4864]{1,0:T(8,128)(2,1)S(1)}, u32[]{:S(2)}, u32[]{:S(2)}) collective-permute-start(bf16[32,4864]{1,0:T(8,128)(2,1)S(1)} %collective-permute-done.26.refs_6_), channel_id=1, source_target_pairs={{0,4},{4,0},{8,12},{12,8},{16,20},{20,16},{24,28},{28,24},{1,5},{5... | collective-permute-start | bytes 933896 | tf_op jit(solution)/shard_map/ppermute | solution.py:332
  126.9 20.9 %collective-permute-start.32 = (bf16[32,4864]{1,0:T(8,128)(2,1)S(1)}, bf16[32,4864]{1,0:T(8,128)(2,1)S(1)}, u32[]{:S(2)}, u32[]{:S(2)}) collective-permute-start(bf16[32,4864]{1,0:T(8,128)(2,1)S(1)} %get-tuple-element.217), channel_id=1, source_target_pairs={{0,1},{1,0},{2,3},{3,2},{4,5},{5,4},{6,7},{7,6},{8,9},{9,8},{10,11... | collective-permute-start | bytes 933896 | tf_op jit(solution)/shard_map/ppermute | solution.py:326
  128.4 19.4 %collective-permute-start.33 = (bf16[32,4864]{1,0:T(8,128)(2,1)S(1)}, bf16[32,4864]{1,0:T(8,128)(2,1)S(1)}, u32[]{:S(2)}, u32[]{:S(2)}) collective-permute-start(bf16[32,4864]{1,0:T(8,128)(2,1)S(1)} %get-tuple-element.218), channel_id=1, source_target_pairs={{0,2},{1,3},{2,0},{3,1},{4,6},{5,7},{6,4},{7,5},{8,10},{9,11},{10,... | collective-permute-start | bytes 933896 | tf_op jit(solution)/shard_map/ppermute | solution.py:326
  129.0 21.8 %copy-start.5 = (s32[128,256]{1,0:T(8,128)S(1)}, s32[128,256]{1,0:T(8,128)}, u32[]{:S(2)}) copy-start(s32[128,256]{1,0:T(8,128)} %refs_13_.1) | copy-start | bytes 393220
  129.0 18.8 %collective-permute-start.34 = (bf16[32,4864]{1,0:T(8,128)(2,1)S(1)}, bf16[32,4864]{1,0:T(8,128)(2,1)S(1)}, u32[]{:S(2)}, u32[]{:S(2)}) collective-permute-start(bf16[32,4864]{1,0:T(8,128)(2,1)S(1)} %get-tuple-element.219), channel_id=1, source_target_pairs={{0,3},{1,2},{2,1},{3,0},{4,7},{5,6},{6,5},{7,4},{8,11},{9,10},{10,... | collective-permute-start | bytes 933896 | tf_op jit(solution)/shard_map/ppermute | solution.py:326
  130.5 0.9 copy-start.12
  147.8 1.7 collective-permute-start.39
  147.9 2.0 %collective-permute-start.40 = (bf16[32,4864]{1,0:T(8,128)(2,1)S(1)}, bf16[32,4864]{1,0:T(8,128)(2,1)S(1)}, u32[]{:S(2)}, u32[]{:S(2)}) collective-permute-start(bf16[32,4864]{1,0:T(8,128)(2,1)S(1)} %collective-permute-done.32.refs_5_), channel_id=1, source_target_pairs={{0,4},{4,0},{8,12},{12,8},{16,20},{20,16},{24,28},{28,24},{1,5},{5... | collective-permute-start | bytes 933896 | tf_op jit(solution)/shard_map/ppermute | solution.py:332
  148.4 2.0 %collective-permute-start.41 = (bf16[32,4864]{1,0:T(8,128)(2,1)S(1)}, bf16[32,4864]{1,0:T(8,128)(2,1)S(1)}, u32[]{:S(2)}, u32[]{:S(2)}) collective-permute-start(bf16[32,4864]{1,0:T(8,128)(2,1)S(1)} %collective-permute-done.33.refs_6_), channel_id=1, source_target_pairs={{0,4},{4,0},{8,12},{12,8},{16,20},{20,16},{24,28},{28,24},{1,5},{5... | collective-permute-start | bytes 933896 | tf_op jit(solution)/shard_map/ppermute | solution.py:332
  148.5 2.4 %collective-permute-start.42 = (bf16[32,4864]{1,0:T(8,128)(2,1)S(1)}, bf16[32,4864]{1,0:T(8,128)(2,1)S(1)}, u32[]{:S(2)}, u32[]{:S(2)}) collective-permute-start(bf16[32,4864]{1,0:T(8,128)(2,1)S(1)} %collective-permute-done.34.refs_7_), channel_id=1, source_target_pairs={{0,4},{4,0},{8,12},{12,8},{16,20},{20,16},{24,28},{28,24},{1,5},{5... | collective-permute-start | bytes 933896 | tf_op jit(solution)/shard_map/ppermute | solution.py:332

commit v7 on v6

--- a/solution.py
+++ b/solution.py
@@ -335,19 +335,19 @@
     half = count // 2
     starts = [u * length for u in range(count)]
     units = list(whiten(traces, fir_taps, seg_flags, [[0]]))
-    several = [starts[1 : half + 1], starts[half:]]
-    *rest, middle, late = whiten(traces, fir_taps, seg_flags, [[start] for start in starts[1:]] + several)
-    units += rest
+    gathered = rows % 16 > 0
+    several = [starts[1 : half + 1]] + ([starts[half:]] if gathered else [])
+    outs = whiten(traces, fir_taps, seg_flags, [[start] for start in starts[1:]] + several)
+    units, several = units + list(outs[: count - 1]), outs[count - 1 :]
     window = units[0].shape[1]
 
     direct = [k for k in range(1, seg_count) if k & (k - 1) == 0][::-1]
     passed = [k for k in range(1, seg_count) if k & (k - 1)]
-    gathered = rows % 16 > 0
     place.append(jnp.zeros((1,), jnp.int32) if gathered else partner)
     place = jnp.concatenate(place).astype(jnp.int32)
 
     state = {("unit", u): unit for u, unit in enumerate(units)}
-    state["middle"], state["late"] = middle, late
+    state.update(zip(("middle", "late"), several))
     state["place"], state["route_place"] = place, route_place
     lines = [{0: (("unit", u), 0)} for u in range(count)]
 

time: 168 us -> 168 us (level)
  no operation moved by 1% of the time
where the time goes in v7:
time: 168 us
  Pallas kernels  81 us (48%)
  waiting for transfers between devices  44.3 us (26%)
  starting transfers between devices  39.1 us (23%)
  local copies, waits for them, and re-layouts  1.91 us (1%)
    pallas_call x4, Pallas kernels, correlate(): pl.pallas_call(functools.partial(correlate_kernel, begins, left_rows, pie...  65.7 us
    ppermute x18, waiting for transfers between devices, to_seg(): return lax.ppermute(value, 'seg', [(i, i ^ k) for i in range(seg_count)])  22.3 us
    ppermute x18, starting transfers between devices, to_seg(): return lax.ppermute(value, 'seg', [(i, i ^ k) for i in range(seg_count)])  20.2 us
    ppermute x9, waiting for transfers between devices, to_plane(): lax.ppermute(value, 'stn', [(i, i ^ k * sides) for i in range(stn_count)])  19.7 us
    ppermute x9, starting transfers between devices, to_plane(): lax.ppermute(value, 'stn', [(i, i ^ k * sides) for i in range(stn_count)])  14.7 us
    pallas_call x2, Pallas kernels, whiten(): pl.pallas_call(functools.partial(whiten_kernel, record_len // LANES, firs...  11.9 us
    ppermute x16, starting transfers between devices, to_side(): return lax.ppermute(value, 'stn', [(i, i ^ j) for i in range(stn_count)])  4.2 us
    pallas_call x4, Pallas kernels, route(): pl.pallas_call(functools.partial(route_kernel, len(parts)), grid=(1,), in...  3.39 us
  transfers between devices with their start and end apart: 43, of which 19 were waited for; matrix products, arithmetic and copies ran while one was open for 0% of the time, Pallas kernels for 35%

profile of v7, /device:TPU:0, one launch (start us, length us, event | category | flops | bytes accessed | tf_op | source)
XLA Modules:
  0.0 168.0 jit_solution(10916749616436261372)
XLA Ops:
  0.0 3.9 %whiten.2.refs_0_ = bf16[32,4864]{1,0:T(8,128)(2,1)} custom-call(f32[31]{0:T(128)} %taps_ref.3, f32[32,19200]{1,0:T(8,128)} %traces_ref.3, s32[32,32]{1,0:T(8,128)} %flags_ref.3), custom_call_target="tpu_custom_call" | custom-call | tf_op jit(solution)/shard_map/whiten/pallas_call | solution.py:127
  3.9 4.0 %collective-permute-start = (bf16[32,4864]{1,0:T(8,128)(2,1)}, bf16[32,4864]{1,0:T(8,128)(2,1)S(1)}, u32[]{:S(2)}, u32[]{:S(2)}) collective-permute-start(bf16[32,4864]{1,0:T(8,128)(2,1)} %whiten.2.refs_0_), channel_id=1, source_target_pairs={{0,16},{4,20},{8,24},{12,28},{16,0},{20,4},{24,8},{28,12},{1,17},{... | collective-permute-start | bytes 933896 | tf_op jit(solution)/shard_map/ppermute | solution.py:329
  8.0 1.6 collective-permute-start.1
  9.5 1.5 collective-permute-start.2
  11.0 1.5 collective-permute-start.3
  12.6 0.5 collective-permute-start.4
  13.0 7.9 %whiten.3 = (bf16[32,4864]{1,0:T(8,128)(2,1)}, bf16[32,4864]{1,0:T(8,128)(2,1)}, bf16[32,4864]{1,0:T(8,128)(2,1)}, bf16[32,9728]{1,0:T(8,128)(2,1)}) custom-call(f32[31]{0:T(128)} %taps_ref.3, f32[32,19200]{1,0:T(8,128)} %traces_ref.3, s32[32,32]{1,0:T(8,128)} %flags_ref.3), custom_call_target="tpu_custom_call" | custom-call | tf_op jit(solution)/shard_map/whiten/pallas_call | solution.py:127
  21.2 1.1 collective-permute-done.refs_2_
  22.5 3.7 %collective-permute-done.3.refs_2_ = bf16[32,4864]{1,0:T(8,128)(2,1)S(1)} collective-permute-done((bf16[32,4864]{1,0:T(8,128)(2,1)}, bf16[32,4864]{1,0:T(8,128)(2,1)S(1)}, u32[]{:S(2)}, u32[]{:S(2)}) %collective-permute-start.3) | collective-permute-done | bytes 311328 | tf_op jit(solution)/shard_map/ppermute | solution.py:326
  26.2 1.1 pad_maximum_fusion
  27.3 0.5 collective-permute-start.6
  27.8 1.2 collective-permute-start.7
  29.1 0.8 collective-permute-start.8
  29.9 0.7 collective-permute-start.5
  30.6 1.1 collective-permute-start.9
  31.7 14.4 %collective-permute-done.5.refs_2_ = bf16[32,4864]{1,0:T(8,128)(2,1)S(1)} collective-permute-done((bf16[32,4864]{1,0:T(8,128)(2,1)S(1)}, bf16[32,4864]{1,0:T(8,128)(2,1)S(1)}, u32[]{:S(2)}, u32[]{:S(2)}) %collective-permute-start.5) | collective-permute-done | bytes 311328 | tf_op jit(solution)/shard_map/ppermute | solution.py:329
  46.1 2.5 %collective-permute-done.9.refs_3_ = bf16[32,4864]{1,0:T(8,128)(2,1)S(1)} collective-permute-done((bf16[32,4864]{1,0:T(8,128)(2,1)S(1)}, bf16[32,4864]{1,0:T(8,128)(2,1)S(1)}, u32[]{:S(2)}, u32[]{:S(2)}) %collective-permute-start.9) | collective-permute-done | bytes 311328 | tf_op jit(solution)/shard_map/ppermute | solution.py:326
  48.6 1.1 collective-permute-done.8.refs_2_
  49.7 0.8 route.4
  50.5 1.3 collective-permute-start.14
  51.8 1.6 collective-permute-start.11
  53.4 0.8 collective-permute-start.12
  54.2 1.5 collective-permute-start.13
  55.7 0.4 collective-permute-start.10
  56.1 13.8 %collective-permute-done.12.refs_5_ = bf16[32,4864]{1,0:T(8,128)(2,1)S(1)} collective-permute-done((bf16[32,4864]{1,0:T(8,128)(2,1)S(1)}, bf16[32,4864]{1,0:T(8,128)(2,1)S(1)}, u32[]{:S(2)}, u32[]{:S(2)}) %collective-permute-start.12) | collective-permute-done | bytes 311328 | tf_op jit(solution)/shard_map/ppermute | solution.py:326
  70.0 0.5 collective-permute-done.10.refs_2_
  70.4 0.9 collective-permute-done.11.refs_3_.refs_1_
  71.3 0.5 collective-permute-start.20
  71.8 0.5 collective-permute-start.22
  72.4 0.9 route.5
  73.3 1.1 collective-permute-start.17
  74.5 0.7 collective-permute-start.18
  75.3 3.5 %collective-permute-start.16 = (bf16[64,4864]{1,0:T(8,128)(2,1)S(1)}, bf16[64,4864]{1,0:T(8,128)(2,1)S(1)}, u32[]{:S(2)}, u32[]{:S(2)}) collective-permute-start(bf16[64,4864]{1,0:T(8,128)(2,1)S(1)} %pad_maximum_fusion.2), channel_id=1, source_target_pairs={{0,8},{4,12},{8,0},{12,4},{16,24},{20,28},{24,16},{28,20},{1,9},{5... | collective-permute-start | bytes 1867784 | tf_op jit(solution)/shard_map/ppermute | solution.py:329
  78.8 1.4 collective-permute-start.19
  80.2 0.8 collective-permute-start.15
  81.0 15.8 %correlate.4.refs_12_ = bf16[3,21,128,256]{3,2,1,0:T(8,128)(2,1)} custom-call(s32[12]{0:T(128)S(1)} %concatenate.13.place_ref, bf16[32,4864]{1,0:T(8,128)(2,1)S(1)} %copy-done.3, bf16[32,4864]{1,0:T(8,128)(2,1)S(1)} %collective-permute-done.2.refs_1_, bf16[32,4864]{1,0:T(8,128)(2,1)S(1)} %collective-permute-done.3.refs_2_, bf16[32,4864]{1,0:T(8,128)(2,1)} %copy-done.15, ...), custom_call_target="tpu_custom_call" | custom-call | tf_op jit(solution)/shard_map/correlate/pallas_call | solution.py:297
  96.9 1.9 %collective-permute-done.15.refs_2_ = bf16[32,4864]{1,0:T(8,128)(2,1)S(1)} collective-permute-done((bf16[32,4864]{1,0:T(8,128)(2,1)S(1)}, bf16[32,4864]{1,0:T(8,128)(2,1)S(1)}, u32[]{:S(2)}, u32[]{:S(2)}) %collective-permute-start.15) | collective-permute-done | bytes 311328 | tf_op jit(solution)/shard_map/ppermute | solution.py:329
  98.8 0.7 collective-permute-done.16.refs_3_.refs_1_
  99.5 0.5 collective-permute-start.30
  100.0 0.5 collective-permute-start.31
  100.5 0.8 route.6
  101.3 1.3 collective-permute-start.27
  102.9 1.4 collective-permute-start.25
  104.3 0.6 collective-permute-start.26
  104.8 1.5 collective-permute-start.24
  106.4 0.8 copy-done.14
  107.3 16.4 %correlate.5.refs_12_ = bf16[3,21,128,256]{3,2,1,0:T(8,128)(2,1)} custom-call(s32[12]{0:T(128)S(1)} %concatenate.13.place_ref, bf16[32,4864]{1,0:T(8,128)(2,1)S(1)} %copy-done.2, bf16[32,9728]{1,0:T(8,128)(2,1)S(1)} %collective-permute-done.7.refs_1_, bf16[32,9728]{1,0:T(8,128)(2,1)} %copy-done.10, ...), custom_call_target="tpu_custom_call", output_to_operand_aliasing={{}: (13, {})} | custom-call | tf_op jit(solution)/shard_map/correlate/pallas_call | solution.py:297
  123.7 0.5 collective-permute-done.25.refs_5_
  124.2 0.7 collective-permute-done.26.refs_6_
  124.9 0.5 collective-permute-start.35
  125.5 0.4 collective-permute-start.37
  126.0 1.0 route.7
  126.9 1.5 collective-permute-start.32
  128.4 0.6 collective-permute-start.33
  129.0 1.5 collective-permute-start.34
  130.5 0.8 copy-done.12
  131.3 16.4 %correlate.6.refs_12_ = bf16[3,21,128,256]{3,2,1,0:T(8,128)(2,1)} custom-call(s32[12]{0:T(128)S(1)} %concatenate.13.place_ref, bf16[32,4864]{1,0:T(8,128)(2,1)S(1)} %copy-done.1, bf16[32,9728]{1,0:T(8,128)(2,1)S(1)} %collective-permute-done.7.refs_1_, bf16[32,9728]{1,0:T(8,128)(2,1)} %copy-done.10, ...), custom_call_target="tpu_custom_call", output_to_operand_aliasing={{}: (13, {})} | custom-call | tf_op jit(solution)/shard_map/correlate/pallas_call | solution.py:297
  147.9 0.5 collective-permute-start.40
  148.5 0.4 collective-permute-start.42
  148.9 0.6 collective-permute-done.39.refs_8_
  149.5 0.4 collective-permute-done.40.refs_9_
  149.9 0.4 collective-permute-done.41.refs_10_
  150.4 0.4 collective-permute-done.42.refs_11_
  150.8 17.0 %correlate.7 = f32[41,128,256]{2,1,0:T(8,128)} custom-call(s32[12]{0:T(128)S(1)} %concatenate.13.place_ref, bf16[32,4864]{1,0:T(8,128)(2,1)S(1)} %copy-done, bf16[64,4864]{1,0:T(8,128)(2,1)} %copy-done.6, bf16[64,4864]{1,0:T(8,128)(2,1)} %copy-done.7, bf16[64,4864]{1,0:T(8,128)(2,1)} %copy-done.8, bf16[32,4864]{1,0:T(8,128)(2,1)S(1)} %get-tuple-element.226.refs_4_, ...), custom_call_target="tpu_custom_call" | custom-call | tf_op jit(solution)/shard_map/correlate/pallas_call | solution.py:297
  (80 shorter events, 1.4 us)
Async XLA Ops:
  3.9 18.4 %collective-permute-start = (bf16[32,4864]{1,0:T(8,128)(2,1)}, bf16[32,4864]{1,0:T(8,128)(2,1)S(1)}, u32[]{:S(2)}, u32[]{:S(2)}) collective-permute-start(bf16[32,4864]{1,0:T(8,128)(2,1)} %whiten.2.refs_0_), channel_id=1, source_target_pairs={{0,16},{4,20},{8,24},{12,28},{16,0},{20,4},{24,8},{28,12},{1,17},{... | collective-permute-start | bytes 933896 | tf_op jit(solution)/shard_map/ppermute | solution.py:329
  8.0 14.5 %collective-permute-start.1 = (bf16[32,4864]{1,0:T(8,128)(2,1)}, bf16[32,4864]{1,0:T(8,128)(2,1)S(1)}, u32[]{:S(2)}, u32[]{:S(2)}) collective-permute-start(bf16[32,4864]{1,0:T(8,128)(2,1)} %whiten.2.refs_0_), channel_id=1, source_target_pairs={{0,8},{4,12},{8,0},{12,4},{16,24},{20,28},{24,16},{28,20},{1,9},{5... | collective-permute-start | bytes 933896 | tf_op jit(solution)/shard_map/ppermute | solution.py:329
  9.5 13.0 %collective-permute-start.2 = (bf16[32,4864]{1,0:T(8,128)(2,1)}, bf16[32,4864]{1,0:T(8,128)(2,1)S(1)}, u32[]{:S(2)}, u32[]{:S(2)}) collective-permute-start(bf16[32,4864]{1,0:T(8,128)(2,1)} %whiten.2.refs_0_), channel_id=1, source_target_pairs={{0,1},{1,0},{2,3},{3,2},{4,5},{5,4},{6,7},{7,6},{8,9},{9,8},{10,11... | collective-permute-start | bytes 933896 | tf_op jit(solution)/shard_map/ppermute | solution.py:326
  11.0 15.1 %collective-permute-start.3 = (bf16[32,4864]{1,0:T(8,128)(2,1)}, bf16[32,4864]{1,0:T(8,128)(2,1)S(1)}, u32[]{:S(2)}, u32[]{:S(2)}) collective-permute-start(bf16[32,4864]{1,0:T(8,128)(2,1)} %whiten.2.refs_0_), channel_id=1, source_target_pairs={{0,2},{1,3},{2,0},{3,1},{4,6},{5,7},{6,4},{7,5},{8,10},{9,11},{10,... | collective-permute-start | bytes 933896 | tf_op jit(solution)/shard_map/ppermute | solution.py:326
  12.6 13.6 %collective-permute-start.4 = (bf16[32,4864]{1,0:T(8,128)(2,1)}, bf16[32,4864]{1,0:T(8,128)(2,1)S(1)}, u32[]{:S(2)}, u32[]{:S(2)}) collective-permute-start(bf16[32,4864]{1,0:T(8,128)(2,1)} %whiten.2.refs_0_), channel_id=1, source_target_pairs={{0,3},{1,2},{2,1},{3,0},{4,7},{5,6},{6,5},{7,4},{8,11},{9,10},{10,... | collective-permute-start | bytes 933896 | tf_op jit(solution)/shard_map/ppermute | solution.py:326
  21.0 8.9 %copy-start.2 = (bf16[32,4864]{1,0:T(8,128)(2,1)S(1)}, bf16[32,4864]{1,0:T(8,128)(2,1)}, u32[]{:S(2)}) copy-start(bf16[32,4864]{1,0:T(8,128)(2,1)} %get-tuple-element.178.refs_0_) | copy-start | bytes 933892
  21.0 28.7 %copy-start.1 = (bf16[32,4864]{1,0:T(8,128)(2,1)S(1)}, bf16[32,4864]{1,0:T(8,128)(2,1)}, u32[]{:S(2)}) copy-start(bf16[32,4864]{1,0:T(8,128)(2,1)} %get-tuple-element.200.refs_4_.refs_0_) | copy-start | bytes 933892
  21.0 28.7 %copy-start.3 = (bf16[32,4864]{1,0:T(8,128)(2,1)S(1)}, bf16[32,4864]{1,0:T(8,128)(2,1)}, u32[]{:S(2)}) copy-start(bf16[32,4864]{1,0:T(8,128)(2,1)} %whiten.2.refs_0_) | copy-start | bytes 933892
  26.2 1.7 copy-start.15
  27.3 45.0 %copy-start = (bf16[32,4864]{1,0:T(8,128)(2,1)S(1)}, bf16[32,4864]{1,0:T(8,128)(2,1)}, u32[]{:S(2)}) copy-start(bf16[32,4864]{1,0:T(8,128)(2,1)} %get-tuple-element.222.refs_4_.refs_0_) | copy-start | bytes 933892
  27.3 21.2 %collective-permute-start.6 = (bf16[64,4864]{1,0:T(8,128)(2,1)S(1)}, bf16[64,4864]{1,0:T(8,128)(2,1)S(1)}, u32[]{:S(2)}, u32[]{:S(2)}) collective-permute-start(bf16[64,4864]{1,0:T(8,128)(2,1)S(1)} %pad_maximum_fusion), channel_id=1, source_target_pairs={{0,8},{4,12},{8,0},{12,4},{16,24},{20,28},{24,16},{28,20},{1,9},{5... | collective-permute-start | bytes 1867784 | tf_op jit(solution)/shard_map/ppermute | solution.py:329
  27.8 20.7 %collective-permute-start.7 = (bf16[32,9728]{1,0:T(8,128)(2,1)}, bf16[32,9728]{1,0:T(8,128)(2,1)S(1)}, u32[]{:S(2)}, u32[]{:S(2)}) collective-permute-start(bf16[32,9728]{1,0:T(8,128)(2,1)} %get-tuple-element.126), channel_id=1, source_target_pairs={{0,1},{1,0},{2,3},{3,2},{4,5},{5,4},{6,7},{7,6},{8,9},{9,8},{10,11... | collective-permute-start | bytes 1867784 | tf_op jit(solution)/shard_map/ppermute | solution.py:326
  29.1 20.6 %collective-permute-start.8 = (bf16[32,9728]{1,0:T(8,128)(2,1)}, bf16[32,9728]{1,0:T(8,128)(2,1)S(1)}, u32[]{:S(2)}, u32[]{:S(2)}) collective-permute-start(bf16[32,9728]{1,0:T(8,128)(2,1)} %get-tuple-element.126), channel_id=1, source_target_pairs={{0,2},{1,3},{2,0},{3,1},{4,6},{5,7},{6,4},{7,5},{8,10},{9,11},{10,... | collective-permute-start | bytes 1867784 | tf_op jit(solution)/shard_map/ppermute | solution.py:326
  29.9 16.2 %collective-permute-start.5 = (bf16[32,4864]{1,0:T(8,128)(2,1)S(1)}, bf16[32,4864]{1,0:T(8,128)(2,1)S(1)}, u32[]{:S(2)}, u32[]{:S(2)}) collective-permute-start(bf16[32,4864]{1,0:T(8,128)(2,1)S(1)} %copy-done.2), channel_id=1, source_target_pairs={{0,16},{4,20},{8,24},{12,28},{16,0},{20,4},{24,8},{28,12},{1,17},{... | collective-permute-start | bytes 933896 | tf_op jit(solution)/shard_map/ppermute | solution.py:329
  30.6 18.0 %collective-permute-start.9 = (bf16[32,4864]{1,0:T(8,128)(2,1)S(1)}, bf16[32,4864]{1,0:T(8,128)(2,1)S(1)}, u32[]{:S(2)}, u32[]{:S(2)}) collective-permute-start(bf16[32,4864]{1,0:T(8,128)(2,1)S(1)} %copy-done.2), channel_id=1, source_target_pairs={{0,3},{1,2},{2,1},{3,0},{4,7},{5,6},{6,5},{7,4},{8,11},{9,10},{10,... | collective-permute-start | bytes 933896 | tf_op jit(solution)/shard_map/ppermute | solution.py:326
  49.7 2.1 %copy-start.10 = (bf16[32,9728]{1,0:T(8,128)(2,1)}, bf16[32,9728]{1,0:T(8,128)(2,1)S(1)}, u32[]{:S(2)}) copy-start(bf16[32,9728]{1,0:T(8,128)(2,1)S(1)} %collective-permute-done.8.refs_2_) | copy-start | bytes 1867780
  50.4 22.9 %copy-start.4 = (bf16[32,4864]{1,0:T(8,128)(2,1)}, bf16[32,4864]{1,0:T(8,128)(2,1)S(1)}, u32[]{:S(2)}) copy-start(bf16[32,4864]{1,0:T(8,128)(2,1)S(1)} %get-tuple-element.170.refs_4_) | copy-start | bytes 933892
  50.5 20.0 %collective-permute-start.14 = (bf16[64,4864]{1,0:T(8,128)(2,1)S(1)}, bf16[64,4864]{1,0:T(8,128)(2,1)S(1)}, u32[]{:S(2)}, u32[]{:S(2)}) collective-permute-start(bf16[64,4864]{1,0:T(8,128)(2,1)S(1)} %get-tuple-element.153), channel_id=1, source_target_pairs={{0,3},{1,2},{2,1},{3,0},{4,7},{5,6},{6,5},{7,4},{8,11},{9,10},{10,... | collective-permute-start | bytes 1867784 | tf_op jit(solution)/shard_map/ppermute | solution.py:326
  51.8 19.5 %collective-permute-start.11 = (bf16[64,4864]{1,0:T(8,128)(2,1)S(1)}, bf16[64,4864]{1,0:T(8,128)(2,1)S(1)}, u32[]{:S(2)}, u32[]{:S(2)}) collective-permute-start(bf16[64,4864]{1,0:T(8,128)(2,1)S(1)} %pad_maximum_fusion.1), channel_id=1, source_target_pairs={{0,8},{4,12},{8,0},{12,4},{16,24},{20,28},{24,16},{28,20},{1,9},{5... | collective-permute-start | bytes 1867784 | tf_op jit(solution)/shard_map/ppermute | solution.py:329
  53.4 16.5 %collective-permute-start.12 = (bf16[32,4864]{1,0:T(8,128)(2,1)S(1)}, bf16[32,4864]{1,0:T(8,128)(2,1)S(1)}, u32[]{:S(2)}, u32[]{:S(2)}) collective-permute-start(bf16[32,4864]{1,0:T(8,128)(2,1)S(1)} %get-tuple-element.151), channel_id=1, source_target_pairs={{0,1},{1,0},{2,3},{3,2},{4,5},{5,4},{6,7},{7,6},{8,9},{9,8},{10,11... | collective-permute-start | bytes 933896 | tf_op jit(solution)/shard_map/ppermute | solution.py:326
  54.2 15.7 %collective-permute-start.13 = (bf16[32,4864]{1,0:T(8,128)(2,1)S(1)}, bf16[32,4864]{1,0:T(8,128)(2,1)S(1)}, u32[]{:S(2)}, u32[]{:S(2)}) collective-permute-start(bf16[32,4864]{1,0:T(8,128)(2,1)S(1)} %get-tuple-element.152), channel_id=1, source_target_pairs={{0,2},{1,3},{2,0},{3,1},{4,6},{5,7},{6,4},{7,5},{8,10},{9,11},{10,... | collective-permute-start | bytes 933896 | tf_op jit(solution)/shard_map/ppermute | solution.py:326
  55.7 14.7 %collective-permute-start.10 = (bf16[32,4864]{1,0:T(8,128)(2,1)S(1)}, bf16[32,4864]{1,0:T(8,128)(2,1)S(1)}, u32[]{:S(2)}, u32[]{:S(2)}) collective-permute-start(bf16[32,4864]{1,0:T(8,128)(2,1)S(1)} %copy-done.1), channel_id=1, source_target_pairs={{0,16},{4,20},{8,24},{12,28},{16,0},{20,4},{24,8},{28,12},{1,17},{... | collective-permute-start | bytes 933896 | tf_op jit(solution)/shard_map/ppermute | solution.py:329
  69.9 4.6 %copy-start.16 = (bf16[32,4864]{1,0:T(8,128)(2,1)}, bf16[32,4864]{1,0:T(8,128)(2,1)S(1)}, u32[]{:S(2)}) copy-start(bf16[32,4864]{1,0:T(8,128)(2,1)S(1)} %collective-permute-done.12.refs_5_) | copy-start | bytes 933892
  70.0 4.5 %copy-start.17 = (bf16[32,4864]{1,0:T(8,128)(2,1)}, bf16[32,4864]{1,0:T(8,128)(2,1)S(1)}, u32[]{:S(2)}) copy-start(bf16[32,4864]{1,0:T(8,128)(2,1)S(1)} %collective-permute-done.13.refs_6_) | copy-start | bytes 933892
  70.4 4.1 %copy-start.9 = (bf16[64,4864]{1,0:T(8,128)(2,1)}, bf16[64,4864]{1,0:T(8,128)(2,1)S(1)}, u32[]{:S(2)}) copy-start(bf16[64,4864]{1,0:T(8,128)(2,1)S(1)} %collective-permute-done.14.refs_7_.refs_3_) | copy-start | bytes 1867780
  71.3 8.8 %collective-permute-start.23 = (bf16[64,4864]{1,0:T(8,128)(2,1)S(1)}, bf16[64,4864]{1,0:T(8,128)(2,1)S(1)}, u32[]{:S(2)}, u32[]{:S(2)}) collective-permute-start(bf16[64,4864]{1,0:T(8,128)(2,1)S(1)} %collective-permute-done.14.refs_7_.refs_3_), channel_id=1, source_target_pairs={{0,4},{4,0},{8,12},{12,8},{16,20},{20,16},{24,28},{28,24},{1,5},{5... | collective-permute-start | bytes 1867784 | tf_op jit(solution)/shard_map/ppermute | solution.py:332
  71.3 3.2 %collective-permute-start.20 = (bf16[32,4864]{1,0:T(8,128)(2,1)S(1)}, bf16[32,4864]{1,0:T(8,128)(2,1)S(1)}, u32[]{:S(2)}, u32[]{:S(2)}) collective-permute-start(bf16[32,4864]{1,0:T(8,128)(2,1)S(1)} %get-tuple-element.170.refs_4_), channel_id=1, source_target_pairs={{0,4},{4,0},{8,12},{12,8},{16,20},{20,16},{24,28},{28,24},{1,5},{5... | collective-permute-start | bytes 933896 | tf_op jit(solution)/shard_map/ppermute | solution.py:332
  71.8 3.4 %collective-permute-start.21 = (bf16[32,4864]{1,0:T(8,128)(2,1)S(1)}, bf16[32,4864]{1,0:T(8,128)(2,1)S(1)}, u32[]{:S(2)}, u32[]{:S(2)}) collective-permute-start(bf16[32,4864]{1,0:T(8,128)(2,1)S(1)} %collective-permute-done.12.refs_5_), channel_id=1, source_target_pairs={{0,4},{4,0},{8,12},{12,8},{16,20},{20,16},{24,28},{28,24},{1,5},{5... | collective-permute-start | bytes 933896 | tf_op jit(solution)/shard_map/ppermute | solution.py:332
  71.8 6.9 %collective-permute-start.22 = (bf16[32,4864]{1,0:T(8,128)(2,1)S(1)}, bf16[32,4864]{1,0:T(8,128)(2,1)S(1)}, u32[]{:S(2)}, u32[]{:S(2)}) collective-permute-start(bf16[32,4864]{1,0:T(8,128)(2,1)S(1)} %collective-permute-done.13.refs_6_), channel_id=1, source_target_pairs={{0,4},{4,0},{8,12},{12,8},{16,20},{20,16},{24,28},{28,24},{1,5},{5... | collective-permute-start | bytes 933896 | tf_op jit(solution)/shard_map/ppermute | solution.py:332
  73.3 25.4 %collective-permute-start.17 = (bf16[64,4864]{1,0:T(8,128)(2,1)S(1)}, bf16[64,4864]{1,0:T(8,128)(2,1)S(1)}, u32[]{:S(2)}, u32[]{:S(2)}) collective-permute-start(bf16[64,4864]{1,0:T(8,128)(2,1)S(1)} %get-tuple-element.175), channel_id=1, source_target_pairs={{0,1},{1,0},{2,3},{3,2},{4,5},{5,4},{6,7},{7,6},{8,9},{9,8},{10,11... | collective-permute-start | bytes 1867784 | tf_op jit(solution)/shard_map/ppermute | solution.py:326
  74.5 6.4 %copy-start.18 = (bf16[32,4864]{1,0:T(8,128)(2,1)}, bf16[32,4864]{1,0:T(8,128)(2,1)S(1)}, u32[]{:S(2)}) copy-start(bf16[32,4864]{1,0:T(8,128)(2,1)S(1)} %collective-permute-done.20.refs_8_) | copy-start | bytes 933892
  74.5 24.2 %collective-permute-start.18 = (bf16[64,4864]{1,0:T(8,128)(2,1)S(1)}, bf16[64,4864]{1,0:T(8,128)(2,1)S(1)}, u32[]{:S(2)}, u32[]{:S(2)}) collective-permute-start(bf16[64,4864]{1,0:T(8,128)(2,1)S(1)} %get-tuple-element.176), channel_id=1, source_target_pairs={{0,2},{1,3},{2,0},{3,1},{4,6},{5,7},{6,4},{7,5},{8,10},{9,11},{10,... | collective-permute-start | bytes 1867784 | tf_op jit(solution)/shard_map/ppermute | solution.py:326
  75.3 3.5 %copy-start.19 = (bf16[32,4864]{1,0:T(8,128)(2,1)}, bf16[32,4864]{1,0:T(8,128)(2,1)S(1)}, u32[]{:S(2)}) copy-start(bf16[32,4864]{1,0:T(8,128)(2,1)S(1)} %collective-permute-done.21.refs_9_) | copy-start | bytes 933892
  75.3 24.2 %collective-permute-start.16 = (bf16[64,4864]{1,0:T(8,128)(2,1)S(1)}, bf16[64,4864]{1,0:T(8,128)(2,1)S(1)}, u32[]{:S(2)}, u32[]{:S(2)}) collective-permute-start(bf16[64,4864]{1,0:T(8,128)(2,1)S(1)} %pad_maximum_fusion.2), channel_id=1, source_target_pairs={{0,8},{4,12},{8,0},{12,4},{16,24},{20,28},{24,16},{28,20},{1,9},{5... | collective-permute-start | bytes 1867784 | tf_op jit(solution)/shard_map/ppermute | solution.py:329
  78.8 1.4 copy-start.20
  78.8 18.1 %collective-permute-start.19 = (bf16[32,4864]{1,0:T(8,128)(2,1)S(1)}, bf16[32,4864]{1,0:T(8,128)(2,1)S(1)}, u32[]{:S(2)}, u32[]{:S(2)}) collective-permute-start(bf16[32,4864]{1,0:T(8,128)(2,1)S(1)} %get-tuple-element.177), channel_id=1, source_target_pairs={{0,3},{1,2},{2,1},{3,0},{4,7},{5,6},{6,5},{7,4},{8,11},{9,10},{10,... | collective-permute-start | bytes 933896 | tf_op jit(solution)/shard_map/ppermute | solution.py:326
  80.2 0.8 copy-start.11
  80.2 18.6 %collective-permute-start.15 = (bf16[32,4864]{1,0:T(8,128)(2,1)S(1)}, bf16[32,4864]{1,0:T(8,128)(2,1)S(1)}, u32[]{:S(2)}, u32[]{:S(2)}) collective-permute-start(bf16[32,4864]{1,0:T(8,128)(2,1)S(1)} %copy-done), channel_id=1, source_target_pairs={{0,16},{4,20},{8,24},{12,28},{16,0},{20,4},{24,8},{28,12},{1,17},{... | collective-permute-start | bytes 933896 | tf_op jit(solution)/shard_map/ppermute | solution.py:329
  98.8 7.6 %copy-start.6 = (bf16[64,4864]{1,0:T(8,128)(2,1)}, bf16[64,4864]{1,0:T(8,128)(2,1)S(1)}, u32[]{:S(2)}) copy-start(bf16[64,4864]{1,0:T(8,128)(2,1)S(1)} %collective-permute-done.17.refs_5_.refs_1_) | copy-start | bytes 1867780
  98.8 7.6 %copy-start.7 = (bf16[64,4864]{1,0:T(8,128)(2,1)}, bf16[64,4864]{1,0:T(8,128)(2,1)S(1)}, u32[]{:S(2)}) copy-start(bf16[64,4864]{1,0:T(8,128)(2,1)S(1)} %collective-permute-done.18.refs_6_.refs_2_) | copy-start | bytes 1867780
  99.5 5.3 %collective-permute-start.29 = (bf16[64,4864]{1,0:T(8,128)(2,1)S(1)}, bf16[64,4864]{1,0:T(8,128)(2,1)S(1)}, u32[]{:S(2)}, u32[]{:S(2)}) collective-permute-start(bf16[64,4864]{1,0:T(8,128)(2,1)S(1)} %collective-permute-done.17.refs_5_.refs_1_), channel_id=1, source_target_pairs={{0,4},{4,0},{8,12},{12,8},{16,20},{20,16},{24,28},{28,24},{1,5},{5... | collective-permute-start | bytes 1867784 | tf_op jit(solution)/shard_map/ppermute | solution.py:332
  99.5 6.9 %collective-permute-start.30 = (bf16[64,4864]{1,0:T(8,128)(2,1)S(1)}, bf16[64,4864]{1,0:T(8,128)(2,1)S(1)}, u32[]{:S(2)}, u32[]{:S(2)}) collective-permute-start(bf16[64,4864]{1,0:T(8,128)(2,1)S(1)} %collective-permute-done.18.refs_6_.refs_2_), channel_id=1, source_target_pairs={{0,4},{4,0},{8,12},{12,8},{16,20},{20,16},{24,28},{28,24},{1,5},{5... | collective-permute-start | bytes 1867784 | tf_op jit(solution)/shard_map/ppermute | solution.py:332
  100.0 2.9 %collective-permute-start.28 = (bf16[32,4864]{1,0:T(8,128)(2,1)S(1)}, bf16[32,4864]{1,0:T(8,128)(2,1)S(1)}, u32[]{:S(2)}, u32[]{:S(2)}) collective-permute-start(bf16[32,4864]{1,0:T(8,128)(2,1)S(1)} %get-tuple-element.191.refs_4_), channel_id=1, source_target_pairs={{0,4},{4,0},{8,12},{12,8},{16,20},{20,16},{24,28},{28,24},{1,5},{5... | collective-permute-start | bytes 933896 | tf_op jit(solution)/shard_map/ppermute | solution.py:332
  100.0 4.3 %collective-permute-start.31 = (bf16[32,4864]{1,0:T(8,128)(2,1)S(1)}, bf16[32,4864]{1,0:T(8,128)(2,1)S(1)}, u32[]{:S(2)}, u32[]{:S(2)}) collective-permute-start(bf16[32,4864]{1,0:T(8,128)(2,1)S(1)} %collective-permute-done.19.refs_7_), channel_id=1, source_target_pairs={{0,4},{4,0},{8,12},{12,8},{16,20},{20,16},{24,28},{28,24},{1,5},{5... | collective-permute-start | bytes 933896 | tf_op jit(solution)/shard_map/ppermute | solution.py:332
  101.3 23.6 %collective-permute-start.27 = (bf16[64,4864]{1,0:T(8,128)(2,1)S(1)}, bf16[64,4864]{1,0:T(8,128)(2,1)S(1)}, u32[]{:S(2)}, u32[]{:S(2)}) collective-permute-start(bf16[64,4864]{1,0:T(8,128)(2,1)S(1)} %get-tuple-element.198), channel_id=1, source_target_pairs={{0,3},{1,2},{2,1},{3,0},{4,7},{5,6},{6,5},{7,4},{8,11},{9,10},{10,... | collective-permute-start | bytes 1867784 | tf_op jit(solution)/shard_map/ppermute | solution.py:326
  102.9 21.3 %collective-permute-start.25 = (bf16[32,4864]{1,0:T(8,128)(2,1)S(1)}, bf16[32,4864]{1,0:T(8,128)(2,1)S(1)}, u32[]{:S(2)}, u32[]{:S(2)}) collective-permute-start(bf16[32,4864]{1,0:T(8,128)(2,1)S(1)} %get-tuple-element.196), channel_id=1, source_target_pairs={{0,1},{1,0},{2,3},{3,2},{4,5},{5,4},{6,7},{7,6},{8,9},{9,8},{10,11... | collective-permute-start | bytes 933896 | tf_op jit(solution)/shard_map/ppermute | solution.py:326
  104.3 20.6 %collective-permute-start.26 = (bf16[32,4864]{1,0:T(8,128)(2,1)S(1)}, bf16[32,4864]{1,0:T(8,128)(2,1)S(1)}, u32[]{:S(2)}, u32[]{:S(2)}) collective-permute-start(bf16[32,4864]{1,0:T(8,128)(2,1)S(1)} %get-tuple-element.197), channel_id=1, source_target_pairs={{0,2},{1,3},{2,0},{3,1},{4,6},{5,7},{6,4},{7,5},{8,10},{9,11},{10,... | collective-permute-start | bytes 933896 | tf_op jit(solution)/shard_map/ppermute | solution.py:326
  104.8 1.5 copy-start.13
  104.8 20.0 %collective-permute-start.24 = (bf16[32,4864]{1,0:T(8,128)(2,1)S(1)}, bf16[32,4864]{1,0:T(8,128)(2,1)S(1)}, u32[]{:S(2)}, u32[]{:S(2)}) collective-permute-start(bf16[32,4864]{1,0:T(8,128)(2,1)S(1)} %collective-permute-done.15.refs_2_), channel_id=1, source_target_pairs={{0,8},{4,12},{8,0},{12,4},{16,24},{20,28},{24,16},{28,20},{1,9},{5... | collective-permute-start | bytes 933896 | tf_op jit(solution)/shard_map/ppermute | solution.py:329
  106.4 0.9 copy-start.14
  124.9 5.6 %copy-start.8 = (bf16[64,4864]{1,0:T(8,128)(2,1)}, bf16[64,4864]{1,0:T(8,128)(2,1)S(1)}, u32[]{:S(2)}) copy-start(bf16[64,4864]{1,0:T(8,128)(2,1)S(1)} %collective-permute-done.27.refs_7_.refs_3_) | copy-start | bytes 1867780
  124.9 5.6 %collective-permute-start.38 = (bf16[64,4864]{1,0:T(8,128)(2,1)S(1)}, bf16[64,4864]{1,0:T(8,128)(2,1)S(1)}, u32[]{:S(2)}, u32[]{:S(2)}) collective-permute-start(bf16[64,4864]{1,0:T(8,128)(2,1)S(1)} %collective-permute-done.27.refs_7_.refs_3_), channel_id=1, source_target_pairs={{0,4},{4,0},{8,12},{12,8},{16,20},{20,16},{24,28},{28,24},{1,5},{5... | collective-permute-start | bytes 1867784 | tf_op jit(solution)/shard_map/ppermute | solution.py:332
  124.9 3.4 %collective-permute-start.35 = (bf16[32,4864]{1,0:T(8,128)(2,1)S(1)}, bf16[32,4864]{1,0:T(8,128)(2,1)S(1)}, u32[]{:S(2)}, u32[]{:S(2)}) collective-permute-start(bf16[32,4864]{1,0:T(8,128)(2,1)S(1)} %get-tuple-element.212.refs_4_), channel_id=1, source_target_pairs={{0,4},{4,0},{8,12},{12,8},{16,20},{20,16},{24,28},{28,24},{1,5},{5... | collective-permute-start | bytes 933896 | tf_op jit(solution)/shard_map/ppermute | solution.py:332
  125.4 3.6 %collective-permute-start.36 = (bf16[32,4864]{1,0:T(8,128)(2,1)S(1)}, bf16[32,4864]{1,0:T(8,128)(2,1)S(1)}, u32[]{:S(2)}, u32[]{:S(2)}) collective-permute-start(bf16[32,4864]{1,0:T(8,128)(2,1)S(1)} %collective-permute-done.25.refs_5_), channel_id=1, source_target_pairs={{0,4},{4,0},{8,12},{12,8},{16,20},{20,16},{24,28},{28,24},{1,5},{5... | collective-permute-start | bytes 933896 | tf_op jit(solution)/shard_map/ppermute | solution.py:332
  125.5 5.0 %collective-permute-start.37 = (bf16[32,4864]{1,0:T(8,128)(2,1)S(1)}, bf16[32,4864]{1,0:T(8,128)(2,1)S(1)}, u32[]{:S(2)}, u32[]{:S(2)}) collective-permute-start(bf16[32,4864]{1,0:T(8,128)(2,1)S(1)} %collective-permute-done.26.refs_6_), channel_id=1, source_target_pairs={{0,4},{4,0},{8,12},{12,8},{16,20},{20,16},{24,28},{28,24},{1,5},{5... | collective-permute-start | bytes 933896 | tf_op jit(solution)/shard_map/ppermute | solution.py:332
  126.9 20.9 %collective-permute-start.32 = (bf16[32,4864]{1,0:T(8,128)(2,1)S(1)}, bf16[32,4864]{1,0:T(8,128)(2,1)S(1)}, u32[]{:S(2)}, u32[]{:S(2)}) collective-permute-start(bf16[32,4864]{1,0:T(8,128)(2,1)S(1)} %get-tuple-element.217), channel_id=1, source_target_pairs={{0,1},{1,0},{2,3},{3,2},{4,5},{5,4},{6,7},{7,6},{8,9},{9,8},{10,11... | collective-permute-start | bytes 933896 | tf_op jit(solution)/shard_map/ppermute | solution.py:326
  128.4 19.4 %collective-permute-start.33 = (bf16[32,4864]{1,0:T(8,128)(2,1)S(1)}, bf16[32,4864]{1,0:T(8,128)(2,1)S(1)}, u32[]{:S(2)}, u32[]{:S(2)}) collective-permute-start(bf16[32,4864]{1,0:T(8,128)(2,1)S(1)} %get-tuple-element.218), channel_id=1, source_target_pairs={{0,2},{1,3},{2,0},{3,1},{4,6},{5,7},{6,4},{7,5},{8,10},{9,11},{10,... | collective-permute-start | bytes 933896 | tf_op jit(solution)/shard_map/ppermute | solution.py:326
  129.0 21.8 %copy-start.5 = (s32[128,256]{1,0:T(8,128)S(1)}, s32[128,256]{1,0:T(8,128)}, u32[]{:S(2)}) copy-start(s32[128,256]{1,0:T(8,128)} %refs_13_.1) | copy-start | bytes 393220
  129.0 18.8 %collective-permute-start.34 = (bf16[32,4864]{1,0:T(8,128)(2,1)S(1)}, bf16[32,4864]{1,0:T(8,128)(2,1)S(1)}, u32[]{:S(2)}, u32[]{:S(2)}) collective-permute-start(bf16[32,4864]{1,0:T(8,128)(2,1)S(1)} %get-tuple-element.219), channel_id=1, source_target_pairs={{0,3},{1,2},{2,1},{3,0},{4,7},{5,6},{6,5},{7,4},{8,11},{9,10},{10,... | collective-permute-start | bytes 933896 | tf_op jit(solution)/shard_map/ppermute | solution.py:326
  130.5 0.9 copy-start.12
  147.8 1.7 collective-permute-start.39
  147.9 2.0 %collective-permute-start.40 = (bf16[32,4864]{1,0:T(8,128)(2,1)S(1)}, bf16[32,4864]{1,0:T(8,128)(2,1)S(1)}, u32[]{:S(2)}, u32[]{:S(2)}) collective-permute-start(bf16[32,4864]{1,0:T(8,128)(2,1)S(1)} %collective-permute-done.32.refs_5_), channel_id=1, source_target_pairs={{0,4},{4,0},{8,12},{12,8},{16,20},{20,16},{24,28},{28,24},{1,5},{5... | collective-permute-start | bytes 933896 | tf_op jit(solution)/shard_map/ppermute | solution.py:332
  148.4 2.0 %collective-permute-start.41 = (bf16[32,4864]{1,0:T(8,128)(2,1)S(1)}, bf16[32,4864]{1,0:T(8,128)(2,1)S(1)}, u32[]{:S(2)}, u32[]{:S(2)}) collective-permute-start(bf16[32,4864]{1,0:T(8,128)(2,1)S(1)} %collective-permute-done.33.refs_6_), channel_id=1, source_target_pairs={{0,4},{4,0},{8,12},{12,8},{16,20},{20,16},{24,28},{28,24},{1,5},{5... | collective-permute-start | bytes 933896 | tf_op jit(solution)/shard_map/ppermute | solution.py:332
  148.5 2.4 %collective-permute-start.42 = (bf16[32,4864]{1,0:T(8,128)(2,1)S(1)}, bf16[32,4864]{1,0:T(8,128)(2,1)S(1)}, u32[]{:S(2)}, u32[]{:S(2)}) collective-permute-start(bf16[32,4864]{1,0:T(8,128)(2,1)S(1)} %collective-permute-done.34.refs_7_), channel_id=1, source_target_pairs={{0,4},{4,0},{8,12},{12,8},{16,20},{20,16},{24,28},{28,24},{1,5},{5... | collective-permute-start | bytes 933896 | tf_op jit(solution)/shard_map/ppermute | solution.py:332
